TPU v7x, 32 devices: a whole 2x2x4 slice. The times are simulated.
32 devices in a mesh: groups: 2 (over x), row: 8 (over z, y), col: 2 (over core).
Axes of the slice: x: 2, y: 2, z: 4, core: 2. Of those that a mesh axis runs over, the one named last changes fastest.
Arguments:
- gradient: bfloat16 [8192, 7168], P(('groups', 'row'), 'col'), parts along dimension 0, may hold values from -0.25 to 0.25
- left_old: float32 [8192, 4096], P(('groups', 'row'), 'col'), parts along dimension 0, may hold values from -6 to 6
- right_old: float32 [4, 3584, 3584], P(('groups', 'col'), 'row'), parts along dimension 0, may hold values from -6 to 6
- left_counts: int32 [16, 2], P(('groups', 'row'), 'col'), parts along dimension 0, may hold values from 0 to 29
- right_counts: int32 [4], P(('groups', 'col')), parts along dimension 0, may hold values from 0 to 29
Outputs:
- left_state: float32 [8192, 4096], P(('groups', 'row'), 'col'), parts along dimension 0
- left_fixed: float32 [8192, 4096], P(('groups', 'row'), 'col'), parts along dimension 0
- right_state: float32 [4, 3584, 3584], P(('groups', 'col'), 'row'), parts along dimension 0
- right_fixed: float32 [4, 3584, 3584], P(('groups', 'col'), 'row'), parts along dimension 0
There are 2 independent parts, one for each index of `groups`. A program takes and returns all parts, laid end to end along the dimension named above; each array names one. Nothing has to cross between parts.
All inputs are finite; a program needn't handle non-finite values.
Results may differ from a plain program's by a relative error of at most 0.0003.
Values may be sent and summed in bfloat16 or wider, within the bound.
No kernel may reach another device: no remote copies, remote signals or barrier semaphores. Data moves between devices by JAX's collectives and lax.ppermute only.
A program may use at most 192 MiB of HBM per device.

v0:
```python
import jax
import jax.numpy as jnp
from jax import lax
from jax.sharding import PartitionSpec as P

BETA = 0.9


def denominator(counters):
    decay_power = jnp.power(jnp.float32(BETA), (counters + 1).astype(jnp.float32))
    return 1.0 - decay_power


def strip_product(incoming, strip_at, strip_wide):
    strip_rows = lax.dynamic_slice_in_dim(incoming, strip_at, strip_wide, 1)
    return lax.dot_general(
        strip_rows, incoming, (((0,), (0,)), ((), ())), preferred_element_type=jnp.float32
    )


def row_product(gradient, incoming):
    return lax.dot_general(
        gradient, incoming, (((1,), (1,)), ((), ())), preferred_element_type=jnp.float32
    )


def local(gradient, left_old, right_old, left_counts, right_counts):
    tile_rows, half_wide = gradient.shape
    device_count = lax.axis_size("row")
    my_index = lax.axis_index("row")
    strip_wide = half_wide // device_count
    strip_at = my_index * strip_wide
    incoming = lax.all_gather(gradient, "row", axis=0, tiled=True)
    product_tile = row_product(gradient, incoming)
    right_acc = strip_product(incoming, strip_at, strip_wide)
    gram_left = lax.psum_scatter(product_tile, "col", scatter_dimension=1, tiled=True)
    left_state = BETA * left_old + (1.0 - BETA) * gram_left
    left_fixed = left_state / denominator(left_counts)
    right_state = BETA * right_old + (1.0 - BETA) * right_acc[None]
    right_fixed = right_state / denominator(right_counts)[:, None, None]
    return (left_state, left_fixed, right_state, right_fixed)


def solution(mesh):
    return jax.shard_map(
        local,
        mesh=mesh,
        in_specs=(
            P(("groups", "row"), "col"),
            P(("groups", "row"), "col"),
            P(("groups", "col"), "row", None),
            P(("groups", "row"), "col"),
            P(("groups", "col")),
        ),
        out_specs=(
            P(("groups", "row"), "col"),
            P(("groups", "row"), "col"),
            P(("groups", "col"), "row", None),
            P(("groups", "col"), "row", None),
        ),
        check_vma=False,
    )
```

profile of v0, /device:TPU:1, one launch (start us, length us, event | category | flops | bytes accessed | tf_op | source)
XLA Modules:
  0.0 636.2 jit_solution(14898300987352108242)
XLA Ops:
  7.2 0.0 all-gather.2.cloned.1.call-start
  7.2 0.7 all-gather.2.cloned.1.call-update
  7.9 0.0 reduce-scatter.2.cloned.1.call-start
  7.9 562.8 %all-gather.2.cloned.1.call-done = bf16[4096,3584]{1,0:T(8,128)(2,1)} async-done(((bf16[512,3584]{1,0:T(8,128)(2,1)}), bf16[4096,3584]{1,0:T(8,128)(2,1)}) %all-gather.2.cloned.1.call-update) | async-done | bytes 29360144 | tf_op jit(solution)/shard_map/all_gather | solution.py:33
  570.7 21.4 %fusion.2 = f32[512,4096]{1,0:T(8,128)} fusion(bf16[512,3584]{1,0:T(8,128)(2,1)} %param.5, bf16[4096,3584]{1,0:T(8,128)(2,1)} %all-gather.2.cloned.1.call-done), kind=kOutput, calls=%fused_computation.6 | convolution fusion | flops 15032385536 | bytes 41418752 | tf_op jit(solution)/shard_map/dot_general | solution.py:22
  592.1 0.0 reduce-scatter.2.cloned.1.call-update
  593.5 27.1 %broadcast_divide_fusion = (f32[1,448,3584]{2,1,0:T(8,128)}, f32[1,448,3584]{2,1,0:T(8,128)}) fusion(f32[]{:T(128)} %bitcast.2, bf16[4096,3584]{1,0:T(8,128)(2,1)} %all-gather.2.cloned.1.call-done, s32[]{:T(128)S(6)} %select_n.3, f32[1,448,3584]{2,1,0:T(8,128)} %param.7), kind=kOutput, calls=%fused_computation.3 | convolution fusion | flops 13159759872 | bytes 52822532 | tf_op jit(solution)/shard_map/dot_general | solution.py:16
  620.6 0.0 reduce-scatter.2.cloned.1.call-done
  620.6 8.8 %broadcast_divide_fusion.1 = (f32[512,2048]{1,0:T(8,128)}, f32[512,2048]{1,0:T(8,128)}) fusion(f32[]{:T(128)} %bitcast, f32[512,2048]{1,0:T(8,128)} %reduce-scatter.2.cloned.1.call-done, f32[512,2048]{1,0:T(8,128)} %param.6), kind=kLoop, calls=%fused_computation.4 | loop fusion | flops 4194304 | bytes 16777220 | tf_op jit(solution)/shard_map/div | solution.py:38
Async XLA Ops:
  7.2 563.6 %all-gather.2.cloned.1.call-start = ((), (), s32[]{:S(2)}) async-start(), calls=%async_computation.1 | async-start | bytes 33030144 | tf_op jit(solution)/shard_map/all_gather | solution.py:33
  7.9 612.7 %reduce-scatter.2.cloned.1.call-start = ((), (), s32[]{:S(2)}) async-start(), calls=%async_computation.2 | async-start | bytes 12582912 | tf_op jit(solution)/shard_map/reduce_scatter | solution.py:36
Sparse Core Ops, SparseCore 0:
  9.5 561.1 all-gather.1
  592.3 17.2 reduce-scatter.1
where the time goes:
time: 637 us; the launch traced here: 636 us
  waiting for transfers between devices  563 us (88%)
  matrix products  48.5 us (8%)
  between operations  15.4 us (2%)
  other arithmetic  8.77 us (1%)
    all_gather x1, waiting for transfers between devices, local(): incoming = lax.all_gather(gradient, 'row', axis=0, tiled=True)  563 us
    dot_general x1, matrix products, strip_product(): lax.dot_general(strip_rows, incoming, (((0,), (0,)), ((), ())), preferred...  27.1 us
    dot_general x1, matrix products, row_product(): lax.dot_general(gradient, incoming, (((1,), (1,)), ((), ())), preferred_e...  21.4 us
  transfers between devices with their start and end apart: 2, of which 1 were waited for; matrix products, arithmetic and copies ran while one was open for 4% of the time, Pallas kernels for 0%

commit v1 on v0

v1 whole, which is shorter than its diff:
```python
import jax
import jax.numpy as jnp
from jax import lax
from jax.sharding import PartitionSpec as P

BETA = 0.9


def denominator(counters):
    decay_power = jnp.power(jnp.float32(BETA), (counters + 1).astype(jnp.float32))
    return 1.0 - decay_power


def ring_order(count):
    if count == 8:
        return [0, 2, 4, 6, 7, 5, 3, 1]
    return list(range(count))


def local(gradient, left_old, right_old, left_counts, right_counts):
    tile_rows, half_wide = gradient.shape
    count = lax.axis_size("row")
    strip_wide = half_wide // count
    order = ring_order(count)
    place = {row: at for at, row in enumerate(order)}
    my_row = lax.axis_index("row")
    my_col = lax.axis_index("col")
    up = [(order[at], order[(at + 1) % count]) for at in range(count)]
    down = [(dest, source) for source, dest in up]
    piece = tile_rows // 2
    strip_at = my_row * strip_wide

    state = {"left": jnp.zeros((tile_rows, count * tile_rows), jnp.float32), "right": None}

    def consume(part, step, offset):
        sources = [order[(place[row] - step) % count] for row in range(count)]
        source = jnp.asarray(sources, jnp.int32)[my_row]
        product = lax.dot_general(
            gradient, part, (((1,), (1,)), ((), ())), preferred_element_type=jnp.float32
        )
        pairs = []
        for row in range(count):
            keeper = sources[row] * 2 // count
            pairs.append((row * 2 + 1 - keeper, row * 2 + keeper))
        other = lax.ppermute(product, ("row", "col"), pairs)
        state["left"] = lax.dynamic_update_slice(
            state["left"], product + other, (0, source * tile_rows + offset)
        )
        strip = lax.dynamic_slice_in_dim(part, strip_at, strip_wide, 1)
        term = lax.dot_general(
            strip, part, (((0,), (0,)), ((), ())), preferred_element_type=jnp.float32
        )
        state["right"] = term if state["right"] is None else state["right"] + term

    halves = [gradient[:piece], gradient[piece:]]
    going_up = list(halves)
    going_down = list(halves)
    last = count // 2
    for step in range(1, last + 1):
        if step < last:
            going_up = [lax.ppermute(part, "row", up) for part in going_up]
            going_down = [lax.ppermute(part, "row", down) for part in going_down]
        else:
            going_up = [lax.ppermute(going_up[0], "row", up)]
            going_down = [lax.ppermute(going_down[1], "row", down)]
        if step == 1:
            consume(halves[0], 0, 0)
            consume(halves[1], 0, piece)
        if step < last:
            for at in range(2):
                consume(going_up[at], step, at * piece)
                consume(going_down[at], -step, at * piece)
        else:
            consume(going_up[0], step, 0)
            consume(going_down[0], step, piece)

    width = count * tile_rows // 2
    gram_left = lax.dynamic_slice_in_dim(state["left"], my_col * width, width, 1)
    left_state = BETA * left_old + (1.0 - BETA) * gram_left
    left_fixed = left_state / denominator(left_counts)
    right_state = BETA * right_old + (1.0 - BETA) * state["right"][None]
    right_fixed = right_state / denominator(right_counts)[:, None, None]
    return (left_state, left_fixed, right_state, right_fixed)


def solution(mesh):
    return jax.shard_map(
        local,
        mesh=mesh,
        in_specs=(
            P(("groups", "row"), "col"),
            P(("groups", "row"), "col"),
            P(("groups", "col"), "row", None),
            P(("groups", "row"), "col"),
            P(("groups", "col")),
        ),
        out_specs=(
            P(("groups", "row"), "col"),
            P(("groups", "row"), "col"),
            P(("groups", "col"), "row", None),
            P(("groups", "col"), "row", None),
        ),
        check_vma=False,
    )
```

time: 637 us -> 371 us (0.58)
  waiting for transfers between devices: 563 us -> 168 us
  matrix products: 48.5 us -> 124 us
  starting transfers between devices: 0.08 us -> 45.1 us
  local copies, waits for them, and re-layouts: 0 us -> 8.93 us
  between operations: 15.4 us -> 7.09 us
    all_gather x1 -> x0, waiting for transfers between devices: 563 us -> none  [local(): incoming = lax.all_gather(gradient, 'row', axis=0, tiled=True)]
    ppermute x0 -> x30, waiting for transfers between devices: none -> 168 us  [the longest x6 110 us: local(): going_up = [lax.ppermute(part, 'row', up) for part in going_up]]
    dot_general x2 -> x32, matrix products: 48.5 us -> 124 us  [the longest x16 101 us: consume(): lax.dot_general(strip, part, (((0,), (0,)), ((), ())), preferred_element_...]
    ppermute x0 -> x30, starting transfers between devices: none -> 45.1 us  [the longest x16 30 us: consume(): other = lax.ppermute(product, ('row', 'col'), pairs)]
  transfers between devices with their start and end apart: 2 -> 30, of which waited for: 1 -> 15; matrix products, arithmetic and copies ran while one was open for 4% -> 36% of each run, Pallas kernels for 0% -> 0%
where the time goes in v1:
time: 371 us; the launch traced here: 367 us
  waiting for transfers between devices  168 us (45%)
  matrix products  124 us (33%)
  starting transfers between devices  45.1 us (12%)
  other arithmetic  14 us (4%)
  local copies, waits for them, and re-layouts  8.93 us (2%)
  between operations  7.09 us (2%)
    ppermute x6, waiting for transfers between devices, local(): going_up = [lax.ppermute(part, 'row', up) for part in going_up]  110 us
    dot_general x16, matrix products, consume(): lax.dot_general(strip, part, (((0,), (0,)), ((), ())), preferred_element_...  101 us
    ppermute x6, waiting for transfers between devices, local(): going_down = [lax.ppermute(part, 'row', down) for part in going_down]  37 us
    ppermute x16, starting transfers between devices, consume(): other = lax.ppermute(product, ('row', 'col'), pairs)  30 us
    dot_general x16, matrix products, consume(): lax.dot_general(gradient, part, (((1,), (1,)), ((), ())), preferred_eleme...  22.7 us
    ppermute x6, starting transfers between devices, local(): going_up = [lax.ppermute(part, 'row', up) for part in going_up]  10.1 us
    ppermute x1, waiting for transfers between devices, local(): going_up = [lax.ppermute(going_up[0], 'row', up)]  9.78 us
    div x1, other arithmetic, local(): left_fixed = left_state / denominator(left_counts)  8.77 us
  transfers between devices with their start and end apart: 30, of which 15 were waited for; matrix products, arithmetic and copies ran while one was open for 36% of the time, Pallas kernels for 0%

profile of v1, /device:TPU:1, one launch (start us, length us, event | category | flops | bytes accessed | tf_op | source)
XLA Modules:
  0.0 366.9 jit_solution(1074293141146606085)
XLA Ops:
  15.6 5.6 %fusion.32 = f32[448,3584]{1,0:T(8,128)} fusion(bf16[256,3584]{1,0:T(8,128)(2,1)} %get-tuple-element.7, s32[]{:T(128)S(6)} %select_n.105), kind=kOutput, calls=%fused_computation.50 | convolution fusion | flops 822083584 | bytes 8519684 | tf_op jit(solution)/shard_map/dot_general | solution.py:50
  31.3 3.8 %fusion.30 = f32[448,3584]{1,0:T(8,128)} fusion(bf16[256,3584]{1,0:T(8,128)(2,1)S(1)} %get-tuple-element.6, s32[]{:T(128)S(6)} %select_n.105), kind=kOutput, calls=%fused_computation.48 | convolution fusion | flops 822083584 | bytes 8519684 | tf_op jit(solution)/shard_map/dot_general | solution.py:50
  37.5 9.0 %collective-permute-done.2 = bf16[256,3584]{1,0:T(8,128)(2,1)} collective-permute-done((bf16[256,3584]{1,0:T(8,128)(2,1)}, bf16[256,3584]{1,0:T(8,128)(2,1)}, u32[]{:S(2)}, u32[]{:S(2)}) %collective-permute-start.2) | collective-permute-done | bytes 1835040 | tf_op jit(solution)/shard_map/ppermute | solution.py:61
  49.1 4.0 %collective-permute-start.3 = (f32[512,256]{1,0:T(8,128)S(1)}, f32[512,256]{1,0:T(8,128)S(1)}, u32[]{:S(2)}, u32[]{:S(2)}) collective-permute-start(f32[512,256]{1,0:T(8,128)S(1)} %fusion.55), channel_id=1, source_target_pairs={{1,0},{3,2},{5,4},{6,7},{9,8},{10,11},{12,13},{14,15},{17,16},{19,... | collective-permute-start | bytes 1572872 | tf_op jit(solution)/shard_map/ppermute | solution.py:45
  57.1 28.7 %collective-permute-done.6 = bf16[256,3584]{1,0:T(8,128)(2,1)} collective-permute-done((bf16[256,3584]{1,0:T(8,128)(2,1)S(1)}, bf16[256,3584]{1,0:T(8,128)(2,1)}, u32[]{:S(2)}, u32[]{:S(2)}) %collective-permute-start.6) | collective-permute-done | bytes 1835040 | tf_op jit(solution)/shard_map/ppermute | solution.py:61
  93.2 5.5 %fusion.24 = f32[448,3584]{1,0:T(8,128)} fusion(bf16[256,3584]{1,0:T(8,128)(2,1)} %collective-permute-done.6, s32[]{:T(128)S(6)} %select_n.105), kind=kOutput, calls=%fused_computation.42 | convolution fusion | flops 822083584 | bytes 8519684 | tf_op jit(solution)/shard_map/dot_general | solution.py:50
  98.6 5.4 %fusion.26 = f32[448,3584]{1,0:T(8,128)} fusion(bf16[256,3584]{1,0:T(8,128)(2,1)} %collective-permute-done.4, s32[]{:T(128)S(6)} %select_n.105), kind=kOutput, calls=%fused_computation.44 | convolution fusion | flops 822083584 | bytes 8519684 | tf_op jit(solution)/shard_map/dot_general | solution.py:50
  104.0 5.5 %fusion.28 = f32[448,3584]{1,0:T(8,128)} fusion(bf16[256,3584]{1,0:T(8,128)(2,1)} %collective-permute-done.2, s32[]{:T(128)S(6)} %select_n.105), kind=kOutput, calls=%fused_computation.46 | convolution fusion | flops 822083584 | bytes 8519684 | tf_op jit(solution)/shard_map/dot_general | solution.py:50
  109.5 3.9 %fusion.22 = f32[448,3584]{1,0:T(8,128)} fusion(bf16[256,3584]{1,0:T(8,128)(2,1)S(1)} %collective-permute-done.8, s32[]{:T(128)S(6)} %select_n.105), kind=kOutput, calls=%fused_computation.40 | convolution fusion | flops 822083584 | bytes 8519684 | tf_op jit(solution)/shard_map/dot_general | solution.py:50
  119.9 13.9 %collective-permute-done.10 = bf16[256,3584]{1,0:T(8,128)(2,1)S(1)} collective-permute-done((bf16[256,3584]{1,0:T(8,128)(2,1)}, bf16[256,3584]{1,0:T(8,128)(2,1)S(1)}, u32[]{:S(2)}, u32[]{:S(2)}) %collective-permute-start.10) | collective-permute-done | bytes 1835040 | tf_op jit(solution)/shard_map/ppermute | solution.py:61
  137.0 14.7 %collective-permute-done.12 = bf16[256,3584]{1,0:T(8,128)(2,1)S(1)} collective-permute-done((bf16[256,3584]{1,0:T(8,128)(2,1)}, bf16[256,3584]{1,0:T(8,128)(2,1)S(1)}, u32[]{:S(2)}, u32[]{:S(2)}) %collective-permute-start.12) | collective-permute-done | bytes 1835040 | tf_op jit(solution)/shard_map/ppermute | solution.py:62
  154.1 18.9 %collective-permute-done.14 = bf16[256,3584]{1,0:T(8,128)(2,1)S(1)} collective-permute-done((bf16[256,3584]{1,0:T(8,128)(2,1)}, bf16[256,3584]{1,0:T(8,128)(2,1)S(1)}, u32[]{:S(2)}, u32[]{:S(2)}) %collective-permute-start.14) | collective-permute-done | bytes 1835040 | tf_op jit(solution)/shard_map/ppermute | solution.py:61
  181.7 3.9 %fusion.18 = f32[448,3584]{1,0:T(8,128)} fusion(bf16[256,3584]{1,0:T(8,128)(2,1)S(1)} %collective-permute-done.12, s32[]{:T(128)S(6)} %select_n.105), kind=kOutput, calls=%fused_computation.36 | convolution fusion | flops 822083584 | bytes 8519684 | tf_op jit(solution)/shard_map/dot_general | solution.py:50
  191.1 3.9 %fusion.14 = f32[448,3584]{1,0:T(8,128)} fusion(bf16[256,3584]{1,0:T(8,128)(2,1)S(1)} %collective-permute-done.16, s32[]{:T(128)S(6)} %select_n.105), kind=kOutput, calls=%fused_computation.32 | convolution fusion | flops 822083584 | bytes 8519684 | tf_op jit(solution)/shard_map/dot_general | solution.py:50
  201.5 16.4 %collective-permute-done.18 = bf16[256,3584]{1,0:T(8,128)(2,1)S(1)} collective-permute-done((bf16[256,3584]{1,0:T(8,128)(2,1)S(1)}, bf16[256,3584]{1,0:T(8,128)(2,1)S(1)}, u32[]{:S(2)}, u32[]{:S(2)}) %collective-permute-start.18) | collective-permute-done | bytes 1835040 | tf_op jit(solution)/shard_map/ppermute | solution.py:61
  220.4 11.7 %collective-permute-done.20 = bf16[256,3584]{1,0:T(8,128)(2,1)S(1)} collective-permute-done((bf16[256,3584]{1,0:T(8,128)(2,1)S(1)}, bf16[256,3584]{1,0:T(8,128)(2,1)S(1)}, u32[]{:S(2)}, u32[]{:S(2)}) %collective-permute-start.20) | collective-permute-done | bytes 1835040 | tf_op jit(solution)/shard_map/ppermute | solution.py:62
  234.5 22.7 %collective-permute-done.22 = bf16[256,3584]{1,0:T(8,128)(2,1)S(1)} collective-permute-done((bf16[256,3584]{1,0:T(8,128)(2,1)S(1)}, bf16[256,3584]{1,0:T(8,128)(2,1)S(1)}, u32[]{:S(2)}, u32[]{:S(2)}) %collective-permute-start.22) | collective-permute-done | bytes 1835040 | tf_op jit(solution)/shard_map/ppermute | solution.py:61
  262.4 9.0 %collective-permute-done.24 = bf16[256,3584]{1,0:T(8,128)(2,1)S(1)} collective-permute-done((bf16[256,3584]{1,0:T(8,128)(2,1)S(1)}, bf16[256,3584]{1,0:T(8,128)(2,1)S(1)}, u32[]{:S(2)}, u32[]{:S(2)}) %collective-permute-start.24) | collective-permute-done | bytes 1835040 | tf_op jit(solution)/shard_map/ppermute | solution.py:62
  271.6 3.9 %fusion.6 = f32[448,3584]{1,0:T(8,128)} fusion(bf16[256,3584]{1,0:T(8,128)(2,1)S(1)} %collective-permute-done.24, s32[]{:T(128)S(6)} %select_n.105), kind=kOutput, calls=%fused_computation.24 | convolution fusion | flops 822083584 | bytes 8519684 | tf_op jit(solution)/shard_map/dot_general | solution.py:50
  292.3 9.8 %collective-permute-done.26 = bf16[256,3584]{1,0:T(8,128)(2,1)S(1)} collective-permute-done((bf16[256,3584]{1,0:T(8,128)(2,1)S(1)}, bf16[256,3584]{1,0:T(8,128)(2,1)S(1)}, u32[]{:S(2)}, u32[]{:S(2)}) %collective-permute-start.26) | collective-permute-done | bytes 1835040 | tf_op jit(solution)/shard_map/ppermute | solution.py:64
  304.5 7.0 %collective-permute-done.28 = bf16[256,3584]{1,0:T(8,128)(2,1)S(1)} collective-permute-done((bf16[256,3584]{1,0:T(8,128)(2,1)S(1)}, bf16[256,3584]{1,0:T(8,128)(2,1)S(1)}, u32[]{:S(2)}, u32[]{:S(2)}) %collective-permute-start.28) | collective-permute-done | bytes 1835040 | tf_op jit(solution)/shard_map/ppermute | solution.py:65
  314.0 3.9 %fusion.4 = f32[448,3584]{1,0:T(8,128)} fusion(bf16[256,3584]{1,0:T(8,128)(2,1)S(1)} %collective-permute-done.26, s32[]{:T(128)S(6)} %select_n.105), kind=kOutput, calls=%fused_computation.22 | convolution fusion | flops 822083584 | bytes 8519684 | tf_op jit(solution)/shard_map/dot_general | solution.py:50
  317.9 37.3 %broadcast_divide_fusion = (f32[1,448,3584]{2,1,0:T(8,128)}, f32[1,448,3584]{2,1,0:T(8,128)}) fusion(f32[]{:T(128)} %bitcast.23, bf16[256,3584]{1,0:T(8,128)(2,1)S(1)} %collective-permute-done.28, s32[]{:T(128)S(6)} %select_n.105, f32[448,3584]{1,0:T(8,128)} %fusion.4, f32[448,3584]{1,0:T(8,128)} %fusion.6, f32[448,3584]{1,0:T(8,128)} %fusion.8, ...), kind=kOutput, calls=%fused_computation.2 | convolution fusion | flops 852590592 | bytes 117702664 | tf_op jit(solution)/shard_map/dot_general | solution.py:50
  358.1 8.8 %broadcast_divide_fusion.1 = (f32[512,2048]{1,0:T(8,128)}, f32[512,2048]{1,0:T(8,128)}) fusion(f32[]{:T(128)} %bitcast.21, f32[512,4096]{1,0:T(8,128)} %add_dynamic-update-slice_fusion, s32[]{:T(128)S(6)} %select_n.104, f32[512,2048]{1,0:T(8,128)} %param.22), kind=kLoop, calls=%fused_computation.3 | loop fusion | flops 4194304 | bytes 16777224 | tf_op jit(solution)/shard_map/div | solution.py:80
  (114 shorter events, 102.7 us)
Async XLA Ops:
  4.3 42.1 %collective-permute-start.2 = (bf16[256,3584]{1,0:T(8,128)(2,1)}, bf16[256,3584]{1,0:T(8,128)(2,1)}, u32[]{:S(2)}, u32[]{:S(2)}) collective-permute-start(bf16[256,3584]{1,0:T(8,128)(2,1)} %get-tuple-element.7), channel_id=1, source_target_pairs={{0,4},{4,8},{8,12},{12,14},{14,10},{10,6},{6,2},{2,0},{1,5},{5,9},... | collective-permute-start | bytes 5505032 | tf_op jit(solution)/shard_map/ppermute | solution.py:61
  6.4 46.6 %collective-permute-start.4 = (bf16[256,3584]{1,0:T(8,128)(2,1)}, bf16[256,3584]{1,0:T(8,128)(2,1)}, u32[]{:S(2)}, u32[]{:S(2)}) collective-permute-start(bf16[256,3584]{1,0:T(8,128)(2,1)} %get-tuple-element.7), channel_id=1, source_target_pairs={{4,0},{8,4},{12,8},{14,12},{10,14},{6,10},{2,6},{0,2},{5,1},{9,5},... | collective-permute-start | bytes 5505032 | tf_op jit(solution)/shard_map/ppermute | solution.py:62
  13.8 72.0 %collective-permute-start.6 = (bf16[256,3584]{1,0:T(8,128)(2,1)S(1)}, bf16[256,3584]{1,0:T(8,128)(2,1)}, u32[]{:S(2)}, u32[]{:S(2)}) collective-permute-start(bf16[256,3584]{1,0:T(8,128)(2,1)S(1)} %get-tuple-element.6), channel_id=1, source_target_pairs={{0,4},{4,8},{8,12},{12,14},{14,10},{10,6},{6,2},{2,0},{1,5},{5,9},... | collective-permute-start | bytes 5505032 | tf_op jit(solution)/shard_map/ppermute | solution.py:61
  35.1 74.4 %collective-permute-start.8 = (bf16[256,3584]{1,0:T(8,128)(2,1)S(1)}, bf16[256,3584]{1,0:T(8,128)(2,1)S(1)}, u32[]{:S(2)}, u32[]{:S(2)}) collective-permute-start(bf16[256,3584]{1,0:T(8,128)(2,1)S(1)} %get-tuple-element.6), channel_id=1, source_target_pairs={{4,0},{8,4},{12,8},{14,12},{10,14},{6,10},{2,6},{0,2},{5,1},{9,5},... | collective-permute-start | bytes 5505032 | tf_op jit(solution)/shard_map/ppermute | solution.py:62
  49.1 65.5 %collective-permute-start.3 = (f32[512,256]{1,0:T(8,128)S(1)}, f32[512,256]{1,0:T(8,128)S(1)}, u32[]{:S(2)}, u32[]{:S(2)}) collective-permute-start(f32[512,256]{1,0:T(8,128)S(1)} %fusion.55), channel_id=1, source_target_pairs={{1,0},{3,2},{5,4},{6,7},{9,8},{10,11},{12,13},{14,15},{17,16},{19,... | collective-permute-start | bytes 1572872 | tf_op jit(solution)/shard_map/ppermute | solution.py:45
  55.7 60.5 %collective-permute-start.5 = (f32[512,256]{1,0:T(8,128)S(1)}, f32[512,256]{1,0:T(8,128)S(1)}, u32[]{:S(2)}, u32[]{:S(2)}) collective-permute-start(f32[512,256]{1,0:T(8,128)S(1)} %fusion.56), channel_id=1, source_target_pairs={{1,0},{3,2},{4,5},{7,6},{8,9},{11,10},{12,13},{14,15},{17,16},{19,... | collective-permute-start | bytes 1572872 | tf_op jit(solution)/shard_map/ppermute | solution.py:45
  88.4 30.1 %collective-permute-start.7 = (f32[512,256]{1,0:T(8,128)S(1)}, f32[512,256]{1,0:T(8,128)S(1)}, u32[]{:S(2)}, u32[]{:S(2)}) collective-permute-start(f32[512,256]{1,0:T(8,128)S(1)} %fusion.57), channel_id=1, source_target_pairs={{1,0},{3,2},{5,4},{6,7},{9,8},{10,11},{12,13},{14,15},{17,16},{19,... | collective-permute-start | bytes 1572872 | tf_op jit(solution)/shard_map/ppermute | solution.py:45
  91.6 42.3 %collective-permute-start.10 = (bf16[256,3584]{1,0:T(8,128)(2,1)}, bf16[256,3584]{1,0:T(8,128)(2,1)S(1)}, u32[]{:S(2)}, u32[]{:S(2)}) collective-permute-start(bf16[256,3584]{1,0:T(8,128)(2,1)} %collective-permute-done.2), channel_id=1, source_target_pairs={{0,4},{4,8},{8,12},{12,14},{14,10},{10,6},{6,2},{2,0},{1,5},{5,9},... | collective-permute-start | bytes 5505032 | tf_op jit(solution)/shard_map/ppermute | solution.py:61
  109.5 42.1 %collective-permute-start.12 = (bf16[256,3584]{1,0:T(8,128)(2,1)}, bf16[256,3584]{1,0:T(8,128)(2,1)S(1)}, u32[]{:S(2)}, u32[]{:S(2)}) collective-permute-start(bf16[256,3584]{1,0:T(8,128)(2,1)} %collective-permute-done.4), channel_id=1, source_target_pairs={{4,0},{8,4},{12,8},{14,12},{10,14},{6,10},{2,6},{0,2},{5,1},{9,5},... | collective-permute-start | bytes 5505032 | tf_op jit(solution)/shard_map/ppermute | solution.py:62
  114.6 58.4 %collective-permute-start.14 = (bf16[256,3584]{1,0:T(8,128)(2,1)}, bf16[256,3584]{1,0:T(8,128)(2,1)S(1)}, u32[]{:S(2)}, u32[]{:S(2)}) collective-permute-start(bf16[256,3584]{1,0:T(8,128)(2,1)} %collective-permute-done.6), channel_id=1, source_target_pairs={{0,4},{4,8},{8,12},{12,14},{14,10},{10,6},{6,2},{2,0},{1,5},{5,9},... | collective-permute-start | bytes 5505032 | tf_op jit(solution)/shard_map/ppermute | solution.py:61
  118.5 72.5 %collective-permute-start.16 = (bf16[256,3584]{1,0:T(8,128)(2,1)S(1)}, bf16[256,3584]{1,0:T(8,128)(2,1)S(1)}, u32[]{:S(2)}, u32[]{:S(2)}) collective-permute-start(bf16[256,3584]{1,0:T(8,128)(2,1)S(1)} %collective-permute-done.8), channel_id=1, source_target_pairs={{4,0},{8,4},{12,8},{14,12},{10,14},{6,10},{2,6},{0,2},{5,1},{9,5},... | collective-permute-start | bytes 5505032 | tf_op jit(solution)/shard_map/ppermute | solution.py:62
  135.0 61.1 %collective-permute-start.11 = (f32[512,256]{1,0:T(8,128)S(1)}, f32[512,256]{1,0:T(8,128)S(1)}, u32[]{:S(2)}, u32[]{:S(2)}) collective-permute-start(f32[512,256]{1,0:T(8,128)S(1)} %fusion.59), channel_id=1, source_target_pairs={{1,0},{2,3},{5,4},{6,7},{9,8},{10,11},{13,12},{14,15},{17,16},{18,... | collective-permute-start | bytes 1572872 | tf_op jit(solution)/shard_map/ppermute | solution.py:45
  152.8 44.8 %collective-permute-start.13 = (f32[512,256]{1,0:T(8,128)S(1)}, f32[512,256]{1,0:T(8,128)S(1)}, u32[]{:S(2)}, u32[]{:S(2)}) collective-permute-start(f32[512,256]{1,0:T(8,128)S(1)} %fusion.60), channel_id=1, source_target_pairs={{0,1},{3,2},{4,5},{7,6},{8,9},{11,10},{12,13},{15,14},{16,17},{19,... | collective-permute-start | bytes 1572872 | tf_op jit(solution)/shard_map/ppermute | solution.py:45
  176.3 41.6 %collective-permute-start.18 = (bf16[256,3584]{1,0:T(8,128)(2,1)S(1)}, bf16[256,3584]{1,0:T(8,128)(2,1)S(1)}, u32[]{:S(2)}, u32[]{:S(2)}) collective-permute-start(bf16[256,3584]{1,0:T(8,128)(2,1)S(1)} %collective-permute-done.10), channel_id=1, source_target_pairs={{0,4},{4,8},{8,12},{12,14},{14,10},{10,6},{6,2},{2,0},{1,5},{5,9},... | collective-permute-start | bytes 5505032 | tf_op jit(solution)/shard_map/ppermute | solution.py:61
  191.0 41.1 %collective-permute-start.20 = (bf16[256,3584]{1,0:T(8,128)(2,1)S(1)}, bf16[256,3584]{1,0:T(8,128)(2,1)S(1)}, u32[]{:S(2)}, u32[]{:S(2)}) collective-permute-start(bf16[256,3584]{1,0:T(8,128)(2,1)S(1)} %collective-permute-done.12), channel_id=1, source_target_pairs={{4,0},{8,4},{12,8},{14,12},{10,14},{6,10},{2,6},{0,2},{5,1},{9,5},... | collective-permute-start | bytes 5505032 | tf_op jit(solution)/shard_map/ppermute | solution.py:62
  196.1 61.2 %collective-permute-start.22 = (bf16[256,3584]{1,0:T(8,128)(2,1)S(1)}, bf16[256,3584]{1,0:T(8,128)(2,1)S(1)}, u32[]{:S(2)}, u32[]{:S(2)}) collective-permute-start(bf16[256,3584]{1,0:T(8,128)(2,1)S(1)} %collective-permute-done.14), channel_id=1, source_target_pairs={{0,4},{4,8},{8,12},{12,14},{14,10},{10,6},{6,2},{2,0},{1,5},{5,9},... | collective-permute-start | bytes 5505032 | tf_op jit(solution)/shard_map/ppermute | solution.py:61
  199.0 72.4 %collective-permute-start.24 = (bf16[256,3584]{1,0:T(8,128)(2,1)S(1)}, bf16[256,3584]{1,0:T(8,128)(2,1)S(1)}, u32[]{:S(2)}, u32[]{:S(2)}) collective-permute-start(bf16[256,3584]{1,0:T(8,128)(2,1)S(1)} %collective-permute-done.16), channel_id=1, source_target_pairs={{4,0},{8,4},{12,8},{14,12},{10,14},{6,10},{2,6},{0,2},{5,1},{9,5},... | collective-permute-start | bytes 5505032 | tf_op jit(solution)/shard_map/ppermute | solution.py:62
  219.1 68.9 %collective-permute-start.19 = (f32[512,256]{1,0:T(8,128)S(1)}, f32[512,256]{1,0:T(8,128)S(1)}, u32[]{:S(2)}, u32[]{:S(2)}) collective-permute-start(f32[512,256]{1,0:T(8,128)S(1)} %fusion.63), channel_id=1, source_target_pairs={{0,1},{2,3},{5,4},{6,7},{9,8},{10,11},{13,12},{15,14},{16,17},{18,... | collective-permute-start | bytes 1572872 | tf_op jit(solution)/shard_map/ppermute | solution.py:45
  233.2 56.2 %collective-permute-start.21 = (f32[512,256]{1,0:T(8,128)S(1)}, f32[512,256]{1,0:T(8,128)S(1)}, u32[]{:S(2)}, u32[]{:S(2)}) collective-permute-start(f32[512,256]{1,0:T(8,128)S(1)} %fusion.64), channel_id=1, source_target_pairs={{0,1},{2,3},{4,5},{7,6},{8,9},{11,10},{13,12},{15,14},{16,17},{18,... | collective-permute-start | bytes 1572872 | tf_op jit(solution)/shard_map/ppermute | solution.py:45
  258.4 31.1 %collective-permute-start.23 = (f32[512,256]{1,0:T(8,128)S(1)}, f32[512,256]{1,0:T(8,128)S(1)}, u32[]{:S(2)}, u32[]{:S(2)}) collective-permute-start(f32[512,256]{1,0:T(8,128)S(1)} %fusion.65), channel_id=1, source_target_pairs={{0,1},{2,3},{5,4},{6,7},{9,8},{10,11},{13,12},{15,14},{16,17},{18,... | collective-permute-start | bytes 1572872 | tf_op jit(solution)/shard_map/ppermute | solution.py:45
  259.7 42.4 %collective-permute-start.26 = (bf16[256,3584]{1,0:T(8,128)(2,1)S(1)}, bf16[256,3584]{1,0:T(8,128)(2,1)S(1)}, u32[]{:S(2)}, u32[]{:S(2)}) collective-permute-start(bf16[256,3584]{1,0:T(8,128)(2,1)S(1)} %collective-permute-done.18), channel_id=1, source_target_pairs={{0,4},{4,8},{8,12},{12,14},{14,10},{10,6},{6,2},{2,0},{1,5},{5,9},... | collective-permute-start | bytes 5505032 | tf_op jit(solution)/shard_map/ppermute | solution.py:64
  271.4 40.2 %collective-permute-start.28 = (bf16[256,3584]{1,0:T(8,128)(2,1)S(1)}, bf16[256,3584]{1,0:T(8,128)(2,1)S(1)}, u32[]{:S(2)}, u32[]{:S(2)}) collective-permute-start(bf16[256,3584]{1,0:T(8,128)(2,1)S(1)} %collective-permute-done.24), channel_id=1, source_target_pairs={{4,0},{8,4},{12,8},{14,12},{10,14},{6,10},{2,6},{0,2},{5,1},{9,5},... | collective-permute-start | bytes 5505032 | tf_op jit(solution)/shard_map/ppermute | solution.py:65
  303.2 52.0 %collective-permute-start.27 = (f32[512,256]{1,0:T(8,128)S(1)}, f32[512,256]{1,0:T(8,128)S(1)}, u32[]{:S(2)}, u32[]{:S(2)}) collective-permute-start(f32[512,256]{1,0:T(8,128)S(1)} %fusion.67), channel_id=1, source_target_pairs={{0,1},{2,3},{4,5},{6,7},{9,8},{11,10},{13,12},{15,14},{16,17},{18,... | collective-permute-start | bytes 1572872 | tf_op jit(solution)/shard_map/ppermute | solution.py:45
  312.7 43.5 %collective-permute-start.29 = (f32[512,256]{1,0:T(8,128)S(1)}, f32[512,256]{1,0:T(8,128)}, u32[]{:S(2)}, u32[]{:S(2)}) collective-permute-start(f32[512,256]{1,0:T(8,128)S(1)} %fusion.68), channel_id=1, source_target_pairs={{0,1},{2,3},{4,5},{6,7},{9,8},{11,10},{13,12},{15,14},{16,17},{18,... | collective-permute-start | bytes 1572872 | tf_op jit(solution)/shard_map/ppermute | solution.py:45
  (16 other events, 191.9 us)

commit v2 on v1

--- a/solution.py
+++ b/solution.py
@@ -17,7 +17,7 @@
     return list(range(count))
 
 
-def local(gradient, left_old, right_old, left_counts, right_counts):
+def ring(gradient, left_old, right_old, left_counts, right_counts):
     tile_rows, half_wide = gradient.shape
     count = lax.axis_size("row")
     strip_wide = half_wide // count
@@ -83,7 +83,204 @@
     return (left_state, left_fixed, right_state, right_fixed)
 
 
+GROUP = 64
+
+
+def encode(values):
+    rows, wide = values.shape
+    grouped = values.reshape(rows // GROUP, GROUP, wide)
+    most = jnp.maximum(jnp.max(jnp.abs(grouped), axis=1), 1e-34)
+    level = jnp.ceil(jnp.log2(most) * 256.0)
+    inverse = 32767.0 * jnp.exp2(level * (-1.0 / 256.0))
+    coded = jnp.clip(jnp.round(grouped * inverse[:, None, :]), -32767.0, 32767.0)
+    extra = -(-(rows // GROUP) // 16) * 16
+    levels = jnp.pad(level, ((0, extra - rows // GROUP), (0, 0)))
+    return jnp.concatenate(
+        [coded.reshape(rows, wide).astype(jnp.int16), levels.astype(jnp.int16)], 0
+    )
+
+
+def decode(coded, rows):
+    wide = coded.shape[1]
+    level = coded[rows : rows + rows // GROUP].astype(jnp.float32)
+    step = jnp.exp2(level * (1.0 / 256.0)) * (1.0 / 32767.0)
+    grouped = coded[:rows].astype(jnp.float32).reshape(rows // GROUP, GROUP, wide)
+    return (grouped * step[:, None, :]).reshape(rows, wide)
+
+
+def dot(a, b, a_dim, b_dim):
+    return lax.dot_general(
+        a, b, (((a_dim,), (b_dim,)), ((), ())), preferred_element_type=jnp.float32
+    )
+
+
+AXES = ("row", "col")
+CHIPS = [(z, y) for z in range(4) for y in range(2)]
+
+
+def at(z, y, c):
+    return (z * 2 + y) * 2 + c
+
+
+MIDDLE = ((1, 0), (2, 3))
+
+
+def moves(rule):
+    pairs = []
+    for z, y in CHIPS:
+        for c in range(2):
+            dest = rule(z, y, c)
+            if dest is not None:
+                pairs.append((at(z, y, c), at(*dest)))
+    return pairs
+
+
+def middle_planes(gradient, left_old, right_old, left_counts, right_counts):
+    tile_rows, half_wide = gradient.shape
+    chunk = half_wide // 4
+    strip = half_wide // 8
+    my_row = lax.axis_index("row")
+    c = lax.axis_index("col")
+    z, y = my_row // 2, my_row % 2
+    side = (z >= 2).astype(jnp.int32)
+    own, mate, near, far = 1 + side, 3 * side, 2 - side, 3 - 3 * side
+    straight = c == y
+
+    def send(value, rule):
+        return lax.ppermute(value, AXES, moves(rule))
+
+    def swap_rule(z, y, c):
+        return (z, c, y) if c != y else None
+
+    def inward(same):
+        return lambda z, y, c: ({0: 1, 3: 2}[z], y, c) if z in (0, 3) and (c == y) == same else None
+
+    def across(same):
+        return lambda z, y, c: (3 - z, y, c) if z in (1, 2) and (same is None or (c == y) == same) else None
+
+    def beside(z, y, c):
+        return (z, y, 1 - c)
+
+    def other_y(z, y, c):
+        return (z, 1 - y, c) if z in (1, 2) else None
+
+    swapped = send(gradient, swap_rule)
+    mate_a = send(gradient, inward(True))
+    near_a = send(gradient, across(True))
+    mine = jnp.where(straight, gradient, swapped)
+    mate_b = send(mine, inward(False))
+    near_b = send(mine, across(False))
+    mine_o = send(mine, beside)
+    mates = jnp.where(straight, mate_a, mate_b)
+    nears = jnp.where(straight, near_a, near_b)
+
+    orders = (far, near, own, mate)
+    chunks = []
+    for plane in orders:
+        part = lax.dynamic_slice_in_dim(mates, plane * chunk, chunk, 1)
+        chunks.append(send(part, across(None)))
+    mates_o = send(mates, beside)
+    nears_o = send(nears, beside)
+    held = jnp.concatenate([mine, mine_o, mates, mates_o, nears, nears_o], 0)
+    plane_rows = 2 * tile_rows
+    lefts = lax.dynamic_slice_in_dim(held, c * plane_rows, plane_rows, 0)
+    kept_at = jnp.where(straight, 0, tile_rows)
+    sent_at = tile_rows - kept_at
+
+    def exchange(product):
+        kept = lax.dynamic_slice_in_dim(product, kept_at, tile_rows, 0)
+        gone = lax.dynamic_slice_in_dim(product, sent_at, tile_rows, 0)
+        return kept, send(encode(gone), other_y)
+
+    def finish_left(kept, coded, name):
+        total = kept + decode(coded, tile_rows)
+        total = jnp.where(
+            c == 0, total, jnp.concatenate([total[:, tile_rows:], total[:, :tile_rows]], 1)
+        )
+
+        def rule(z, y, c):
+            if z not in (1, 2):
+                return None
+            plane = {"own": z, "mate": {1: 0, 2: 3}[z], "near": 3 - z, "far": {1: 3, 2: 0}[z]}[name]
+            half = plane // 2
+            return (z, y, half) if c == 0 else ({1: 0, 2: 3}[z], y, half)
+
+        return send(encode(total), rule)
+
+    halves = {}
+    for index, name in enumerate(("own", "mate", "near")):
+        rows = held[index * plane_rows : (index + 1) * plane_rows]
+        halves[name] = exchange(dot(lefts, rows, 1, 1))
+
+    target = jnp.where(c == 0, own, mate)
+    strips = lax.dynamic_slice_in_dim(held, target * chunk, chunk, 1)
+    bases = [
+        dot(strips, lax.dynamic_slice_in_dim(held, plane * chunk, chunk, 1), 0, 0)
+        for plane in (mate, own, near, far)
+    ]
+
+    def same_rule(z, y, c):
+        if z not in (1, 2):
+            return None
+        return (z, y, y) if c == 0 else ({1: 0, 2: 3}[z], y, y)
+
+    def cross_rule(z, y, c):
+        if z not in (1, 2):
+            return None
+        return (z, 1 - y, y) if c == 0 else ({1: 0, 2: 3}[z], 1 - y, y)
+
+    def finish_right(value):
+        same = lax.dynamic_slice_in_dim(value, y * strip, strip, 0)
+        cross = lax.dynamic_slice_in_dim(value, (1 - y) * strip, strip, 0)
+        same = send(encode(same), same_rule)
+        cross = send(encode(cross), cross_rule)
+        return jnp.where(straight, same, cross)
+
+    lefts_out = {}
+    rights = []
+    far_rows = []
+    far_product = None
+    names = ["own", "mate", "near"]
+    for index, plane in enumerate((mate, own, near, far)):
+        part = jnp.concatenate([chunks[index], send(chunks[index], beside)], 0)
+        far_rows.append(part)
+        piece = lax.dynamic_slice_in_dim(lefts, plane * chunk, chunk, 1)
+        term = dot(piece, part, 1, 1)
+        far_product = term if far_product is None else far_product + term
+        if index == 1:
+            far_strips = jnp.where(c == 0, far_rows[1], far_rows[0])
+            rights.append(finish_right(bases[0] + dot(far_strips, far_rows[0], 0, 0)))
+        if index >= 1:
+            rights.append(finish_right(bases[index] + dot(far_strips, part, 0, 0)))
+            name = names[index - 1]
+            lefts_out[name] = finish_left(*halves[name], name)
+    halves["far"] = exchange(far_product)
+    lefts_out["far"] = finish_left(*halves["far"], "far")
+
+    same_half = c == side
+    first = jnp.where(same_half, lefts_out["own"], lefts_out["near"])
+    second = jnp.where(same_half, lefts_out["mate"], lefts_out["far"])
+    first, second = decode(first, tile_rows), decode(second, tile_rows)
+    ahead = c == 0
+    gram_left = jnp.concatenate(
+        [jnp.where(ahead, second, first), jnp.where(ahead, first, second)], 1
+    )
+    gram_right = jnp.concatenate(
+        [
+            decode(jnp.where(side == 0, rights[index], rights[3 - index]), strip)
+            for index in range(4)
+        ],
+        1,
+    )
+    left_state = BETA * left_old + (1.0 - BETA) * gram_left
+    left_fixed = left_state / denominator(left_counts)
+    right_state = BETA * right_old + (1.0 - BETA) * gram_right[None]
+    right_fixed = right_state / denominator(right_counts)[:, None, None]
+    return (left_state, left_fixed, right_state, right_fixed)
+
+
 def solution(mesh):
+    local = middle_planes if mesh.shape["row"] == 8 else ring
     return jax.shard_map(
         local,
         mesh=mesh,

time: 371 us -> 635 us (1.71)
  the two profiles are of different devices: /device:TPU:1 before, /device:TPU:14 now
where the time goes in v2:
time: 635 us; the launch traced here: 626 us
  waiting for transfers between devices  342 us (54%)
  matrix products  107 us (17%)
  starting transfers between devices  71.1 us (11%)
  other arithmetic  68 us (11%)
  local copies, waits for them, and re-layouts  35.1 us (6%)
    ppermute x32, waiting for transfers between devices, send(): return lax.ppermute(value, AXES, moves(rule))  342 us
    dot_general x15, matrix products, dot(): lax.dot_general(a, b, (((a_dim,), (b_dim,)), ((), ())), preferred_element...  107 us
    ppermute x32, starting transfers between devices, send(): return lax.ppermute(value, AXES, moves(rule))  71.1 us
    unnamed x82, local copies, waits for them, and re-layouts  20.5 us
    reduce_max x16, other arithmetic, encode(): most = jnp.maximum(jnp.max(jnp.abs(grouped), axis=1), 1e-34)  15.8 us
  transfers between devices with their start and end apart: 32, of which 15 were waited for; matrix products, arithmetic and copies ran while one was open for 13% of the time, Pallas kernels for 0%

profile of v2, /device:TPU:14, one launch (start us, length us, event | category | flops | bytes accessed | tf_op | source)
XLA Modules:
  0.0 626.0 jit_solution(7518574865118467764)
XLA Ops:
  2.6 42.6 %collective-permute-done = bf16[512,3584]{1,0:T(8,128)(2,1)} collective-permute-done((bf16[512,3584]{1,0:T(8,128)(2,1)}, bf16[512,3584]{1,0:T(8,128)(2,1)}, u32[]{:S(2)}, u32[]{:S(2)}) %collective-permute-start) | collective-permute-done | bytes 3670048 | tf_op jit(solution)/shard_map/ppermute | solution.py:150
  59.4 74.2 %collective-permute-done.3 = bf16[512,3584]{1,0:T(8,128)(2,1)S(1)} collective-permute-done((bf16[512,3584]{1,0:T(8,128)(2,1)S(1)}, bf16[512,3584]{1,0:T(8,128)(2,1)S(1)}, u32[]{:S(2)}, u32[]{:S(2)}) %collective-permute-start.3) | collective-permute-done | bytes 3670048 | tf_op jit(solution)/shard_map/ppermute | solution.py:150
  145.8 74.2 %collective-permute-done.6 = bf16[512,3584]{1,0:T(8,128)(2,1)S(1)} collective-permute-done((bf16[512,3584]{1,0:T(8,128)(2,1)S(1)}, bf16[512,3584]{1,0:T(8,128)(2,1)S(1)}, u32[]{:S(2)}, u32[]{:S(2)}) %collective-permute-start.6) | collective-permute-done | bytes 3670048 | tf_op jit(solution)/shard_map/ppermute | solution.py:150
  238.9 13.4 %collective-permute-done.14 = bf16[512,896]{1,0:T(8,128)(2,1)} collective-permute-done((bf16[512,896]{1,0:T(8,128)(2,1)S(1)}, bf16[512,896]{1,0:T(8,128)(2,1)}, u32[]{:S(2)}, u32[]{:S(2)}) %collective-permute-start.14) | collective-permute-done | bytes 917536 | tf_op jit(solution)/shard_map/ppermute | solution.py:150
  252.3 19.6 %collective-permute-done.10 = bf16[512,896]{1,0:T(8,128)(2,1)S(1)} collective-permute-done((bf16[512,896]{1,0:T(8,128)(2,1)S(1)}, bf16[512,896]{1,0:T(8,128)(2,1)S(1)}, u32[]{:S(2)}, u32[]{:S(2)}) %collective-permute-start.10) | collective-permute-done | bytes 917536 | tf_op jit(solution)/shard_map/ppermute | solution.py:150
  271.9 19.7 %collective-permute-done.12 = bf16[512,896]{1,0:T(8,128)(2,1)S(1)} collective-permute-done((bf16[512,896]{1,0:T(8,128)(2,1)S(1)}, bf16[512,896]{1,0:T(8,128)(2,1)S(1)}, u32[]{:S(2)}, u32[]{:S(2)}) %collective-permute-start.12) | collective-permute-done | bytes 917536 | tf_op jit(solution)/shard_map/ppermute | solution.py:150
  293.0 17.9 %collective-permute-done.16 = bf16[512,896]{1,0:T(8,128)(2,1)S(1)} collective-permute-done((bf16[512,896]{1,0:T(8,128)(2,1)}, bf16[512,896]{1,0:T(8,128)(2,1)S(1)}, u32[]{:S(2)}, u32[]{:S(2)}) %collective-permute-start.16) | collective-permute-done | bytes 917536 | tf_op jit(solution)/shard_map/ppermute | solution.py:150
  324.3 11.2 %fusion.18 = f32[896,896]{1,0:T(8,128)} fusion(bf16[3072,3584]{1,0:T(8,128)(2,1)} %constant_dynamic-update-slice_fusion, s32[]{:T(128)S(6)} %select_n.194, s32[]{:T(128)S(6)} %select_n.209), kind=kOutput, calls=%fused_computation.19 | convolution fusion | flops 4932501504 | bytes 14221320 | tf_op jit(solution)/shard_map/dot_general | solution.py:112
  336.2 7.8 %fusion.16 = f32[896,896]{1,0:T(8,128)} fusion(bf16[3072,3584]{1,0:T(8,128)(2,1)S(1)} %copy-done.18, s32[]{:T(128)S(6)} %select_n.196, s32[]{:T(128)S(6)} %select_n.209), kind=kOutput, calls=%fused_computation.17 | convolution fusion | flops 4932501504 | bytes 14221320 | tf_op jit(solution)/shard_map/dot_general | solution.py:112
  343.9 7.8 %fusion.22 = f32[896,896]{1,0:T(8,128)} fusion(bf16[3072,3584]{1,0:T(8,128)(2,1)S(1)} %copy-done.18, s32[]{:T(128)S(6)} %select_n.191, s32[]{:T(128)S(6)} %select_n.209), kind=kOutput, calls=%fused_computation.23 | convolution fusion | flops 4932501504 | bytes 14221320 | tf_op jit(solution)/shard_map/dot_general | solution.py:112
  351.7 11.5 %fusion.20 = f32[896,896]{1,0:T(8,128)} fusion(bf16[3072,3584]{1,0:T(8,128)(2,1)} %constant_dynamic-update-slice_fusion, s32[]{:T(128)S(6)} %select_n.193, s32[]{:T(128)S(6)} %select_n.209), kind=kOutput, calls=%fused_computation.21 | convolution fusion | flops 4932501504 | bytes 14221320 | tf_op jit(solution)/shard_map/dot_general | solution.py:112
  363.2 10.0 %fusion.4 = f32[1024,1024]{1,0:T(8,128)S(1)} fusion(bf16[512,3584]{1,0:T(8,128)(2,1)S(1)} %copy-done.12, bf16[512,3584]{1,0:T(8,128)(2,1)S(1)} %copy-done.17, bf16[3072,3584]{1,0:T(8,128)(2,1)} %constant_dynamic-update-slice_fusion, s32[]{:T(128)S(6)} %select_n.186), kind=kOutput, calls=%fused_computation.4 | convolution fusion | flops 7530872832 | bytes 18874372 | tf_op jit(solution)/shard_map/dot_general | solution.py:112
  375.4 12.6 %fusion.8 = f32[1024,1024]{1,0:T(8,128)S(1)} fusion(bf16[512,3584]{1,0:T(8,128)(2,1)} %collective-permute-done.7, bf16[512,3584]{1,0:T(8,128)(2,1)} %get-tuple-element.9, bf16[3072,3584]{1,0:T(8,128)(2,1)} %constant_dynamic-update-slice_fusion, s32[]{:T(128)S(6)} %select_n.186), kind=kOutput, calls=%fused_computation.8 | convolution fusion | flops 7530872832 | bytes 18874372 | tf_op jit(solution)/shard_map/dot_general | solution.py:112
  390.6 10.2 %fusion = f32[1024,1024]{1,0:T(8,128)S(1)} fusion(bf16[512,3584]{1,0:T(8,128)(2,1)S(1)} %copy-done.14, bf16[512,3584]{1,0:T(8,128)(2,1)S(1)} %copy-done.1, bf16[3072,3584]{1,0:T(8,128)(2,1)} %constant_dynamic-update-slice_fusion, s32[]{:T(128)S(6)} %select_n.186), kind=kOutput, calls=%fused_computation | convolution fusion | flops 7530872832 | bytes 18874372 | tf_op jit(solution)/shard_map/dot_general | solution.py:112
  403.7 6.2 fusion.65
  409.8 6.2 fusion.63
  477.3 6.1 add_add_fusion
  492.5 18.7 %collective-permute-start.20 = (s16[528,1024]{1,0:T(8,128)(2,1)S(1)}, s16[528,1024]{1,0:T(8,128)(2,1)S(1)}, u32[]{:S(2)}, u32[]{:S(2)}) collective-permute-start(s16[528,1024]{1,0:T(8,128)(2,1)S(1)} %pad_add_fusion.3), channel_id=1, source_target_pairs={{4,6},{5,7},{6,4},{7,5},{8,10},{9,11},{10,8},{11,9},{20,22},{21,23... | collective-permute-start | bytes 3244040 | tf_op jit(solution)/shard_map/ppermute | solution.py:150
  513.2 8.8 %collective-permute-done.25 = s16[464,896]{1,0:T(8,128)(2,1)S(1)} collective-permute-done((s16[464,896]{1,0:T(8,128)(2,1)S(1)}, s16[464,896]{1,0:T(8,128)(2,1)S(1)}, u32[]{:S(2)}, u32[]{:S(2)}) %collective-permute-start.25) | collective-permute-done | bytes 831520 | tf_op jit(solution)/shard_map/ppermute | solution.py:150
  528.2 11.6 %collective-permute-done.27 = s16[464,896]{1,0:T(8,128)(2,1)} collective-permute-done((s16[464,896]{1,0:T(8,128)(2,1)S(1)}, s16[464,896]{1,0:T(8,128)(2,1)}, u32[]{:S(2)}, u32[]{:S(2)}) %collective-permute-start.27) | collective-permute-done | bytes 831520 | tf_op jit(solution)/shard_map/ppermute | solution.py:150
  543.7 19.2 %collective-permute-done.20 = s16[528,1024]{1,0:T(8,128)(2,1)S(1)} collective-permute-done((s16[528,1024]{1,0:T(8,128)(2,1)S(1)}, s16[528,1024]{1,0:T(8,128)(2,1)S(1)}, u32[]{:S(2)}, u32[]{:S(2)}) %collective-permute-start.20) | collective-permute-done | bytes 1081376 | tf_op jit(solution)/shard_map/ppermute | solution.py:150
  565.5 18.0 %collective-permute-done.22 = s16[528,1024]{1,0:T(8,128)(2,1)S(1)} collective-permute-done((s16[528,1024]{1,0:T(8,128)(2,1)S(1)}, s16[528,1024]{1,0:T(8,128)(2,1)S(1)}, u32[]{:S(2)}, u32[]{:S(2)}) %collective-permute-start.22) | collective-permute-done | bytes 1081376 | tf_op jit(solution)/shard_map/ppermute | solution.py:150
  586.8 8.3 %collective-permute-done.8 = s16[528,1024]{1,0:T(8,128)(2,1)S(1)} collective-permute-done((s16[528,1024]{1,0:T(8,128)(2,1)S(1)}, s16[528,1024]{1,0:T(8,128)(2,1)S(1)}, u32[]{:S(2)}, u32[]{:S(2)}) %collective-permute-start.8) | collective-permute-done | bytes 1081376 | tf_op jit(solution)/shard_map/ppermute | solution.py:150
  598.7 8.0 %collective-permute-done.18 = s16[528,1024]{1,0:T(8,128)(2,1)S(1)} collective-permute-done((s16[528,1024]{1,0:T(8,128)(2,1)S(1)}, s16[528,1024]{1,0:T(8,128)(2,1)S(1)}, u32[]{:S(2)}, u32[]{:S(2)}) %collective-permute-start.18) | collective-permute-done | bytes 1081376 | tf_op jit(solution)/shard_map/ppermute | solution.py:150
  (239 shorter events, 178.9 us)
Async XLA Ops:
  0.6 44.5 %collective-permute-start = (bf16[512,3584]{1,0:T(8,128)(2,1)}, bf16[512,3584]{1,0:T(8,128)(2,1)}, u32[]{:S(2)}, u32[]{:S(2)}) collective-permute-start(bf16[512,3584]{1,0:T(8,128)(2,1)} %param.5), channel_id=1, source_target_pairs={{1,2},{2,1},{5,6},{6,5},{9,10},{10,9},{13,14},{14,13},{17,18},{18,... | collective-permute-start | bytes 11010056 | tf_op jit(solution)/shard_map/ppermute | solution.py:150
  50.8 82.7 %collective-permute-start.3 = (bf16[512,3584]{1,0:T(8,128)(2,1)S(1)}, bf16[512,3584]{1,0:T(8,128)(2,1)S(1)}, u32[]{:S(2)}, u32[]{:S(2)}) collective-permute-start(bf16[512,3584]{1,0:T(8,128)(2,1)S(1)} %get-tuple-element.13), channel_id=1, source_target_pairs={{1,5},{2,6},{13,9},{14,10},{17,21},{18,22},{29,25},{30,26}} | collective-permute-start | bytes 11010056 | tf_op jit(solution)/shard_map/ppermute | solution.py:150
  137.2 82.7 %collective-permute-start.6 = (bf16[512,3584]{1,0:T(8,128)(2,1)S(1)}, bf16[512,3584]{1,0:T(8,128)(2,1)S(1)}, u32[]{:S(2)}, u32[]{:S(2)}) collective-permute-start(bf16[512,3584]{1,0:T(8,128)(2,1)S(1)} %get-tuple-element.13), channel_id=1, source_target_pairs={{5,9},{6,10},{9,5},{10,6},{21,25},{22,26},{25,21},{26,22}} | collective-permute-start | bytes 11010056 | tf_op jit(solution)/shard_map/ppermute | solution.py:150
  223.9 96.2 %collective-permute-start.7 = (bf16[512,3584]{1,0:T(8,128)(2,1)}, bf16[512,3584]{1,0:T(8,128)(2,1)}, u32[]{:S(2)}, u32[]{:S(2)}) collective-permute-start(bf16[512,3584]{1,0:T(8,128)(2,1)} %get-tuple-element.9), channel_id=1, source_target_pairs={{0,1},{1,0},{2,3},{3,2},{4,5},{5,4},{6,7},{7,6},{8,9},{9,8},{10,11... | collective-permute-start | bytes 11010056 | tf_op jit(solution)/shard_map/ppermute | solution.py:150
  227.2 25.1 %collective-permute-start.14 = (bf16[512,896]{1,0:T(8,128)(2,1)S(1)}, bf16[512,896]{1,0:T(8,128)(2,1)}, u32[]{:S(2)}, u32[]{:S(2)}) collective-permute-start(bf16[512,896]{1,0:T(8,128)(2,1)S(1)} %get-tuple-element.15), channel_id=1, source_target_pairs={{4,8},{5,9},{6,10},{7,11},{8,4},{9,5},{10,6},{11,7},{20,24},{21,25... | collective-permute-start | bytes 2752520 | tf_op jit(solution)/shard_map/ppermute | solution.py:150
  230.7 41.2 %collective-permute-start.10 = (bf16[512,896]{1,0:T(8,128)(2,1)S(1)}, bf16[512,896]{1,0:T(8,128)(2,1)S(1)}, u32[]{:S(2)}, u32[]{:S(2)}) collective-permute-start(bf16[512,896]{1,0:T(8,128)(2,1)S(1)} %get-tuple-element.17), channel_id=1, source_target_pairs={{4,8},{5,9},{6,10},{7,11},{8,4},{9,5},{10,6},{11,7},{20,24},{21,25... | collective-permute-start | bytes 2752520 | tf_op jit(solution)/shard_map/ppermute | solution.py:150
  233.0 58.5 %collective-permute-start.12 = (bf16[512,896]{1,0:T(8,128)(2,1)S(1)}, bf16[512,896]{1,0:T(8,128)(2,1)S(1)}, u32[]{:S(2)}, u32[]{:S(2)}) collective-permute-start(bf16[512,896]{1,0:T(8,128)(2,1)S(1)} %get-tuple-element.16), channel_id=1, source_target_pairs={{4,8},{5,9},{6,10},{7,11},{8,4},{9,5},{10,6},{11,7},{20,24},{21,25... | collective-permute-start | bytes 2752520 | tf_op jit(solution)/shard_map/ppermute | solution.py:150
  236.5 74.3 %collective-permute-start.16 = (bf16[512,896]{1,0:T(8,128)(2,1)}, bf16[512,896]{1,0:T(8,128)(2,1)S(1)}, u32[]{:S(2)}, u32[]{:S(2)}) collective-permute-start(bf16[512,896]{1,0:T(8,128)(2,1)} %get-tuple-element.14), channel_id=1, source_target_pairs={{4,8},{5,9},{6,10},{7,11},{8,4},{9,5},{10,6},{11,7},{20,24},{21,25... | collective-permute-start | bytes 2752520 | tf_op jit(solution)/shard_map/ppermute | solution.py:150
  252.3 60.9 %collective-permute-start.15 = (bf16[512,896]{1,0:T(8,128)(2,1)}, bf16[512,896]{1,0:T(8,128)(2,1)}, u32[]{:S(2)}, u32[]{:S(2)}) collective-permute-start(bf16[512,896]{1,0:T(8,128)(2,1)} %collective-permute-done.14), channel_id=1, source_target_pairs={{0,1},{1,0},{2,3},{3,2},{4,5},{5,4},{6,7},{7,6},{8,9},{9,8},{10,11... | collective-permute-start | bytes 2752520 | tf_op jit(solution)/shard_map/ppermute | solution.py:150
  271.9 42.7 %collective-permute-start.11 = (bf16[512,896]{1,0:T(8,128)(2,1)S(1)}, bf16[512,896]{1,0:T(8,128)(2,1)}, u32[]{:S(2)}, u32[]{:S(2)}) collective-permute-start(bf16[512,896]{1,0:T(8,128)(2,1)S(1)} %collective-permute-done.10), channel_id=1, source_target_pairs={{0,1},{1,0},{2,3},{3,2},{4,5},{5,4},{6,7},{7,6},{8,9},{9,8},{10,11... | collective-permute-start | bytes 2752520 | tf_op jit(solution)/shard_map/ppermute | solution.py:150
  424.8 58.6 %collective-permute-start.28 = (s16[464,896]{1,0:T(8,128)(2,1)}, s16[464,896]{1,0:T(8,128)(2,1)}, u32[]{:S(2)}, u32[]{:S(2)}) collective-permute-start(s16[464,896]{1,0:T(8,128)(2,1)} %pad_add_fusion.11), channel_id=1, source_target_pairs={{4,4},{5,0},{6,7},{7,3},{8,8},{9,12},{10,11},{11,15},{20,20},{21,1... | collective-permute-start | bytes 2494472 | tf_op jit(solution)/shard_map/ppermute | solution.py:150
  428.9 56.5 %collective-permute-start.29 = (s16[464,896]{1,0:T(8,128)(2,1)}, s16[464,896]{1,0:T(8,128)(2,1)}, u32[]{:S(2)}, u32[]{:S(2)}) collective-permute-start(s16[464,896]{1,0:T(8,128)(2,1)} %pad_add_fusion.10), channel_id=1, source_target_pairs={{4,6},{5,2},{6,5},{7,1},{8,10},{9,14},{10,9},{11,13},{20,22},{21,1... | collective-permute-start | bytes 2494472 | tf_op jit(solution)/shard_map/ppermute | solution.py:150
  446.2 40.5 %collective-permute-start.30 = (s16[464,896]{1,0:T(8,128)(2,1)}, s16[464,896]{1,0:T(8,128)(2,1)}, u32[]{:S(2)}, u32[]{:S(2)}) collective-permute-start(s16[464,896]{1,0:T(8,128)(2,1)} %pad_add_fusion.9), channel_id=1, source_target_pairs={{4,4},{5,0},{6,7},{7,3},{8,8},{9,12},{10,11},{11,15},{20,20},{21,1... | collective-permute-start | bytes 2494472 | tf_op jit(solution)/shard_map/ppermute | solution.py:150
  449.7 42.8 %collective-permute-start.31 = (s16[464,896]{1,0:T(8,128)(2,1)}, s16[464,896]{1,0:T(8,128)(2,1)}, u32[]{:S(2)}, u32[]{:S(2)}) collective-permute-start(s16[464,896]{1,0:T(8,128)(2,1)} %pad_add_fusion.8), channel_id=1, source_target_pairs={{4,6},{5,2},{6,5},{7,1},{8,10},{9,14},{10,9},{11,13},{20,22},{21,1... | collective-permute-start | bytes 2494472 | tf_op jit(solution)/shard_map/ppermute | solution.py:150
  461.2 50.0 %collective-permute-start.24 = (s16[464,896]{1,0:T(8,128)(2,1)}, s16[464,896]{1,0:T(8,128)(2,1)}, u32[]{:S(2)}, u32[]{:S(2)}) collective-permute-start(s16[464,896]{1,0:T(8,128)(2,1)} %pad_add_fusion.15), channel_id=1, source_target_pairs={{4,4},{5,0},{6,7},{7,3},{8,8},{9,12},{10,11},{11,15},{20,20},{21,1... | collective-permute-start | bytes 2494472 | tf_op jit(solution)/shard_map/ppermute | solution.py:150
  483.5 38.4 %collective-permute-start.25 = (s16[464,896]{1,0:T(8,128)(2,1)S(1)}, s16[464,896]{1,0:T(8,128)(2,1)S(1)}, u32[]{:S(2)}, u32[]{:S(2)}) collective-permute-start(s16[464,896]{1,0:T(8,128)(2,1)S(1)} %pad_add_fusion.14), channel_id=1, source_target_pairs={{4,6},{5,2},{6,5},{7,1},{8,10},{9,14},{10,9},{11,13},{20,22},{21,1... | collective-permute-start | bytes 2494472 | tf_op jit(solution)/shard_map/ppermute | solution.py:150
  485.4 38.4 %collective-permute-start.26 = (s16[464,896]{1,0:T(8,128)(2,1)S(1)}, s16[464,896]{1,0:T(8,128)(2,1)S(1)}, u32[]{:S(2)}, u32[]{:S(2)}) collective-permute-start(s16[464,896]{1,0:T(8,128)(2,1)S(1)} %pad_add_fusion.13), channel_id=1, source_target_pairs={{4,4},{5,0},{6,7},{7,3},{8,8},{9,12},{10,11},{11,15},{20,20},{21,1... | collective-permute-start | bytes 2494472 | tf_op jit(solution)/shard_map/ppermute | solution.py:150
  486.8 53.1 %collective-permute-start.27 = (s16[464,896]{1,0:T(8,128)(2,1)S(1)}, s16[464,896]{1,0:T(8,128)(2,1)}, u32[]{:S(2)}, u32[]{:S(2)}) collective-permute-start(s16[464,896]{1,0:T(8,128)(2,1)S(1)} %pad_add_fusion.12), channel_id=1, source_target_pairs={{4,6},{5,2},{6,5},{7,1},{8,10},{9,14},{10,9},{11,13},{20,22},{21,1... | collective-permute-start | bytes 2494472 | tf_op jit(solution)/shard_map/ppermute | solution.py:150
  492.5 70.4 %collective-permute-start.20 = (s16[528,1024]{1,0:T(8,128)(2,1)S(1)}, s16[528,1024]{1,0:T(8,128)(2,1)S(1)}, u32[]{:S(2)}, u32[]{:S(2)}) collective-permute-start(s16[528,1024]{1,0:T(8,128)(2,1)S(1)} %pad_add_fusion.3), channel_id=1, source_target_pairs={{4,6},{5,7},{6,4},{7,5},{8,10},{9,11},{10,8},{11,9},{20,22},{21,23... | collective-permute-start | bytes 3244040 | tf_op jit(solution)/shard_map/ppermute | solution.py:150
  511.2 72.3 %collective-permute-start.22 = (s16[528,1024]{1,0:T(8,128)(2,1)S(1)}, s16[528,1024]{1,0:T(8,128)(2,1)S(1)}, u32[]{:S(2)}, u32[]{:S(2)}) collective-permute-start(s16[528,1024]{1,0:T(8,128)(2,1)S(1)} %pad_add_fusion.1), channel_id=1, source_target_pairs={{4,6},{5,7},{6,4},{7,5},{8,10},{9,11},{10,8},{11,9},{20,22},{21,23... | collective-permute-start | bytes 3244040 | tf_op jit(solution)/shard_map/ppermute | solution.py:150
  521.9 73.2 %collective-permute-start.8 = (s16[528,1024]{1,0:T(8,128)(2,1)S(1)}, s16[528,1024]{1,0:T(8,128)(2,1)S(1)}, u32[]{:S(2)}, u32[]{:S(2)}) collective-permute-start(s16[528,1024]{1,0:T(8,128)(2,1)S(1)} %pad_add_fusion.7), channel_id=1, source_target_pairs={{4,6},{5,7},{6,4},{7,5},{8,10},{9,11},{10,8},{11,9},{20,22},{21,23... | collective-permute-start | bytes 3244040 | tf_op jit(solution)/shard_map/ppermute | solution.py:150
  523.9 82.8 %collective-permute-start.18 = (s16[528,1024]{1,0:T(8,128)(2,1)S(1)}, s16[528,1024]{1,0:T(8,128)(2,1)S(1)}, u32[]{:S(2)}, u32[]{:S(2)}) collective-permute-start(s16[528,1024]{1,0:T(8,128)(2,1)S(1)} %pad_add_fusion.5), channel_id=1, source_target_pairs={{4,6},{5,7},{6,4},{7,5},{8,10},{9,11},{10,8},{11,9},{20,22},{21,23... | collective-permute-start | bytes 3244040 | tf_op jit(solution)/shard_map/ppermute | solution.py:150
  564.8 52.2 %collective-permute-start.21 = (s16[528,1024]{1,0:T(8,128)(2,1)S(1)}, s16[528,1024]{1,0:T(8,128)(2,1)S(1)}, u32[]{:S(2)}, u32[]{:S(2)}) collective-permute-start(s16[528,1024]{1,0:T(8,128)(2,1)S(1)} %pad_add_fusion.2), channel_id=1, source_target_pairs={{4,4},{5,0},{6,6},{7,2},{8,9},{9,13},{10,11},{11,15},{20,20},{21,1... | collective-permute-start | bytes 3244040 | tf_op jit(solution)/shard_map/ppermute | solution.py:150
  585.5 31.5 %collective-permute-start.23 = (s16[528,1024]{1,0:T(8,128)(2,1)S(1)}, s16[528,1024]{1,0:T(8,128)(2,1)S(1)}, u32[]{:S(2)}, u32[]{:S(2)}) collective-permute-start(s16[528,1024]{1,0:T(8,128)(2,1)S(1)} %pad_add_fusion), channel_id=1, source_target_pairs={{4,5},{5,1},{6,7},{7,3},{8,8},{9,12},{10,10},{11,14},{20,21},{21,1... | collective-permute-start | bytes 3244040 | tf_op jit(solution)/shard_map/ppermute | solution.py:150
  (46 other events, 462.3 us)

commit v3 on v1

--- a/solution.py
+++ b/solution.py
@@ -1,6 +1,10 @@
+import math
+
 import jax
 import jax.numpy as jnp
 from jax import lax
+from jax.experimental import pallas as pl
+from jax.experimental.pallas import tpu as pltpu
 from jax.sharding import PartitionSpec as P
 
 BETA = 0.9
@@ -17,7 +21,7 @@
     return list(range(count))
 
 
-def local(gradient, left_old, right_old, left_counts, right_counts):
+def ring(gradient, left_old, right_old, left_counts, right_counts):
     tile_rows, half_wide = gradient.shape
     count = lax.axis_size("row")
     strip_wide = half_wide // count
@@ -83,7 +87,388 @@
     return (left_state, left_fixed, right_state, right_fixed)
 
 
+GROUP = 64
+LEVELS = 16
+
+
+def pack(values, out_ref, at):
+    levels = []
+    for first in range(0, values.shape[0], GROUP):
+        block = values[first : first + GROUP]
+        most = jnp.maximum(jnp.max(jnp.abs(block), axis=0, keepdims=True), 1e-34)
+        level = jnp.ceil(jnp.log2(most) * 256.0)
+        inverse = 32767.0 * jnp.exp2(level * (-1.0 / 256.0))
+        coded = jnp.clip(jnp.round(block * inverse), -32767.0, 32767.0)
+        out_ref[at + first : at + first + GROUP] = coded.astype(jnp.int32).astype(jnp.int16)
+        levels.append(level)
+    return levels
+
+
+def put_levels(levels, out_ref, at):
+    levels = levels + [jnp.zeros_like(levels[0])] * (LEVELS - len(levels))
+    out_ref[at : at + LEVELS] = jnp.concatenate(levels, 0).astype(jnp.int32).astype(jnp.int16)
+
+
+def unpack(ref, index, rows, many):
+    level = ref[many * rows : many * rows + LEVELS].astype(jnp.int32).astype(jnp.float32)
+    step = jnp.exp2(level * (1.0 / 256.0)) * (1.0 / 32767.0)
+    parts = []
+    for group in range(rows // GROUP):
+        at = index * rows + group * GROUP
+        row = index * (rows // GROUP) + group
+        block = ref[at : at + GROUP].astype(jnp.int32).astype(jnp.float32)
+        parts.append(block * step[row : row + 1])
+    return jnp.concatenate(parts, 0)
+
+
+def decode(coded, rows):
+    wide = coded.shape[1]
+    level = coded[rows : rows + rows // GROUP].astype(jnp.float32)
+    step = jnp.exp2(level * (1.0 / 256.0)) * (1.0 / 32767.0)
+    grouped = coded[:rows].astype(jnp.float32).reshape(rows // GROUP, GROUP, wide)
+    return (grouped * step[:, None, :]).reshape(rows, wide)
+
+
+PARAMS = pltpu.CompilerParams(vmem_limit_bytes=48 * 2**20)
+FREE = pl.CostEstimate(flops=1, bytes_accessed=1, transcendentals=0)
+WHOLE = pl.BlockSpec(memory_space=pltpu.VMEM)
+SCALAR = pl.BlockSpec(memory_space=pltpu.SMEM)
+
+
+def kernel_call(body, flags, arrays, outs):
+    return pl.pallas_call(
+        body,
+        in_specs=[SCALAR] + [WHOLE] * len(arrays),
+        out_specs=[WHOLE] * len(outs),
+        out_shape=[jax.ShapeDtypeStruct(s, d) for s, d in outs],
+        compiler_params=PARAMS,
+        cost_estimate=FREE,
+    )(flags, *arrays)
+
+
+def pick(flag, size):
+    return pl.multiple_of(flag * size, GROUP)
+
+
+def left_terms(flags, rows, slots, before=None, last=True):
+    many, pieces = len(slots), len(rows)
+    tall, wide = rows[0][0].shape
+    block = math.gcd(wide, 896)
+    size = 2 * tall
+
+    def body(flag_ref, *refs):
+        rows_in, refs = refs[: 2 * pieces], refs[2 * pieces :]
+        slots_in, refs = refs[: many * pieces], refs[many * pieces :]
+        if before is not None:
+            before_in, refs = refs[:many], refs[many:]
+        outs = refs[:many]
+        step = pl.program_id(0)
+
+        @pl.when(step == 0)
+        def _():
+            for index in range(many):
+                outs[index][...] = jnp.zeros_like(outs[index]) if before is None else before_in[index][...]
+
+        for index in range(many):
+            for piece in range(pieces):
+                for half in range(2):
+                    outs[index][half * tall : (half + 1) * tall] += dot(
+                        rows_in[2 * piece + half][...], slots_in[index * pieces + piece][...], 1, 1
+                    )
+
+        if last:
+
+            @pl.when(step == pl.num_programs(0) - 1)
+            def _():
+                gone = 1 - flag_ref[0]
+                levels = []
+                for index in range(many):
+                    part = outs[index][pl.ds(pick(gone, tall), tall), :]
+                    levels += pack(part, refs[many], index * tall)
+                put_levels(levels, refs[many], many * tall)
+
+    moving = pl.BlockSpec((tall, block), lambda k: (0, k))
+    still = pl.BlockSpec((size, tall), lambda k: (0, 0))
+    arrays = [a for pair in rows for a in pair] + [b for slot in slots for b in slot]
+    specs = [SCALAR] + [moving] * len(arrays)
+    if before is not None:
+        arrays += before
+        specs += [still] * many
+    out_shape = [jax.ShapeDtypeStruct((size, tall), jnp.float32)] * many
+    out_specs = [still] * many
+    if last:
+        out_shape.append(jax.ShapeDtypeStruct((many * tall + LEVELS, tall), jnp.int16))
+        out_specs.append(pl.BlockSpec((many * tall + LEVELS, tall), lambda k: (0, 0)))
+    return pl.pallas_call(
+        body,
+        grid=(wide // block,),
+        in_specs=specs,
+        out_specs=out_specs,
+        out_shape=out_shape,
+        compiler_params=PARAMS,
+        cost_estimate=FREE,
+    )(flags, *arrays)
+
+
+def right_terms(terms, before=None, last=False):
+    wide = terms[0][1].shape[1]
+    strip = terms[0][0].shape[1]
+    block = math.gcd(wide, 896)
+
+    def body(*refs):
+        total = None if before is None else refs[2 * len(terms)][...]
+        for index in range(len(terms)):
+            term = dot(refs[2 * index][...], refs[2 * index + 1][...], 0, 0)
+            total = term if total is None else total + term
+        outs = refs[2 * len(terms) + (before is not None) :]
+        outs[0][...] = total
+        if last:
+            put_levels(pack(total, outs[1], 0), outs[1], strip)
+
+    specs = []
+    arrays = []
+    for strips, columns in terms:
+        arrays += [strips, columns]
+        specs += [
+            pl.BlockSpec(strips.shape, lambda k: (0, 0)),
+            pl.BlockSpec((columns.shape[0], block), lambda k: (0, k)),
+        ]
+    out = pl.BlockSpec((strip, block), lambda k: (0, k))
+    if before is not None:
+        arrays.append(before)
+        specs.append(out)
+    out_shape = [jax.ShapeDtypeStruct((strip, wide), jnp.float32)]
+    out_specs = [out]
+    if last:
+        out_shape.append(jax.ShapeDtypeStruct((strip + LEVELS, wide), jnp.int16))
+        out_specs.append(pl.BlockSpec((strip + LEVELS, block), lambda k: (0, k)))
+    return pl.pallas_call(
+        body,
+        grid=(wide // block,),
+        in_specs=specs,
+        out_specs=out_specs,
+        out_shape=out_shape,
+        compiler_params=PARAMS,
+        cost_estimate=FREE,
+    )(*arrays)
+
+
+def add_up(flags, products, coded):
+    rows, wide = products[0].shape[0] // 2, products[0].shape[1]
+    many = len(products)
+
+    def body(flag_ref, *refs):
+        coded_ref, total_ref, out_ref = refs[many:]
+        levels = []
+        for index in range(many):
+            kept = refs[index][pl.ds(pick(flag_ref[0], rows), rows), :]
+            total = kept + unpack(coded_ref, index, rows, many)
+            total_ref[index * rows : (index + 1) * rows] = total
+            levels += pack(total, out_ref, index * rows)
+        put_levels(levels, out_ref, many * rows)
+
+    outs = [((many * rows, wide), jnp.float32), ((many * rows + LEVELS, wide), jnp.int16)]
+    return kernel_call(body, flags, list(products) + [coded], outs)
+
+
+def dot(a, b, a_dim, b_dim):
+    return lax.dot_general(
+        a, b, (((a_dim,), (b_dim,)), ((), ())), preferred_element_type=jnp.float32
+    )
+
+
+AXES = ("row", "col")
+CHIPS = [(z, y) for z in range(4) for y in range(2)]
+
+
+def at(z, y, c):
+    return (z * 2 + y) * 2 + c
+
+
+def send(value, rule):
+    pairs = []
+    for z, y in CHIPS:
+        for c in range(2):
+            dest = rule(z, y, c)
+            if dest is not None:
+                pairs.append((at(z, y, c), at(*dest)))
+    return lax.ppermute(value, AXES, pairs)
+
+
+def middle(z):
+    return z in (1, 2)
+
+
+def to_line(z, y, c):
+    return (z, c, y) if c != y else None
+
+
+def pair_line(z, y, c):
+    return (z ^ 1, c, y)
+
+
+def across_line(z, y, c):
+    return (3 - z, c, y) if middle(z) else None
+
+
+def across(z, y, c):
+    return (3 - z, y, c) if middle(z) else None
+
+
+def outward(z, y, c):
+    return (z ^ 1, y, c) if middle(z) else None
+
+
+def beside(z, y, c):
+    return (z, y, 1 - c)
+
+
+def other_y(z, y, c):
+    return (z, 1 - y, c)
+
+
+def to_home(z, y, c):
+    return (z, y, 1 - c) if c != z // 2 else None
+
+
+def to_away(z, y, c):
+    return (z, y, 1 - c) if c == z // 2 else None
+
+
+def line_gather(gradient, left_old, right_old, left_counts, right_counts):
+    tile_rows, half_wide = gradient.shape
+    wide = half_wide // 2
+    chunk = half_wide // 4
+    strip = half_wide // 8
+    my_row = lax.axis_index("row")
+    c = lax.axis_index("col")
+    z, y = my_row // 2, my_row % 2
+    side = (z >= 2).astype(jnp.int32)
+    is_middle = (z == 1) | (z == 2)
+    straight = c == y
+    flags = jnp.stack([jnp.where(straight, 0, 1)]).astype(jnp.int32)
+    strip_at = (2 * (z - 2 * side) + c) * strip
+
+    def tie(*values):
+        return lax.optimization_barrier(tuple(values))
+
+    def strips_of(pair):
+        return [lax.dynamic_slice_in_dim(part, strip_at + side * wide, strip, 1) for part in pair]
+
+    def half_of(value, which):
+        return lax.dynamic_slice_in_dim(value, which * wide, wide, 1)
+
+    def terms(strips, pair):
+        return list(zip(strips, pair))
+
+    mate = send(gradient, pair_line)
+    cross = send(gradient, across_line)
+    gradient_t, mate, cross = tie(gradient, mate, cross)
+    far = send(mate, across)
+    near = send(cross, outward)
+    swapped = send(gradient_t, to_line)
+    mates = (mate, send(mate, beside))
+    [right] = right_terms(terms(strips_of(mates), mates))
+
+    right, swapped = tie(right, swapped)
+    mine = jnp.where(straight, gradient, swapped)
+    own = (mine, jnp.concatenate([send(mine[:, at : at + chunk], beside) for at in range(0, half_wide, chunk)], 1))
+    own_product, mate_product, same_coded = left_terms(flags, [own], [[mine], [mate]])
+    same_products = [own_product, mate_product]
+    same_got = send(same_coded, other_y)
+    [right] = right_terms(terms(strips_of(own), own), right)
+    own_home = tuple(half_of(part, side) for part in own)
+    own_away = tuple(half_of(part, 1 - side) for part in own)
+
+    right, same_coded, near, far = tie(right, same_coded, near, far)
+    far_home, far_away = half_of(far, side), half_of(far, 1 - side)
+    far_first, far_second = far_away[:, :chunk], far_away[:, chunk:]
+    end_home = send(far_home, outward)
+    near = jnp.where(is_middle, cross, near)
+    nears = (near, send(near, beside))
+    same_total, same_out = add_up(flags, same_products, same_got)
+    same_other = send(same_out, to_home)
+    near_product, near_coded = left_terms(flags, [own], [[near]])
+    near_got = send(near_coded, other_y)
+    far_first, far_second, near_coded, same_out = tie(far_first, far_second, near_coded, same_out)
+    end_first = send(far_first, outward)
+    end_second = send(far_second, outward)
+    [right] = right_terms(terms(strips_of(nears), nears), right)
+    right_home, right_away = half_of(right, side), half_of(right, 1 - side)
+
+    right_home, right_away, end_home = tie(right_home, right_away, end_home)
+    end_home = jnp.where(is_middle, far_home, end_home)
+    ends_home = (end_home, send(end_home, beside))
+    [far_product] = left_terms(flags, [own_home], [[end_home]], last=False)
+    near_total, near_out = add_up(flags, [near_product], near_got)
+    near_other = send(near_out, to_away)
+    strips = [lax.dynamic_slice_in_dim(part, strip_at, strip, 1) for part in ends_home]
+    right_home, home_coded = right_terms(terms(strips, ends_home), right_home, last=True)
+    home_got = send(home_coded, to_line)
+
+    home_coded, far_product, end_first = tie(home_coded, far_product, end_first)
+    end_first = jnp.where(is_middle, far_first, end_first)
+    ends_first = (end_first, send(end_first, beside))
+    first_rows = tuple(part[:, :chunk] for part in own_away)
+    [far_product] = left_terms(flags, [first_rows], [[end_first]], [far_product], last=False)
+    right_first, first_coded = right_terms(terms(strips, ends_first), right_away[:, :chunk], last=True)
+    first_got = send(first_coded, to_line)
+
+    first_coded, far_product, end_second = tie(first_coded, far_product, end_second)
+    end_second = jnp.where(is_middle, far_second, end_second)
+    ends_second = (end_second, send(end_second, beside))
+    second_rows = tuple(part[:, chunk:] for part in own_away)
+    far_product, far_coded = left_terms(flags, [second_rows], [[end_second]], [far_product])
+    far_got = send(far_coded, other_y)
+    right_second, second_coded = right_terms(terms(strips, ends_second), right_away[:, chunk:], last=True)
+    second_coded, far_got = tie(second_coded, far_got)
+    second_got = send(second_coded, to_line)
+    far_total, far_out = add_up(flags, [far_product], far_got)
+    far_other = send(far_out, to_away)
+
+    home = jnp.where(straight, right_home, decode(home_got, strip))
+    away = jnp.concatenate(
+        [
+            jnp.where(straight, right_first, decode(first_got, strip)),
+            jnp.where(straight, right_second, decode(second_got, strip)),
+        ],
+        1,
+    )
+    gram_right = jnp.concatenate(
+        [jnp.where(side == 0, home, away), jnp.where(side == 0, away, home)], 1
+    )
+    right_state = BETA * right_old + (1.0 - BETA) * gram_right[None]
+    right_fixed = right_state / denominator(right_counts)[:, None, None]
+
+    same_decoded = decode(jnp.concatenate([same_other[:tile_rows], same_other[2 * tile_rows : 2 * tile_rows + LEVELS]], 0), tile_rows), decode(
+        jnp.concatenate([same_other[tile_rows : 2 * tile_rows], same_other[2 * tile_rows + tile_rows // GROUP : 2 * tile_rows + LEVELS]], 0), tile_rows
+    )
+    own_pair = (same_total[:tile_rows], same_decoded[0])
+    mate_pair = (same_total[tile_rows:], same_decoded[1])
+    near_pair = (near_total, decode(near_other, tile_rows))
+    far_pair = (far_total, decode(far_other, tile_rows))
+    keeps_home = c == side
+    inner, outer = [], []
+    for index in range(2):
+        home_inner = jnp.where(is_middle, own_pair[index], mate_pair[index])
+        home_outer = jnp.where(is_middle, mate_pair[index], own_pair[index])
+        inner.append(jnp.where(keeps_home, home_inner, near_pair[index]))
+        outer.append(jnp.where(keeps_home, home_outer, far_pair[index]))
+    first_core = c == 0
+    inner = [jnp.where(first_core, inner[0], inner[1]), jnp.where(first_core, inner[1], inner[0])]
+    outer = [jnp.where(first_core, outer[0], outer[1]), jnp.where(first_core, outer[1], outer[0])]
+    gram_left = jnp.concatenate(
+        [jnp.where(first_core, outer[i], inner[i]) for i in range(2)]
+        + [jnp.where(first_core, inner[i], outer[i]) for i in range(2)],
+        1,
+    )
+    left_state = BETA * left_old + (1.0 - BETA) * gram_left
+    left_fixed = left_state / denominator(left_counts)
+    return (left_state, left_fixed, right_state, right_fixed)
+
+
 def solution(mesh):
+    local = line_gather if mesh.shape["row"] == 8 else ring
     return jax.shard_map(
         local,
         mesh=mesh,

time: 371 us -> 366 us (0.987)
  matrix products: 124 us -> 0 us
  Pallas kernels: 0 us -> 75.4 us
  local copies, waits for them, and re-layouts: 8.93 us -> 52.3 us
  other arithmetic: 14 us -> 31.6 us
  starting transfers between devices: 45.1 us -> 39.3 us
  waiting for transfers between devices: 168 us -> 163 us
  between operations: 7.09 us -> 2.84 us
    dot_general x32 -> x0, matrix products: 124 us -> none  [the longest x16 101 us: consume(): lax.dot_general(strip, part, (((0,), (0,)), ((), ())), preferred_element_...]
    pallas_call x0 -> x14, Pallas kernels: none -> 75.4 us  [the longest x6 38.3 us: right_terms(): pl.pallas_call(body, grid=(wide // block,), in_specs=specs, out_specs=out...]
    unnamed x20 -> x67, local copies, waits for them, and re-layouts: 0.05 us -> 20.3 us
    select_n x0 -> x10, other arithmetic: none -> 17.3 us  [the longest x2 4.87 us: line_gather(): jnp.where(first_core, outer[i], inner[i])]
    dynamic_slice x7 -> x12, local copies, waits for them, and re-layouts: 4.21 us -> 20.8 us  [the longest x4 12.7 us: half_of(): return lax.dynamic_slice_in_dim(value, which * wide, wide, 1)]
    slice x1 -> x4, local copies, waits for them, and re-layouts: 3.67 us -> 9.89 us  [the longest x1 3.82 us: line_gather(): right_away[:, chunk:]]
    ppermute x30 -> x26, starting transfers between devices: 45.1 us -> 39.3 us  [send(): return lax.ppermute(value, AXES, pairs)]
    dynamic_update_slice x16 -> x0, other arithmetic: 5.2 us -> none  [consume(): lax.dynamic_update_slice(state['left'], product + other, (0, source * til...]
  transfers between devices with their start and end apart: 30 -> 26, of which waited for: 15 -> 10; matrix products, arithmetic and copies ran while one was open for 36% -> 15% of each run, Pallas kernels for 0% -> 21%
where the time goes in v3:
time: 366 us; the launch traced here: 364 us
  waiting for transfers between devices  163 us (45%)
  Pallas kernels  75.4 us (21%)
  local copies, waits for them, and re-layouts  52.3 us (14%)
  starting transfers between devices  39.3 us (11%)
  other arithmetic  31.6 us (9%)
    ppermute x26, waiting for transfers between devices, send(): return lax.ppermute(value, AXES, pairs)  163 us
    ppermute x26, starting transfers between devices, send(): return lax.ppermute(value, AXES, pairs)  39.3 us
    pallas_call x6, Pallas kernels, right_terms(): pl.pallas_call(body, grid=(wide // block,), in_specs=specs, out_specs=out...  38.3 us
    pallas_call x5, Pallas kernels, left_terms(): pl.pallas_call(body, grid=(wide // block,), in_specs=specs, out_specs=out...  31.6 us
    unnamed x67, local copies, waits for them, and re-layouts  20.3 us
    dynamic_slice x4, local copies, waits for them, and re-layouts, half_of(): return lax.dynamic_slice_in_dim(value, which * wide, wide, 1)  12.7 us
  transfers between devices with their start and end apart: 26, of which 10 were waited for; matrix products, arithmetic and copies ran while one was open for 15% of the time, Pallas kernels for 21%

profile of v3, /device:TPU:1, one launch (start us, length us, event | category | flops | bytes accessed | tf_op | source)
XLA Modules:
  0.0 364.1 jit_solution(15521235439788261511)
XLA Ops:
  0.6 3.7 %collective-permute-start = (bf16[512,3584]{1,0:T(8,128)(2,1)}, bf16[512,3584]{1,0:T(8,128)(2,1)}, u32[]{:S(2)}, u32[]{:S(2)}) collective-permute-start(bf16[512,3584]{1,0:T(8,128)(2,1)} %param.5), channel_id=1, source_target_pairs={{0,4},{1,6},{2,5},{3,7},{4,0},{5,2},{6,1},{7,3},{8,12},{9,14},{10,... | collective-permute-start | bytes 11010056 | tf_op jit(solution)/shard_map/ppermute | solution.py:295
  6.8 77.1 %collective-permute-done.refs_1_.refs_3_ = bf16[512,3584]{1,0:T(8,128)(2,1)} collective-permute-done((bf16[512,3584]{1,0:T(8,128)(2,1)}, bf16[512,3584]{1,0:T(8,128)(2,1)}, u32[]{:S(2)}, u32[]{:S(2)}) %collective-permute-start) | collective-permute-done | bytes 3670048 | tf_op jit(solution)/shard_map/ppermute | solution.py:295
  94.1 8.3 %shard_map.84.refs_4_ = f32[448,3584]{1,0:T(8,128)} custom-call(bf16[512,448]{1,0:T(8,128)(2,1)S(1)} %constant_dynamic-slice_fusion.18.refs_0_, bf16[512,3584]{1,0:T(8,128)(2,1)} %collective-permute-done.refs_1_.refs_3_, bf16[512,448]{1,0:T(8,128)(2,1)S(1)} %constant_dynamic-slice_fusion.17.refs_2_, bf16[512,3584]{1,0:T(8,128)(2,1)} %collective-permute-done.2.refs_3_), custom_call_target="tpu_custom_call" | custom-call | flops 1 | bytes 1 | tf_op jit(solution)/shard_map/pallas_call | solution.py:245
  102.4 26.3 %collective-permute-done.3 = bf16[512,3584]{1,0:T(8,128)(2,1)} collective-permute-done((bf16[512,3584]{1,0:T(8,128)(2,1)}, bf16[512,3584]{1,0:T(8,128)(2,1)}, u32[]{:S(2)}, u32[]{:S(2)}) %collective-permute-start.3) | collective-permute-done | bytes 3670048 | tf_op jit(solution)/shard_map/ppermute | solution.py:295
  146.8 12.4 %shard_map.85 = (f32[1024,512]{1,0:T(8,128)S(1)}, f32[1024,512]{1,0:T(8,128)S(1)}, s16[1040,512]{1,0:T(8,128)(2,1)S(1)}) custom-call(s32[1]{0:T(128)} %bitcast.flag_ref, bf16[512,3584]{1,0:T(8,128)(2,1)} %copy-done, bf16[512,3584]{1,0:T(8,128)(2,1)} %copy-done.20, bf16[512,3584]{1,0:T(8,128)(2,1)} %copy-done, ...), custom_call_target="tpu_custom_call" | custom-call | flops 1 | bytes 1 | tf_op jit(solution)/shard_map/pallas_call | solution.py:202
  162.4 9.0 %shard_map.87.refs_4_ = f32[448,3584]{1,0:T(8,128)} custom-call(bf16[512,448]{1,0:T(8,128)(2,1)S(1)} %constant_dynamic-slice_fusion.14.refs_0_, bf16[512,3584]{1,0:T(8,128)(2,1)S(1)} %copy-done.1, bf16[512,448]{1,0:T(8,128)(2,1)S(1)} %constant_dynamic-slice_fusion.13.refs_2_, bf16[512,3584]{1,0:T(8,128)(2,1)} %copy-done.20, f32[448,3584]{1,0:T(8,128)} %shard_map.84.refs_4_), custom_call_target="tpu_custom_call" | custom-call | flops 1 | bytes 1 | tf_op jit(solution)/shard_map/pallas_call | solution.py:245
  171.4 8.2 %collective-permute-done.9 = bf16[512,3584]{1,0:T(8,128)(2,1)} collective-permute-done((bf16[512,3584]{1,0:T(8,128)(2,1)}, bf16[512,3584]{1,0:T(8,128)(2,1)}, u32[]{:S(2)}, u32[]{:S(2)}) %collective-permute-start.9) | collective-permute-done | bytes 3670048 | tf_op jit(solution)/shard_map/ppermute | solution.py:295
  190.5 9.0 %shard_map.89 = f32[448,3584]{1,0:T(8,128)} custom-call(bf16[512,448]{1,0:T(8,128)(2,1)S(1)} %constant_dynamic-slice_fusion.10.refs_0_, bf16[512,3584]{1,0:T(8,128)(2,1)S(1)} %broadcast_select_fusion.refs_2_.refs_1_, bf16[512,448]{1,0:T(8,128)(2,1)S(1)} %constant_dynamic-slice_fusion.9.refs_2_, bf16[512,3584]{1,0:T(8,128)(2,1)} %copy-done.23, ...), custom_call_target="tpu_custom_call" | custom-call | flops 1 | bytes 1 | tf_op jit(solution)/shard_map/pallas_call | solution.py:245
  199.5 6.1 %constant_dynamic-slice_fusion.7 = (f32[448,1792]{1,0:T(8,128)}, f32[448,1792]{1,0:T(8,128)}) fusion(f32[448,3584]{1,0:T(8,128)} %shard_map.89, s32[]{:T(128)S(6)} %select_n.183, s32[]{:T(128)S(6)} %mul.173), kind=kLoop, calls=%fused_computation.54 | loop fusion | bytes 12845064 | tf_op jit(solution)/shard_map/dynamic_slice | solution.py:359
  205.6 22.2 %collective-permute-done.12 = bf16[512,1792]{1,0:T(8,128)(2,1)S(1)} collective-permute-done((bf16[512,1792]{1,0:T(8,128)(2,1)S(1)}, bf16[512,1792]{1,0:T(8,128)(2,1)S(1)}, u32[]{:S(2)}, u32[]{:S(2)}) %collective-permute-start.12) | collective-permute-done | bytes 1835040 | tf_op jit(solution)/shard_map/ppermute | solution.py:295
  231.3 7.8 %shard_map.88 = (f32[1024,512]{1,0:T(8,128)S(1)}, s16[528,512]{1,0:T(8,128)(2,1)S(1)}) custom-call(s32[1]{0:T(128)} %bitcast.flag_ref, bf16[512,3584]{1,0:T(8,128)(2,1)} %copy-done, bf16[512,3584]{1,0:T(8,128)(2,1)} %copy-done.20, bf16[512,3584]{1,0:T(8,128)(2,1)} %copy-done.2), custom_call_target="tpu_custom_call" | custom-call | flops 1 | bytes 1 | tf_op jit(solution)/shard_map/pallas_call | solution.py:202
  239.1 3.6 constant_dynamic-slice_fusion.12
  242.7 4.0 %shard_map.86 = (f32[1024,512]{1,0:T(8,128)S(1)}, s16[1040,512]{1,0:T(8,128)(2,1)}) custom-call(s32[1]{0:T(128)} %bitcast.flag_ref, f32[1024,512]{1,0:T(8,128)} %copy-done.14, f32[1024,512]{1,0:T(8,128)} %copy-done.15, s16[1040,512]{1,0:T(8,128)(2,1)S(1)} %collective-permute-done.8.refs_2_), custom_call_target="tpu_custom_call" | custom-call | flops 1 | bytes 1 | tf_op jit(solution)/shard_map/pallas_call | solution.py:139
  256.7 4.5 %shard_map.91.refs_3_ = f32[1024,512]{1,0:T(8,128)} custom-call(s32[1]{0:T(128)} %bitcast.flag_ref, bf16[512,1792]{1,0:T(8,128)(2,1)S(1)} %copy-done.4, bf16[512,1792]{1,0:T(8,128)(2,1)S(1)} %copy-done.5, bf16[512,1792]{1,0:T(8,128)(2,1)S(1)} %broadcast_select_fusion.2.refs_1_.refs_2_), custom_call_target="tpu_custom_call" | custom-call | flops 1 | bytes 1 | tf_op jit(solution)/shard_map/pallas_call | solution.py:202
  262.8 6.1 %shard_map.90 = (f32[448,1792]{1,0:T(8,128)}, s16[464,1792]{1,0:T(8,128)(2,1)}) custom-call(bf16[512,448]{1,0:T(8,128)(2,1)S(1)} %constant_dynamic-slice_fusion.6.refs_0_, bf16[512,1792]{1,0:T(8,128)(2,1)S(1)} %broadcast_select_fusion.2.refs_1_.refs_2_, bf16[512,448]{1,0:T(8,128)(2,1)S(1)} %constant_dynamic-slice_fusion.5.refs_2_, ...), custom_call_target="tpu_custom_call" | custom-call | flops 1 | bytes 1 | tf_op jit(solution)/shard_map/pallas_call | solution.py:245
  275.7 3.5 collective-permute-start.23
  279.4 10.1 %collective-permute-done.21.refs_1_ = s16[528,512]{1,0:T(8,128)(2,1)S(1)} collective-permute-done((s16[528,512]{1,0:T(8,128)(2,1)S(1)}, s16[528,512]{1,0:T(8,128)(2,1)S(1)}, u32[]{:S(2)}, u32[]{:S(2)}) %collective-permute-start.21) | collective-permute-done | bytes 540704 | tf_op jit(solution)/shard_map/ppermute | solution.py:295
  293.1 4.8 %collective-permute-start.19 = (s16[1040,512]{1,0:T(8,128)(2,1)}, s16[1040,512]{1,0:T(8,128)(2,1)}, u32[]{:S(2)}, u32[]{:S(2)}) collective-permute-start(s16[1040,512]{1,0:T(8,128)(2,1)} %get-tuple-element.54), channel_id=1, source_target_pairs={{1,0},{3,2},{5,4},{7,6},{8,9},{10,11},{12,13},{14,15},{17,16},{19,... | collective-permute-start | bytes 3194888 | tf_op jit(solution)/shard_map/ppermute | solution.py:295
  298.0 3.8 %fusion.9 = (f32[448,896]{1,0:T(8,128)}, f32[448,896]{1,0:T(8,128)}) fusion(f32[448,1792]{1,0:T(8,128)} %get-tuple-element.62), kind=kLoop, calls=%fused_computation.66 | loop fusion | bytes 6422528 | tf_op jit(solution)/shard_map/slice | solution.py:423
  311.3 3.9 %shard_map.94 = (f32[1024,512]{1,0:T(8,128)S(1)}, s16[528,512]{1,0:T(8,128)(2,1)}) custom-call(s32[1]{0:T(128)} %bitcast.flag_ref, bf16[512,896]{1,0:T(8,128)(2,1)S(1)} %copy-done.6, bf16[512,896]{1,0:T(8,128)(2,1)S(1)} %get-tuple-element.94.refs_1_, bf16[512,896]{1,0:T(8,128)(2,1)S(1)} %broadcast_select_fusion.3.refs_2_.refs_1_, f32[1024,512]{1,0:T(8,128)} %copy-done.3), custom_call_target="tpu_custom_call" | custom-call | flops 1 | bytes 1 | tf_op jit(solution)/shard_map/pallas_call | solution.py:202
  318.1 4.1 %collective-permute-start.24 = (s16[464,896]{1,0:T(8,128)(2,1)S(1)}, s16[464,896]{1,0:T(8,128)(2,1)S(1)}, u32[]{:S(2)}, u32[]{:S(2)}) collective-permute-start(s16[464,896]{1,0:T(8,128)(2,1)S(1)} %get-tuple-element.63), channel_id=1, source_target_pairs={{1,2},{2,1},{5,6},{6,5},{9,10},{10,9},{13,14},{14,13},{17,18},{18,... | collective-permute-start | bytes 2494472 | tf_op jit(solution)/shard_map/ppermute | solution.py:295
  332.5 7.1 %collective-permute-done.24 = s16[464,896]{1,0:T(8,128)(2,1)S(1)} collective-permute-done((s16[464,896]{1,0:T(8,128)(2,1)S(1)}, s16[464,896]{1,0:T(8,128)(2,1)S(1)}, u32[]{:S(2)}, u32[]{:S(2)}) %collective-permute-start.24) | collective-permute-done | bytes 831520 | tf_op jit(solution)/shard_map/ppermute | solution.py:295
  350.1 3.9 %broadcast_divide_fusion.1 = (f32[512,2048]{1,0:T(8,128)}, f32[512,2048]{1,0:T(8,128)}) fusion(f32[]{:T(128)} %bitcast.5, f32[512,512]{1,0:T(8,128)S(1)} %broadcast_select_fusion.5, f32[512,512]{1,0:T(8,128)S(1)} %get-tuple-element.92, f32[512,512]{1,0:T(8,128)S(1)} %get-tuple-element.91, f32[512,512]{1,0:T(8,128)S(1)} %get-tuple-element.84, ...), kind=kLoop, calls=%fused_computation.12 | loop fusion | flops 7340032 | bytes 16777220 | tf_op jit(solution)/shard_map/div | solution.py:466
  358.5 5.7 %broadcast_divide_fusion = (f32[1,448,3584]{2,1,0:T(8,128)}, f32[1,448,3584]{2,1,0:T(8,128)}) fusion(f32[]{:T(128)} %bitcast.11, f32[1,448,1792]{2,1,0:T(8,128)S(1)} %get-tuple-element.88, f32[1,448,1792]{2,1,0:T(8,128)S(1)} %get-tuple-element.87, f32[1,448,3584]{2,1,0:T(8,128)S(1)} %bitcast.92), kind=kLoop, calls=%fused_computation.9 | loop fusion | flops 8028160 | bytes 25690116 | tf_op jit(solution)/shard_map/div | solution.py:441
  (146 shorter events, 106.0 us)
Async XLA Ops:
  0.6 83.2 %collective-permute-start = (bf16[512,3584]{1,0:T(8,128)(2,1)}, bf16[512,3584]{1,0:T(8,128)(2,1)}, u32[]{:S(2)}, u32[]{:S(2)}) collective-permute-start(bf16[512,3584]{1,0:T(8,128)(2,1)} %param.5), channel_id=1, source_target_pairs={{0,4},{1,6},{2,5},{3,7},{4,0},{5,2},{6,1},{7,3},{8,12},{9,14},{10,... | collective-permute-start | bytes 11010056 | tf_op jit(solution)/shard_map/ppermute | solution.py:295
  4.3 79.5 %collective-permute-start.1 = (bf16[512,3584]{1,0:T(8,128)(2,1)}, bf16[512,3584]{1,0:T(8,128)(2,1)}, u32[]{:S(2)}, u32[]{:S(2)}) collective-permute-start(bf16[512,3584]{1,0:T(8,128)(2,1)} %param.5), channel_id=1, source_target_pairs={{4,8},{5,10},{6,9},{7,11},{8,4},{9,6},{10,5},{11,7},{20,24},{21,26... | collective-permute-start | bytes 11010056 | tf_op jit(solution)/shard_map/ppermute | solution.py:295
  83.9 7.3 %collective-permute-start.2 = (bf16[512,3584]{1,0:T(8,128)(2,1)}, bf16[512,3584]{1,0:T(8,128)(2,1)}, u32[]{:S(2)}, u32[]{:S(2)}) collective-permute-start(bf16[512,3584]{1,0:T(8,128)(2,1)} %collective-permute-done.refs_1_.refs_3_), channel_id=1, source_target_pairs={{0,1},{1,0},{2,3},{3,2},{4,5},{5,4},{6,7},{7,6},{8,9},{9,8},{10,11... | collective-permute-start | bytes 11010056 | tf_op jit(solution)/shard_map/ppermute | solution.py:295
  83.9 44.8 %collective-permute-start.3 = (bf16[512,3584]{1,0:T(8,128)(2,1)}, bf16[512,3584]{1,0:T(8,128)(2,1)}, u32[]{:S(2)}, u32[]{:S(2)}) collective-permute-start(bf16[512,3584]{1,0:T(8,128)(2,1)} %param.5), channel_id=1, source_target_pairs={{1,2},{2,1},{5,6},{6,5},{9,10},{10,9},{13,14},{14,13},{17,18},{18,... | collective-permute-start | bytes 11010056 | tf_op jit(solution)/shard_map/ppermute | solution.py:295
  87.3 84.1 %collective-permute-start.10 = (bf16[512,3584]{1,0:T(8,128)(2,1)}, bf16[512,3584]{1,0:T(8,128)(2,1)}, u32[]{:S(2)}, u32[]{:S(2)}) collective-permute-start(bf16[512,3584]{1,0:T(8,128)(2,1)} %collective-permute-done.refs_1_.refs_3_), channel_id=1, source_target_pairs={{4,8},{5,9},{6,10},{7,11},{8,4},{9,5},{10,6},{11,7},{20,24},{21,25... | collective-permute-start | bytes 11010056 | tf_op jit(solution)/shard_map/ppermute | solution.py:295
  92.6 87.1 %collective-permute-start.9 = (bf16[512,3584]{1,0:T(8,128)(2,1)}, bf16[512,3584]{1,0:T(8,128)(2,1)}, u32[]{:S(2)}, u32[]{:S(2)}) collective-permute-start(bf16[512,3584]{1,0:T(8,128)(2,1)} %collective-permute-done.1), channel_id=1, source_target_pairs={{4,0},{5,1},{6,2},{7,3},{8,12},{9,13},{10,14},{11,15},{20,16},{21,... | collective-permute-start | bytes 11010056 | tf_op jit(solution)/shard_map/ppermute | solution.py:295
  133.5 7.4 %collective-permute-start.5 = (bf16[512,896]{1,0:T(8,128)(2,1)S(1)}, bf16[512,896]{1,0:T(8,128)(2,1)}, u32[]{:S(2)}, u32[]{:S(2)}) collective-permute-start(bf16[512,896]{1,0:T(8,128)(2,1)S(1)} %get-tuple-element.99), channel_id=1, source_target_pairs={{0,1},{1,0},{2,3},{3,2},{4,5},{5,4},{6,7},{7,6},{8,9},{9,8},{10,11... | collective-permute-start | bytes 2752520 | tf_op jit(solution)/shard_map/ppermute | solution.py:295
  134.0 8.3 %collective-permute-start.6 = (bf16[512,896]{1,0:T(8,128)(2,1)S(1)}, bf16[512,896]{1,0:T(8,128)(2,1)}, u32[]{:S(2)}, u32[]{:S(2)}) collective-permute-start(bf16[512,896]{1,0:T(8,128)(2,1)S(1)} %get-tuple-element.98), channel_id=1, source_target_pairs={{0,1},{1,0},{2,3},{3,2},{4,5},{5,4},{6,7},{7,6},{8,9},{9,8},{10,11... | collective-permute-start | bytes 2752520 | tf_op jit(solution)/shard_map/ppermute | solution.py:295
  182.1 6.6 %collective-permute-start.11 = (bf16[512,3584]{1,0:T(8,128)(2,1)S(1)}, bf16[512,3584]{1,0:T(8,128)(2,1)S(1)}, u32[]{:S(2)}, u32[]{:S(2)}) collective-permute-start(bf16[512,3584]{1,0:T(8,128)(2,1)S(1)} %broadcast_select_fusion.refs_2_.refs_1_), channel_id=1, source_target_pairs={{0,1},{1,0},{2,3},{3,2},{4,5},{5,4},{6,7},{7,6},{8,9},{9,8},{10,11... | collective-permute-start | bytes 11010056 | tf_op jit(solution)/shard_map/ppermute | solution.py:295
  185.0 42.9 %collective-permute-start.12 = (bf16[512,1792]{1,0:T(8,128)(2,1)S(1)}, bf16[512,1792]{1,0:T(8,128)(2,1)S(1)}, u32[]{:S(2)}, u32[]{:S(2)}) collective-permute-start(bf16[512,1792]{1,0:T(8,128)(2,1)S(1)} %constant_dynamic-slice_fusion.11), channel_id=1, source_target_pairs={{4,0},{5,1},{6,2},{7,3},{8,12},{9,13},{10,14},{11,15},{20,16},{21,... | collective-permute-start | bytes 5505032 | tf_op jit(solution)/shard_map/ppermute | solution.py:295
  186.4 56.3 %collective-permute-start.8 = (s16[1040,512]{1,0:T(8,128)(2,1)S(1)}, s16[1040,512]{1,0:T(8,128)(2,1)S(1)}, u32[]{:S(2)}, u32[]{:S(2)}) collective-permute-start(s16[1040,512]{1,0:T(8,128)(2,1)S(1)} %get-tuple-element.47), channel_id=1, source_target_pairs={{0,2},{1,3},{2,0},{3,1},{4,6},{5,7},{6,4},{7,5},{8,10},{9,11},{10,... | collective-permute-start | bytes 3194888 | tf_op jit(solution)/shard_map/ppermute | solution.py:295
  229.7 31.7 %collective-permute-start.13 = (bf16[512,1792]{1,0:T(8,128)(2,1)S(1)}, bf16[512,1792]{1,0:T(8,128)(2,1)}, u32[]{:S(2)}, u32[]{:S(2)}) collective-permute-start(bf16[512,1792]{1,0:T(8,128)(2,1)S(1)} %broadcast_select_fusion.2.refs_1_.refs_2_), channel_id=1, source_target_pairs={{0,1},{1,0},{2,3},{3,2},{4,5},{5,4},{6,7},{7,6},{8,9},{9,8},{10,11... | collective-permute-start | bytes 5505032 | tf_op jit(solution)/shard_map/ppermute | solution.py:295
  248.0 24.2 %collective-permute-start.14 = (bf16[512,896]{1,0:T(8,128)(2,1)}, bf16[512,896]{1,0:T(8,128)(2,1)}, u32[]{:S(2)}, u32[]{:S(2)}) collective-permute-start(bf16[512,896]{1,0:T(8,128)(2,1)} %get-tuple-element.58), channel_id=1, source_target_pairs={{4,0},{5,1},{6,2},{7,3},{8,12},{9,13},{10,14},{11,15},{20,16},{21,... | collective-permute-start | bytes 2752520 | tf_op jit(solution)/shard_map/ppermute | solution.py:295
  273.4 32.6 %collective-permute-start.15 = (bf16[512,896]{1,0:T(8,128)(2,1)S(1)}, bf16[512,896]{1,0:T(8,128)(2,1)S(1)}, u32[]{:S(2)}, u32[]{:S(2)}) collective-permute-start(bf16[512,896]{1,0:T(8,128)(2,1)S(1)} %broadcast_select_fusion.4.refs_1_.refs_2_), channel_id=1, source_target_pairs={{0,1},{1,0},{2,3},{3,2},{4,5},{5,4},{6,7},{7,6},{8,9},{9,8},{10,11... | collective-permute-start | bytes 2752520 | tf_op jit(solution)/shard_map/ppermute | solution.py:295
  274.3 34.6 %collective-permute-start.16 = (bf16[512,896]{1,0:T(8,128)(2,1)S(1)}, bf16[512,896]{1,0:T(8,128)(2,1)S(1)}, u32[]{:S(2)}, u32[]{:S(2)}) collective-permute-start(bf16[512,896]{1,0:T(8,128)(2,1)S(1)} %copy-done.26), channel_id=1, source_target_pairs={{4,0},{5,1},{6,2},{7,3},{8,12},{9,13},{10,14},{11,15},{20,16},{21,... | collective-permute-start | bytes 2752520 | tf_op jit(solution)/shard_map/ppermute | solution.py:295
  275.6 13.9 %collective-permute-start.21 = (s16[528,512]{1,0:T(8,128)(2,1)S(1)}, s16[528,512]{1,0:T(8,128)(2,1)S(1)}, u32[]{:S(2)}, u32[]{:S(2)}) collective-permute-start(s16[528,512]{1,0:T(8,128)(2,1)S(1)} %get-tuple-element.53), channel_id=1, source_target_pairs={{0,2},{1,3},{2,0},{3,1},{4,6},{5,7},{6,4},{7,5},{8,10},{9,11},{10,... | collective-permute-start | bytes 1622024 | tf_op jit(solution)/shard_map/ppermute | solution.py:295
  275.7 56.1 %collective-permute-start.23 = (s16[464,1792]{1,0:T(8,128)(2,1)}, s16[464,1792]{1,0:T(8,128)(2,1)}, u32[]{:S(2)}, u32[]{:S(2)}) collective-permute-start(s16[464,1792]{1,0:T(8,128)(2,1)} %get-tuple-element.60), channel_id=1, source_target_pairs={{1,2},{2,1},{5,6},{6,5},{9,10},{10,9},{13,14},{14,13},{17,18},{18,... | collective-permute-start | bytes 4988936 | tf_op jit(solution)/shard_map/ppermute | solution.py:295
  291.7 26.4 %collective-permute-start.22 = (s16[528,512]{1,0:T(8,128)(2,1)}, s16[528,512]{1,0:T(8,128)(2,1)}, u32[]{:S(2)}, u32[]{:S(2)}) collective-permute-start(s16[528,512]{1,0:T(8,128)(2,1)} %get-tuple-element.75), channel_id=1, source_target_pairs={{0,1},{2,3},{4,5},{6,7},{9,8},{11,10},{13,12},{15,14},{16,17},{18,... | collective-permute-start | bytes 1622024 | tf_op jit(solution)/shard_map/ppermute | solution.py:295
  293.1 29.8 %collective-permute-start.19 = (s16[1040,512]{1,0:T(8,128)(2,1)}, s16[1040,512]{1,0:T(8,128)(2,1)}, u32[]{:S(2)}, u32[]{:S(2)}) collective-permute-start(s16[1040,512]{1,0:T(8,128)(2,1)} %get-tuple-element.54), channel_id=1, source_target_pairs={{1,0},{3,2},{5,4},{7,6},{8,9},{10,11},{12,13},{14,15},{17,16},{19,... | collective-permute-start | bytes 3194888 | tf_op jit(solution)/shard_map/ppermute | solution.py:295
  311.2 12.5 %collective-permute-start.17 = (bf16[512,896]{1,0:T(8,128)(2,1)S(1)}, bf16[512,896]{1,0:T(8,128)(2,1)}, u32[]{:S(2)}, u32[]{:S(2)}) collective-permute-start(bf16[512,896]{1,0:T(8,128)(2,1)S(1)} %broadcast_select_fusion.3.refs_2_.refs_1_), channel_id=1, source_target_pairs={{0,1},{1,0},{2,3},{3,2},{4,5},{5,4},{6,7},{7,6},{8,9},{9,8},{10,11... | collective-permute-start | bytes 2752520 | tf_op jit(solution)/shard_map/ppermute | solution.py:295
  316.5 13.6 %collective-permute-start.18 = (s16[528,512]{1,0:T(8,128)(2,1)}, s16[528,512]{1,0:T(8,128)(2,1)S(1)}, u32[]{:S(2)}, u32[]{:S(2)}) collective-permute-start(s16[528,512]{1,0:T(8,128)(2,1)} %get-tuple-element.69), channel_id=1, source_target_pairs={{0,2},{1,3},{2,0},{3,1},{4,6},{5,7},{6,4},{7,5},{8,10},{9,11},{10,... | collective-permute-start | bytes 1622024 | tf_op jit(solution)/shard_map/ppermute | solution.py:295
  318.1 21.5 %collective-permute-start.24 = (s16[464,896]{1,0:T(8,128)(2,1)S(1)}, s16[464,896]{1,0:T(8,128)(2,1)S(1)}, u32[]{:S(2)}, u32[]{:S(2)}) collective-permute-start(s16[464,896]{1,0:T(8,128)(2,1)S(1)} %get-tuple-element.63), channel_id=1, source_target_pairs={{1,2},{2,1},{5,6},{6,5},{9,10},{10,9},{13,14},{14,13},{17,18},{18,... | collective-permute-start | bytes 2494472 | tf_op jit(solution)/shard_map/ppermute | solution.py:295
  330.5 12.1 %collective-permute-start.20 = (s16[528,512]{1,0:T(8,128)(2,1)S(1)}, s16[528,512]{1,0:T(8,128)(2,1)S(1)}, u32[]{:S(2)}, u32[]{:S(2)}) collective-permute-start(s16[528,512]{1,0:T(8,128)(2,1)S(1)} %get-tuple-element.72), channel_id=1, source_target_pairs={{0,1},{2,3},{4,5},{6,7},{9,8},{11,10},{13,12},{15,14},{16,17},{18,... | collective-permute-start | bytes 1622024 | tf_op jit(solution)/shard_map/ppermute | solution.py:295
  340.0 14.0 %collective-permute-start.25 = (s16[464,896]{1,0:T(8,128)(2,1)S(1)}, s16[464,896]{1,0:T(8,128)(2,1)S(1)}, u32[]{:S(2)}, u32[]{:S(2)}) collective-permute-start(s16[464,896]{1,0:T(8,128)(2,1)S(1)} %get-tuple-element.79), channel_id=1, source_target_pairs={{1,2},{2,1},{5,6},{6,5},{9,10},{10,9},{13,14},{14,13},{17,18},{18,... | collective-permute-start | bytes 2494472 | tf_op jit(solution)/shard_map/ppermute | solution.py:295
  (34 other events, 257.1 us)

commit v4 on v1

--- a/solution.py
+++ b/solution.py
@@ -1,6 +1,10 @@
+import math
+
 import jax
 import jax.numpy as jnp
 from jax import lax
+from jax.experimental import pallas as pl
+from jax.experimental.pallas import tpu as pltpu
 from jax.sharding import PartitionSpec as P
 
 BETA = 0.9
@@ -17,7 +21,7 @@
     return list(range(count))
 
 
-def local(gradient, left_old, right_old, left_counts, right_counts):
+def ring(gradient, left_old, right_old, left_counts, right_counts):
     tile_rows, half_wide = gradient.shape
     count = lax.axis_size("row")
     strip_wide = half_wide // count
@@ -83,7 +87,448 @@
     return (left_state, left_fixed, right_state, right_fixed)
 
 
+GROUP = 64
+LEVELS = 16
+
+
+def pack(values, out_ref, at):
+    levels = []
+    for first in range(0, values.shape[0], GROUP):
+        block = values[first : first + GROUP]
+        most = jnp.maximum(jnp.max(jnp.abs(block), axis=0, keepdims=True), 1e-34)
+        level = jnp.ceil(jnp.log2(most) * 256.0)
+        inverse = 32767.0 * jnp.exp2(level * (-1.0 / 256.0))
+        coded = jnp.clip(jnp.round(block * inverse), -32767.0, 32767.0)
+        out_ref[at + first : at + first + GROUP] = coded.astype(jnp.int32).astype(jnp.int16)
+        levels.append(level)
+    return levels
+
+
+def put_levels(levels, out_ref, at):
+    levels = levels + [jnp.zeros_like(levels[0])] * (LEVELS - len(levels))
+    out_ref[at : at + LEVELS] = jnp.concatenate(levels, 0).astype(jnp.int32).astype(jnp.int16)
+
+
+def unpack(ref, index, rows, many):
+    level = ref[many * rows : many * rows + LEVELS].astype(jnp.int32).astype(jnp.float32)
+    step = jnp.exp2(level * (1.0 / 256.0)) * (1.0 / 32767.0)
+    parts = []
+    for group in range(rows // GROUP):
+        at = index * rows + group * GROUP
+        row = index * (rows // GROUP) + group
+        block = ref[at : at + GROUP].astype(jnp.int32).astype(jnp.float32)
+        parts.append(block * step[row : row + 1])
+    return jnp.concatenate(parts, 0)
+
+
+def decode(coded, rows):
+    wide = coded.shape[1]
+    level = coded[rows : rows + rows // GROUP].astype(jnp.float32)
+    step = jnp.exp2(level * (1.0 / 256.0)) * (1.0 / 32767.0)
+    grouped = coded[:rows].astype(jnp.float32).reshape(rows // GROUP, GROUP, wide)
+    return (grouped * step[:, None, :]).reshape(rows, wide)
+
+
+PARAMS = pltpu.CompilerParams(vmem_limit_bytes=48 * 2**20)
+FREE = pl.CostEstimate(flops=1, bytes_accessed=1, transcendentals=0)
+KEPT, PIECE_A, PIECE_B, SAME_HALF, MIDDLE, CORE = range(6)
+
+
+def spec(shape, index=None):
+    if index is None:
+        return pl.BlockSpec(shape, lambda k, flags: (0, 0))
+    return pl.BlockSpec(shape, lambda k, flags: (0, index(k, flags)))
+
+
+def whole(array):
+    return spec(array.shape)
+
+
+def kernel_call(body, flags, steps, ins, outs, aliases=None):
+    results = pl.pallas_call(
+        body,
+        grid_spec=pltpu.PrefetchScalarGridSpec(
+            num_scalar_prefetch=1,
+            grid=(steps,),
+            in_specs=[s for _, s in ins],
+            out_specs=[s for _, _, s in outs],
+        ),
+        out_shape=[jax.ShapeDtypeStruct(shape, dtype) for shape, dtype, _ in outs],
+        input_output_aliases=aliases or {},
+        compiler_params=PARAMS,
+        cost_estimate=FREE,
+    )(flags, *[array for array, _ in ins])
+    return list(results)
+
+
+def pick(flag, size):
+    return pl.multiple_of(flag * size, GROUP)
+
+
+def left_terms(flags, rows, slots, block, steps, at=None, before=None, last=True):
+    many = len(slots)
+    tall = rows[0].shape[0]
+    size = 2 * tall
+
+    def body(flag_ref, first_ref, second_ref, *refs):
+        slots_in, refs = refs[:many], refs[many:]
+        if before is not None:
+            before_in, refs = refs[:many], refs[many:]
+        outs = refs[:many]
+        step = pl.program_id(0)
+
+        @pl.when(step == 0)
+        def _():
+            for index in range(many):
+                outs[index][...] = jnp.zeros_like(outs[index]) if before is None else before_in[index][...]
+
+        for index in range(many):
+            for half, ref in enumerate((first_ref, second_ref)):
+                outs[index][half * tall : (half + 1) * tall] += dot(ref[...], slots_in[index][...], 1, 1)
+
+        if last:
+
+            @pl.when(step == pl.num_programs(0) - 1)
+            def _():
+                gone = 1 - flag_ref[KEPT]
+                levels = []
+                for index in range(many):
+                    part = outs[index][pl.ds(pick(gone, tall), tall), :]
+                    levels += pack(part, refs[many], index * tall)
+                put_levels(levels, refs[many], many * tall)
+
+    from_flag = lambda k, flags: k if at is None else k + flags[at]
+    ins = [(part, spec((tall, block), from_flag)) for part in rows]
+    ins += [(slot, spec((tall, block), lambda k, flags: k)) for slot in slots]
+    if before is not None:
+        ins += [(part, whole(part)) for part in before]
+    outs = [((size, tall), jnp.float32, spec((size, tall)))] * many
+    if last:
+        shape = (many * tall + LEVELS, tall)
+        outs.append((shape, jnp.int16, spec(shape)))
+    return kernel_call(body, flags, steps, ins, outs)
+
+
+def right_terms(flags, terms, block, steps, at=None, before=None, last=False):
+    wide = block * steps
+    strip = terms[0][0].shape[1]
+
+    def body(flag_ref, *refs):
+        total = None if before is None else refs[2 * len(terms)][...]
+        for index in range(len(terms)):
+            term = dot(refs[2 * index][...], refs[2 * index + 1][...], 0, 0)
+            total = term if total is None else total + term
+        outs = refs[2 * len(terms) + (before is not None) :]
+        outs[0][...] = total
+        if last:
+            put_levels(pack(total, outs[1], 0), outs[1], strip)
+
+    here = lambda k, flags: k
+    from_flag = lambda k, flags: k if at is None else k + flags[at]
+    ins = []
+    for strips, columns in terms:
+        ins += [(strips, whole(strips)), (columns, spec((columns.shape[0], block), here))]
+    if before is not None:
+        ins.append((before, spec((strip, block), from_flag)))
+    outs = [((strip, wide), jnp.float32, spec((strip, block), here))]
+    if last:
+        outs.append(((strip + LEVELS, wide), jnp.int16, spec((strip + LEVELS, block), here)))
+    return kernel_call(body, flags, steps, ins, outs)
+
+
+def add_up(flags, products, coded):
+    rows, wide = products[0].shape[0] // 2, products[0].shape[1]
+    many = len(products)
+
+    def body(flag_ref, *refs):
+        coded_ref, total_ref, out_ref = refs[many:]
+        levels = []
+        for index in range(many):
+            kept = refs[index][pl.ds(pick(flag_ref[KEPT], rows), rows), :]
+            total = kept + unpack(coded_ref, index, rows, many)
+            total_ref[index * rows : (index + 1) * rows] = total
+            levels += pack(total, out_ref, index * rows)
+        put_levels(levels, out_ref, many * rows)
+
+    ins = [(array, whole(array)) for array in list(products) + [coded]]
+    shapes = [((many * rows, wide), jnp.float32), ((many * rows + LEVELS, wide), jnp.int16)]
+    return kernel_call(body, flags, 1, ins, [(s, d, spec(s)) for s, d in shapes])
+
+
+def write_states(old, gram, scale, state_ref, fixed_ref, where):
+    state = BETA * old + (1.0 - BETA) * gram
+    state_ref[:, where] = state
+    fixed_ref[:, where] = state * scale
+
+
+def finish_right(flags, scale, old, value, coded, at, block, steps, written=None):
+    strip, wide = old.shape
+
+    def body(flag_ref, scale_ref, old_ref, value_ref, coded_ref, *refs):
+        state_ref, fixed_ref = refs[-2:]
+        everything = slice(None)
+
+        @pl.when(flag_ref[KEPT] == 0)
+        def _():
+            write_states(old_ref[...], value_ref[...], scale_ref[0], state_ref, fixed_ref, everything)
+
+        @pl.when(flag_ref[KEPT] == 1)
+        def _():
+            write_states(
+                old_ref[...], unpack(coded_ref, 0, strip, 1), scale_ref[0], state_ref, fixed_ref, everything
+            )
+
+    here = lambda k, flags: k
+    there = lambda k, flags: k + flags[at]
+    ins = [
+        (scale, pl.BlockSpec(memory_space=pltpu.SMEM)),
+        (old, spec((strip, block), there)),
+        (value, spec((strip, block), here)),
+        (coded, spec((strip + LEVELS, block), here)),
+    ]
+    aliases = None
+    if written is not None:
+        ins += [(array, pl.BlockSpec(memory_space=pl.ANY)) for array in written]
+        aliases = {5: 0, 6: 1}
+    outs = [((strip, wide), jnp.float32, spec((strip, block), there))] * 2
+    return kernel_call(body, flags, steps, ins, outs, aliases)
+
+
+def finish_left(flags, scale, old, same_total, same_other, total, other, inner, written=None):
+    tall, wide = total.shape
+    plane = 2 * wide
+
+    def body(flag_ref, scale_ref, old_ref, same_ref, same_other_ref, total_ref, other_ref, *refs):
+        state_ref, fixed_ref = refs[-2:]
+
+        def put(core, value):
+            where = slice(core * wide, (core + 1) * wide)
+            write_states(old_ref[:, where], value, scale_ref[0], state_ref, fixed_ref, where)
+
+        is_mate = 1 - flag_ref[MIDDLE] if inner else flag_ref[MIDDLE]
+        for core in range(2):
+            mine = flag_ref[CORE] == core
+            same = flag_ref[SAME_HALF] == 1
+
+            @pl.when(mine & same)
+            def _():
+                put(core, same_ref[pl.ds(pick(is_mate, tall), tall), :])
+
+            @pl.when(mine & jnp.logical_not(same))
+            def _():
+                put(core, total_ref[...])
+
+            for index in range(2):
+
+                @pl.when(jnp.logical_not(mine) & same & (is_mate == index))
+                def _():
+                    put(core, unpack(same_other_ref, index, tall, 2))
+
+            @pl.when(jnp.logical_not(mine) & jnp.logical_not(same))
+            def _():
+                put(core, unpack(other_ref, 0, tall, 1))
+
+    there = (lambda k, flags: 1 - flags[CORE]) if inner else (lambda k, flags: flags[CORE])
+    ins = [(scale, pl.BlockSpec(memory_space=pltpu.SMEM)), (old, spec((tall, plane), there))]
+    ins += [(array, whole(array)) for array in (same_total, same_other, total, other)]
+    aliases = None
+    if written is not None:
+        ins += [(array, pl.BlockSpec(memory_space=pl.ANY)) for array in written]
+        aliases = {7: 0, 8: 1}
+    outs = [(old.shape, jnp.float32, spec((tall, plane), there))] * 2
+    return kernel_call(body, flags, 1, ins, outs, aliases)
+
+
+def dot(a, b, a_dim, b_dim):
+    return lax.dot_general(
+        a, b, (((a_dim,), (b_dim,)), ((), ())), preferred_element_type=jnp.float32
+    )
+
+
+AXES = ("row", "col")
+CHIPS = [(z, y) for z in range(4) for y in range(2)]
+
+
+def at(z, y, c):
+    return (z * 2 + y) * 2 + c
+
+
+def send(value, rule):
+    pairs = []
+    for z, y in CHIPS:
+        for c in range(2):
+            dest = rule(z, y, c)
+            if dest is not None:
+                pairs.append((at(z, y, c), at(*dest)))
+    return lax.ppermute(value, AXES, pairs)
+
+
+def middle(z):
+    return z in (1, 2)
+
+
+def to_line(z, y, c):
+    return (z, c, y) if c != y else None
+
+
+def pair_line(z, y, c):
+    return (z ^ 1, c, y)
+
+
+def across_line(z, y, c):
+    return (3 - z, c, y) if middle(z) else None
+
+
+def across(z, y, c):
+    return (3 - z, y, c) if middle(z) else None
+
+
+def outward(z, y, c):
+    return (z ^ 1, y, c) if middle(z) else None
+
+
+def beside(z, y, c):
+    return (z, y, 1 - c)
+
+
+def other_y(z, y, c):
+    return (z, 1 - y, c)
+
+
+def to_home(z, y, c):
+    return (z, y, 1 - c) if c != z // 2 else None
+
+
+def to_away(z, y, c):
+    return (z, y, 1 - c) if c == z // 2 else None
+
+
+def line_gather(gradient, left_old, right_old, left_counts, right_counts):
+    tile_rows, half_wide = gradient.shape
+    block = half_wide // 4
+    strip = half_wide // 8
+    my_row = lax.axis_index("row")
+    c = lax.axis_index("col")
+    z, y = my_row // 2, my_row % 2
+    side = (z >= 2).astype(jnp.int32)
+    is_middle = (z == 1) | (z == 2)
+    straight = c == y
+    flags = jnp.stack(
+        [
+            jnp.where(straight, 0, 1),
+            side,
+            3 * (1 - side),
+            (c == side).astype(jnp.int32),
+            is_middle.astype(jnp.int32),
+            c,
+        ]
+    ).astype(jnp.int32)
+    strip_at = (2 * z + c) * strip
+
+    def tie(*values):
+        return lax.optimization_barrier(tuple(values))
+
+    def columns(value, first, count):
+        return lax.dynamic_slice_in_dim(value, first * block, count * block, 1)
+
+    def strips_of(pair, first=0):
+        return [lax.dynamic_slice_in_dim(part, strip_at - first, strip, 1) for part in pair]
+
+    def terms(strips, pair):
+        return list(zip(strips, pair))
+
+    mate_b = send(columns(gradient, 3 * side, 1), pair_line)
+    mate_a = send(columns(gradient, 1 - side, 3), pair_line)
+    cross = send(gradient, across_line)
+    gradient_t, mate_a, mate_b, cross = tie(gradient, mate_a, mate_b, cross)
+    far_a = send(mate_a, across)
+    far_b = send(mate_b, across)
+    near = send(cross, outward)
+    swapped = send(gradient_t, to_line)
+
+    def in_order(part_a, part_b):
+        return jnp.where(
+            side == 0, jnp.concatenate([part_b, part_a], 1), jnp.concatenate([part_a, part_b], 1)
+        )
+
+    mate = in_order(mate_a, mate_b)
+    mates = (mate, send(mate, beside))
+    mine = jnp.where(straight, gradient, swapped)
+    starts = range(0, half_wide, block)
+    own = (
+        mine,
+        jnp.concatenate(
+            [send(mine[:, first : first + block], beside) for first in starts], 1
+        ),
+    )
+    own_product, mate_product, same_coded = left_terms(flags, own, [mine, mate], block, 4)
+    same_products = [own_product, mate_product]
+    same_got = send(same_coded, other_y)
+    [right] = right_terms(
+        flags, terms(strips_of(own), own) + terms(strips_of(mates), mates), block, 4
+    )
+
+    right, same_coded, near, far_a, far_b = tie(right, same_coded, near, far_a, far_b)
+    end_a = send(far_a, outward)
+    near = jnp.where(is_middle, cross, near)
+    nears = (near, send(near, beside))
+    near_product, near_coded = left_terms(flags, own, [near], block, 4)
+    near_got = send(near_coded, other_y)
+    [right] = right_terms(flags, terms(strips_of(nears), nears), block, 4, before=right)
+    same_total, same_out = add_up(flags, same_products, same_got)
+    same_other = send(same_out, to_home)
+    near_got, right, same_out = tie(near_got, right, same_out)
+    near_total, near_out = add_up(flags, [near_product], near_got)
+    near_other = send(near_out, to_away)
+
+    right, near_out, end_a, same_other, near_other = tie(right, near_out, end_a, same_other, near_other)
+    far_b, end_a = tie(far_b, end_a)
+    end_b = send(far_b, outward)
+    end_a = jnp.where(is_middle, far_a, end_a)
+    ends_a = (end_a, send(end_a, beside))
+    [far_product] = left_terms(flags, own, [end_a], block, 3, at=PIECE_A, last=False)
+    strips = strips_of(ends_a, side * block)
+    right_a, coded_a = right_terms(
+        flags, terms(strips, ends_a), block, 3, at=PIECE_A, before=right, last=True
+    )
+    got_a = send(coded_a, to_line)
+    left_scale = 1.0 / denominator(left_counts).reshape(1)
+    right_scale = 1.0 / denominator(right_counts)
+    coded_a, near_other, same_other = tie(coded_a, near_other, same_other)
+    left_done = finish_left(
+        flags, left_scale, left_old, same_total, same_other, near_total, near_other, True
+    )
+
+    left_done[0], coded_a, far_product, end_b = tie(left_done[0], coded_a, far_product, end_b)
+    end_b = jnp.where(is_middle, far_b, end_b)
+    ends_b = (end_b, send(end_b, beside))
+    far_product, far_coded = left_terms(
+        flags, own, [end_b], block, 1, at=PIECE_B, before=[far_product]
+    )
+    far_got = send(far_coded, other_y)
+    right_b, coded_b = right_terms(
+        flags, terms(strips, ends_b), block, 1, at=PIECE_B, before=right, last=True
+    )
+    got_b = send(coded_b, to_line)
+    old = right_old[0]
+    coded_b, far_got = tie(coded_b, far_got)
+    far_total, far_out = add_up(flags, [far_product], far_got)
+    far_other = send(far_out, to_away)
+    far_out, got_a = tie(far_out, got_a)
+    right_done = finish_right(flags, right_scale, old, right_a, got_a, PIECE_A, block, 3)
+    right_done[0], got_b = tie(right_done[0], got_b)
+    right_state, right_fixed = finish_right(
+        flags, right_scale, old, right_b, got_b, PIECE_B, block, 1, right_done
+    )
+    far_other, right_state = tie(far_other, right_state)
+    left_state, left_fixed = finish_left(
+        flags, left_scale, left_old, same_total, same_other, far_total, far_other, False, left_done
+    )
+    return (left_state, left_fixed, right_state[None], right_fixed[None])
+
+
 def solution(mesh):
+    local = line_gather if mesh.shape["row"] == 8 else ring
     return jax.shard_map(
         local,
         mesh=mesh,

time: 371 us -> 342 us (0.922)
  matrix products: 124 us -> 0 us
  Pallas kernels: 0 us -> 97.1 us
  local copies, waits for them, and re-layouts: 8.93 us -> 27.7 us
  starting transfers between devices: 45.1 us -> 34.7 us
  waiting for transfers between devices: 168 us -> 160 us
  between operations: 7.09 us -> 2.6 us
    dot_general x32 -> x0, matrix products: 124 us -> none  [the longest x16 101 us: consume(): lax.dot_general(strip, part, (((0,), (0,)), ((), ())), preferred_element_...]
    pallas_call x0 -> x15, Pallas kernels: none -> 97.1 us  [kernel_call(): pl.pallas_call(body, grid_spec=pltpu.PrefetchScalarGridSpec(num_scalar_pr...]
    select_n x0 -> x5, other arithmetic: none -> 15.6 us  [the longest x1 5.52 us: in_order(): jnp.where(side == 0, jnp.concatenate([part_b, part_a], 1), jnp.concatenat...]
    unnamed x20 -> x43, local copies, waits for them, and re-layouts: 0.05 us -> 15.2 us
    ppermute x30 -> x25, starting transfers between devices: 45.1 us -> 34.7 us  [send(): return lax.ppermute(value, AXES, pairs)]
    div x1 -> x0, other arithmetic: 8.77 us -> none  [local(): left_fixed = left_state / denominator(left_counts)]
    ppermute x30 -> x25, waiting for transfers between devices: 168 us -> 160 us  [send(): return lax.ppermute(value, AXES, pairs)]
    dynamic_slice x7 -> x10, local copies, waits for them, and re-layouts: 4.21 us -> 10.9 us  [the longest x8 7.63 us: strips_of(): lax.dynamic_slice_in_dim(part, strip_at - first, strip, 1)]
  transfers between devices with their start and end apart: 30 -> 25, of which waited for: 15 -> 7; matrix products, arithmetic and copies ran while one was open for 36% -> 7% of each run, Pallas kernels for 0% -> 27%
where the time goes in v4:
time: 342 us; the launch traced here: 338 us
  waiting for transfers between devices  160 us (47%)
  Pallas kernels  97.1 us (28%)
  starting transfers between devices  34.7 us (10%)
  local copies, waits for them, and re-layouts  27.7 us (8%)
  other arithmetic  15.6 us (5%)
    ppermute x25, waiting for transfers between devices, send(): return lax.ppermute(value, AXES, pairs)  160 us
    pallas_call x15, Pallas kernels, kernel_call(): pl.pallas_call(body, grid_spec=pltpu.PrefetchScalarGridSpec(num_scalar_pr...  97.1 us
    ppermute x25, starting transfers between devices, send(): return lax.ppermute(value, AXES, pairs)  34.7 us
    unnamed x43, local copies, waits for them, and re-layouts  15.2 us
    dynamic_slice x8, local copies, waits for them, and re-layouts, strips_of(): lax.dynamic_slice_in_dim(part, strip_at - first, strip, 1)  7.63 us
  transfers between devices with their start and end apart: 25, of which 7 were waited for; matrix products, arithmetic and copies ran while one was open for 7% of the time, Pallas kernels for 27%

profile of v4, /device:TPU:1, one launch (start us, length us, event | category | flops | bytes accessed | tf_op | source)
XLA Modules:
  0.0 337.7 jit_solution(11559577877189132095)
XLA Ops:
  5.1 4.2 %collective-permute-start = (bf16[512,2688]{1,0:T(8,128)(2,1)S(1)}, bf16[512,2688]{1,0:T(8,128)(2,1)}, u32[]{:S(2)}, u32[]{:S(2)}) collective-permute-start(bf16[512,2688]{1,0:T(8,128)(2,1)S(1)} %constant_dynamic-slice_fusion.9), channel_id=1, source_target_pairs={{0,4},{1,6},{2,5},{3,7},{4,0},{5,2},{6,1},{7,3},{8,12},{9,14},{10,... | collective-permute-start | bytes 8257544 | tf_op jit(solution)/shard_map/ppermute | solution.py:363
  10.6 78.0 %collective-permute-done.1 = bf16[512,896]{1,0:T(8,128)(2,1)S(1)} collective-permute-done((bf16[512,896]{1,0:T(8,128)(2,1)S(1)}, bf16[512,896]{1,0:T(8,128)(2,1)S(1)}, u32[]{:S(2)}, u32[]{:S(2)}) %collective-permute-start.1) | collective-permute-done | bytes 917536 | tf_op jit(solution)/shard_map/ppermute | solution.py:363
  89.6 3.8 %collective-permute-start.3 = (bf16[512,3584]{1,0:T(8,128)(2,1)}, bf16[512,3584]{1,0:T(8,128)(2,1)}, u32[]{:S(2)}, u32[]{:S(2)}) collective-permute-start(bf16[512,3584]{1,0:T(8,128)(2,1)} %param.5), channel_id=1, source_target_pairs={{1,2},{2,1},{5,6},{6,5},{9,10},{10,9},{13,14},{14,13},{17,18},{18,... | collective-permute-start | bytes 11010056 | tf_op jit(solution)/shard_map/ppermute | solution.py:363
  93.4 5.5 %maximum_select_fusion.refs_1_.refs_5_ = bf16[512,3584]{1,0:T(8,128)(2,1)} fusion(bf16[512,2688]{1,0:T(8,128)(2,1)} %collective-permute-done, bf16[512,896]{1,0:T(8,128)(2,1)} %copy-done.19, pred[]{:T(512)S(6)} %eq.21), kind=kLoop, calls=%fused_computation | loop fusion | flops 16515072 | bytes 7340033 | tf_op jit(solution)/shard_map/jit(_where)/select_n | solution.py:450
  102.5 32.0 %collective-permute-done.3 = bf16[512,3584]{1,0:T(8,128)(2,1)} collective-permute-done((bf16[512,3584]{1,0:T(8,128)(2,1)}, bf16[512,3584]{1,0:T(8,128)(2,1)}, u32[]{:S(2)}, u32[]{:S(2)}) %collective-permute-start.3) | collective-permute-done | bytes 3670048 | tf_op jit(solution)/shard_map/ppermute | solution.py:363
  155.5 13.2 %shard_map.84 = (f32[1024,512]{1,0:T(8,128)S(1)}, f32[1024,512]{1,0:T(8,128)S(1)}, s16[1040,512]{1,0:T(8,128)(2,1)S(1)}) custom-call(s32[6]{0:T(128)S(1)} %stack.35.flag_ref, bf16[512,3584]{1,0:T(8,128)(2,1)} %copy-done, bf16[512,3584]{1,0:T(8,128)(2,1)} %copy-done.14, bf16[512,3584]{1,0:T(8,128)(2,1)} %copy-done, ...), custom_call_target="tpu_custom_call" | custom-call | flops 1 | bytes 1 | tf_op jit(solution)/shard_map/pallas_call | solution.py:148
  168.8 13.2 %shard_map.86.refs_4_ = f32[448,3584]{1,0:T(8,128)} custom-call(s32[6]{0:T(128)S(1)} %stack.35.flag_ref, bf16[512,448]{1,0:T(8,128)(2,1)S(1)} %constant_dynamic-slice_fusion.7.refs_0_, bf16[512,3584]{1,0:T(8,128)(2,1)S(1)} %copy-done.1, bf16[512,448]{1,0:T(8,128)(2,1)S(1)} %constant_dynamic-slice_fusion.6.refs_2_, bf16[512,3584]{1,0:T(8,128)(2,1)} %copy-done.14, ...), custom_call_target="tpu_custom_call" | custom-call | flops 1 | bytes 1 | tf_op jit(solution)/shard_map/pallas_call | solution.py:148
  182.0 4.3 %broadcast_select_fusion.refs_0_.refs_1_ = bf16[512,3584]{1,0:T(8,128)(2,1)} fusion(bf16[512,3584]{1,0:T(8,128)(2,1)} %collective-permute-done.2, bf16[512,3584]{1,0:T(8,128)(2,1)} %collective-permute-done.10, pred[]{:T(512)S(6)} %or.3), kind=kLoop, calls=%fused_computation.1 | loop fusion | flops 1835008 | bytes 11010049 | tf_op jit(solution)/shard_map/jit(_where)/select_n | solution.py:473
  189.1 8.4 %shard_map.87 = (f32[1024,512]{1,0:T(8,128)S(1)}, s16[528,512]{1,0:T(8,128)(2,1)S(1)}) custom-call(s32[6]{0:T(128)S(1)} %stack.35.flag_ref, bf16[512,3584]{1,0:T(8,128)(2,1)} %copy-done, bf16[512,3584]{1,0:T(8,128)(2,1)} %copy-done.14, bf16[512,3584]{1,0:T(8,128)(2,1)} %broadcast_select_fusion.refs_0_.refs_1_), custom_call_target="tpu_custom_call" | custom-call | flops 1 | bytes 1 | tf_op jit(solution)/shard_map/pallas_call | solution.py:148
  198.4 15.2 %collective-permute-done.8.refs_2_ = s16[1040,512]{1,0:T(8,128)(2,1)S(1)} collective-permute-done((s16[1040,512]{1,0:T(8,128)(2,1)S(1)}, s16[1040,512]{1,0:T(8,128)(2,1)S(1)}, u32[]{:S(2)}, u32[]{:S(2)}) %collective-permute-start.8) | collective-permute-done | bytes 1064992 | tf_op jit(solution)/shard_map/ppermute | solution.py:363
  213.6 3.5 %shard_map.85 = (f32[1024,512]{1,0:T(8,128)S(1)}, s16[1040,512]{1,0:T(8,128)(2,1)S(1)}) custom-call(s32[6]{0:T(128)S(1)} %stack.35.flag_ref, f32[1024,512]{1,0:T(8,128)} %copy-done.8, f32[1024,512]{1,0:T(8,128)} %copy-done.9, s16[1040,512]{1,0:T(8,128)(2,1)S(1)} %collective-permute-done.8.refs_2_), custom_call_target="tpu_custom_call" | custom-call | flops 1 | bytes 1 | tf_op jit(solution)/shard_map/pallas_call | solution.py:148
  218.4 3.3 collective-permute-start.16
  225.0 10.4 %shard_map.88.refs_4_ = f32[448,3584]{1,0:T(8,128)} custom-call(s32[6]{0:T(128)S(1)} %stack.35.flag_ref, bf16[512,448]{1,0:T(8,128)(2,1)S(1)} %constant_dynamic-slice_fusion.3.refs_0_, bf16[512,3584]{1,0:T(8,128)(2,1)} %broadcast_select_fusion.refs_0_.refs_1_, bf16[512,448]{1,0:T(8,128)(2,1)S(1)} %constant_dynamic-slice_fusion.2.refs_2_, ...), custom_call_target="tpu_custom_call" | custom-call | flops 1 | bytes 1 | tf_op jit(solution)/shard_map/pallas_call | solution.py:148
  237.6 16.6 %collective-permute-done.15 = bf16[512,2688]{1,0:T(8,128)(2,1)S(1)} collective-permute-done((bf16[512,2688]{1,0:T(8,128)(2,1)}, bf16[512,2688]{1,0:T(8,128)(2,1)S(1)}, u32[]{:S(2)}, u32[]{:S(2)}) %collective-permute-start.15) | collective-permute-done | bytes 2752544 | tf_op jit(solution)/shard_map/ppermute | solution.py:363
  260.0 3.3 collective-permute-done.18.refs_3_
  264.7 10.4 %shard_map.90 = (f32[448,2688]{1,0:T(8,128)}, s16[464,2688]{1,0:T(8,128)(2,1)}) custom-call(s32[6]{0:T(128)S(1)} %stack.35.flag_ref, bf16[512,448]{1,0:T(8,128)(2,1)S(1)} %constant_dynamic-slice_fusion.1.refs_0_, bf16[512,2688]{1,0:T(8,128)(2,1)} %copy-done.2, bf16[512,448]{1,0:T(8,128)(2,1)S(1)} %constant_dynamic-slice_fusion.refs_2_, ...), custom_call_target="tpu_custom_call" | custom-call | flops 1 | bytes 1 | tf_op jit(solution)/shard_map/pallas_call | solution.py:148
  279.8 6.5 %shard_map.92.refs_1_ = f32[1024,512]{1,0:T(8,128)S(1)} custom-call(s32[6]{0:T(128)S(1)} %stack.35.flag_ref, bf16[512,3584]{1,0:T(8,128)(2,1)} %copy-done, bf16[512,3584]{1,0:T(8,128)(2,1)} %copy-done.14, bf16[512,2688]{1,0:T(8,128)(2,1)S(1)} %copy-done.3), custom_call_target="tpu_custom_call" | custom-call | flops 1 | bytes 1 | tf_op jit(solution)/shard_map/pallas_call | solution.py:148
  286.4 4.7 %shard_map.91 = (f32[512,2048]{1,0:T(8,128)}, f32[512,2048]{1,0:T(8,128)}) custom-call(s32[6]{0:T(128)S(1)} %stack.35.flag_ref, f32[1]{0:T(128)} %bitcast.6.scale_ref, f32[512,2048]{1,0:T(8,128)} %old_ref.3, f32[1024,512]{1,0:T(8,128)S(1)} %copy-done.5, s16[1040,512]{1,0:T(8,128)(2,1)S(1)} %copy-done.7, f32[512,512]{1,0:T(8,128)S(1)} %copy-done.13, ...), custom_call_target="tpu_custom_call" | custom-call | flops 1 | bytes 1 | tf_op jit(solution)/shard_map/pallas_call | solution.py:148
  292.5 3.5 %shard_map.93 = (f32[1024,512]{1,0:T(8,128)S(1)}, s16[528,512]{1,0:T(8,128)(2,1)S(1)}) custom-call(s32[6]{0:T(128)S(1)} %stack.35.flag_ref, bf16[512,3584]{1,0:T(8,128)(2,1)} %copy-done, bf16[512,3584]{1,0:T(8,128)(2,1)} %copy-done.14, bf16[512,896]{1,0:T(8,128)(2,1)S(1)} %broadcast_select_fusion.3.refs_0_.refs_1_, f32[1024,512]{1,0:T(8,128)S(1)} %shard_map.92.refs_1_), custom_call_target="tpu_custom_call" | custom-call | flops 1 | bytes 1 | tf_op jit(solution)/shard_map/pallas_call | solution.py:148
  298.9 3.3 shard_map.94
  304.8 11.6 %collective-permute-done.21.refs_1_ = s16[528,512]{1,0:T(8,128)(2,1)S(1)} collective-permute-done((s16[528,512]{1,0:T(8,128)(2,1)S(1)}, s16[528,512]{1,0:T(8,128)(2,1)S(1)}, u32[]{:S(2)}, u32[]{:S(2)}) %collective-permute-start.21) | collective-permute-done | bytes 540704 | tf_op jit(solution)/shard_map/ppermute | solution.py:363
  319.5 9.3 %shard_map.96 = (f32[448,3584]{1,0:T(8,128)}, f32[448,3584]{1,0:T(8,128)}) custom-call(s32[6]{0:T(128)S(1)} %stack.35.flag_ref, f32[1]{0:T(128)S(6)} %div.21.scale_ref, f32[448,3584]{1,0:T(8,128)} %bitcast.10, f32[448,2688]{1,0:T(8,128)} %get-tuple-element.94.value_ref, s16[464,2688]{1,0:T(8,128)(2,1)S(1)} %collective-permute-done.23.coded_ref), custom_call_target="tpu_custom_call" | custom-call | flops 1 | bytes 1 | tf_op jit(solution)/shard_map/pallas_call | solution.py:148
  328.9 4.1 %shard_map.97 = (f32[448,3584]{1,0:T(8,128)}, f32[448,3584]{1,0:T(8,128)}) custom-call(s32[6]{0:T(128)S(1)} %stack.35.flag_ref, f32[1]{0:T(128)S(6)} %div.21.scale_ref, f32[448,3584]{1,0:T(8,128)} %bitcast.11, f32[448,896]{1,0:T(8,128)S(1)} %get-tuple-element.93.value_ref, ...), custom_call_target="tpu_custom_call", output_to_operand_aliasing={{0}: (5, {}), {1}: (6, {})} | custom-call | flops 1 | bytes 1 | tf_op jit(solution)/shard_map/pallas_call | solution.py:148
  333.0 4.7 %shard_map.98 = (f32[512,2048]{1,0:T(8,128)}, f32[512,2048]{1,0:T(8,128)}) custom-call(s32[6]{0:T(128)S(1)} %stack.35.flag_ref, f32[1]{0:T(128)} %bitcast.6.scale_ref, f32[512,2048]{1,0:T(8,128)} %old_ref.3, f32[1024,512]{1,0:T(8,128)S(1)} %copy-done.5, s16[1040,512]{1,0:T(8,128)(2,1)S(1)} %copy-done.7, ...), custom_call_target="tpu_custom_call", output_to_operand_aliasing={{0}: (7, {}), {1}: (8, {})} | custom-call | flops 1 | bytes 1 | tf_op jit(solution)/shard_map/pallas_call | solution.py:148
  (102 shorter events, 62.0 us)
Async XLA Ops:
  0.6 88.9 %collective-permute-start.2 = (bf16[512,3584]{1,0:T(8,128)(2,1)}, bf16[512,3584]{1,0:T(8,128)(2,1)}, u32[]{:S(2)}, u32[]{:S(2)}) collective-permute-start(bf16[512,3584]{1,0:T(8,128)(2,1)} %param.5), channel_id=1, source_target_pairs={{4,8},{5,10},{6,9},{7,11},{8,4},{9,6},{10,5},{11,7},{20,24},{21,26... | collective-permute-start | bytes 11010056 | tf_op jit(solution)/shard_map/ppermute | solution.py:363
  5.1 83.5 %collective-permute-start = (bf16[512,2688]{1,0:T(8,128)(2,1)S(1)}, bf16[512,2688]{1,0:T(8,128)(2,1)}, u32[]{:S(2)}, u32[]{:S(2)}) collective-permute-start(bf16[512,2688]{1,0:T(8,128)(2,1)S(1)} %constant_dynamic-slice_fusion.9), channel_id=1, source_target_pairs={{0,4},{1,6},{2,5},{3,7},{4,0},{5,2},{6,1},{7,3},{8,12},{9,14},{10,... | collective-permute-start | bytes 8257544 | tf_op jit(solution)/shard_map/ppermute | solution.py:363
  10.5 78.1 %collective-permute-start.1 = (bf16[512,896]{1,0:T(8,128)(2,1)S(1)}, bf16[512,896]{1,0:T(8,128)(2,1)S(1)}, u32[]{:S(2)}, u32[]{:S(2)}) collective-permute-start(bf16[512,896]{1,0:T(8,128)(2,1)S(1)} %constant_dynamic-slice_fusion.8), channel_id=1, source_target_pairs={{0,4},{1,6},{2,5},{3,7},{4,0},{5,2},{6,1},{7,3},{8,12},{9,14},{10,... | collective-permute-start | bytes 2752520 | tf_op jit(solution)/shard_map/ppermute | solution.py:363
  89.6 45.0 %collective-permute-start.3 = (bf16[512,3584]{1,0:T(8,128)(2,1)}, bf16[512,3584]{1,0:T(8,128)(2,1)}, u32[]{:S(2)}, u32[]{:S(2)}) collective-permute-start(bf16[512,3584]{1,0:T(8,128)(2,1)} %param.5), channel_id=1, source_target_pairs={{1,2},{2,1},{5,6},{6,5},{9,10},{10,9},{13,14},{14,13},{17,18},{18,... | collective-permute-start | bytes 11010056 | tf_op jit(solution)/shard_map/ppermute | solution.py:363
  98.9 40.4 %collective-permute-start.9 = (bf16[512,3584]{1,0:T(8,128)(2,1)}, bf16[512,3584]{1,0:T(8,128)(2,1)}, u32[]{:S(2)}, u32[]{:S(2)}) collective-permute-start(bf16[512,3584]{1,0:T(8,128)(2,1)} %maximum_select_fusion.refs_1_.refs_5_), channel_id=1, source_target_pairs={{0,1},{1,0},{2,3},{3,2},{4,5},{5,4},{6,7},{7,6},{8,9},{9,8},{10,11... | collective-permute-start | bytes 11010056 | tf_op jit(solution)/shard_map/ppermute | solution.py:363
  98.9 83.0 %collective-permute-start.10 = (bf16[512,3584]{1,0:T(8,128)(2,1)}, bf16[512,3584]{1,0:T(8,128)(2,1)}, u32[]{:S(2)}, u32[]{:S(2)}) collective-permute-start(bf16[512,3584]{1,0:T(8,128)(2,1)} %collective-permute-done.2), channel_id=1, source_target_pairs={{4,0},{5,1},{6,2},{7,3},{8,12},{9,13},{10,14},{11,15},{20,16},{21,... | collective-permute-start | bytes 11010056 | tf_op jit(solution)/shard_map/ppermute | solution.py:363
  100.2 81.7 %collective-permute-start.11 = (bf16[512,2688]{1,0:T(8,128)(2,1)}, bf16[512,2688]{1,0:T(8,128)(2,1)}, u32[]{:S(2)}, u32[]{:S(2)}) collective-permute-start(bf16[512,2688]{1,0:T(8,128)(2,1)} %collective-permute-done), channel_id=1, source_target_pairs={{4,8},{5,9},{6,10},{7,11},{8,4},{9,5},{10,6},{11,7},{20,24},{21,25... | collective-permute-start | bytes 8257544 | tf_op jit(solution)/shard_map/ppermute | solution.py:363
  138.8 4.9 %collective-permute-start.5 = (bf16[512,896]{1,0:T(8,128)(2,1)S(1)}, bf16[512,896]{1,0:T(8,128)(2,1)}, u32[]{:S(2)}, u32[]{:S(2)}) collective-permute-start(bf16[512,896]{1,0:T(8,128)(2,1)S(1)} %get-tuple-element.110), channel_id=1, source_target_pairs={{0,1},{1,0},{2,3},{3,2},{4,5},{5,4},{6,7},{7,6},{8,9},{9,8},{10,11... | collective-permute-start | bytes 2752520 | tf_op jit(solution)/shard_map/ppermute | solution.py:363
  139.3 11.7 %collective-permute-start.6 = (bf16[512,896]{1,0:T(8,128)(2,1)S(1)}, bf16[512,896]{1,0:T(8,128)(2,1)}, u32[]{:S(2)}, u32[]{:S(2)}) collective-permute-start(bf16[512,896]{1,0:T(8,128)(2,1)S(1)} %get-tuple-element.109), channel_id=1, source_target_pairs={{0,1},{1,0},{2,3},{3,2},{4,5},{5,4},{6,7},{7,6},{8,9},{9,8},{10,11... | collective-permute-start | bytes 2752520 | tf_op jit(solution)/shard_map/ppermute | solution.py:363
  143.5 8.8 %collective-permute-start.7 = (bf16[512,896]{1,0:T(8,128)(2,1)S(1)}, bf16[512,896]{1,0:T(8,128)(2,1)}, u32[]{:S(2)}, u32[]{:S(2)}) collective-permute-start(bf16[512,896]{1,0:T(8,128)(2,1)S(1)} %get-tuple-element.108), channel_id=1, source_target_pairs={{0,1},{1,0},{2,3},{3,2},{4,5},{5,4},{6,7},{7,6},{8,9},{9,8},{10,11... | collective-permute-start | bytes 2752520 | tf_op jit(solution)/shard_map/ppermute | solution.py:363
  143.7 38.3 %collective-permute-start.12 = (bf16[512,896]{1,0:T(8,128)(2,1)}, bf16[512,896]{1,0:T(8,128)(2,1)}, u32[]{:S(2)}, u32[]{:S(2)}) collective-permute-start(bf16[512,896]{1,0:T(8,128)(2,1)} %copy-done.19), channel_id=1, source_target_pairs={{4,8},{5,9},{6,10},{7,11},{8,4},{9,5},{10,6},{11,7},{20,24},{21,25... | collective-permute-start | bytes 2752520 | tf_op jit(solution)/shard_map/ppermute | solution.py:363
  186.2 36.9 %collective-permute-start.14 = (bf16[512,3584]{1,0:T(8,128)(2,1)}, bf16[512,3584]{1,0:T(8,128)(2,1)S(1)}, u32[]{:S(2)}, u32[]{:S(2)}) collective-permute-start(bf16[512,3584]{1,0:T(8,128)(2,1)} %broadcast_select_fusion.refs_0_.refs_1_), channel_id=1, source_target_pairs={{0,1},{1,0},{2,3},{3,2},{4,5},{5,4},{6,7},{7,6},{8,9},{9,8},{10,11... | collective-permute-start | bytes 11010056 | tf_op jit(solution)/shard_map/ppermute | solution.py:363
  187.1 67.0 %collective-permute-start.15 = (bf16[512,2688]{1,0:T(8,128)(2,1)}, bf16[512,2688]{1,0:T(8,128)(2,1)S(1)}, u32[]{:S(2)}, u32[]{:S(2)}) collective-permute-start(bf16[512,2688]{1,0:T(8,128)(2,1)} %collective-permute-done.11), channel_id=1, source_target_pairs={{4,0},{5,1},{6,2},{7,3},{8,12},{9,13},{10,14},{11,15},{20,16},{21,... | collective-permute-start | bytes 8257544 | tf_op jit(solution)/shard_map/ppermute | solution.py:363
  188.4 25.2 %collective-permute-start.8 = (s16[1040,512]{1,0:T(8,128)(2,1)S(1)}, s16[1040,512]{1,0:T(8,128)(2,1)S(1)}, u32[]{:S(2)}, u32[]{:S(2)}) collective-permute-start(s16[1040,512]{1,0:T(8,128)(2,1)S(1)} %get-tuple-element.61), channel_id=1, source_target_pairs={{0,2},{1,3},{2,0},{3,1},{4,6},{5,7},{6,4},{7,5},{8,10},{9,11},{10,... | collective-permute-start | bytes 3194888 | tf_op jit(solution)/shard_map/ppermute | solution.py:363
  197.6 37.8 %collective-permute-start.13 = (s16[528,512]{1,0:T(8,128)(2,1)S(1)}, s16[528,512]{1,0:T(8,128)(2,1)S(1)}, u32[]{:S(2)}, u32[]{:S(2)}) collective-permute-start(s16[528,512]{1,0:T(8,128)(2,1)S(1)} %get-tuple-element.67), channel_id=1, source_target_pairs={{0,2},{1,3},{2,0},{3,1},{4,6},{5,7},{6,4},{7,5},{8,10},{9,11},{10,... | collective-permute-start | bytes 1622024 | tf_op jit(solution)/shard_map/ppermute | solution.py:363
  218.4 19.2 %collective-permute-start.16 = (s16[1040,512]{1,0:T(8,128)(2,1)S(1)}, s16[1040,512]{1,0:T(8,128)(2,1)S(1)}, u32[]{:S(2)}, u32[]{:S(2)}) collective-permute-start(s16[1040,512]{1,0:T(8,128)(2,1)S(1)} %get-tuple-element.69), channel_id=1, source_target_pairs={{1,0},{3,2},{5,4},{7,6},{8,9},{10,11},{12,13},{14,15},{17,16},{19,... | collective-permute-start | bytes 3194888 | tf_op jit(solution)/shard_map/ppermute | solution.py:363
  236.3 19.4 %collective-permute-start.17 = (s16[528,512]{1,0:T(8,128)(2,1)S(1)}, s16[528,512]{1,0:T(8,128)(2,1)S(1)}, u32[]{:S(2)}, u32[]{:S(2)}) collective-permute-start(s16[528,512]{1,0:T(8,128)(2,1)S(1)} %get-tuple-element.73), channel_id=1, source_target_pairs={{0,1},{2,3},{4,5},{6,7},{9,8},{11,10},{13,12},{15,14},{16,17},{18,... | collective-permute-start | bytes 1622024 | tf_op jit(solution)/shard_map/ppermute | solution.py:363
  257.8 5.5 %collective-permute-start.18 = (bf16[512,2688]{1,0:T(8,128)(2,1)S(1)}, bf16[512,2688]{1,0:T(8,128)(2,1)}, u32[]{:S(2)}, u32[]{:S(2)}) collective-permute-start(bf16[512,2688]{1,0:T(8,128)(2,1)S(1)} %broadcast_select_fusion.2.refs_1_.refs_0_), channel_id=1, source_target_pairs={{0,1},{1,0},{2,3},{3,2},{4,5},{5,4},{6,7},{7,6},{8,9},{9,8},{10,11... | collective-permute-start | bytes 8257544 | tf_op jit(solution)/shard_map/ppermute | solution.py:363
  258.4 32.7 %collective-permute-start.19 = (bf16[512,896]{1,0:T(8,128)(2,1)}, bf16[512,896]{1,0:T(8,128)(2,1)}, u32[]{:S(2)}, u32[]{:S(2)}) collective-permute-start(bf16[512,896]{1,0:T(8,128)(2,1)} %collective-permute-done.12), channel_id=1, source_target_pairs={{4,0},{5,1},{6,2},{7,3},{8,12},{9,13},{10,14},{11,15},{20,16},{21,... | collective-permute-start | bytes 2752520 | tf_op jit(solution)/shard_map/ppermute | solution.py:363
  275.0 44.5 %collective-permute-start.23 = (s16[464,2688]{1,0:T(8,128)(2,1)}, s16[464,2688]{1,0:T(8,128)(2,1)S(1)}, u32[]{:S(2)}, u32[]{:S(2)}) collective-permute-start(s16[464,2688]{1,0:T(8,128)(2,1)} %get-tuple-element.77), channel_id=1, source_target_pairs={{1,2},{2,1},{5,6},{6,5},{9,10},{10,9},{13,14},{14,13},{17,18},{18,... | collective-permute-start | bytes 7483400 | tf_op jit(solution)/shard_map/ppermute | solution.py:363
  292.4 6.5 %collective-permute-start.20 = (bf16[512,896]{1,0:T(8,128)(2,1)S(1)}, bf16[512,896]{1,0:T(8,128)(2,1)S(1)}, u32[]{:S(2)}, u32[]{:S(2)}) collective-permute-start(bf16[512,896]{1,0:T(8,128)(2,1)S(1)} %broadcast_select_fusion.3.refs_0_.refs_1_), channel_id=1, source_target_pairs={{0,1},{1,0},{2,3},{3,2},{4,5},{5,4},{6,7},{7,6},{8,9},{9,8},{10,11... | collective-permute-start | bytes 2752520 | tf_op jit(solution)/shard_map/ppermute | solution.py:363
  297.4 19.0 %collective-permute-start.21 = (s16[528,512]{1,0:T(8,128)(2,1)S(1)}, s16[528,512]{1,0:T(8,128)(2,1)S(1)}, u32[]{:S(2)}, u32[]{:S(2)}) collective-permute-start(s16[528,512]{1,0:T(8,128)(2,1)S(1)} %get-tuple-element.89), channel_id=1, source_target_pairs={{0,2},{1,3},{2,0},{3,1},{4,6},{5,7},{6,4},{7,5},{8,10},{9,11},{10,... | collective-permute-start | bytes 1622024 | tf_op jit(solution)/shard_map/ppermute | solution.py:363
  302.2 26.7 %collective-permute-start.24 = (s16[464,896]{1,0:T(8,128)(2,1)S(1)}, s16[464,896]{1,0:T(8,128)(2,1)S(1)}, u32[]{:S(2)}, u32[]{:S(2)}) collective-permute-start(s16[464,896]{1,0:T(8,128)(2,1)S(1)} %get-tuple-element.88), channel_id=1, source_target_pairs={{1,2},{2,1},{5,6},{6,5},{9,10},{10,9},{13,14},{14,13},{17,18},{18,... | collective-permute-start | bytes 2494472 | tf_op jit(solution)/shard_map/ppermute | solution.py:363
  317.3 15.7 %collective-permute-start.22 = (s16[528,512]{1,0:T(8,128)(2,1)S(1)}, s16[528,512]{1,0:T(8,128)(2,1)S(1)}, u32[]{:S(2)}, u32[]{:S(2)}) collective-permute-start(s16[528,512]{1,0:T(8,128)(2,1)S(1)} %get-tuple-element.92), channel_id=1, source_target_pairs={{0,1},{2,3},{4,5},{6,7},{9,8},{11,10},{13,12},{15,14},{16,17},{18,... | collective-permute-start | bytes 1622024 | tf_op jit(solution)/shard_map/ppermute | solution.py:363
  (21 other events, 149.8 us)

commit v5 on v4

--- a/solution.py
+++ b/solution.py
@@ -1,4 +1,4 @@
-import math
+import functools
 
 import jax
 import jax.numpy as jnp
@@ -131,7 +131,7 @@
 
 PARAMS = pltpu.CompilerParams(vmem_limit_bytes=48 * 2**20)
 FREE = pl.CostEstimate(flops=1, bytes_accessed=1, transcendentals=0)
-KEPT, PIECE_A, PIECE_B, SAME_HALF, MIDDLE, CORE = range(6)
+KEPT, START, HOME, AWAY, LAST, SAME_HALF, MIDDLE, CORE = range(8)
 
 
 def spec(shape, index=None):
@@ -144,7 +144,7 @@
     return spec(array.shape)
 
 
-def kernel_call(body, flags, steps, ins, outs, aliases=None):
+def kernel_call(body, flags, steps, ins, outs, aliases=None, scratch=()):
     results = pl.pallas_call(
         body,
         grid_spec=pltpu.PrefetchScalarGridSpec(
@@ -152,6 +152,7 @@
             grid=(steps,),
             in_specs=[s for _, s in ins],
             out_specs=[s for _, _, s in outs],
+            scratch_shapes=list(scratch),
         ),
         out_shape=[jax.ShapeDtypeStruct(shape, dtype) for shape, dtype, _ in outs],
         input_output_aliases=aliases or {},
@@ -165,13 +166,21 @@
     return pl.multiple_of(flag * size, GROUP)
 
 
-def left_terms(flags, rows, slots, block, steps, at=None, before=None, last=True):
+def blocks_from(at):
+    return lambda k, flags: k + flags[at]
+
+
+def left_terms(flags, rows, slots, block, steps, at=START, before=None, last=True):
     many = len(slots)
+    choices = [len(slot) for slot in slots]
     tall = rows[0].shape[0]
     size = 2 * tall
 
     def body(flag_ref, first_ref, second_ref, *refs):
-        slots_in, refs = refs[:many], refs[many:]
+        slots_in = []
+        for count in choices:
+            slots_in.append(refs[:count])
+            refs = refs[count:]
         if before is not None:
             before_in, refs = refs[:many], refs[many:]
         outs = refs[:many]
@@ -182,9 +191,18 @@
             for index in range(many):
                 outs[index][...] = jnp.zeros_like(outs[index]) if before is None else before_in[index][...]
 
+        def add(index, ref):
+            for half, row_ref in enumerate((first_ref, second_ref)):
+                outs[index][half * tall : (half + 1) * tall] += dot(row_ref[...], ref[...], 1, 1)
+
         for index in range(many):
-            for half, ref in enumerate((first_ref, second_ref)):
-                outs[index][half * tall : (half + 1) * tall] += dot(ref[...], slots_in[index][...], 1, 1)
+            if choices[index] == 1:
+                add(index, slots_in[index][0])
+            else:
+                for choice in range(2):
+                    pl.when(flag_ref[MIDDLE] == choice)(
+                        functools.partial(add, index, slots_in[index][choice])
+                    )
 
         if last:
 
@@ -197,9 +215,9 @@
                     levels += pack(part, refs[many], index * tall)
                 put_levels(levels, refs[many], many * tall)
 
-    from_flag = lambda k, flags: k if at is None else k + flags[at]
-    ins = [(part, spec((tall, block), from_flag)) for part in rows]
-    ins += [(slot, spec((tall, block), lambda k, flags: k)) for slot in slots]
+    ins = [(part, spec((tall, block), blocks_from(at))) for part in rows]
+    for slot in slots:
+        ins += [(array, spec((tall, block), blocks_from(start))) for array, start in slot]
     if before is not None:
         ins += [(part, whole(part)) for part in before]
     outs = [((size, tall), jnp.float32, spec((size, tall)))] * many
@@ -209,31 +227,54 @@
     return kernel_call(body, flags, steps, ins, outs)
 
 
-def right_terms(flags, terms, block, steps, at=None, before=None, last=False):
+def right_terms(flags, strips, columns, block, steps, at=START, before=None, last=False):
     wide = block * steps
-    strip = terms[0][0].shape[1]
+    rows, strip = strips[0].shape
+    many = len(strips)
 
     def body(flag_ref, *refs):
-        total = None if before is None else refs[2 * len(terms)][...]
-        for index in range(len(terms)):
-            term = dot(refs[2 * index][...], refs[2 * index + 1][...], 0, 0)
-            total = term if total is None else total + term
-        outs = refs[2 * len(terms) + (before is not None) :]
-        outs[0][...] = total
+        strips_in, refs = refs[:many], refs[many:]
+        columns_in = []
+        for choice in columns:
+            columns_in.append(refs[: len(choice)])
+            refs = refs[len(choice) :]
+        if before is not None:
+            before_in, refs = refs[0], refs[1:]
+        outs, turned = refs[:-1], refs[-1]
+
+        @pl.when(pl.program_id(0) == 0)
+        def _():
+            for index in range(many):
+                turned[index] = strips_in[index][...].T
+
+        def add(choice):
+            total = None if before is None else before_in[...]
+            for index in range(many):
+                refs_here = columns_in[index]
+                ref = refs_here[choice if len(refs_here) == 2 else 0]
+                term = dot(turned[index], ref[...], 1, 0)
+                total = term if total is None else total + term
+            outs[0][...] = total
+
+        if max(len(choice) for choice in columns) == 1:
+            add(0)
+        else:
+            for choice in range(2):
+                pl.when(flag_ref[MIDDLE] == choice)(functools.partial(add, choice))
         if last:
-            put_levels(pack(total, outs[1], 0), outs[1], strip)
+            put_levels(pack(outs[0][...], outs[1], 0), outs[1], strip)
 
     here = lambda k, flags: k
-    from_flag = lambda k, flags: k if at is None else k + flags[at]
-    ins = []
-    for strips, columns in terms:
-        ins += [(strips, whole(strips)), (columns, spec((columns.shape[0], block), here))]
+    ins = [(part, whole(part)) for part in strips]
+    for choice in columns:
+        ins += [(array, spec((rows, block), blocks_from(start))) for array, start in choice]
     if before is not None:
-        ins.append((before, spec((strip, block), from_flag)))
+        ins.append((before, spec((strip, block), blocks_from(at))))
     outs = [((strip, wide), jnp.float32, spec((strip, block), here))]
     if last:
         outs.append(((strip + LEVELS, wide), jnp.int16, spec((strip + LEVELS, block), here)))
-    return kernel_call(body, flags, steps, ins, outs)
+    scratch = [pltpu.VMEM((many, strip, rows), jnp.bfloat16)]
+    return kernel_call(body, flags, steps, ins, outs, scratch=scratch)
 
 
 def add_up(flags, products, coded):
@@ -416,8 +457,10 @@
     flags = jnp.stack(
         [
             jnp.where(straight, 0, 1),
-            side,
-            3 * (1 - side),
+            0,
+            2 * side,
+            2 * (1 - side),
+            2 * (1 - side) + 1,
             (c == side).astype(jnp.int32),
             is_middle.astype(jnp.int32),
             c,
@@ -434,25 +477,17 @@
     def strips_of(pair, first=0):
         return [lax.dynamic_slice_in_dim(part, strip_at - first, strip, 1) for part in pair]
 
-    def terms(strips, pair):
-        return list(zip(strips, pair))
-
-    mate_b = send(columns(gradient, 3 * side, 1), pair_line)
-    mate_a = send(columns(gradient, 1 - side, 3), pair_line)
+    def one(array, at=START):
+        return [(array, at)]
+
+    mate = send(gradient, pair_line)
     cross = send(gradient, across_line)
-    gradient_t, mate_a, mate_b, cross = tie(gradient, mate_a, mate_b, cross)
-    far_a = send(mate_a, across)
-    far_b = send(mate_b, across)
+    gradient_t, mate, cross = tie(gradient, mate, cross)
+    far = send(mate, across)
     near = send(cross, outward)
     swapped = send(gradient_t, to_line)
-
-    def in_order(part_a, part_b):
-        return jnp.where(
-            side == 0, jnp.concatenate([part_b, part_a], 1), jnp.concatenate([part_a, part_b], 1)
-        )
-
-    mate = in_order(mate_a, mate_b)
     mates = (mate, send(mate, beside))
+    cross_o = send(cross, beside)
     mine = jnp.where(straight, gradient, swapped)
     starts = range(0, half_wide, block)
     own = (
@@ -461,64 +496,106 @@
             [send(mine[:, first : first + block], beside) for first in starts], 1
         ),
     )
-    own_product, mate_product, same_coded = left_terms(flags, own, [mine, mate], block, 4)
+    own_product, mate_product, same_coded = left_terms(flags, own, [one(mine), one(mate)], block, 4)
     same_products = [own_product, mate_product]
     same_got = send(same_coded, other_y)
     [right] = right_terms(
-        flags, terms(strips_of(own), own) + terms(strips_of(mates), mates), block, 4
-    )
-
-    right, same_coded, near, far_a, far_b = tie(right, same_coded, near, far_a, far_b)
-    end_a = send(far_a, outward)
-    near = jnp.where(is_middle, cross, near)
-    nears = (near, send(near, beside))
-    near_product, near_coded = left_terms(flags, own, [near], block, 4)
+        flags, strips_of(own) + strips_of(mates), [one(part) for part in own + mates], block, 4
+    )
+
+    right, same_coded, near, far, cross_o = tie(right, same_coded, near, far, cross_o)
+    end_home = send(columns(far, 2 * side, 2), outward)
+    near_o = send(near, beside)
+    far_o = send(far, beside)
+    near_product, near_coded = left_terms(
+        flags, own, [[(near, START), (cross, START)]], block, 4
+    )
     near_got = send(near_coded, other_y)
-    [right] = right_terms(flags, terms(strips_of(nears), nears), block, 4, before=right)
+    near_strips = strips_of((jnp.where(is_middle, cross, near), jnp.where(is_middle, cross_o, near_o)))
+    [right] = right_terms(
+        flags,
+        near_strips,
+        [[(near, START), (cross, START)], [(near_o, START), (cross_o, START)]],
+        block,
+        4,
+        before=right,
+    )
+    same_got, right = tie(same_got, right)
     same_total, same_out = add_up(flags, same_products, same_got)
     same_other = send(same_out, to_home)
-    near_got, right, same_out = tie(near_got, right, same_out)
+
+    right, same_out, end_home, far_o = tie(right, same_out, end_home, far_o)
+    far, end_home = tie(far, end_home)
+    end_first = send(columns(far, 2 * (1 - side), 1), outward)
+    end_home_o = send(end_home, beside)
+    [far_product] = left_terms(
+        flags, own, [[(end_home, START), (far, HOME)]], block, 2, at=HOME, last=False
+    )
+    strips = [
+        jnp.where(is_middle, strips_of([a])[0], strips_of([b], 2 * side * block)[0])
+        for a, b in ((far, end_home), (far_o, end_home_o))
+    ]
+    right_home, home_coded = right_terms(
+        flags,
+        strips,
+        [[(end_home, START), (far, HOME)], [(end_home_o, START), (far_o, HOME)]],
+        block,
+        2,
+        at=HOME,
+        before=right,
+        last=True,
+    )
+    home_got = send(home_coded, to_line)
+    near_got, home_coded = tie(near_got, home_coded)
     near_total, near_out = add_up(flags, [near_product], near_got)
     near_other = send(near_out, to_away)
 
-    right, near_out, end_a, same_other, near_other = tie(right, near_out, end_a, same_other, near_other)
-    far_b, end_a = tie(far_b, end_a)
-    end_b = send(far_b, outward)
-    end_a = jnp.where(is_middle, far_a, end_a)
-    ends_a = (end_a, send(end_a, beside))
-    [far_product] = left_terms(flags, own, [end_a], block, 3, at=PIECE_A, last=False)
-    strips = strips_of(ends_a, side * block)
-    right_a, coded_a = right_terms(
-        flags, terms(strips, ends_a), block, 3, at=PIECE_A, before=right, last=True
-    )
-    got_a = send(coded_a, to_line)
+    def quarter(end, at, far_product, last):
+        end_o = send(end, beside)
+        lefts = left_terms(
+            flags, own, [[(end, START), (far, at)]], block, 1, at=at, before=[far_product], last=last
+        )
+        value, coded = right_terms(
+            flags,
+            strips,
+            [[(end, START), (far, at)], [(end_o, START), (far_o, at)]],
+            block,
+            1,
+            at=at,
+            before=right,
+            last=True,
+        )
+        return lefts, value, coded
+
     left_scale = 1.0 / denominator(left_counts).reshape(1)
     right_scale = 1.0 / denominator(right_counts)
-    coded_a, near_other, same_other = tie(coded_a, near_other, same_other)
+    old = right_old[0]
+    near_out, far_product, end_first = tie(near_out, far_product, end_first)
+    far, end_first = tie(far, end_first)
+    end_last = send(columns(far, 2 * (1 - side) + 1, 1), outward)
+    [far_product], right_first, first_coded = quarter(end_first, AWAY, far_product, False)
+    first_got = send(first_coded, to_line)
+    first_coded, home_got = tie(first_coded, home_got)
+    right_done = finish_right(flags, right_scale, old, right_home, home_got, HOME, block, 2)
+    right_done[0], near_other, same_other = tie(right_done[0], near_other, same_other)
     left_done = finish_left(
         flags, left_scale, left_old, same_total, same_other, near_total, near_other, True
     )
 
-    left_done[0], coded_a, far_product, end_b = tie(left_done[0], coded_a, far_product, end_b)
-    end_b = jnp.where(is_middle, far_b, end_b)
-    ends_b = (end_b, send(end_b, beside))
-    far_product, far_coded = left_terms(
-        flags, own, [end_b], block, 1, at=PIECE_B, before=[far_product]
-    )
+    left_done[0], far_product, end_last = tie(left_done[0], far_product, end_last)
+    [far_product, far_coded], right_last, last_coded = quarter(end_last, LAST, far_product, True)
     far_got = send(far_coded, other_y)
-    right_b, coded_b = right_terms(
-        flags, terms(strips, ends_b), block, 1, at=PIECE_B, before=right, last=True
-    )
-    got_b = send(coded_b, to_line)
-    old = right_old[0]
-    coded_b, far_got = tie(coded_b, far_got)
+    last_got = send(last_coded, to_line)
+    last_coded, first_got = tie(last_coded, first_got)
+    right_done = finish_right(
+        flags, right_scale, old, right_first, first_got, AWAY, block, 1, right_done
+    )
+    right_done[0], far_got = tie(right_done[0], far_got)
     far_total, far_out = add_up(flags, [far_product], far_got)
     far_other = send(far_out, to_away)
-    far_out, got_a = tie(far_out, got_a)
-    right_done = finish_right(flags, right_scale, old, right_a, got_a, PIECE_A, block, 3)
-    right_done[0], got_b = tie(right_done[0], got_b)
+    far_out, last_got = tie(far_out, last_got)
     right_state, right_fixed = finish_right(
-        flags, right_scale, old, right_b, got_b, PIECE_B, block, 1, right_done
+        flags, right_scale, old, right_last, last_got, LAST, block, 1, right_done
     )
     far_other, right_state = tie(far_other, right_state)
     left_state, left_fixed = finish_left(

time: 342 us -> 364 us (1.064)
  Pallas kernels: 97.1 us -> 120 us
  other arithmetic: 15.6 us -> 9.14 us
  starting transfers between devices: 34.7 us -> 41 us
  local copies, waits for them, and re-layouts: 27.7 us -> 23.2 us
    pallas_call x15 -> x18, Pallas kernels: 97.1 us -> 120 us  [kernel_call(): pl.pallas_call(body, grid_spec=pltpu.PrefetchScalarGridSpec(num_scalar_pr...]
    select_n x4, other arithmetic: 13.1 us -> 6.72 us  [the longest x2 3.32 us: line_gather(): jnp.where(is_middle, strips_of([a])[0], strips_of([b], 2 * side * block)[0])]
    ppermute x25 -> x28, starting transfers between devices: 34.7 us -> 41 us  [send(): return lax.ppermute(value, AXES, pairs)]
    unnamed x43, local copies, waits for them, and re-layouts: 15.2 us -> 9.77 us
    dynamic_slice x8 -> x4, local copies, waits for them, and re-layouts: 7.63 us -> 4.51 us  [strips_of(): lax.dynamic_slice_in_dim(part, strip_at - first, strip, 1)]
    ppermute x25 -> x28, waiting for transfers between devices: 160 us -> 163 us  [send(): return lax.ppermute(value, AXES, pairs)]
  transfers between devices with their start and end apart: 25 -> 28, of which waited for: 7 -> 11; matrix products, arithmetic and copies ran while one was open for 7% -> 7% of each run, Pallas kernels for 27% -> 32%
where the time goes in v5:
time: 364 us; the launch traced here: 358 us
  waiting for transfers between devices  163 us (45%)
  Pallas kernels  120 us (33%)
  starting transfers between devices  41 us (11%)
  local copies, waits for them, and re-layouts  23.2 us (6%)
  other arithmetic  9.14 us (3%)
    ppermute x28, waiting for transfers between devices, send(): return lax.ppermute(value, AXES, pairs)  163 us
    pallas_call x18, Pallas kernels, kernel_call(): pl.pallas_call(body, grid_spec=pltpu.PrefetchScalarGridSpec(num_scalar_pr...  120 us
    ppermute x28, starting transfers between devices, send(): return lax.ppermute(value, AXES, pairs)  41 us
    unnamed x43, local copies, waits for them, and re-layouts  9.77 us
  transfers between devices with their start and end apart: 28, of which 11 were waited for; matrix products, arithmetic and copies ran while one was open for 7% of the time, Pallas kernels for 32%

profile of v5, /device:TPU:1, one launch (start us, length us, event | category | flops | bytes accessed | tf_op | source)
XLA Modules:
  0.0 358.3 jit_solution(8994681125113054078)
XLA Ops:
  3.1 4.1 %collective-permute-start = (bf16[512,3584]{1,0:T(8,128)(2,1)}, bf16[512,3584]{1,0:T(8,128)(2,1)}, u32[]{:S(2)}, u32[]{:S(2)}) collective-permute-start(bf16[512,3584]{1,0:T(8,128)(2,1)} %param.5), channel_id=1, source_target_pairs={{0,4},{1,6},{2,5},{3,7},{4,0},{5,2},{6,1},{7,3},{8,12},{9,14},{10,... | collective-permute-start | bytes 11010056 | tf_op jit(solution)/shard_map/ppermute | solution.py:404
  7.2 79.7 %collective-permute-done.refs_1_.refs_6_ = bf16[512,3584]{1,0:T(8,128)(2,1)} collective-permute-done((bf16[512,3584]{1,0:T(8,128)(2,1)}, bf16[512,3584]{1,0:T(8,128)(2,1)}, u32[]{:S(2)}, u32[]{:S(2)}) %collective-permute-start) | collective-permute-done | bytes 3670048 | tf_op jit(solution)/shard_map/ppermute | solution.py:404
  95.2 36.7 %collective-permute-done.2 = bf16[512,3584]{1,0:T(8,128)(2,1)} collective-permute-done((bf16[512,3584]{1,0:T(8,128)(2,1)}, bf16[512,3584]{1,0:T(8,128)(2,1)}, u32[]{:S(2)}, u32[]{:S(2)}) %collective-permute-start.2) | collective-permute-done | bytes 3670048 | tf_op jit(solution)/shard_map/ppermute | solution.py:404
  150.7 13.2 %shard_map.84 = (f32[1024,512]{1,0:T(8,128)S(1)}, f32[1024,512]{1,0:T(8,128)S(1)}, s16[1040,512]{1,0:T(8,128)(2,1)S(1)}) custom-call(s32[8]{0:T(128)S(1)} %stack.39.flag_ref, bf16[512,3584]{1,0:T(8,128)(2,1)} %copy-done, bf16[512,3584]{1,0:T(8,128)(2,1)} %copy-done.15, bf16[512,3584]{1,0:T(8,128)(2,1)} %copy-done, ...), custom_call_target="tpu_custom_call" | custom-call | flops 1 | bytes 1 | tf_op jit(solution)/shard_map/pallas_call | solution.py:148
  164.0 13.6 %shard_map.85.refs_6_ = f32[448,3584]{1,0:T(8,128)} custom-call(s32[8]{0:T(128)S(1)} %stack.39.flag_ref, bf16[512,448]{1,0:T(8,128)(2,1)S(1)} %constant_dynamic-slice_fusion.6.refs_0_, bf16[512,448]{1,0:T(8,128)(2,1)S(1)} %constant_dynamic-slice_fusion.5.refs_1_, bf16[512,448]{1,0:T(8,128)(2,1)S(1)} %constant_dynamic-slice_fusion.4.refs_2_, ...), custom_call_target="tpu_custom_call" | custom-call | flops 1 | bytes 1 | tf_op jit(solution)/shard_map/pallas_call | solution.py:148
  186.1 12.3 %shard_map.86.refs_6_ = f32[448,3584]{1,0:T(8,128)} custom-call(s32[8]{0:T(128)S(1)} %stack.39.flag_ref, bf16[512,448]{1,0:T(8,128)(2,1)S(1)} %dynamic-slice_select_fusion.1.refs_0_, bf16[512,448]{1,0:T(8,128)(2,1)S(1)} %dynamic-slice_select_fusion.refs_1_, bf16[512,3584]{1,0:T(8,128)(2,1)} %collective-permute-done.9.refs_2_.refs_0_, ...), custom_call_target="tpu_custom_call" | custom-call | flops 1 | bytes 1 | tf_op jit(solution)/shard_map/pallas_call | solution.py:148
  198.4 7.5 %collective-permute-done.7.refs_2_ = s16[1040,512]{1,0:T(8,128)(2,1)S(1)} collective-permute-done((s16[1040,512]{1,0:T(8,128)(2,1)S(1)}, s16[1040,512]{1,0:T(8,128)(2,1)S(1)}, u32[]{:S(2)}, u32[]{:S(2)}) %collective-permute-start.7) | collective-permute-done | bytes 1064992 | tf_op jit(solution)/shard_map/ppermute | solution.py:404
  205.9 4.5 %shard_map.87 = (f32[1024,512]{1,0:T(8,128)S(1)}, s16[1040,512]{1,0:T(8,128)(2,1)}) custom-call(s32[8]{0:T(128)S(1)} %stack.39.flag_ref, f32[1024,512]{1,0:T(8,128)} %copy-done.5, f32[1024,512]{1,0:T(8,128)} %copy-done.6, s16[1040,512]{1,0:T(8,128)(2,1)S(1)} %collective-permute-done.7.refs_2_), custom_call_target="tpu_custom_call" | custom-call | flops 1 | bytes 1 | tf_op jit(solution)/shard_map/pallas_call | solution.py:148
  211.6 11.2 %collective-permute-done.13.refs_2_.refs_0_ = bf16[512,1792]{1,0:T(8,128)(2,1)S(1)} collective-permute-done((bf16[512,1792]{1,0:T(8,128)(2,1)S(1)}, bf16[512,1792]{1,0:T(8,128)(2,1)S(1)}, u32[]{:S(2)}, u32[]{:S(2)}) %collective-permute-start.13) | collective-permute-done | bytes 1835040 | tf_op jit(solution)/shard_map/ppermute | solution.py:404
  231.2 7.3 %shard_map.88 = (f32[448,1792]{1,0:T(8,128)}, s16[464,1792]{1,0:T(8,128)(2,1)}) custom-call(s32[8]{0:T(128)S(1)} %stack.39.flag_ref, bf16[512,448]{1,0:T(8,128)(2,1)S(1)} %dynamic-slice_select_fusion.3.refs_0_, bf16[512,448]{1,0:T(8,128)(2,1)S(1)} %dynamic-slice_select_fusion.2.refs_1_, bf16[512,1792]{1,0:T(8,128)(2,1)S(1)} %collective-permute-done.13.refs_2_.refs_0_, ...), custom_call_target="tpu_custom_call" | custom-call | flops 1 | bytes 1 | tf_op jit(solution)/shard_map/pallas_call | solution.py:148
  241.8 9.9 %shard_map.89 = (f32[1024,512]{1,0:T(8,128)S(1)}, s16[528,512]{1,0:T(8,128)(2,1)}) custom-call(s32[8]{0:T(128)S(1)} %stack.39.flag_ref, bf16[512,3584]{1,0:T(8,128)(2,1)} %copy-done, bf16[512,3584]{1,0:T(8,128)(2,1)} %copy-done.15, bf16[512,3584]{1,0:T(8,128)(2,1)} %collective-permute-done.9.refs_2_.refs_0_, ...), custom_call_target="tpu_custom_call" | custom-call | flops 1 | bytes 1 | tf_op jit(solution)/shard_map/pallas_call | solution.py:148
  256.7 5.2 %shard_map.91.refs_2_ = f32[1024,512]{1,0:T(8,128)S(1)} custom-call(s32[8]{0:T(128)S(1)} %stack.39.flag_ref, bf16[512,3584]{1,0:T(8,128)(2,1)} %copy-done, bf16[512,3584]{1,0:T(8,128)(2,1)} %copy-done.15, bf16[512,1792]{1,0:T(8,128)(2,1)S(1)} %collective-permute-done.13.refs_2_.refs_0_, bf16[512,3584]{1,0:T(8,128)(2,1)} %collective-permute-done.10.refs_3_.refs_1_), custom_call_target="tpu_custom_call" | custom-call | flops 1 | bytes 1 | tf_op jit(solution)/shard_map/pallas_call | solution.py:148
  261.9 10.1 %collective-permute-done.16.refs_1_ = s16[528,512]{1,0:T(8,128)(2,1)S(1)} collective-permute-done((s16[528,512]{1,0:T(8,128)(2,1)}, s16[528,512]{1,0:T(8,128)(2,1)S(1)}, u32[]{:S(2)}, u32[]{:S(2)}) %collective-permute-start.16) | collective-permute-done | bytes 540704 | tf_op jit(solution)/shard_map/ppermute | solution.py:404
  281.7 4.0 %shard_map.95.refs_2_ = f32[1024,512]{1,0:T(8,128)S(1)} custom-call(s32[8]{0:T(128)S(1)} %stack.39.flag_ref, bf16[512,3584]{1,0:T(8,128)(2,1)} %copy-done, bf16[512,3584]{1,0:T(8,128)(2,1)} %copy-done.15, bf16[512,896]{1,0:T(8,128)(2,1)} %collective-permute-done.17.refs_2_.refs_0_, bf16[512,3584]{1,0:T(8,128)(2,1)} %collective-permute-done.10.refs_3_.refs_1_, ...), custom_call_target="tpu_custom_call" | custom-call | flops 1 | bytes 1 | tf_op jit(solution)/shard_map/pallas_call | solution.py:148
  285.7 14.7 %shard_map.92 = (f32[448,896]{1,0:T(8,128)S(1)}, s16[464,896]{1,0:T(8,128)(2,1)S(1)}) custom-call(s32[8]{0:T(128)S(1)} %stack.39.flag_ref, bf16[512,448]{1,0:T(8,128)(2,1)S(1)} %dynamic-slice_select_fusion.3.refs_0_, bf16[512,448]{1,0:T(8,128)(2,1)S(1)} %dynamic-slice_select_fusion.2.refs_1_, bf16[512,896]{1,0:T(8,128)(2,1)} %collective-permute-done.17.refs_2_.refs_0_, ...), custom_call_target="tpu_custom_call" | custom-call | flops 1 | bytes 1 | tf_op jit(solution)/shard_map/pallas_call | solution.py:148
  301.3 6.0 %shard_map.93 = (f32[448,3584]{1,0:T(8,128)}, f32[448,3584]{1,0:T(8,128)}) custom-call(s32[8]{0:T(128)S(1)} %stack.39.flag_ref, f32[1]{0:T(128)S(6)} %div.21.scale_ref, f32[448,3584]{1,0:T(8,128)} %bitcast.11, f32[448,1792]{1,0:T(8,128)S(1)} %copy-done.4, s16[464,1792]{1,0:T(8,128)(2,1)} %collective-permute-done.19.coded_ref), custom_call_target="tpu_custom_call" | custom-call | flops 1 | bytes 1 | tf_op jit(solution)/shard_map/pallas_call | solution.py:148
  308.6 5.0 %shard_map.94 = (f32[512,2048]{1,0:T(8,128)}, f32[512,2048]{1,0:T(8,128)}) custom-call(s32[8]{0:T(128)S(1)} %stack.39.flag_ref, f32[1]{0:T(128)} %bitcast.7.scale_ref, f32[512,2048]{1,0:T(8,128)} %old_ref.3, f32[1024,512]{1,0:T(8,128)S(1)} %copy-done.3, s16[1040,512]{1,0:T(8,128)(2,1)} %collective-permute-done.21.same_other_ref, f32[512,512]{1,0:T(8,128)S(1)} %copy-done.12, ...), custom_call_target="tpu_custom_call" | custom-call | flops 1 | bytes 1 | tf_op jit(solution)/shard_map/pallas_call | solution.py:148
  317.1 3.9 %shard_map.96 = (f32[1024,512]{1,0:T(8,128)S(1)}, s16[528,512]{1,0:T(8,128)(2,1)S(1)}) custom-call(s32[8]{0:T(128)S(1)} %stack.39.flag_ref, bf16[512,3584]{1,0:T(8,128)(2,1)} %copy-done, bf16[512,3584]{1,0:T(8,128)(2,1)} %copy-done.15, bf16[512,896]{1,0:T(8,128)(2,1)S(1)} %collective-permute-done.22.refs_0_.refs_2_, ...), custom_call_target="tpu_custom_call" | custom-call | flops 1 | bytes 1 | tf_op jit(solution)/shard_map/pallas_call | solution.py:148
  321.1 4.3 %shard_map.97 = (f32[448,896]{1,0:T(8,128)S(1)}, s16[464,896]{1,0:T(8,128)(2,1)S(1)}) custom-call(s32[8]{0:T(128)S(1)} %stack.39.flag_ref, bf16[512,448]{1,0:T(8,128)(2,1)S(1)} %dynamic-slice_select_fusion.3.refs_0_, bf16[512,448]{1,0:T(8,128)(2,1)S(1)} %dynamic-slice_select_fusion.2.refs_1_, bf16[512,896]{1,0:T(8,128)(2,1)S(1)} %collective-permute-done.22.refs_0_.refs_2_, ...), custom_call_target="tpu_custom_call" | custom-call | flops 1 | bytes 1 | tf_op jit(solution)/shard_map/pallas_call | solution.py:148
  328.7 4.8 %collective-permute-done.24.coded_ref = s16[464,896]{1,0:T(8,128)(2,1)S(1)} collective-permute-done((s16[464,896]{1,0:T(8,128)(2,1)S(1)}, s16[464,896]{1,0:T(8,128)(2,1)S(1)}, u32[]{:S(2)}, u32[]{:S(2)}) %collective-permute-start.24) | collective-permute-done | bytes 831520 | tf_op jit(solution)/shard_map/ppermute | solution.py:404
  333.5 4.1 %shard_map.98 = (f32[448,3584]{1,0:T(8,128)}, f32[448,3584]{1,0:T(8,128)}) custom-call(s32[8]{0:T(128)S(1)} %stack.39.flag_ref, f32[1]{0:T(128)S(6)} %div.21.scale_ref, f32[448,3584]{1,0:T(8,128)} %bitcast.12, f32[448,896]{1,0:T(8,128)S(1)} %copy-done.10, ...), custom_call_target="tpu_custom_call", output_to_operand_aliasing={{0}: (5, {}), {1}: (6, {})} | custom-call | flops 1 | bytes 1 | tf_op jit(solution)/shard_map/pallas_call | solution.py:148
  340.3 8.8 %collective-permute-done.27.coded_ref = s16[464,896]{1,0:T(8,128)(2,1)S(1)} collective-permute-done((s16[464,896]{1,0:T(8,128)(2,1)S(1)}, s16[464,896]{1,0:T(8,128)(2,1)S(1)}, u32[]{:S(2)}, u32[]{:S(2)}) %collective-permute-start.27) | collective-permute-done | bytes 831520 | tf_op jit(solution)/shard_map/ppermute | solution.py:404
  349.0 4.1 %shard_map.100 = (f32[448,3584]{1,0:T(8,128)}, f32[448,3584]{1,0:T(8,128)}) custom-call(s32[8]{0:T(128)S(1)} %stack.39.flag_ref, f32[1]{0:T(128)S(6)} %div.21.scale_ref, f32[448,3584]{1,0:T(8,128)} %bitcast.13, f32[448,896]{1,0:T(8,128)S(1)} %get-tuple-element.114.value_ref, ...), custom_call_target="tpu_custom_call", output_to_operand_aliasing={{0}: (5, {}), {1}: (6, {})} | custom-call | flops 1 | bytes 1 | tf_op jit(solution)/shard_map/pallas_call | solution.py:148
  353.1 5.0 %shard_map.101 = (f32[512,2048]{1,0:T(8,128)}, f32[512,2048]{1,0:T(8,128)}) custom-call(s32[8]{0:T(128)S(1)} %stack.39.flag_ref, f32[1]{0:T(128)} %bitcast.7.scale_ref, f32[512,2048]{1,0:T(8,128)} %old_ref.3, f32[1024,512]{1,0:T(8,128)S(1)} %copy-done.3, ...), custom_call_target="tpu_custom_call", output_to_operand_aliasing={{0}: (7, {}), {1}: (8, {})} | custom-call | flops 1 | bytes 1 | tf_op jit(solution)/shard_map/pallas_call | solution.py:148
  (108 shorter events, 75.6 us)
Async XLA Ops:
  0.6 6.6 %collective-permute-start.1 = (bf16[512,3584]{1,0:T(8,128)(2,1)}, bf16[512,3584]{1,0:T(8,128)(2,1)}, u32[]{:S(2)}, u32[]{:S(2)}) collective-permute-start(bf16[512,3584]{1,0:T(8,128)(2,1)} %param.5), channel_id=1, source_target_pairs={{4,8},{5,10},{6,9},{7,11},{8,4},{9,6},{10,5},{11,7},{20,24},{21,26... | collective-permute-start | bytes 11010056 | tf_op jit(solution)/shard_map/ppermute | solution.py:404
  3.1 83.8 %collective-permute-start = (bf16[512,3584]{1,0:T(8,128)(2,1)}, bf16[512,3584]{1,0:T(8,128)(2,1)}, u32[]{:S(2)}, u32[]{:S(2)}) collective-permute-start(bf16[512,3584]{1,0:T(8,128)(2,1)} %param.5), channel_id=1, source_target_pairs={{0,4},{1,6},{2,5},{3,7},{4,0},{5,2},{6,1},{7,3},{8,12},{9,14},{10,... | collective-permute-start | bytes 11010056 | tf_op jit(solution)/shard_map/ppermute | solution.py:404
  86.9 45.0 %collective-permute-start.2 = (bf16[512,3584]{1,0:T(8,128)(2,1)}, bf16[512,3584]{1,0:T(8,128)(2,1)}, u32[]{:S(2)}, u32[]{:S(2)}) collective-permute-start(bf16[512,3584]{1,0:T(8,128)(2,1)} %param.5), channel_id=1, source_target_pairs={{1,2},{2,1},{5,6},{6,5},{9,10},{10,9},{13,14},{14,13},{17,18},{18,... | collective-permute-start | bytes 11010056 | tf_op jit(solution)/shard_map/ppermute | solution.py:404
  90.8 45.8 %collective-permute-start.8 = (bf16[512,3584]{1,0:T(8,128)(2,1)}, bf16[512,3584]{1,0:T(8,128)(2,1)}, u32[]{:S(2)}, u32[]{:S(2)}) collective-permute-start(bf16[512,3584]{1,0:T(8,128)(2,1)} %collective-permute-done.refs_1_.refs_6_), channel_id=1, source_target_pairs={{0,1},{1,0},{2,3},{3,2},{4,5},{5,4},{6,7},{7,6},{8,9},{9,8},{10,11... | collective-permute-start | bytes 11010056 | tf_op jit(solution)/shard_map/ppermute | solution.py:404
  90.8 86.7 %collective-permute-start.10 = (bf16[512,3584]{1,0:T(8,128)(2,1)}, bf16[512,3584]{1,0:T(8,128)(2,1)}, u32[]{:S(2)}, u32[]{:S(2)}) collective-permute-start(bf16[512,3584]{1,0:T(8,128)(2,1)} %collective-permute-done.refs_1_.refs_6_), channel_id=1, source_target_pairs={{4,8},{5,9},{6,10},{7,11},{8,4},{9,5},{10,6},{11,7},{20,24},{21,25... | collective-permute-start | bytes 11010056 | tf_op jit(solution)/shard_map/ppermute | solution.py:404
  93.4 84.1 %collective-permute-start.11 = (bf16[512,3584]{1,0:T(8,128)(2,1)}, bf16[512,3584]{1,0:T(8,128)(2,1)}, u32[]{:S(2)}, u32[]{:S(2)}) collective-permute-start(bf16[512,3584]{1,0:T(8,128)(2,1)} %collective-permute-done.1.refs_3_.refs_1_), channel_id=1, source_target_pairs={{0,1},{1,0},{2,3},{3,2},{4,5},{5,4},{6,7},{7,6},{8,9},{9,8},{10,11... | collective-permute-start | bytes 11010056 | tf_op jit(solution)/shard_map/ppermute | solution.py:404
  93.9 83.7 %collective-permute-start.9 = (bf16[512,3584]{1,0:T(8,128)(2,1)}, bf16[512,3584]{1,0:T(8,128)(2,1)}, u32[]{:S(2)}, u32[]{:S(2)}) collective-permute-start(bf16[512,3584]{1,0:T(8,128)(2,1)} %collective-permute-done.1.refs_3_.refs_1_), channel_id=1, source_target_pairs={{4,0},{5,1},{6,2},{7,3},{8,12},{9,13},{10,14},{11,15},{20,16},{21,... | collective-permute-start | bytes 11010056 | tf_op jit(solution)/shard_map/ppermute | solution.py:404
  139.0 7.0 %collective-permute-start.5 = (bf16[512,896]{1,0:T(8,128)(2,1)}, bf16[512,896]{1,0:T(8,128)(2,1)}, u32[]{:S(2)}, u32[]{:S(2)}) collective-permute-start(bf16[512,896]{1,0:T(8,128)(2,1)} %get-tuple-element.127), channel_id=1, source_target_pairs={{0,1},{1,0},{2,3},{3,2},{4,5},{5,4},{6,7},{7,6},{8,9},{9,8},{10,11... | collective-permute-start | bytes 2752520 | tf_op jit(solution)/shard_map/ppermute | solution.py:404
  177.6 6.8 %collective-permute-start.12 = (bf16[512,3584]{1,0:T(8,128)(2,1)}, bf16[512,3584]{1,0:T(8,128)(2,1)}, u32[]{:S(2)}, u32[]{:S(2)}) collective-permute-start(bf16[512,3584]{1,0:T(8,128)(2,1)} %collective-permute-done.9.refs_2_.refs_0_), channel_id=1, source_target_pairs={{0,1},{1,0},{2,3},{3,2},{4,5},{5,4},{6,7},{7,6},{8,9},{9,8},{10,11... | collective-permute-start | bytes 11010056 | tf_op jit(solution)/shard_map/ppermute | solution.py:404
  178.0 44.9 %collective-permute-start.14 = (bf16[512,3584]{1,0:T(8,128)(2,1)}, bf16[512,3584]{1,0:T(8,128)(2,1)}, u32[]{:S(2)}, u32[]{:S(2)}) collective-permute-start(bf16[512,3584]{1,0:T(8,128)(2,1)} %collective-permute-done.10.refs_3_.refs_1_), channel_id=1, source_target_pairs={{0,1},{1,0},{2,3},{3,2},{4,5},{5,4},{6,7},{7,6},{8,9},{9,8},{10,11... | collective-permute-start | bytes 11010056 | tf_op jit(solution)/shard_map/ppermute | solution.py:404
  179.8 43.1 %collective-permute-start.13 = (bf16[512,1792]{1,0:T(8,128)(2,1)S(1)}, bf16[512,1792]{1,0:T(8,128)(2,1)S(1)}, u32[]{:S(2)}, u32[]{:S(2)}) collective-permute-start(bf16[512,1792]{1,0:T(8,128)(2,1)S(1)} %constant_dynamic-slice_fusion.2), channel_id=1, source_target_pairs={{4,0},{5,1},{6,2},{7,3},{8,12},{9,13},{10,14},{11,15},{20,16},{21,... | collective-permute-start | bytes 5505032 | tf_op jit(solution)/shard_map/ppermute | solution.py:404
  181.1 24.8 %collective-permute-start.7 = (s16[1040,512]{1,0:T(8,128)(2,1)S(1)}, s16[1040,512]{1,0:T(8,128)(2,1)S(1)}, u32[]{:S(2)}, u32[]{:S(2)}) collective-permute-start(s16[1040,512]{1,0:T(8,128)(2,1)S(1)} %get-tuple-element.69), channel_id=1, source_target_pairs={{0,2},{1,3},{2,0},{3,1},{4,6},{5,7},{6,4},{7,5},{8,10},{9,11},{10,... | collective-permute-start | bytes 3194888 | tf_op jit(solution)/shard_map/ppermute | solution.py:404
  226.3 47.4 %collective-permute-start.17 = (bf16[512,896]{1,0:T(8,128)(2,1)}, bf16[512,896]{1,0:T(8,128)(2,1)}, u32[]{:S(2)}, u32[]{:S(2)}) collective-permute-start(bf16[512,896]{1,0:T(8,128)(2,1)} %constant_dynamic-slice_fusion), channel_id=1, source_target_pairs={{4,0},{5,1},{6,2},{7,3},{8,12},{9,13},{10,14},{11,15},{20,16},{21,... | collective-permute-start | bytes 2752520 | tf_op jit(solution)/shard_map/ppermute | solution.py:404
  238.5 62.8 %collective-permute-start.19 = (s16[464,1792]{1,0:T(8,128)(2,1)}, s16[464,1792]{1,0:T(8,128)(2,1)}, u32[]{:S(2)}, u32[]{:S(2)}) collective-permute-start(s16[464,1792]{1,0:T(8,128)(2,1)} %get-tuple-element.87), channel_id=1, source_target_pairs={{1,2},{2,1},{5,6},{6,5},{9,10},{10,9},{13,14},{14,13},{17,18},{18,... | collective-permute-start | bytes 4988936 | tf_op jit(solution)/shard_map/ppermute | solution.py:404
  253.0 19.0 %collective-permute-start.16 = (s16[528,512]{1,0:T(8,128)(2,1)}, s16[528,512]{1,0:T(8,128)(2,1)S(1)}, u32[]{:S(2)}, u32[]{:S(2)}) collective-permute-start(s16[528,512]{1,0:T(8,128)(2,1)} %get-tuple-element.86), channel_id=1, source_target_pairs={{0,2},{1,3},{2,0},{3,1},{4,6},{5,7},{6,4},{7,5},{8,10},{9,11},{10,... | collective-permute-start | bytes 1622024 | tf_op jit(solution)/shard_map/ppermute | solution.py:404
  253.0 54.3 %collective-permute-start.21 = (s16[1040,512]{1,0:T(8,128)(2,1)}, s16[1040,512]{1,0:T(8,128)(2,1)}, u32[]{:S(2)}, u32[]{:S(2)}) collective-permute-start(s16[1040,512]{1,0:T(8,128)(2,1)} %get-tuple-element.78), channel_id=1, source_target_pairs={{1,0},{3,2},{5,4},{7,6},{8,9},{10,11},{12,13},{14,15},{17,16},{19,... | collective-permute-start | bytes 3194888 | tf_op jit(solution)/shard_map/ppermute | solution.py:404
  273.7 12.0 %collective-permute-start.18 = (bf16[512,896]{1,0:T(8,128)(2,1)}, bf16[512,896]{1,0:T(8,128)(2,1)S(1)}, u32[]{:S(2)}, u32[]{:S(2)}) collective-permute-start(bf16[512,896]{1,0:T(8,128)(2,1)} %collective-permute-done.17.refs_2_.refs_0_), channel_id=1, source_target_pairs={{0,1},{1,0},{2,3},{3,2},{4,5},{5,4},{6,7},{7,6},{8,9},{9,8},{10,11... | collective-permute-start | bytes 2752520 | tf_op jit(solution)/shard_map/ppermute | solution.py:404
  277.6 36.0 %collective-permute-start.22 = (bf16[512,896]{1,0:T(8,128)(2,1)}, bf16[512,896]{1,0:T(8,128)(2,1)S(1)}, u32[]{:S(2)}, u32[]{:S(2)}) collective-permute-start(bf16[512,896]{1,0:T(8,128)(2,1)} %constant_dynamic-slice_fusion.1), channel_id=1, source_target_pairs={{4,0},{5,1},{6,2},{7,3},{8,12},{9,13},{10,14},{11,15},{20,16},{21,... | collective-permute-start | bytes 2752520 | tf_op jit(solution)/shard_map/ppermute | solution.py:404
  278.9 28.5 %collective-permute-start.20 = (s16[528,512]{1,0:T(8,128)(2,1)}, s16[528,512]{1,0:T(8,128)(2,1)S(1)}, u32[]{:S(2)}, u32[]{:S(2)}) collective-permute-start(s16[528,512]{1,0:T(8,128)(2,1)} %get-tuple-element.89), channel_id=1, source_target_pairs={{0,1},{2,3},{4,5},{6,7},{9,8},{11,10},{13,12},{15,14},{16,17},{18,... | collective-permute-start | bytes 1622024 | tf_op jit(solution)/shard_map/ppermute | solution.py:404
  313.6 7.5 %collective-permute-start.23 = (bf16[512,896]{1,0:T(8,128)(2,1)S(1)}, bf16[512,896]{1,0:T(8,128)(2,1)S(1)}, u32[]{:S(2)}, u32[]{:S(2)}) collective-permute-start(bf16[512,896]{1,0:T(8,128)(2,1)S(1)} %collective-permute-done.22.refs_0_.refs_2_), channel_id=1, source_target_pairs={{0,1},{1,0},{2,3},{3,2},{4,5},{5,4},{6,7},{7,6},{8,9},{9,8},{10,11... | collective-permute-start | bytes 2752520 | tf_op jit(solution)/shard_map/ppermute | solution.py:404
  314.7 18.8 %collective-permute-start.24 = (s16[464,896]{1,0:T(8,128)(2,1)S(1)}, s16[464,896]{1,0:T(8,128)(2,1)S(1)}, u32[]{:S(2)}, u32[]{:S(2)}) collective-permute-start(s16[464,896]{1,0:T(8,128)(2,1)S(1)} %copy-done.14), channel_id=1, source_target_pairs={{1,2},{2,1},{5,6},{6,5},{9,10},{10,9},{13,14},{14,13},{17,18},{18,... | collective-permute-start | bytes 2494472 | tf_op jit(solution)/shard_map/ppermute | solution.py:404
  321.0 17.0 %collective-permute-start.25 = (s16[528,512]{1,0:T(8,128)(2,1)S(1)}, s16[528,512]{1,0:T(8,128)(2,1)S(1)}, u32[]{:S(2)}, u32[]{:S(2)}) collective-permute-start(s16[528,512]{1,0:T(8,128)(2,1)S(1)} %get-tuple-element.110), channel_id=1, source_target_pairs={{0,2},{1,3},{2,0},{3,1},{4,6},{5,7},{6,4},{7,5},{8,10},{9,11},{10,... | collective-permute-start | bytes 1622024 | tf_op jit(solution)/shard_map/ppermute | solution.py:404
  325.4 23.6 %collective-permute-start.27 = (s16[464,896]{1,0:T(8,128)(2,1)S(1)}, s16[464,896]{1,0:T(8,128)(2,1)S(1)}, u32[]{:S(2)}, u32[]{:S(2)}) collective-permute-start(s16[464,896]{1,0:T(8,128)(2,1)S(1)} %get-tuple-element.105), channel_id=1, source_target_pairs={{1,2},{2,1},{5,6},{6,5},{9,10},{10,9},{13,14},{14,13},{17,18},{18,... | collective-permute-start | bytes 2494472 | tf_op jit(solution)/shard_map/ppermute | solution.py:404
  339.0 14.2 %collective-permute-start.26 = (s16[528,512]{1,0:T(8,128)(2,1)S(1)}, s16[528,512]{1,0:T(8,128)(2,1)S(1)}, u32[]{:S(2)}, u32[]{:S(2)}) collective-permute-start(s16[528,512]{1,0:T(8,128)(2,1)S(1)} %get-tuple-element.113), channel_id=1, source_target_pairs={{0,1},{2,3},{4,5},{6,7},{9,8},{11,10},{13,12},{15,14},{16,17},{18,... | collective-permute-start | bytes 1622024 | tf_op jit(solution)/shard_map/ppermute | solution.py:404
  (24 other events, 152.5 us)

commit v6 on v5

--- a/solution.py
+++ b/solution.py
@@ -166,8 +166,14 @@
     return pl.multiple_of(flag * size, GROUP)
 
 
-def blocks_from(at):
-    return lambda k, flags: k + flags[at]
+def blocks_from(at, choice=None):
+    if choice is None:
+        return lambda k, flags: k + flags[at]
+    return lambda k, flags: jnp.where(flags[MIDDLE] == choice, k, 0) + flags[at]
+
+
+def choice_of(options, index):
+    return None if len(options) == 1 else index
 
 
 def left_terms(flags, rows, slots, block, steps, at=START, before=None, last=True):
@@ -217,7 +223,10 @@
 
     ins = [(part, spec((tall, block), blocks_from(at))) for part in rows]
     for slot in slots:
-        ins += [(array, spec((tall, block), blocks_from(start))) for array, start in slot]
+        ins += [
+            (array, spec((tall, block), blocks_from(start, choice_of(slot, index))))
+            for index, (array, start) in enumerate(slot)
+        ]
     if before is not None:
         ins += [(part, whole(part)) for part in before]
     outs = [((size, tall), jnp.float32, spec((size, tall)))] * many
@@ -267,7 +276,10 @@
     here = lambda k, flags: k
     ins = [(part, whole(part)) for part in strips]
     for choice in columns:
-        ins += [(array, spec((rows, block), blocks_from(start))) for array, start in choice]
+        ins += [
+            (array, spec((rows, block), blocks_from(start, choice_of(choice, index))))
+            for index, (array, start) in enumerate(choice)
+        ]
     if before is not None:
         ins.append((before, spec((strip, block), blocks_from(at))))
     outs = [((strip, wide), jnp.float32, spec((strip, block), here))]
@@ -489,36 +501,35 @@
     mates = (mate, send(mate, beside))
     cross_o = send(cross, beside)
     mine = jnp.where(straight, gradient, swapped)
-    starts = range(0, half_wide, block)
+    half = half_wide // 2
     own = (
         mine,
-        jnp.concatenate(
-            [send(mine[:, first : first + block], beside) for first in starts], 1
-        ),
-    )
-    own_product, mate_product, same_coded = left_terms(flags, own, [one(mine), one(mate)], block, 4)
+        jnp.concatenate([send(mine[:, :half], beside), send(mine[:, half:], beside)], 1),
+    )
+    own_product, mate_product, same_coded = left_terms(
+        flags, own, [one(mine), one(mate)], half, 2
+    )
     same_products = [own_product, mate_product]
     same_got = send(same_coded, other_y)
-    [right] = right_terms(
-        flags, strips_of(own) + strips_of(mates), [one(part) for part in own + mates], block, 4
-    )
-
-    right, same_coded, near, far, cross_o = tie(right, same_coded, near, far, cross_o)
+
+    same_coded, near, far, cross_o = tie(same_coded, near, far, cross_o)
     end_home = send(columns(far, 2 * side, 2), outward)
     near_o = send(near, beside)
     far_o = send(far, beside)
     near_product, near_coded = left_terms(
-        flags, own, [[(near, START), (cross, START)]], block, 4
+        flags, own, [[(near, START), (cross, START)]], half, 2
     )
     near_got = send(near_coded, other_y)
+    near_coded, near_o, own_o, mate_o = tie(near_coded, near_o, own[1], mates[1])
+    own, mates = (mine, own_o), (mate, mate_o)
     near_strips = strips_of((jnp.where(is_middle, cross, near), jnp.where(is_middle, cross_o, near_o)))
     [right] = right_terms(
         flags,
-        near_strips,
-        [[(near, START), (cross, START)], [(near_o, START), (cross_o, START)]],
+        strips_of(own) + strips_of(mates) + near_strips,
+        [one(part) for part in own + mates]
+        + [[(near, START), (cross, START)], [(near_o, START), (cross_o, START)]],
         block,
         4,
-        before=right,
     )
     same_got, right = tie(same_got, right)
     same_total, same_out = add_up(flags, same_products, same_got)
@@ -527,10 +538,9 @@
     right, same_out, end_home, far_o = tie(right, same_out, end_home, far_o)
     far, end_home = tie(far, end_home)
     end_first = send(columns(far, 2 * (1 - side), 1), outward)
+    far_next, _ = tie(far, end_first)
+    end_last = send(columns(far_next, 2 * (1 - side) + 1, 1), outward)
     end_home_o = send(end_home, beside)
-    [far_product] = left_terms(
-        flags, own, [[(end_home, START), (far, HOME)]], block, 2, at=HOME, last=False
-    )
     strips = [
         jnp.where(is_middle, strips_of([a])[0], strips_of([b], 2 * side * block)[0])
         for a, b in ((far, end_home), (far_o, end_home_o))
@@ -546,9 +556,10 @@
         last=True,
     )
     home_got = send(home_coded, to_line)
-    near_got, home_coded = tie(near_got, home_coded)
-    near_total, near_out = add_up(flags, [near_product], near_got)
-    near_other = send(near_out, to_away)
+    home_coded, end_home = tie(home_coded, end_home)
+    [far_product] = left_terms(
+        flags, own, [[(end_home, START), (far, HOME)]], block, 2, at=HOME, last=False
+    )
 
     def quarter(end, at, far_product, last):
         end_o = send(end, beside)
@@ -570,14 +581,17 @@
     left_scale = 1.0 / denominator(left_counts).reshape(1)
     right_scale = 1.0 / denominator(right_counts)
     old = right_old[0]
-    near_out, far_product, end_first = tie(near_out, far_product, end_first)
-    far, end_first = tie(far, end_first)
-    end_last = send(columns(far, 2 * (1 - side) + 1, 1), outward)
+    far_product, end_first = tie(far_product, end_first)
     [far_product], right_first, first_coded = quarter(end_first, AWAY, far_product, False)
     first_got = send(first_coded, to_line)
-    first_coded, home_got = tie(first_coded, home_got)
+    first_coded, near_got = tie(first_coded, near_got)
+    near_total, near_out = add_up(flags, [near_product], near_got)
+    near_other = send(near_out, to_away)
+    near_out, home_got = tie(near_out, home_got)
     right_done = finish_right(flags, right_scale, old, right_home, home_got, HOME, block, 2)
-    right_done[0], near_other, same_other = tie(right_done[0], near_other, same_other)
+    right_done[0], near_other, same_other, first_got = tie(
+        right_done[0], near_other, same_other, first_got
+    )
     left_done = finish_left(
         flags, left_scale, left_old, same_total, same_other, near_total, near_other, True
     )

time: 364 us -> 349 us (0.959)
  Pallas kernels: 120 us -> 101 us
  local copies, waits for them, and re-layouts: 23.2 us -> 30.7 us
    pallas_call x18 -> x17, Pallas kernels: 120 us -> 101 us  [kernel_call(): pl.pallas_call(body, grid_spec=pltpu.PrefetchScalarGridSpec(num_scalar_pr...]
    unnamed x43 -> x31, local copies, waits for them, and re-layouts: 9.77 us -> 15.8 us
    ppermute x28 -> x26, starting transfers between devices: 41 us -> 37.5 us  [send(): return lax.ppermute(value, AXES, pairs)]
    ppermute x28 -> x26, waiting for transfers between devices: 163 us -> 163 us  [send(): return lax.ppermute(value, AXES, pairs)]
  transfers between devices with their start and end apart: 28 -> 26, of which waited for: 11 -> 9; matrix products, arithmetic and copies ran while one was open for 7% -> 7% of each run, Pallas kernels for 32% -> 28%
where the time goes in v6:
time: 349 us; the launch traced here: 344 us
  waiting for transfers between devices  163 us (47%)
  Pallas kernels  101 us (29%)
  starting transfers between devices  37.5 us (11%)
  local copies, waits for them, and re-layouts  30.7 us (9%)
  other arithmetic  9.15 us (3%)
    ppermute x26, waiting for transfers between devices, send(): return lax.ppermute(value, AXES, pairs)  163 us
    pallas_call x17, Pallas kernels, kernel_call(): pl.pallas_call(body, grid_spec=pltpu.PrefetchScalarGridSpec(num_scalar_pr...  101 us
    ppermute x26, starting transfers between devices, send(): return lax.ppermute(value, AXES, pairs)  37.5 us
    unnamed x31, local copies, waits for them, and re-layouts  15.8 us
    dynamic_slice x3, local copies, waits for them, and re-layouts, columns(): return lax.dynamic_slice_in_dim(value, first * block, count * block, 1)  7.2 us
  transfers between devices with their start and end apart: 26, of which 9 were waited for; matrix products, arithmetic and copies ran while one was open for 7% of the time, Pallas kernels for 28%

profile of v6, /device:TPU:1, one launch (start us, length us, event | category | flops | bytes accessed | tf_op | source)
XLA Modules:
  0.0 344.1 jit_solution(7017357761428498849)
XLA Ops:
  0.6 3.7 %collective-permute-start = (bf16[512,3584]{1,0:T(8,128)(2,1)}, bf16[512,3584]{1,0:T(8,128)(2,1)}, u32[]{:S(2)}, u32[]{:S(2)}) collective-permute-start(bf16[512,3584]{1,0:T(8,128)(2,1)} %param.5), channel_id=1, source_target_pairs={{0,4},{1,6},{2,5},{3,7},{4,0},{5,2},{6,1},{7,3},{8,12},{9,14},{10,... | collective-permute-start | bytes 11010056 | tf_op jit(solution)/shard_map/ppermute | solution.py:416
  6.8 77.1 %collective-permute-done.refs_1_.refs_8_ = bf16[512,3584]{1,0:T(8,128)(2,1)} collective-permute-done((bf16[512,3584]{1,0:T(8,128)(2,1)}, bf16[512,3584]{1,0:T(8,128)(2,1)}, u32[]{:S(2)}, u32[]{:S(2)}) %collective-permute-start) | collective-permute-done | bytes 3670048 | tf_op jit(solution)/shard_map/ppermute | solution.py:416
  91.2 37.4 %collective-permute-done.2 = bf16[512,3584]{1,0:T(8,128)(2,1)} collective-permute-done((bf16[512,3584]{1,0:T(8,128)(2,1)}, bf16[512,3584]{1,0:T(8,128)(2,1)}, u32[]{:S(2)}, u32[]{:S(2)}) %collective-permute-start.2) | collective-permute-done | bytes 3670048 | tf_op jit(solution)/shard_map/ppermute | solution.py:416
  135.1 6.1 %collective-permute-done.3 = bf16[512,1792]{1,0:T(8,128)(2,1)} collective-permute-done((bf16[512,1792]{1,0:T(8,128)(2,1)}, bf16[512,1792]{1,0:T(8,128)(2,1)}, u32[]{:S(2)}, u32[]{:S(2)}) %collective-permute-start.3) | collective-permute-done | bytes 1835040 | tf_op jit(solution)/shard_map/ppermute | solution.py:416
  146.3 13.6 %shard_map.84 = (f32[1024,512]{1,0:T(8,128)S(1)}, f32[1024,512]{1,0:T(8,128)S(1)}, s16[1040,512]{1,0:T(8,128)(2,1)}) custom-call(s32[8]{0:T(128)S(1)} %stack.39.flag_ref, bf16[512,3584]{1,0:T(8,128)(2,1)} %copy-done.13, bf16[512,3584]{1,0:T(8,128)(2,1)} %copy-done.14, bf16[512,3584]{1,0:T(8,128)(2,1)} %copy-done.13, ...), custom_call_target="tpu_custom_call" | custom-call | flops 1 | bytes 1 | tf_op jit(solution)/shard_map/pallas_call | solution.py:148
  162.5 10.0 %collective-permute-done.6.refs_0_.refs_10_ = bf16[512,3584]{1,0:T(8,128)(2,1)} collective-permute-done((bf16[512,3584]{1,0:T(8,128)(2,1)}, bf16[512,3584]{1,0:T(8,128)(2,1)}, u32[]{:S(2)}, u32[]{:S(2)}) %collective-permute-start.6) | collective-permute-done | bytes 3670048 | tf_op jit(solution)/shard_map/ppermute | solution.py:416
  180.2 8.4 %shard_map.85 = (f32[1024,512]{1,0:T(8,128)S(1)}, s16[528,512]{1,0:T(8,128)(2,1)S(1)}) custom-call(s32[8]{0:T(128)S(1)} %stack.39.flag_ref, bf16[512,3584]{1,0:T(8,128)(2,1)} %copy-done.13, bf16[512,3584]{1,0:T(8,128)(2,1)} %copy-done.14, bf16[512,3584]{1,0:T(8,128)(2,1)} %collective-permute-done.6.refs_0_.refs_10_, ...), custom_call_target="tpu_custom_call" | custom-call | flops 1 | bytes 1 | tf_op jit(solution)/shard_map/pallas_call | solution.py:148
  195.1 18.2 %shard_map.86.refs_6_ = f32[448,3584]{1,0:T(8,128)} custom-call(s32[8]{0:T(128)S(1)} %stack.39.flag_ref, bf16[512,448]{1,0:T(8,128)(2,1)S(1)} %constant_dynamic-slice_fusion.6.refs_0_, bf16[512,448]{1,0:T(8,128)(2,1)S(1)} %get-tuple-element.135.refs_1_, bf16[512,448]{1,0:T(8,128)(2,1)S(1)} %constant_dynamic-slice_fusion.4.refs_2_, ...), custom_call_target="tpu_custom_call" | custom-call | flops 1 | bytes 1 | tf_op jit(solution)/shard_map/pallas_call | solution.py:148
  213.4 4.5 %shard_map.87 = (f32[1024,512]{1,0:T(8,128)S(1)}, s16[1040,512]{1,0:T(8,128)(2,1)}) custom-call(s32[8]{0:T(128)S(1)} %stack.39.flag_ref, f32[1024,512]{1,0:T(8,128)} %copy-done.7, f32[1024,512]{1,0:T(8,128)} %copy-done.8, s16[1040,512]{1,0:T(8,128)(2,1)S(1)} %collective-permute-done.5.refs_2_), custom_call_target="tpu_custom_call" | custom-call | flops 1 | bytes 1 | tf_op jit(solution)/shard_map/pallas_call | solution.py:148
  219.1 4.2 %collective-permute-done.11.refs_2_.refs_0_ = bf16[512,1792]{1,0:T(8,128)(2,1)S(1)} collective-permute-done((bf16[512,1792]{1,0:T(8,128)(2,1)}, bf16[512,1792]{1,0:T(8,128)(2,1)S(1)}, u32[]{:S(2)}, u32[]{:S(2)}) %collective-permute-start.11) | collective-permute-done | bytes 1835040 | tf_op jit(solution)/shard_map/ppermute | solution.py:416
  231.4 7.4 %shard_map.88 = (f32[448,1792]{1,0:T(8,128)}, s16[464,1792]{1,0:T(8,128)(2,1)}) custom-call(s32[8]{0:T(128)S(1)} %stack.39.flag_ref, bf16[512,448]{1,0:T(8,128)(2,1)S(1)} %dynamic-slice_select_fusion.3.refs_0_, bf16[512,448]{1,0:T(8,128)(2,1)S(1)} %dynamic-slice_select_fusion.2.refs_1_, bf16[512,1792]{1,0:T(8,128)(2,1)S(1)} %collective-permute-done.11.refs_2_.refs_0_, ...), custom_call_target="tpu_custom_call" | custom-call | flops 1 | bytes 1 | tf_op jit(solution)/shard_map/pallas_call | solution.py:148
  238.8 5.2 %shard_map.89.refs_2_ = f32[1024,512]{1,0:T(8,128)S(1)} custom-call(s32[8]{0:T(128)S(1)} %stack.39.flag_ref, bf16[512,3584]{1,0:T(8,128)(2,1)} %copy-done.13, bf16[512,3584]{1,0:T(8,128)(2,1)} %copy-done.14, bf16[512,1792]{1,0:T(8,128)(2,1)S(1)} %collective-permute-done.11.refs_2_.refs_0_, bf16[512,3584]{1,0:T(8,128)(2,1)} %collective-permute-done.7.refs_3_.refs_1_), custom_call_target="tpu_custom_call" | custom-call | flops 1 | bytes 1 | tf_op jit(solution)/shard_map/pallas_call | solution.py:148
  245.3 5.4 %collective-permute-done.14.refs_2_.refs_0_ = bf16[512,896]{1,0:T(8,128)(2,1)} collective-permute-done((bf16[512,896]{1,0:T(8,128)(2,1)}, bf16[512,896]{1,0:T(8,128)(2,1)}, u32[]{:S(2)}, u32[]{:S(2)}) %collective-permute-start.14) | collective-permute-done | bytes 917536 | tf_op jit(solution)/shard_map/ppermute | solution.py:416
  261.2 5.8 %shard_map.90 = (f32[448,896]{1,0:T(8,128)S(1)}, s16[464,896]{1,0:T(8,128)(2,1)}) custom-call(s32[8]{0:T(128)S(1)} %stack.39.flag_ref, bf16[512,448]{1,0:T(8,128)(2,1)S(1)} %dynamic-slice_select_fusion.3.refs_0_, bf16[512,448]{1,0:T(8,128)(2,1)S(1)} %dynamic-slice_select_fusion.2.refs_1_, bf16[512,896]{1,0:T(8,128)(2,1)} %collective-permute-done.14.refs_2_.refs_0_, ...), custom_call_target="tpu_custom_call" | custom-call | flops 1 | bytes 1 | tf_op jit(solution)/shard_map/pallas_call | solution.py:148
  270.2 14.2 %collective-permute-done.16.refs_1_ = s16[528,512]{1,0:T(8,128)(2,1)S(1)} collective-permute-done((s16[528,512]{1,0:T(8,128)(2,1)S(1)}, s16[528,512]{1,0:T(8,128)(2,1)S(1)}, u32[]{:S(2)}, u32[]{:S(2)}) %collective-permute-start.16) | collective-permute-done | bytes 540704 | tf_op jit(solution)/shard_map/ppermute | solution.py:416
  289.1 4.0 %shard_map.94.refs_2_ = f32[1024,512]{1,0:T(8,128)S(1)} custom-call(s32[8]{0:T(128)S(1)} %stack.39.flag_ref, bf16[512,3584]{1,0:T(8,128)(2,1)} %copy-done.13, bf16[512,3584]{1,0:T(8,128)(2,1)} %copy-done.14, bf16[512,896]{1,0:T(8,128)(2,1)} %collective-permute-done.14.refs_2_.refs_0_, bf16[512,3584]{1,0:T(8,128)(2,1)} %collective-permute-done.7.refs_3_.refs_1_, ...), custom_call_target="tpu_custom_call" | custom-call | flops 1 | bytes 1 | tf_op jit(solution)/shard_map/pallas_call | solution.py:148
  295.0 5.7 %shard_map.92 = (f32[448,3584]{1,0:T(8,128)}, f32[448,3584]{1,0:T(8,128)}) custom-call(s32[8]{0:T(128)S(1)} %stack.39.flag_ref, f32[1]{0:T(128)S(6)} %div.21.scale_ref, f32[448,3584]{1,0:T(8,128)} %bitcast.11, f32[448,1792]{1,0:T(8,128)S(1)} %copy-done.4, s16[464,1792]{1,0:T(8,128)(2,1)} %collective-permute-done.17.coded_ref), custom_call_target="tpu_custom_call" | custom-call | flops 1 | bytes 1 | tf_op jit(solution)/shard_map/pallas_call | solution.py:148
  300.8 4.9 %shard_map.93 = (f32[512,2048]{1,0:T(8,128)}, f32[512,2048]{1,0:T(8,128)}) custom-call(s32[8]{0:T(128)S(1)} %stack.39.flag_ref, f32[1]{0:T(128)} %bitcast.7.scale_ref, f32[512,2048]{1,0:T(8,128)} %old_ref.3, f32[1024,512]{1,0:T(8,128)S(1)} %copy-done.1, s16[1040,512]{1,0:T(8,128)(2,1)S(1)} %collective-permute-done.19.same_other_ref, ...), custom_call_target="tpu_custom_call" | custom-call | flops 1 | bytes 1 | tf_op jit(solution)/shard_map/pallas_call | solution.py:148
  308.0 3.9 %shard_map.95 = (f32[1024,512]{1,0:T(8,128)S(1)}, s16[528,512]{1,0:T(8,128)(2,1)S(1)}) custom-call(s32[8]{0:T(128)S(1)} %stack.39.flag_ref, bf16[512,3584]{1,0:T(8,128)(2,1)} %copy-done.13, bf16[512,3584]{1,0:T(8,128)(2,1)} %copy-done.14, bf16[512,896]{1,0:T(8,128)(2,1)S(1)} %collective-permute-done.21.refs_0_.refs_2_, ...), custom_call_target="tpu_custom_call" | custom-call | flops 1 | bytes 1 | tf_op jit(solution)/shard_map/pallas_call | solution.py:148
  312.9 4.3 %shard_map.96 = (f32[448,896]{1,0:T(8,128)S(1)}, s16[464,896]{1,0:T(8,128)(2,1)S(1)}) custom-call(s32[8]{0:T(128)S(1)} %stack.39.flag_ref, bf16[512,448]{1,0:T(8,128)(2,1)S(1)} %dynamic-slice_select_fusion.3.refs_0_, bf16[512,448]{1,0:T(8,128)(2,1)S(1)} %dynamic-slice_select_fusion.2.refs_1_, bf16[512,896]{1,0:T(8,128)(2,1)S(1)} %collective-permute-done.21.refs_0_.refs_2_, ...), custom_call_target="tpu_custom_call" | custom-call | flops 1 | bytes 1 | tf_op jit(solution)/shard_map/pallas_call | solution.py:148
  319.9 4.3 %shard_map.97 = (f32[448,3584]{1,0:T(8,128)}, f32[448,3584]{1,0:T(8,128)}) custom-call(s32[8]{0:T(128)S(1)} %stack.39.flag_ref, f32[1]{0:T(128)S(6)} %div.21.scale_ref, f32[448,3584]{1,0:T(8,128)} %bitcast.12, f32[448,896]{1,0:T(8,128)S(1)} %copy-done.10, ...), custom_call_target="tpu_custom_call", output_to_operand_aliasing={{0}: (5, {}), {1}: (6, {})} | custom-call | flops 1 | bytes 1 | tf_op jit(solution)/shard_map/pallas_call | solution.py:148
  328.1 6.8 %collective-permute-done.25.coded_ref = s16[464,896]{1,0:T(8,128)(2,1)S(1)} collective-permute-done((s16[464,896]{1,0:T(8,128)(2,1)S(1)}, s16[464,896]{1,0:T(8,128)(2,1)S(1)}, u32[]{:S(2)}, u32[]{:S(2)}) %collective-permute-start.25) | collective-permute-done | bytes 831520 | tf_op jit(solution)/shard_map/ppermute | solution.py:416
  334.9 4.1 %shard_map.99 = (f32[448,3584]{1,0:T(8,128)}, f32[448,3584]{1,0:T(8,128)}) custom-call(s32[8]{0:T(128)S(1)} %stack.39.flag_ref, f32[1]{0:T(128)S(6)} %div.21.scale_ref, f32[448,3584]{1,0:T(8,128)} %bitcast.13, f32[448,896]{1,0:T(8,128)S(1)} %get-tuple-element.120.value_ref, ...), custom_call_target="tpu_custom_call", output_to_operand_aliasing={{0}: (5, {}), {1}: (6, {})} | custom-call | flops 1 | bytes 1 | tf_op jit(solution)/shard_map/pallas_call | solution.py:148
  339.0 4.7 %shard_map.100 = (f32[512,2048]{1,0:T(8,128)}, f32[512,2048]{1,0:T(8,128)}) custom-call(s32[8]{0:T(128)S(1)} %stack.39.flag_ref, f32[1]{0:T(128)} %bitcast.7.scale_ref, f32[512,2048]{1,0:T(8,128)} %old_ref.3, f32[1024,512]{1,0:T(8,128)S(1)} %copy-done.1, ...), custom_call_target="tpu_custom_call", output_to_operand_aliasing={{0}: (7, {}), {1}: (8, {})} | custom-call | flops 1 | bytes 1 | tf_op jit(solution)/shard_map/pallas_call | solution.py:148
  (90 shorter events, 77.1 us)
Async XLA Ops:
  0.6 83.2 %collective-permute-start = (bf16[512,3584]{1,0:T(8,128)(2,1)}, bf16[512,3584]{1,0:T(8,128)(2,1)}, u32[]{:S(2)}, u32[]{:S(2)}) collective-permute-start(bf16[512,3584]{1,0:T(8,128)(2,1)} %param.5), channel_id=1, source_target_pairs={{0,4},{1,6},{2,5},{3,7},{4,0},{5,2},{6,1},{7,3},{8,12},{9,14},{10,... | collective-permute-start | bytes 11010056 | tf_op jit(solution)/shard_map/ppermute | solution.py:416
  4.3 79.5 %collective-permute-start.1 = (bf16[512,3584]{1,0:T(8,128)(2,1)}, bf16[512,3584]{1,0:T(8,128)(2,1)}, u32[]{:S(2)}, u32[]{:S(2)}) collective-permute-start(bf16[512,3584]{1,0:T(8,128)(2,1)} %param.5), channel_id=1, source_target_pairs={{4,8},{5,10},{6,9},{7,11},{8,4},{9,6},{10,5},{11,7},{20,24},{21,26... | collective-permute-start | bytes 11010056 | tf_op jit(solution)/shard_map/ppermute | solution.py:416
  83.9 44.8 %collective-permute-start.2 = (bf16[512,3584]{1,0:T(8,128)(2,1)}, bf16[512,3584]{1,0:T(8,128)(2,1)}, u32[]{:S(2)}, u32[]{:S(2)}) collective-permute-start(bf16[512,3584]{1,0:T(8,128)(2,1)} %param.5), channel_id=1, source_target_pairs={{1,2},{2,1},{5,6},{6,5},{9,10},{10,9},{13,14},{14,13},{17,18},{18,... | collective-permute-start | bytes 11010056 | tf_op jit(solution)/shard_map/ppermute | solution.py:416
  87.3 85.3 %collective-permute-start.6 = (bf16[512,3584]{1,0:T(8,128)(2,1)}, bf16[512,3584]{1,0:T(8,128)(2,1)}, u32[]{:S(2)}, u32[]{:S(2)}) collective-permute-start(bf16[512,3584]{1,0:T(8,128)(2,1)} %collective-permute-done.1.refs_1_.refs_11_), channel_id=1, source_target_pairs={{4,0},{5,1},{6,2},{7,3},{8,12},{9,13},{10,14},{11,15},{20,16},{21,... | collective-permute-start | bytes 11010056 | tf_op jit(solution)/shard_map/ppermute | solution.py:416
  88.6 84.0 %collective-permute-start.8 = (bf16[512,3584]{1,0:T(8,128)(2,1)}, bf16[512,3584]{1,0:T(8,128)(2,1)}, u32[]{:S(2)}, u32[]{:S(2)}) collective-permute-start(bf16[512,3584]{1,0:T(8,128)(2,1)} %collective-permute-done.1.refs_1_.refs_11_), channel_id=1, source_target_pairs={{0,1},{1,0},{2,3},{3,2},{4,5},{5,4},{6,7},{7,6},{8,9},{9,8},{10,11... | collective-permute-start | bytes 11010056 | tf_op jit(solution)/shard_map/ppermute | solution.py:416
  88.7 83.9 %collective-permute-start.7 = (bf16[512,3584]{1,0:T(8,128)(2,1)}, bf16[512,3584]{1,0:T(8,128)(2,1)}, u32[]{:S(2)}, u32[]{:S(2)}) collective-permute-start(bf16[512,3584]{1,0:T(8,128)(2,1)} %collective-permute-done.refs_1_.refs_8_), channel_id=1, source_target_pairs={{4,8},{5,9},{6,10},{7,11},{8,4},{9,5},{10,6},{11,7},{20,24},{21,25... | collective-permute-start | bytes 11010056 | tf_op jit(solution)/shard_map/ppermute | solution.py:416
  134.5 8.4 %collective-permute-start.4 = (bf16[512,1792]{1,0:T(8,128)(2,1)S(1)}, bf16[512,1792]{1,0:T(8,128)(2,1)}, u32[]{:S(2)}, u32[]{:S(2)}) collective-permute-start(bf16[512,1792]{1,0:T(8,128)(2,1)S(1)} %get-tuple-element.132), channel_id=1, source_target_pairs={{0,1},{1,0},{2,3},{3,2},{4,5},{5,4},{6,7},{7,6},{8,9},{9,8},{10,11... | collective-permute-start | bytes 5505032 | tf_op jit(solution)/shard_map/ppermute | solution.py:416
  144.5 47.2 %collective-permute-start.10 = (bf16[512,3584]{1,0:T(8,128)(2,1)}, bf16[512,3584]{1,0:T(8,128)(2,1)}, u32[]{:S(2)}, u32[]{:S(2)}) collective-permute-start(bf16[512,3584]{1,0:T(8,128)(2,1)} %collective-permute-done.refs_1_.refs_8_), channel_id=1, source_target_pairs={{0,1},{1,0},{2,3},{3,2},{4,5},{5,4},{6,7},{7,6},{8,9},{9,8},{10,11... | collective-permute-start | bytes 11010056 | tf_op jit(solution)/shard_map/ppermute | solution.py:416
  172.6 19.1 %collective-permute-start.9 = (bf16[512,3584]{1,0:T(8,128)(2,1)}, bf16[512,3584]{1,0:T(8,128)(2,1)}, u32[]{:S(2)}, u32[]{:S(2)}) collective-permute-start(bf16[512,3584]{1,0:T(8,128)(2,1)} %collective-permute-done.6.refs_0_.refs_10_), channel_id=1, source_target_pairs={{0,1},{1,0},{2,3},{3,2},{4,5},{5,4},{6,7},{7,6},{8,9},{9,8},{10,11... | collective-permute-start | bytes 11010056 | tf_op jit(solution)/shard_map/ppermute | solution.py:416
  172.6 50.7 %collective-permute-start.12 = (bf16[512,3584]{1,0:T(8,128)(2,1)}, bf16[512,3584]{1,0:T(8,128)(2,1)}, u32[]{:S(2)}, u32[]{:S(2)}) collective-permute-start(bf16[512,3584]{1,0:T(8,128)(2,1)} %collective-permute-done.7.refs_3_.refs_1_), channel_id=1, source_target_pairs={{0,1},{1,0},{2,3},{3,2},{4,5},{5,4},{6,7},{7,6},{8,9},{9,8},{10,11... | collective-permute-start | bytes 11010056 | tf_op jit(solution)/shard_map/ppermute | solution.py:416
  175.9 47.4 %collective-permute-start.11 = (bf16[512,1792]{1,0:T(8,128)(2,1)}, bf16[512,1792]{1,0:T(8,128)(2,1)S(1)}, u32[]{:S(2)}, u32[]{:S(2)}) collective-permute-start(bf16[512,1792]{1,0:T(8,128)(2,1)} %constant_dynamic-slice_fusion.2), channel_id=1, source_target_pairs={{4,0},{5,1},{6,2},{7,3},{8,12},{9,13},{10,14},{11,15},{20,16},{21,... | collective-permute-start | bytes 5505032 | tf_op jit(solution)/shard_map/ppermute | solution.py:416
  177.4 36.0 %collective-permute-start.5 = (s16[1040,512]{1,0:T(8,128)(2,1)}, s16[1040,512]{1,0:T(8,128)(2,1)S(1)}, u32[]{:S(2)}, u32[]{:S(2)}) collective-permute-start(s16[1040,512]{1,0:T(8,128)(2,1)} %get-tuple-element.72), channel_id=1, source_target_pairs={{0,2},{1,3},{2,0},{3,1},{4,6},{5,7},{6,4},{7,5},{8,10},{9,11},{10,... | collective-permute-start | bytes 3194888 | tf_op jit(solution)/shard_map/ppermute | solution.py:416
  226.6 24.2 %collective-permute-start.14 = (bf16[512,896]{1,0:T(8,128)(2,1)}, bf16[512,896]{1,0:T(8,128)(2,1)}, u32[]{:S(2)}, u32[]{:S(2)}) collective-permute-start(bf16[512,896]{1,0:T(8,128)(2,1)} %constant_dynamic-slice_fusion), channel_id=1, source_target_pairs={{4,0},{5,1},{6,2},{7,3},{8,12},{9,13},{10,14},{11,15},{20,16},{21,... | collective-permute-start | bytes 2752520 | tf_op jit(solution)/shard_map/ppermute | solution.py:416
  250.7 10.5 %collective-permute-start.15 = (bf16[512,896]{1,0:T(8,128)(2,1)}, bf16[512,896]{1,0:T(8,128)(2,1)}, u32[]{:S(2)}, u32[]{:S(2)}) collective-permute-start(bf16[512,896]{1,0:T(8,128)(2,1)} %collective-permute-done.14.refs_2_.refs_0_), channel_id=1, source_target_pairs={{0,1},{1,0},{2,3},{3,2},{4,5},{5,4},{6,7},{7,6},{8,9},{9,8},{10,11... | collective-permute-start | bytes 2752520 | tf_op jit(solution)/shard_map/ppermute | solution.py:416
  251.5 41.6 %collective-permute-start.17 = (s16[464,1792]{1,0:T(8,128)(2,1)}, s16[464,1792]{1,0:T(8,128)(2,1)}, u32[]{:S(2)}, u32[]{:S(2)}) collective-permute-start(s16[464,1792]{1,0:T(8,128)(2,1)} %get-tuple-element.92), channel_id=1, source_target_pairs={{1,2},{2,1},{5,6},{6,5},{9,10},{10,9},{13,14},{14,13},{17,18},{18,... | collective-permute-start | bytes 4988936 | tf_op jit(solution)/shard_map/ppermute | solution.py:416
  254.4 30.1 %collective-permute-start.16 = (s16[528,512]{1,0:T(8,128)(2,1)S(1)}, s16[528,512]{1,0:T(8,128)(2,1)S(1)}, u32[]{:S(2)}, u32[]{:S(2)}) collective-permute-start(s16[528,512]{1,0:T(8,128)(2,1)S(1)} %get-tuple-element.75), channel_id=1, source_target_pairs={{0,2},{1,3},{2,0},{3,1},{4,6},{5,7},{6,4},{7,5},{8,10},{9,11},{10,... | collective-permute-start | bytes 1622024 | tf_op jit(solution)/shard_map/ppermute | solution.py:416
  254.5 46.3 %collective-permute-start.19 = (s16[1040,512]{1,0:T(8,128)(2,1)}, s16[1040,512]{1,0:T(8,128)(2,1)S(1)}, u32[]{:S(2)}, u32[]{:S(2)}) collective-permute-start(s16[1040,512]{1,0:T(8,128)(2,1)} %get-tuple-element.84), channel_id=1, source_target_pairs={{1,0},{3,2},{5,4},{7,6},{8,9},{10,11},{12,13},{14,15},{17,16},{19,... | collective-permute-start | bytes 3194888 | tf_op jit(solution)/shard_map/ppermute | solution.py:416
  259.8 46.0 %collective-permute-start.21 = (bf16[512,896]{1,0:T(8,128)(2,1)}, bf16[512,896]{1,0:T(8,128)(2,1)S(1)}, u32[]{:S(2)}, u32[]{:S(2)}) collective-permute-start(bf16[512,896]{1,0:T(8,128)(2,1)} %constant_dynamic-slice_fusion.1), channel_id=1, source_target_pairs={{4,0},{5,1},{6,2},{7,3},{8,12},{9,13},{10,14},{11,15},{20,16},{21,... | collective-permute-start | bytes 2752520 | tf_op jit(solution)/shard_map/ppermute | solution.py:416
  268.2 32.6 %collective-permute-start.20 = (s16[464,896]{1,0:T(8,128)(2,1)}, s16[464,896]{1,0:T(8,128)(2,1)}, u32[]{:S(2)}, u32[]{:S(2)}) collective-permute-start(s16[464,896]{1,0:T(8,128)(2,1)} %get-tuple-element.95), channel_id=1, source_target_pairs={{1,2},{2,1},{5,6},{6,5},{9,10},{10,9},{13,14},{14,13},{17,18},{18,... | collective-permute-start | bytes 2494472 | tf_op jit(solution)/shard_map/ppermute | solution.py:416
  286.3 14.4 %collective-permute-start.18 = (s16[528,512]{1,0:T(8,128)(2,1)S(1)}, s16[528,512]{1,0:T(8,128)(2,1)S(1)}, u32[]{:S(2)}, u32[]{:S(2)}) collective-permute-start(s16[528,512]{1,0:T(8,128)(2,1)S(1)} %get-tuple-element.97), channel_id=1, source_target_pairs={{0,1},{2,3},{4,5},{6,7},{9,8},{11,10},{13,12},{15,14},{16,17},{18,... | collective-permute-start | bytes 1622024 | tf_op jit(solution)/shard_map/ppermute | solution.py:416
  305.7 7.1 %collective-permute-start.22 = (bf16[512,896]{1,0:T(8,128)(2,1)S(1)}, bf16[512,896]{1,0:T(8,128)(2,1)S(1)}, u32[]{:S(2)}, u32[]{:S(2)}) collective-permute-start(bf16[512,896]{1,0:T(8,128)(2,1)S(1)} %collective-permute-done.21.refs_0_.refs_2_), channel_id=1, source_target_pairs={{0,1},{1,0},{2,3},{3,2},{4,5},{5,4},{6,7},{7,6},{8,9},{9,8},{10,11... | collective-permute-start | bytes 2752520 | tf_op jit(solution)/shard_map/ppermute | solution.py:416
  311.9 14.0 %collective-permute-start.23 = (s16[528,512]{1,0:T(8,128)(2,1)S(1)}, s16[528,512]{1,0:T(8,128)(2,1)S(1)}, u32[]{:S(2)}, u32[]{:S(2)}) collective-permute-start(s16[528,512]{1,0:T(8,128)(2,1)S(1)} %get-tuple-element.116), channel_id=1, source_target_pairs={{0,2},{1,3},{2,0},{3,1},{4,6},{5,7},{6,4},{7,5},{8,10},{9,11},{10,... | collective-permute-start | bytes 1622024 | tf_op jit(solution)/shard_map/ppermute | solution.py:416
  317.2 17.7 %collective-permute-start.25 = (s16[464,896]{1,0:T(8,128)(2,1)S(1)}, s16[464,896]{1,0:T(8,128)(2,1)S(1)}, u32[]{:S(2)}, u32[]{:S(2)}) collective-permute-start(s16[464,896]{1,0:T(8,128)(2,1)S(1)} %get-tuple-element.110), channel_id=1, source_target_pairs={{1,2},{2,1},{5,6},{6,5},{9,10},{10,9},{13,14},{14,13},{17,18},{18,... | collective-permute-start | bytes 2494472 | tf_op jit(solution)/shard_map/ppermute | solution.py:416
  326.8 12.2 %collective-permute-start.24 = (s16[528,512]{1,0:T(8,128)(2,1)S(1)}, s16[528,512]{1,0:T(8,128)(2,1)S(1)}, u32[]{:S(2)}, u32[]{:S(2)}) collective-permute-start(s16[528,512]{1,0:T(8,128)(2,1)S(1)} %get-tuple-element.119), channel_id=1, source_target_pairs={{0,1},{2,3},{4,5},{6,7},{9,8},{11,10},{13,12},{15,14},{16,17},{18,... | collective-permute-start | bytes 1622024 | tf_op jit(solution)/shard_map/ppermute | solution.py:416
  (17 other events, 92.5 us)

commit v7 on v6

--- a/solution.py
+++ b/solution.py
@@ -1,4 +1,5 @@
 import functools
+import math
 
 import jax
 import jax.numpy as jnp
@@ -131,7 +132,7 @@
 
 PARAMS = pltpu.CompilerParams(vmem_limit_bytes=48 * 2**20)
 FREE = pl.CostEstimate(flops=1, bytes_accessed=1, transcendentals=0)
-KEPT, START, HOME, AWAY, LAST, SAME_HALF, MIDDLE, CORE = range(8)
+KEPT, START, NEXT, HOME, AWAY, LAST, SAME_HALF, MIDDLE, CORE = range(9)
 
 
 def spec(shape, index=None):
@@ -331,65 +332,62 @@
                 old_ref[...], unpack(coded_ref, 0, strip, 1), scale_ref[0], state_ref, fixed_ref, everything
             )
 
-    here = lambda k, flags: k
-    there = lambda k, flags: k + flags[at]
+    part = math.gcd(block * steps, 256)
+    there = lambda k, flags: k + flags[at] * block // part
     ins = [
         (scale, pl.BlockSpec(memory_space=pltpu.SMEM)),
-        (old, spec((strip, block), there)),
-        (value, spec((strip, block), here)),
-        (coded, spec((strip + LEVELS, block), here)),
+        (old, spec((strip, part), there)),
+        (value, spec((strip, part), lambda k, flags: k * (1 - flags[KEPT]))),
+        (coded, spec((strip + LEVELS, part), lambda k, flags: k * flags[KEPT])),
     ]
     aliases = None
     if written is not None:
         ins += [(array, pl.BlockSpec(memory_space=pl.ANY)) for array in written]
         aliases = {5: 0, 6: 1}
-    outs = [((strip, wide), jnp.float32, spec((strip, block), there))] * 2
-    return kernel_call(body, flags, steps, ins, outs, aliases)
+    outs = [((strip, wide), jnp.float32, spec((strip, part), there))] * 2
+    return kernel_call(body, flags, steps * block // part, ins, outs, aliases)
 
 
 def finish_left(flags, scale, old, same_total, same_other, total, other, inner, written=None):
     tall, wide = total.shape
-    plane = 2 * wide
 
     def body(flag_ref, scale_ref, old_ref, same_ref, same_other_ref, total_ref, other_ref, *refs):
         state_ref, fixed_ref = refs[-2:]
 
-        def put(core, value):
-            where = slice(core * wide, (core + 1) * wide)
-            write_states(old_ref[:, where], value, scale_ref[0], state_ref, fixed_ref, where)
+        def put(value):
+            write_states(old_ref[...], value, scale_ref[0], state_ref, fixed_ref, slice(None))
 
         is_mate = 1 - flag_ref[MIDDLE] if inner else flag_ref[MIDDLE]
-        for core in range(2):
-            mine = flag_ref[CORE] == core
-            same = flag_ref[SAME_HALF] == 1
-
-            @pl.when(mine & same)
+        mine = flag_ref[CORE] == pl.program_id(0)
+        same = flag_ref[SAME_HALF] == 1
+
+        @pl.when(mine & same)
+        def _():
+            put(same_ref[pl.ds(pick(is_mate, tall), tall), :])
+
+        @pl.when(mine & jnp.logical_not(same))
+        def _():
+            put(total_ref[...])
+
+        for index in range(2):
+
+            @pl.when(jnp.logical_not(mine) & same & (is_mate == index))
             def _():
-                put(core, same_ref[pl.ds(pick(is_mate, tall), tall), :])
-
-            @pl.when(mine & jnp.logical_not(same))
-            def _():
-                put(core, total_ref[...])
-
-            for index in range(2):
-
-                @pl.when(jnp.logical_not(mine) & same & (is_mate == index))
-                def _():
-                    put(core, unpack(same_other_ref, index, tall, 2))
-
-            @pl.when(jnp.logical_not(mine) & jnp.logical_not(same))
-            def _():
-                put(core, unpack(other_ref, 0, tall, 1))
-
-    there = (lambda k, flags: 1 - flags[CORE]) if inner else (lambda k, flags: flags[CORE])
-    ins = [(scale, pl.BlockSpec(memory_space=pltpu.SMEM)), (old, spec((tall, plane), there))]
+                put(unpack(same_other_ref, index, tall, 2))
+
+        @pl.when(jnp.logical_not(mine) & jnp.logical_not(same))
+        def _():
+            put(unpack(other_ref, 0, tall, 1))
+
+    there = lambda k, flags: 2 * (1 - flags[CORE] if inner else flags[CORE]) + k
+    ins = [(scale, pl.BlockSpec(memory_space=pltpu.SMEM)), (old, spec((tall, wide), there))]
     ins += [(array, whole(array)) for array in (same_total, same_other, total, other)]
     aliases = None
     if written is not None:
         ins += [(array, pl.BlockSpec(memory_space=pl.ANY)) for array in written]
         aliases = {7: 0, 8: 1}
-    outs = [(old.shape, jnp.float32, spec((tall, plane), there))] * 2
-    return kernel_call(body, flags, 1, ins, outs, aliases)
+    outs = [(old.shape, jnp.float32, spec((tall, wide), there))] * 2
+    return kernel_call(body, flags, 2, ins, outs, aliases)
 
 
 def dot(a, b, a_dim, b_dim):
@@ -470,6 +468,7 @@
         [
             jnp.where(straight, 0, 1),
             0,
+            1,
             2 * side,
             2 * (1 - side),
             2 * (1 - side) + 1,
@@ -499,7 +498,15 @@
     near = send(cross, outward)
     swapped = send(gradient_t, to_line)
     mates = (mate, send(mate, beside))
-    cross_o = send(cross, beside)
+    crosses = (cross, send(cross, beside))
+    [right] = right_terms(
+        flags,
+        strips_of(mates) + strips_of(crosses),
+        [one(part) for part in mates + crosses],
+        block,
+        4,
+    )
+    right, swapped = tie(right, swapped)
     mine = jnp.where(straight, gradient, swapped)
     half = half_wide // 2
     own = (
@@ -511,109 +518,95 @@
     )
     same_products = [own_product, mate_product]
     same_got = send(same_coded, other_y)
-
-    same_coded, near, far, cross_o = tie(same_coded, near, far, cross_o)
+    same_coded, own_o = tie(same_coded, own[1])
+    own = (mine, own_o)
+    [right] = right_terms(
+        flags, strips_of(own), [one(part) for part in own], block, 4, before=right
+    )
+
+    right, near, far = tie(right, near, far)
     end_home = send(columns(far, 2 * side, 2), outward)
-    near_o = send(near, beside)
+    nears = (near, send(near, beside))
     far_o = send(far, beside)
     near_product, near_coded = left_terms(
         flags, own, [[(near, START), (cross, START)]], half, 2
     )
     near_got = send(near_coded, other_y)
-    near_coded, near_o, own_o, mate_o = tie(near_coded, near_o, own[1], mates[1])
-    own, mates = (mine, own_o), (mate, mate_o)
-    near_strips = strips_of((jnp.where(is_middle, cross, near), jnp.where(is_middle, cross_o, near_o)))
+    near_coded, near, near_o = tie(near_coded, *nears)
+    nears = (near, near_o)
     [right] = right_terms(
-        flags,
-        strips_of(own) + strips_of(mates) + near_strips,
-        [one(part) for part in own + mates]
-        + [[(near, START), (cross, START)], [(near_o, START), (cross_o, START)]],
-        block,
-        4,
+        flags, strips_of(nears), [one(part) for part in nears], block, 4, before=right
     )
     same_got, right = tie(same_got, right)
     same_total, same_out = add_up(flags, same_products, same_got)
     same_other = send(same_out, to_home)
-
-    right, same_out, end_home, far_o = tie(right, same_out, end_home, far_o)
+    same_out, near_got = tie(same_out, near_got)
+    near_total, near_out = add_up(flags, [near_product], near_got)
+    near_other = send(near_out, to_away)
+
+    right, near_out, end_home, far_o = tie(right, near_out, end_home, far_o)
     far, end_home = tie(far, end_home)
-    end_first = send(columns(far, 2 * (1 - side), 1), outward)
-    far_next, _ = tie(far, end_first)
-    end_last = send(columns(far_next, 2 * (1 - side) + 1, 1), outward)
+    end_away = send(columns(far, 2 * (1 - side), 2), outward)
     end_home_o = send(end_home, beside)
     strips = [
         jnp.where(is_middle, strips_of([a])[0], strips_of([b], 2 * side * block)[0])
         for a, b in ((far, end_home), (far_o, end_home_o))
     ]
-    right_home, home_coded = right_terms(
-        flags,
-        strips,
-        [[(end_home, START), (far, HOME)], [(end_home_o, START), (far_o, HOME)]],
-        block,
-        2,
-        at=HOME,
-        before=right,
-        last=True,
-    )
+
+    def last_right(end, end_o, start, at, steps):
+        return right_terms(
+            flags,
+            strips,
+            [[(end, start), (far, at)], [(end_o, start), (far_o, at)]],
+            block,
+            steps,
+            at=at,
+            before=right,
+            last=True,
+        )
+
+    right_home, home_coded = last_right(end_home, end_home_o, START, HOME, 2)
     home_got = send(home_coded, to_line)
     home_coded, end_home = tie(home_coded, end_home)
     [far_product] = left_terms(
         flags, own, [[(end_home, START), (far, HOME)]], block, 2, at=HOME, last=False
     )
-
-    def quarter(end, at, far_product, last):
-        end_o = send(end, beside)
-        lefts = left_terms(
-            flags, own, [[(end, START), (far, at)]], block, 1, at=at, before=[far_product], last=last
-        )
-        value, coded = right_terms(
-            flags,
-            strips,
-            [[(end, START), (far, at)], [(end_o, START), (far_o, at)]],
-            block,
-            1,
-            at=at,
-            before=right,
-            last=True,
-        )
-        return lefts, value, coded
-
     left_scale = 1.0 / denominator(left_counts).reshape(1)
     right_scale = 1.0 / denominator(right_counts)
     old = right_old[0]
-    far_product, end_first = tie(far_product, end_first)
-    [far_product], right_first, first_coded = quarter(end_first, AWAY, far_product, False)
-    first_got = send(first_coded, to_line)
-    first_coded, near_got = tie(first_coded, near_got)
-    near_total, near_out = add_up(flags, [near_product], near_got)
-    near_other = send(near_out, to_away)
-    near_out, home_got = tie(near_out, home_got)
-    right_done = finish_right(flags, right_scale, old, right_home, home_got, HOME, block, 2)
-    right_done[0], near_other, same_other, first_got = tie(
-        right_done[0], near_other, same_other, first_got
-    )
+    far_product, near_other, same_other = tie(far_product, near_other, same_other)
     left_done = finish_left(
         flags, left_scale, left_old, same_total, same_other, near_total, near_other, True
     )
-
-    left_done[0], far_product, end_last = tie(left_done[0], far_product, end_last)
-    [far_product, far_coded], right_last, last_coded = quarter(end_last, LAST, far_product, True)
+    left_done[0], home_got = tie(left_done[0], home_got)
+    right_done = finish_right(flags, right_scale, old, right_home, home_got, HOME, block, 2)
+
+    right_done[0], far_product, end_away = tie(right_done[0], far_product, end_away)
+    end_away_o = send(end_away, beside)
+    far_product, far_coded = left_terms(
+        flags, own, [[(end_away, START), (far, AWAY)]], block, 2, at=AWAY, before=[far_product]
+    )
     far_got = send(far_coded, other_y)
+    far_coded, end_away_o = tie(far_coded, end_away_o)
+    right_away, away_coded = last_right(end_away, end_away_o, START, AWAY, 1)
+    away_got = send(away_coded, to_line)
+    away_coded, end_away_o = tie(away_coded, end_away_o)
+    right_last, last_coded = last_right(end_away, end_away_o, NEXT, LAST, 1)
     last_got = send(last_coded, to_line)
-    last_coded, first_got = tie(last_coded, first_got)
-    right_done = finish_right(
-        flags, right_scale, old, right_first, first_got, AWAY, block, 1, right_done
-    )
-    right_done[0], far_got = tie(right_done[0], far_got)
+    last_coded, far_got = tie(last_coded, far_got)
     far_total, far_out = add_up(flags, [far_product], far_got)
     far_other = send(far_out, to_away)
-    far_out, last_got = tie(far_out, last_got)
+    far_out, away_got = tie(far_out, away_got)
+    right_done = finish_right(
+        flags, right_scale, old, right_away, away_got, AWAY, block, 1, right_done
+    )
+    right_done[0], far_other = tie(right_done[0], far_other)
+    left_state, left_fixed = finish_left(
+        flags, left_scale, left_old, same_total, same_other, far_total, far_other, False, left_done
+    )
+    left_state, last_got = tie(left_state, last_got)
     right_state, right_fixed = finish_right(
         flags, right_scale, old, right_last, last_got, LAST, block, 1, right_done
-    )
-    far_other, right_state = tie(far_other, right_state)
-    left_state, left_fixed = finish_left(
-        flags, left_scale, left_old, same_total, same_other, far_total, far_other, False, left_done
     )
     return (left_state, left_fixed, right_state[None], right_fixed[None])
 

time: 349 us -> 320 us (0.917)
  waiting for transfers between devices: 163 us -> 135 us
  Pallas kernels: 101 us -> 117 us
  local copies, waits for them, and re-layouts: 30.7 us -> 25.4 us
  starting transfers between devices: 37.5 us -> 32.8 us
    ppermute x26 -> x24, waiting for transfers between devices: 163 us -> 135 us  [send(): return lax.ppermute(value, AXES, pairs)]
    pallas_call x17 -> x18, Pallas kernels: 101 us -> 117 us  [kernel_call(): pl.pallas_call(body, grid_spec=pltpu.PrefetchScalarGridSpec(num_scalar_pr...]
    dynamic_slice x3 -> x7, local copies, waits for them, and re-layouts: 4.5 us -> 9.31 us  [strips_of(): lax.dynamic_slice_in_dim(part, strip_at - first, strip, 1)]
    unnamed x31 -> x35, local copies, waits for them, and re-layouts: 15.8 us -> 11.1 us
    ppermute x26 -> x24, starting transfers between devices: 37.5 us -> 32.8 us  [send(): return lax.ppermute(value, AXES, pairs)]
    dynamic_slice x3 -> x2, local copies, waits for them, and re-layouts: 7.2 us -> 4.55 us  [columns(): return lax.dynamic_slice_in_dim(value, first * block, count * block, 1)]
  transfers between devices with their start and end apart: 26 -> 24, of which waited for: 9 -> 11; matrix products, arithmetic and copies ran while one was open for 7% -> 6% of each run, Pallas kernels for 28% -> 35%
where the time goes in v7:
time: 320 us; the launch traced here: 319 us
  waiting for transfers between devices  135 us (42%)
  Pallas kernels  117 us (37%)
  starting transfers between devices  32.8 us (10%)
  local copies, waits for them, and re-layouts  25.4 us (8%)
  other arithmetic  5.78 us (2%)
    ppermute x24, waiting for transfers between devices, send(): return lax.ppermute(value, AXES, pairs)  135 us
    pallas_call x18, Pallas kernels, kernel_call(): pl.pallas_call(body, grid_spec=pltpu.PrefetchScalarGridSpec(num_scalar_pr...  117 us
    ppermute x24, starting transfers between devices, send(): return lax.ppermute(value, AXES, pairs)  32.8 us
    unnamed x35, local copies, waits for them, and re-layouts  11.1 us
    dynamic_slice x7, local copies, waits for them, and re-layouts, strips_of(): lax.dynamic_slice_in_dim(part, strip_at - first, strip, 1)  9.31 us
  transfers between devices with their start and end apart: 24, of which 11 were waited for; matrix products, arithmetic and copies ran while one was open for 6% of the time, Pallas kernels for 35%

profile of v7, /device:TPU:1, one launch (start us, length us, event | category | flops | bytes accessed | tf_op | source)
XLA Modules:
  0.0 318.5 jit_solution(1484059654057242944)
XLA Ops:
  0.6 3.7 %collective-permute-start = (bf16[512,3584]{1,0:T(8,128)(2,1)}, bf16[512,3584]{1,0:T(8,128)(2,1)}, u32[]{:S(2)}, u32[]{:S(2)}) collective-permute-start(bf16[512,3584]{1,0:T(8,128)(2,1)} %param.5), channel_id=1, source_target_pairs={{0,4},{1,6},{2,5},{3,7},{4,0},{5,2},{6,1},{7,3},{8,12},{9,14},{10,... | collective-permute-start | bytes 11010056 | tf_op jit(solution)/shard_map/ppermute | solution.py:414
  6.8 77.1 %collective-permute-done.refs_4_.refs_1_ = bf16[512,3584]{1,0:T(8,128)(2,1)} collective-permute-done((bf16[512,3584]{1,0:T(8,128)(2,1)}, bf16[512,3584]{1,0:T(8,128)(2,1)}, u32[]{:S(2)}, u32[]{:S(2)}) %collective-permute-start) | collective-permute-done | bytes 3670048 | tf_op jit(solution)/shard_map/ppermute | solution.py:414
  97.2 13.6 %shard_map.84.refs_4_ = f32[448,3584]{1,0:T(8,128)} custom-call(s32[9]{0:T(128)S(1)} %stack.39.flag_ref, bf16[512,448]{1,0:T(8,128)(2,1)S(1)} %get-tuple-element.137.refs_0_, bf16[512,448]{1,0:T(8,128)(2,1)S(1)} %constant_dynamic-slice_fusion.8.refs_1_, bf16[512,448]{1,0:T(8,128)(2,1)S(1)} %get-tuple-element.136.refs_2_, ...), custom_call_target="tpu_custom_call" | custom-call | flops 1 | bytes 1 | tf_op jit(solution)/shard_map/pallas_call | solution.py:149
  110.8 18.4 %collective-permute-done.4 = bf16[512,3584]{1,0:T(8,128)(2,1)} collective-permute-done((bf16[512,3584]{1,0:T(8,128)(2,1)}, bf16[512,3584]{1,0:T(8,128)(2,1)}, u32[]{:S(2)}, u32[]{:S(2)}) %collective-permute-start.4) | collective-permute-done | bytes 3670048 | tf_op jit(solution)/shard_map/ppermute | solution.py:414
  140.4 12.7 %shard_map.85 = (f32[1024,512]{1,0:T(8,128)S(1)}, f32[1024,512]{1,0:T(8,128)S(1)}, s16[1040,512]{1,0:T(8,128)(2,1)S(1)}) custom-call(s32[9]{0:T(128)S(1)} %stack.39.flag_ref, bf16[512,3584]{1,0:T(8,128)(2,1)} %copy-done, bf16[512,3584]{1,0:T(8,128)(2,1)} %copy-done.14, bf16[512,3584]{1,0:T(8,128)(2,1)} %copy-done, ...), custom_call_target="tpu_custom_call" | custom-call | flops 1 | bytes 1 | tf_op jit(solution)/shard_map/pallas_call | solution.py:149
  156.3 9.8 %shard_map.86.refs_4_ = f32[448,3584]{1,0:T(8,128)} custom-call(s32[9]{0:T(128)S(1)} %stack.39.flag_ref, bf16[512,448]{1,0:T(8,128)(2,1)S(1)} %constant_dynamic-slice_fusion.5.refs_0_, bf16[512,448]{1,0:T(8,128)(2,1)S(1)} %constant_dynamic-slice_fusion.4.refs_1_, bf16[512,3584]{1,0:T(8,128)(2,1)S(1)} %copy-done.1, bf16[512,3584]{1,0:T(8,128)(2,1)} %copy-done.14, ...), custom_call_target="tpu_custom_call" | custom-call | flops 1 | bytes 1 | tf_op jit(solution)/shard_map/pallas_call | solution.py:149
  166.1 7.0 %collective-permute-done.8.refs_0_.refs_2_ = bf16[512,3584]{1,0:T(8,128)(2,1)} collective-permute-done((bf16[512,3584]{1,0:T(8,128)(2,1)}, bf16[512,3584]{1,0:T(8,128)(2,1)}, u32[]{:S(2)}, u32[]{:S(2)}) %collective-permute-start.8) | collective-permute-done | bytes 3670048 | tf_op jit(solution)/shard_map/ppermute | solution.py:414
  177.8 8.4 %shard_map.87 = (f32[1024,512]{1,0:T(8,128)S(1)}, s16[528,512]{1,0:T(8,128)(2,1)S(1)}) custom-call(s32[9]{0:T(128)S(1)} %stack.39.flag_ref, bf16[512,3584]{1,0:T(8,128)(2,1)} %copy-done, bf16[512,3584]{1,0:T(8,128)(2,1)} %copy-done.14, bf16[512,3584]{1,0:T(8,128)(2,1)} %collective-permute-done.8.refs_0_.refs_2_, ...), custom_call_target="tpu_custom_call" | custom-call | flops 1 | bytes 1 | tf_op jit(solution)/shard_map/pallas_call | solution.py:149
  189.5 10.7 %shard_map.88.refs_6_ = f32[448,3584]{1,0:T(8,128)} custom-call(s32[9]{0:T(128)S(1)} %stack.39.flag_ref, bf16[512,448]{1,0:T(8,128)(2,1)S(1)} %constant_dynamic-slice_fusion.3.refs_0_, bf16[512,448]{1,0:T(8,128)(2,1)S(1)} %constant_dynamic-slice_fusion.2.refs_1_, bf16[512,3584]{1,0:T(8,128)(2,1)} %collective-permute-done.8.refs_0_.refs_2_, ...), custom_call_target="tpu_custom_call" | custom-call | flops 1 | bytes 1 | tf_op jit(solution)/shard_map/pallas_call | solution.py:149
  201.9 3.5 %shard_map.89 = (f32[1024,512]{1,0:T(8,128)S(1)}, s16[1040,512]{1,0:T(8,128)(2,1)S(1)}) custom-call(s32[9]{0:T(128)S(1)} %stack.39.flag_ref, f32[1024,512]{1,0:T(8,128)} %copy-done.6, f32[1024,512]{1,0:T(8,128)} %copy-done.7, s16[1040,512]{1,0:T(8,128)(2,1)S(1)} %collective-permute-done.7.refs_2_), custom_call_target="tpu_custom_call" | custom-call | flops 1 | bytes 1 | tf_op jit(solution)/shard_map/pallas_call | solution.py:149
  206.8 6.8 %collective-permute-done.11.refs_1_ = s16[528,512]{1,0:T(8,128)(2,1)S(1)} collective-permute-done((s16[528,512]{1,0:T(8,128)(2,1)S(1)}, s16[528,512]{1,0:T(8,128)(2,1)S(1)}, u32[]{:S(2)}, u32[]{:S(2)}) %collective-permute-start.11) | collective-permute-done | bytes 540704 | tf_op jit(solution)/shard_map/ppermute | solution.py:414
  215.4 6.8 %collective-permute-done.12.refs_2_.refs_0_ = bf16[512,1792]{1,0:T(8,128)(2,1)S(1)} collective-permute-done((bf16[512,1792]{1,0:T(8,128)(2,1)S(1)}, bf16[512,1792]{1,0:T(8,128)(2,1)S(1)}, u32[]{:S(2)}, u32[]{:S(2)}) %collective-permute-start.12) | collective-permute-done | bytes 1835040 | tf_op jit(solution)/shard_map/ppermute | solution.py:414
  230.7 7.4 %shard_map.91 = (f32[448,1792]{1,0:T(8,128)}, s16[464,1792]{1,0:T(8,128)(2,1)}) custom-call(s32[9]{0:T(128)S(1)} %stack.39.flag_ref, bf16[512,448]{1,0:T(8,128)(2,1)S(1)} %dynamic-slice_select_fusion.1.refs_0_, bf16[512,448]{1,0:T(8,128)(2,1)S(1)} %dynamic-slice_select_fusion.refs_1_, bf16[512,1792]{1,0:T(8,128)(2,1)S(1)} %collective-permute-done.12.refs_2_.refs_0_, ...), custom_call_target="tpu_custom_call" | custom-call | flops 1 | bytes 1 | tf_op jit(solution)/shard_map/pallas_call | solution.py:149
  244.8 5.5 %shard_map.92.refs_2_ = f32[1024,512]{1,0:T(8,128)S(1)} custom-call(s32[9]{0:T(128)S(1)} %stack.39.flag_ref, bf16[512,3584]{1,0:T(8,128)(2,1)} %copy-done, bf16[512,3584]{1,0:T(8,128)(2,1)} %copy-done.14, bf16[512,1792]{1,0:T(8,128)(2,1)S(1)} %collective-permute-done.12.refs_2_.refs_0_, bf16[512,3584]{1,0:T(8,128)(2,1)} %collective-permute-done.9.refs_3_.refs_1_), custom_call_target="tpu_custom_call" | custom-call | flops 1 | bytes 1 | tf_op jit(solution)/shard_map/pallas_call | solution.py:149
  250.4 4.2 %shard_map.93 = (f32[512,2048]{1,0:T(8,128)}, f32[512,2048]{1,0:T(8,128)}) custom-call(s32[9]{0:T(128)S(1)} %stack.39.flag_ref, f32[1]{0:T(128)} %bitcast.7.scale_ref, f32[512,2048]{1,0:T(8,128)} %old_ref.3, f32[1024,512]{1,0:T(8,128)S(1)} %copy-done.3, s16[1040,512]{1,0:T(8,128)(2,1)S(1)} %collective-permute-done.16.same_other_ref, ...), custom_call_target="tpu_custom_call" | custom-call | flops 1 | bytes 1 | tf_op jit(solution)/shard_map/pallas_call | solution.py:149
  254.6 6.7 %collective-permute-done.17.coded_ref = s16[464,1792]{1,0:T(8,128)(2,1)S(1)} collective-permute-done((s16[464,1792]{1,0:T(8,128)(2,1)}, s16[464,1792]{1,0:T(8,128)(2,1)S(1)}, u32[]{:S(2)}, u32[]{:S(2)}) %collective-permute-start.17) | collective-permute-done | bytes 1663008 | tf_op jit(solution)/shard_map/ppermute | solution.py:414
  265.8 7.3 %shard_map.94 = (f32[448,3584]{1,0:T(8,128)}, f32[448,3584]{1,0:T(8,128)}) custom-call(s32[9]{0:T(128)S(1)} %stack.39.flag_ref, f32[1]{0:T(128)S(6)} %div.21.scale_ref, f32[448,3584]{1,0:T(8,128)} %bitcast.11, f32[448,1792]{1,0:T(8,128)S(1)} %copy-done.5, s16[464,1792]{1,0:T(8,128)(2,1)S(1)} %copy-done.9), custom_call_target="tpu_custom_call" | custom-call | flops 1 | bytes 1 | tf_op jit(solution)/shard_map/pallas_call | solution.py:149
  273.1 6.1 %shard_map.95 = (f32[1024,512]{1,0:T(8,128)S(1)}, s16[528,512]{1,0:T(8,128)(2,1)S(1)}) custom-call(s32[9]{0:T(128)S(1)} %stack.39.flag_ref, bf16[512,3584]{1,0:T(8,128)(2,1)} %copy-done, bf16[512,3584]{1,0:T(8,128)(2,1)} %copy-done.14, bf16[512,1792]{1,0:T(8,128)(2,1)S(1)} %collective-permute-done.18.refs_0_.refs_2_, ...), custom_call_target="tpu_custom_call" | custom-call | flops 1 | bytes 1 | tf_op jit(solution)/shard_map/pallas_call | solution.py:149
  280.8 5.5 %shard_map.96 = (f32[448,896]{1,0:T(8,128)S(1)}, s16[464,896]{1,0:T(8,128)(2,1)}) custom-call(s32[9]{0:T(128)S(1)} %stack.39.flag_ref, bf16[512,448]{1,0:T(8,128)(2,1)S(1)} %dynamic-slice_select_fusion.1.refs_0_, bf16[512,448]{1,0:T(8,128)(2,1)S(1)} %dynamic-slice_select_fusion.refs_1_, bf16[512,1792]{1,0:T(8,128)(2,1)S(1)} %collective-permute-done.18.refs_0_.refs_2_, ...), custom_call_target="tpu_custom_call" | custom-call | flops 1 | bytes 1 | tf_op jit(solution)/shard_map/pallas_call | solution.py:149
  286.3 3.7 %collective-permute-start.21 = (s16[464,896]{1,0:T(8,128)(2,1)}, s16[464,896]{1,0:T(8,128)(2,1)S(1)}, u32[]{:S(2)}, u32[]{:S(2)}) collective-permute-start(s16[464,896]{1,0:T(8,128)(2,1)} %get-tuple-element.111), channel_id=1, source_target_pairs={{1,2},{2,1},{5,6},{6,5},{9,10},{10,9},{13,14},{14,13},{17,18},{18,... | collective-permute-start | bytes 2494472 | tf_op jit(solution)/shard_map/ppermute | solution.py:414
  290.0 4.6 %shard_map.97 = (f32[448,896]{1,0:T(8,128)S(1)}, s16[464,896]{1,0:T(8,128)(2,1)S(1)}) custom-call(s32[9]{0:T(128)S(1)} %stack.39.flag_ref, bf16[512,448]{1,0:T(8,128)(2,1)S(1)} %dynamic-slice_select_fusion.1.refs_0_, bf16[512,448]{1,0:T(8,128)(2,1)S(1)} %dynamic-slice_select_fusion.refs_1_, bf16[512,1792]{1,0:T(8,128)(2,1)S(1)} %collective-permute-done.18.refs_0_.refs_2_, ...), custom_call_target="tpu_custom_call" | custom-call | flops 1 | bytes 1 | tf_op jit(solution)/shard_map/pallas_call | solution.py:149
  302.2 6.1 %shard_map.99 = (f32[448,3584]{1,0:T(8,128)}, f32[448,3584]{1,0:T(8,128)}) custom-call(s32[9]{0:T(128)S(1)} %stack.39.flag_ref, f32[1]{0:T(128)S(6)} %div.21.scale_ref, f32[448,3584]{1,0:T(8,128)} %bitcast.12, f32[448,896]{1,0:T(8,128)S(1)} %get-tuple-element.116.value_ref, ...), custom_call_target="tpu_custom_call", output_to_operand_aliasing={{0}: (5, {}), {1}: (6, {})} | custom-call | flops 1 | bytes 1 | tf_op jit(solution)/shard_map/pallas_call | solution.py:149
  308.3 4.1 %shard_map.100 = (f32[512,2048]{1,0:T(8,128)}, f32[512,2048]{1,0:T(8,128)}) custom-call(s32[9]{0:T(128)S(1)} %stack.39.flag_ref, f32[1]{0:T(128)} %bitcast.7.scale_ref, f32[512,2048]{1,0:T(8,128)} %old_ref.3, f32[1024,512]{1,0:T(8,128)S(1)} %copy-done.3, ...), custom_call_target="tpu_custom_call", output_to_operand_aliasing={{0}: (7, {}), {1}: (8, {})} | custom-call | flops 1 | bytes 1 | tf_op jit(solution)/shard_map/pallas_call | solution.py:149
  312.4 6.1 %shard_map.101 = (f32[448,3584]{1,0:T(8,128)}, f32[448,3584]{1,0:T(8,128)}) custom-call(s32[9]{0:T(128)S(1)} %stack.39.flag_ref, f32[1]{0:T(128)S(6)} %div.21.scale_ref, f32[448,3584]{1,0:T(8,128)} %bitcast.13, f32[448,896]{1,0:T(8,128)S(1)} %get-tuple-element.128.value_ref, ...), custom_call_target="tpu_custom_call", output_to_operand_aliasing={{0}: (5, {}), {1}: (6, {})} | custom-call | flops 1 | bytes 1 | tf_op jit(solution)/shard_map/pallas_call | solution.py:149
  (92 shorter events, 70.3 us)
Async XLA Ops:
  0.6 83.2 %collective-permute-start = (bf16[512,3584]{1,0:T(8,128)(2,1)}, bf16[512,3584]{1,0:T(8,128)(2,1)}, u32[]{:S(2)}, u32[]{:S(2)}) collective-permute-start(bf16[512,3584]{1,0:T(8,128)(2,1)} %param.5), channel_id=1, source_target_pairs={{0,4},{1,6},{2,5},{3,7},{4,0},{5,2},{6,1},{7,3},{8,12},{9,14},{10,... | collective-permute-start | bytes 11010056 | tf_op jit(solution)/shard_map/ppermute | solution.py:414
  4.3 79.5 %collective-permute-start.1 = (bf16[512,3584]{1,0:T(8,128)(2,1)}, bf16[512,3584]{1,0:T(8,128)(2,1)}, u32[]{:S(2)}, u32[]{:S(2)}) collective-permute-start(bf16[512,3584]{1,0:T(8,128)(2,1)} %param.5), channel_id=1, source_target_pairs={{4,8},{5,10},{6,9},{7,11},{8,4},{9,6},{10,5},{11,7},{20,24},{21,26... | collective-permute-start | bytes 11010056 | tf_op jit(solution)/shard_map/ppermute | solution.py:414
  83.9 9.7 %collective-permute-start.3 = (bf16[512,3584]{1,0:T(8,128)(2,1)}, bf16[512,3584]{1,0:T(8,128)(2,1)}, u32[]{:S(2)}, u32[]{:S(2)}) collective-permute-start(bf16[512,3584]{1,0:T(8,128)(2,1)} %collective-permute-done.1.refs_6_.refs_1_), channel_id=1, source_target_pairs={{0,1},{1,0},{2,3},{3,2},{4,5},{5,4},{6,7},{7,6},{8,9},{9,8},{10,11... | collective-permute-start | bytes 11010056 | tf_op jit(solution)/shard_map/ppermute | solution.py:414
  83.9 12.0 %collective-permute-start.2 = (bf16[512,3584]{1,0:T(8,128)(2,1)}, bf16[512,3584]{1,0:T(8,128)(2,1)}, u32[]{:S(2)}, u32[]{:S(2)}) collective-permute-start(bf16[512,3584]{1,0:T(8,128)(2,1)} %collective-permute-done.refs_4_.refs_1_), channel_id=1, source_target_pairs={{0,1},{1,0},{2,3},{3,2},{4,5},{5,4},{6,7},{7,6},{8,9},{9,8},{10,11... | collective-permute-start | bytes 11010056 | tf_op jit(solution)/shard_map/ppermute | solution.py:414
  84.4 44.8 %collective-permute-start.4 = (bf16[512,3584]{1,0:T(8,128)(2,1)}, bf16[512,3584]{1,0:T(8,128)(2,1)}, u32[]{:S(2)}, u32[]{:S(2)}) collective-permute-start(bf16[512,3584]{1,0:T(8,128)(2,1)} %param.5), channel_id=1, source_target_pairs={{1,2},{2,1},{5,6},{6,5},{9,10},{10,9},{13,14},{14,13},{17,18},{18,... | collective-permute-start | bytes 11010056 | tf_op jit(solution)/shard_map/ppermute | solution.py:414
  87.9 85.2 %collective-permute-start.8 = (bf16[512,3584]{1,0:T(8,128)(2,1)}, bf16[512,3584]{1,0:T(8,128)(2,1)}, u32[]{:S(2)}, u32[]{:S(2)}) collective-permute-start(bf16[512,3584]{1,0:T(8,128)(2,1)} %collective-permute-done.1.refs_6_.refs_1_), channel_id=1, source_target_pairs={{4,0},{5,1},{6,2},{7,3},{8,12},{9,13},{10,14},{11,15},{20,16},{21,... | collective-permute-start | bytes 11010056 | tf_op jit(solution)/shard_map/ppermute | solution.py:414
  89.2 84.0 %collective-permute-start.9 = (bf16[512,3584]{1,0:T(8,128)(2,1)}, bf16[512,3584]{1,0:T(8,128)(2,1)}, u32[]{:S(2)}, u32[]{:S(2)}) collective-permute-start(bf16[512,3584]{1,0:T(8,128)(2,1)} %collective-permute-done.refs_4_.refs_1_), channel_id=1, source_target_pairs={{4,8},{5,9},{6,10},{7,11},{8,4},{9,5},{10,6},{11,7},{20,24},{21,25... | collective-permute-start | bytes 11010056 | tf_op jit(solution)/shard_map/ppermute | solution.py:414
  131.9 3.9 %collective-permute-start.5 = (bf16[512,1792]{1,0:T(8,128)(2,1)S(1)}, bf16[512,1792]{1,0:T(8,128)(2,1)S(1)}, u32[]{:S(2)}, u32[]{:S(2)}) collective-permute-start(bf16[512,1792]{1,0:T(8,128)(2,1)S(1)} %get-tuple-element.135), channel_id=1, source_target_pairs={{0,1},{1,0},{2,3},{3,2},{4,5},{5,4},{6,7},{7,6},{8,9},{9,8},{10,11... | collective-permute-start | bytes 5505032 | tf_op jit(solution)/shard_map/ppermute | solution.py:414
  132.0 6.4 %collective-permute-start.6 = (bf16[512,1792]{1,0:T(8,128)(2,1)S(1)}, bf16[512,1792]{1,0:T(8,128)(2,1)S(1)}, u32[]{:S(2)}, u32[]{:S(2)}) collective-permute-start(bf16[512,1792]{1,0:T(8,128)(2,1)S(1)} %get-tuple-element.134), channel_id=1, source_target_pairs={{0,1},{1,0},{2,3},{3,2},{4,5},{5,4},{6,7},{7,6},{8,9},{9,8},{10,11... | collective-permute-start | bytes 5505032 | tf_op jit(solution)/shard_map/ppermute | solution.py:414
  173.2 13.6 %collective-permute-start.10 = (bf16[512,3584]{1,0:T(8,128)(2,1)}, bf16[512,3584]{1,0:T(8,128)(2,1)}, u32[]{:S(2)}, u32[]{:S(2)}) collective-permute-start(bf16[512,3584]{1,0:T(8,128)(2,1)} %collective-permute-done.8.refs_0_.refs_2_), channel_id=1, source_target_pairs={{0,1},{1,0},{2,3},{3,2},{4,5},{5,4},{6,7},{7,6},{8,9},{9,8},{10,11... | collective-permute-start | bytes 11010056 | tf_op jit(solution)/shard_map/ppermute | solution.py:414
  173.2 49.0 %collective-permute-start.13 = (bf16[512,3584]{1,0:T(8,128)(2,1)}, bf16[512,3584]{1,0:T(8,128)(2,1)}, u32[]{:S(2)}, u32[]{:S(2)}) collective-permute-start(bf16[512,3584]{1,0:T(8,128)(2,1)} %collective-permute-done.9.refs_3_.refs_1_), channel_id=1, source_target_pairs={{0,1},{1,0},{2,3},{3,2},{4,5},{5,4},{6,7},{7,6},{8,9},{9,8},{10,11... | collective-permute-start | bytes 11010056 | tf_op jit(solution)/shard_map/ppermute | solution.py:414
  175.3 46.9 %collective-permute-start.12 = (bf16[512,1792]{1,0:T(8,128)(2,1)S(1)}, bf16[512,1792]{1,0:T(8,128)(2,1)S(1)}, u32[]{:S(2)}, u32[]{:S(2)}) collective-permute-start(bf16[512,1792]{1,0:T(8,128)(2,1)S(1)} %constant_dynamic-slice_fusion.1), channel_id=1, source_target_pairs={{4,0},{5,1},{6,2},{7,3},{8,12},{9,13},{10,14},{11,15},{20,16},{21,... | collective-permute-start | bytes 5505032 | tf_op jit(solution)/shard_map/ppermute | solution.py:414
  176.8 25.2 %collective-permute-start.7 = (s16[1040,512]{1,0:T(8,128)(2,1)S(1)}, s16[1040,512]{1,0:T(8,128)(2,1)S(1)}, u32[]{:S(2)}, u32[]{:S(2)}) collective-permute-start(s16[1040,512]{1,0:T(8,128)(2,1)S(1)} %get-tuple-element.75), channel_id=1, source_target_pairs={{0,2},{1,3},{2,0},{3,1},{4,6},{5,7},{6,4},{7,5},{8,10},{9,11},{10,... | collective-permute-start | bytes 3194888 | tf_op jit(solution)/shard_map/ppermute | solution.py:414
  186.2 27.3 %collective-permute-start.11 = (s16[528,512]{1,0:T(8,128)(2,1)S(1)}, s16[528,512]{1,0:T(8,128)(2,1)S(1)}, u32[]{:S(2)}, u32[]{:S(2)}) collective-permute-start(s16[528,512]{1,0:T(8,128)(2,1)S(1)} %get-tuple-element.79), channel_id=1, source_target_pairs={{0,2},{1,3},{2,0},{3,1},{4,6},{5,7},{6,4},{7,5},{8,10},{9,11},{10,... | collective-permute-start | bytes 1622024 | tf_op jit(solution)/shard_map/ppermute | solution.py:414
  222.2 6.7 %collective-permute-start.14 = (bf16[512,1792]{1,0:T(8,128)(2,1)S(1)}, bf16[512,1792]{1,0:T(8,128)(2,1)}, u32[]{:S(2)}, u32[]{:S(2)}) collective-permute-start(bf16[512,1792]{1,0:T(8,128)(2,1)S(1)} %collective-permute-done.12.refs_2_.refs_0_), channel_id=1, source_target_pairs={{0,1},{1,0},{2,3},{3,2},{4,5},{5,4},{6,7},{7,6},{8,9},{9,8},{10,11... | collective-permute-start | bytes 5505032 | tf_op jit(solution)/shard_map/ppermute | solution.py:414
  226.1 47.0 %collective-permute-start.18 = (bf16[512,1792]{1,0:T(8,128)(2,1)}, bf16[512,1792]{1,0:T(8,128)(2,1)S(1)}, u32[]{:S(2)}, u32[]{:S(2)}) collective-permute-start(bf16[512,1792]{1,0:T(8,128)(2,1)} %constant_dynamic-slice_fusion), channel_id=1, source_target_pairs={{4,0},{5,1},{6,2},{7,3},{8,12},{9,13},{10,14},{11,15},{20,16},{21,... | collective-permute-start | bytes 5505032 | tf_op jit(solution)/shard_map/ppermute | solution.py:414
  238.1 23.2 %collective-permute-start.17 = (s16[464,1792]{1,0:T(8,128)(2,1)}, s16[464,1792]{1,0:T(8,128)(2,1)S(1)}, u32[]{:S(2)}, u32[]{:S(2)}) collective-permute-start(s16[464,1792]{1,0:T(8,128)(2,1)} %get-tuple-element.96), channel_id=1, source_target_pairs={{1,2},{2,1},{5,6},{6,5},{9,10},{10,9},{13,14},{14,13},{17,18},{18,... | collective-permute-start | bytes 4988936 | tf_op jit(solution)/shard_map/ppermute | solution.py:414
  240.5 9.9 %collective-permute-start.16 = (s16[1040,512]{1,0:T(8,128)(2,1)S(1)}, s16[1040,512]{1,0:T(8,128)(2,1)S(1)}, u32[]{:S(2)}, u32[]{:S(2)}) collective-permute-start(s16[1040,512]{1,0:T(8,128)(2,1)S(1)} %copy-done.13), channel_id=1, source_target_pairs={{1,0},{3,2},{5,4},{7,6},{8,9},{10,11},{12,13},{14,15},{17,16},{19,... | collective-permute-start | bytes 3194888 | tf_op jit(solution)/shard_map/ppermute | solution.py:414
  241.8 8.5 %collective-permute-start.15 = (s16[528,512]{1,0:T(8,128)(2,1)S(1)}, s16[528,512]{1,0:T(8,128)(2,1)S(1)}, u32[]{:S(2)}, u32[]{:S(2)}) collective-permute-start(s16[528,512]{1,0:T(8,128)(2,1)S(1)} %get-tuple-element.90), channel_id=1, source_target_pairs={{0,1},{2,3},{4,5},{6,7},{9,8},{11,10},{13,12},{15,14},{16,17},{18,... | collective-permute-start | bytes 1622024 | tf_op jit(solution)/shard_map/ppermute | solution.py:414
  273.1 6.5 %collective-permute-start.19 = (bf16[512,1792]{1,0:T(8,128)(2,1)S(1)}, bf16[512,1792]{1,0:T(8,128)(2,1)S(1)}, u32[]{:S(2)}, u32[]{:S(2)}) collective-permute-start(bf16[512,1792]{1,0:T(8,128)(2,1)S(1)} %collective-permute-done.18.refs_0_.refs_2_), channel_id=1, source_target_pairs={{0,1},{1,0},{2,3},{3,2},{4,5},{5,4},{6,7},{7,6},{8,9},{9,8},{10,11... | collective-permute-start | bytes 5505032 | tf_op jit(solution)/shard_map/ppermute | solution.py:414
  279.2 17.3 %collective-permute-start.20 = (s16[528,512]{1,0:T(8,128)(2,1)S(1)}, s16[528,512]{1,0:T(8,128)(2,1)S(1)}, u32[]{:S(2)}, u32[]{:S(2)}) collective-permute-start(s16[528,512]{1,0:T(8,128)(2,1)S(1)} %get-tuple-element.109), channel_id=1, source_target_pairs={{0,2},{1,3},{2,0},{3,1},{4,6},{5,7},{6,4},{7,5},{8,10},{9,11},{10,... | collective-permute-start | bytes 1622024 | tf_op jit(solution)/shard_map/ppermute | solution.py:414
  286.3 15.9 %collective-permute-start.21 = (s16[464,896]{1,0:T(8,128)(2,1)}, s16[464,896]{1,0:T(8,128)(2,1)S(1)}, u32[]{:S(2)}, u32[]{:S(2)}) collective-permute-start(s16[464,896]{1,0:T(8,128)(2,1)} %get-tuple-element.111), channel_id=1, source_target_pairs={{1,2},{2,1},{5,6},{6,5},{9,10},{10,9},{13,14},{14,13},{17,18},{18,... | collective-permute-start | bytes 2494472 | tf_op jit(solution)/shard_map/ppermute | solution.py:414
  294.6 17.8 %collective-permute-start.23 = (s16[464,896]{1,0:T(8,128)(2,1)S(1)}, s16[464,896]{1,0:T(8,128)(2,1)S(1)}, u32[]{:S(2)}, u32[]{:S(2)}) collective-permute-start(s16[464,896]{1,0:T(8,128)(2,1)S(1)} %get-tuple-element.113), channel_id=1, source_target_pairs={{1,2},{2,1},{5,6},{6,5},{9,10},{10,9},{13,14},{14,13},{17,18},{18,... | collective-permute-start | bytes 2494472 | tf_op jit(solution)/shard_map/ppermute | solution.py:414
  297.5 10.8 %collective-permute-start.22 = (s16[528,512]{1,0:T(8,128)(2,1)S(1)}, s16[528,512]{1,0:T(8,128)(2,1)S(1)}, u32[]{:S(2)}, u32[]{:S(2)}) collective-permute-start(s16[528,512]{1,0:T(8,128)(2,1)S(1)} %get-tuple-element.117), channel_id=1, source_target_pairs={{0,1},{2,3},{4,5},{6,7},{9,8},{11,10},{13,12},{15,14},{16,17},{18,... | collective-permute-start | bytes 1622024 | tf_op jit(solution)/shard_map/ppermute | solution.py:414
  (17 other events, 125.0 us)

commit v8 on v7

--- a/solution.py
+++ b/solution.py
@@ -89,7 +89,10 @@
 
 
 GROUP = 64
-LEVELS = 16
+
+
+def level_rows(rows):
+    return -(-(rows // GROUP) // 16) * 16
 
 
 def pack(values, out_ref, at):
@@ -106,13 +109,17 @@
 
 
 def put_levels(levels, out_ref, at):
-    levels = levels + [jnp.zeros_like(levels[0])] * (LEVELS - len(levels))
-    out_ref[at : at + LEVELS] = jnp.concatenate(levels, 0).astype(jnp.int32).astype(jnp.int16)
+    count = out_ref.shape[0] - at
+    levels = levels + [jnp.zeros_like(levels[0])] * (count - len(levels))
+    out_ref[at : at + count] = jnp.concatenate(levels, 0).astype(jnp.int32).astype(jnp.int16)
+
+
+def step_of(level):
+    return jnp.exp2(level.astype(jnp.int32).astype(jnp.float32) * (1.0 / 256.0)) * (1.0 / 32767.0)
 
 
 def unpack(ref, index, rows, many):
-    level = ref[many * rows : many * rows + LEVELS].astype(jnp.int32).astype(jnp.float32)
-    step = jnp.exp2(level * (1.0 / 256.0)) * (1.0 / 32767.0)
+    step = step_of(ref[many * rows : many * rows + level_rows(many * rows)])
     parts = []
     for group in range(rows // GROUP):
         at = index * rows + group * GROUP
@@ -122,17 +129,9 @@
     return jnp.concatenate(parts, 0)
 
 
-def decode(coded, rows):
-    wide = coded.shape[1]
-    level = coded[rows : rows + rows // GROUP].astype(jnp.float32)
-    step = jnp.exp2(level * (1.0 / 256.0)) * (1.0 / 32767.0)
-    grouped = coded[:rows].astype(jnp.float32).reshape(rows // GROUP, GROUP, wide)
-    return (grouped * step[:, None, :]).reshape(rows, wide)
-
-
 PARAMS = pltpu.CompilerParams(vmem_limit_bytes=48 * 2**20)
 FREE = pl.CostEstimate(flops=1, bytes_accessed=1, transcendentals=0)
-KEPT, START, NEXT, HOME, AWAY, LAST, SAME_HALF, MIDDLE, CORE = range(9)
+KEPT, START, THIRD, SAME_HALF, MIDDLE, CORE = range(6)
 
 
 def spec(shape, index=None):
@@ -232,12 +231,12 @@
         ins += [(part, whole(part)) for part in before]
     outs = [((size, tall), jnp.float32, spec((size, tall)))] * many
     if last:
-        shape = (many * tall + LEVELS, tall)
+        shape = (many * tall + level_rows(many * tall), tall)
         outs.append((shape, jnp.int16, spec(shape)))
     return kernel_call(body, flags, steps, ins, outs)
 
 
-def right_terms(flags, strips, columns, block, steps, at=START, before=None, last=False):
+def right_terms(flags, strips, columns, block, steps, before=None, keep=True, last=False):
     wide = block * steps
     rows, strip = strips[0].shape
     many = len(strips)
@@ -250,7 +249,8 @@
             refs = refs[len(choice) :]
         if before is not None:
             before_in, refs = refs[0], refs[1:]
-        outs, turned = refs[:-1], refs[-1]
+        outs, turned = refs[: keep + last], refs[keep + last]
+        total_ref = outs[0] if keep else refs[-1]
 
         @pl.when(pl.program_id(0) == 0)
         def _():
@@ -264,7 +264,7 @@
                 ref = refs_here[choice if len(refs_here) == 2 else 0]
                 term = dot(turned[index], ref[...], 1, 0)
                 total = term if total is None else total + term
-            outs[0][...] = total
+            total_ref[...] = total
 
         if max(len(choice) for choice in columns) == 1:
             add(0)
@@ -272,7 +272,7 @@
             for choice in range(2):
                 pl.when(flag_ref[MIDDLE] == choice)(functools.partial(add, choice))
         if last:
-            put_levels(pack(outs[0][...], outs[1], 0), outs[1], strip)
+            put_levels(pack(total_ref[...], outs[-1], 0), outs[-1], strip)
 
     here = lambda k, flags: k
     ins = [(part, whole(part)) for part in strips]
@@ -282,11 +282,14 @@
             for index, (array, start) in enumerate(choice)
         ]
     if before is not None:
-        ins.append((before, spec((strip, block), blocks_from(at))))
-    outs = [((strip, wide), jnp.float32, spec((strip, block), here))]
+        ins.append((before, spec((strip, block), here)))
+    outs = [((strip, wide), jnp.float32, spec((strip, block), here))] if keep else []
     if last:
-        outs.append(((strip + LEVELS, wide), jnp.int16, spec((strip + LEVELS, block), here)))
+        tall = strip + level_rows(strip)
+        outs.append(((tall, wide), jnp.int16, spec((tall, block), here)))
     scratch = [pltpu.VMEM((many, strip, rows), jnp.bfloat16)]
+    if not keep:
+        scratch.append(pltpu.VMEM((strip, block), jnp.float32))
     return kernel_call(body, flags, steps, ins, outs, scratch=scratch)
 
 
@@ -305,89 +308,106 @@
         put_levels(levels, out_ref, many * rows)
 
     ins = [(array, whole(array)) for array in list(products) + [coded]]
-    shapes = [((many * rows, wide), jnp.float32), ((many * rows + LEVELS, wide), jnp.int16)]
+    shapes = [((many * rows, wide), jnp.float32), ((many * rows + level_rows(many * rows), wide), jnp.int16)]
     return kernel_call(body, flags, 1, ins, [(s, d, spec(s)) for s, d in shapes])
 
 
-def write_states(old, gram, scale, state_ref, fixed_ref, where):
-    state = BETA * old + (1.0 - BETA) * gram
-    state_ref[:, where] = state
-    fixed_ref[:, where] = state * scale
-
-
-def finish_right(flags, scale, old, value, coded, at, block, steps, written=None):
-    strip, wide = old.shape
-
-    def body(flag_ref, scale_ref, old_ref, value_ref, coded_ref, *refs):
-        state_ref, fixed_ref = refs[-2:]
-        everything = slice(None)
+def write_states(old_ref, gram, scale_ref, state_ref, fixed_ref):
+    state = BETA * old_ref[...] + (1.0 - BETA) * gram
+    state_ref[...] = state
+    fixed_ref[...] = state * scale_ref[0]
+
+
+def outputs_of(old, block, index, written, count):
+    ins, aliases = [], None
+    if written is not None:
+        ins = [(array, pl.BlockSpec(memory_space=pl.ANY)) for array in written]
+        aliases = {count + 1: 0, count + 2: 1}
+    return ins, [(old.shape, jnp.float32, pl.BlockSpec(block, index))] * 2, aliases
+
+
+def finish_right(flags, scale, old, value, coded, share, half, written=None):
+    strip, wide = old.shape[0], old.shape[1] // 2
+
+    def body(flag_ref, scale_ref, old_ref, value_ref, coded_ref, level_ref, share_ref, share_level_ref, *refs):
+        group = pl.program_id(0)
+
+        def decoded(ref, levels):
+            rows = lax.broadcasted_iota(jnp.int32, levels.shape, 0)
+            level = jnp.sum(
+                jnp.where(rows == group, levels[...].astype(jnp.int32), 0), axis=0, keepdims=True
+            )
+            step = jnp.exp2(level.astype(jnp.float32) * (1.0 / 256.0)) * (1.0 / 32767.0)
+            return ref[...].astype(jnp.int32).astype(jnp.float32) * step
+
+        def put(gram):
+            gram = gram + decoded(share_ref, share_level_ref)
+            write_states(old_ref, gram, scale_ref, *refs[-2:])
 
         @pl.when(flag_ref[KEPT] == 0)
         def _():
-            write_states(old_ref[...], value_ref[...], scale_ref[0], state_ref, fixed_ref, everything)
+            put(value_ref[...])
 
         @pl.when(flag_ref[KEPT] == 1)
         def _():
-            write_states(
-                old_ref[...], unpack(coded_ref, 0, strip, 1), scale_ref[0], state_ref, fixed_ref, everything
-            )
-
-    part = math.gcd(block * steps, 256)
-    there = lambda k, flags: k + flags[at] * block // part
+            put(decoded(coded_ref, level_ref))
+
+    rows = (GROUP, wide)
+    levels = (level_rows(strip), wide)
+    last = strip // level_rows(strip)
+    there = lambda k, flags: (k, half)
     ins = [
         (scale, pl.BlockSpec(memory_space=pltpu.SMEM)),
-        (old, spec((strip, part), there)),
-        (value, spec((strip, part), lambda k, flags: k * (1 - flags[KEPT]))),
-        (coded, spec((strip + LEVELS, part), lambda k, flags: k * flags[KEPT])),
+        (old, pl.BlockSpec(rows, there)),
+        (value, pl.BlockSpec(rows, lambda k, flags: (k * (1 - flags[KEPT]), half))),
+        (coded, pl.BlockSpec(rows, lambda k, flags: (k * flags[KEPT], 0))),
+        (coded, pl.BlockSpec(levels, lambda k, flags: (last, 0))),
+        (share, pl.BlockSpec(rows, there)),
+        (share, pl.BlockSpec(levels, lambda k, flags: (last, half))),
     ]
-    aliases = None
-    if written is not None:
-        ins += [(array, pl.BlockSpec(memory_space=pl.ANY)) for array in written]
-        aliases = {5: 0, 6: 1}
-    outs = [((strip, wide), jnp.float32, spec((strip, part), there))] * 2
-    return kernel_call(body, flags, steps * block // part, ins, outs, aliases)
-
-
-def finish_left(flags, scale, old, same_total, same_other, total, other, inner, written=None):
-    tall, wide = total.shape
-
-    def body(flag_ref, scale_ref, old_ref, same_ref, same_other_ref, total_ref, other_ref, *refs):
-        state_ref, fixed_ref = refs[-2:]
+    more, outs, aliases = outputs_of(old, rows, there, written, len(ins))
+    return kernel_call(body, flags, strip // GROUP, ins + more, outs, aliases)
+
+
+def finish_left(flags, scale, old, same_total, same_other, late_total, late_other, sent, inner, written=None):
+    tall, wide = late_total.shape
+
+    def body(flag_ref, scale_ref, old_ref, same_ref, same_other_ref, late_ref, late_other_ref, *refs):
+        sent_refs = refs[:2]
 
         def put(value):
-            write_states(old_ref[...], value, scale_ref[0], state_ref, fixed_ref, slice(None))
-
-        is_mate = 1 - flag_ref[MIDDLE] if inner else flag_ref[MIDDLE]
-        mine = flag_ref[CORE] == pl.program_id(0)
+            write_states(old_ref, value, scale_ref, *refs[-2:])
+
+        def put_same(index, mine):
+            put(same_ref[index * tall : (index + 1) * tall] if mine else unpack(same_other_ref, index, tall, 3))
+
+        def put_late(mine):
+            put(late_ref[...] if mine else unpack(late_other_ref, 0, tall, 1))
+
+        def put_sent(mine):
+            put(unpack(sent_refs[0 if mine else 1], 0, tall, 1))
+
         same = flag_ref[SAME_HALF] == 1
-
-        @pl.when(mine & same)
-        def _():
-            put(same_ref[pl.ds(pick(is_mate, tall), tall), :])
-
-        @pl.when(mine & jnp.logical_not(same))
-        def _():
-            put(total_ref[...])
-
-        for index in range(2):
-
-            @pl.when(jnp.logical_not(mine) & same & (is_mate == index))
-            def _():
-                put(unpack(same_other_ref, index, tall, 2))
-
-        @pl.when(jnp.logical_not(mine) & jnp.logical_not(same))
-        def _():
-            put(unpack(other_ref, 0, tall, 1))
-
-    there = lambda k, flags: 2 * (1 - flags[CORE] if inner else flags[CORE]) + k
-    ins = [(scale, pl.BlockSpec(memory_space=pltpu.SMEM)), (old, spec((tall, wide), there))]
-    ins += [(array, whole(array)) for array in (same_total, same_other, total, other)]
-    aliases = None
-    if written is not None:
-        ins += [(array, pl.BlockSpec(memory_space=pl.ANY)) for array in written]
-        aliases = {7: 0, 8: 1}
-    outs = [(old.shape, jnp.float32, spec((tall, wide), there))] * 2
-    return kernel_call(body, flags, 2, ins, outs, aliases)
+        is_middle = flag_ref[MIDDLE] == 1
+        for mine in (True, False):
+            here = (flag_ref[CORE] == pl.program_id(0)) == mine
+            at_middle = here & is_middle
+            at_end = here & jnp.logical_not(is_middle)
+            other = jnp.logical_not(same)
+            pl.when(at_middle & same)(functools.partial(put_same, 0 if inner else 1, mine))
+            pl.when(at_end & same)(functools.partial(put_same, 1 if inner else 0, mine))
+            if inner:
+                pl.when(at_middle & other)(functools.partial(put_same, 2, mine))
+                pl.when(at_end & other)(functools.partial(put_late, mine))
+            else:
+                pl.when(at_middle & other)(functools.partial(put_late, mine))
+                pl.when(at_end & other)(functools.partial(put_sent, mine))
+
+    there = lambda k, flags: (0, 2 * (1 - flags[CORE] if inner else flags[CORE]) + k)
+    ins = [(scale, pl.BlockSpec(memory_space=pltpu.SMEM)), (old, pl.BlockSpec((tall, wide), there))]
+    ins += [(array, whole(array)) for array in (same_total, same_other, late_total, late_other) + sent]
+    more, outs, aliases = outputs_of(old, (tall, wide), there, written, len(ins))
+    return kernel_call(body, flags, 2, ins + more, outs, aliases)
 
 
 def dot(a, b, a_dim, b_dim):
@@ -446,12 +466,16 @@
     return (z, 1 - y, c)
 
 
-def to_home(z, y, c):
-    return (z, y, 1 - c) if c != z // 2 else None
-
-
-def to_away(z, y, c):
-    return (z, y, 1 - c) if c == z // 2 else None
+def share_out(z, y, c):
+    return (z ^ 1, c, y) if middle(z) else None
+
+
+def far_straight(z, y, c):
+    return (z ^ 1, y, c) if middle(z) and c != z // 2 else None
+
+
+def far_cross(z, y, c):
+    return (z ^ 1, y, 1 - c) if middle(z) and c == z // 2 else None
 
 
 def line_gather(gradient, left_old, right_old, left_counts, right_counts):
@@ -468,10 +492,7 @@
         [
             jnp.where(straight, 0, 1),
             0,
-            1,
-            2 * side,
-            2 * (1 - side),
-            2 * (1 - side) + 1,
+            2,
             (c == side).astype(jnp.int32),
             is_middle.astype(jnp.int32),
             c,
@@ -482,11 +503,8 @@
     def tie(*values):
         return lax.optimization_barrier(tuple(values))
 
-    def columns(value, first, count):
-        return lax.dynamic_slice_in_dim(value, first * block, count * block, 1)
-
-    def strips_of(pair, first=0):
-        return [lax.dynamic_slice_in_dim(part, strip_at - first, strip, 1) for part in pair]
+    def strips_of(pair, at=strip_at):
+        return [lax.dynamic_slice_in_dim(part, at, strip, 1) for part in pair]
 
     def one(array, at=START):
         return [(array, at)]
@@ -513,10 +531,9 @@
         mine,
         jnp.concatenate([send(mine[:, :half], beside), send(mine[:, half:], beside)], 1),
     )
-    own_product, mate_product, same_coded = left_terms(
-        flags, own, [one(mine), one(mate)], half, 2
-    )
-    same_products = [own_product, mate_product]
+    *same_products, same_coded = left_terms(
+        flags, own, [one(mine), one(mate), one(cross)], block, 4
+    )
     same_got = send(same_coded, other_y)
     same_coded, own_o = tie(same_coded, own[1])
     own = (mine, own_o)
@@ -525,88 +542,60 @@
     )
 
     right, near, far = tie(right, near, far)
-    end_home = send(columns(far, 2 * side, 2), outward)
-    nears = (near, send(near, beside))
     far_o = send(far, beside)
-    near_product, near_coded = left_terms(
-        flags, own, [[(near, START), (cross, START)]], half, 2
-    )
-    near_got = send(near_coded, other_y)
-    near_coded, near, near_o = tie(near_coded, *nears)
-    nears = (near, near_o)
-    [right] = right_terms(
-        flags, strips_of(nears), [one(part) for part in nears], block, 4, before=right
-    )
-    same_got, right = tie(same_got, right)
+    near_o = send(near, beside)
+    far_product, far_coded = left_terms(flags, mates, [one(far)], half, 2)
+    far_got = send(far_coded, other_y)
+    end_strips = strips_of((far, far_o), (2 * (z ^ 1) + c) * strip)
+
+    far_coded, far_o = tie(far_coded, far_o)
+    [share] = right_terms(
+        flags, end_strips, [one(far), one(far_o)], block, 4, keep=False, last=True
+    )
+    share_got = send(share, share_out)
+    share, near_o = tie(share, near_o)
+    late_strips = [
+        jnp.where(is_middle, a, b) for a, b in zip(strips_of((far, far_o)), strips_of((near, near_o)))
+    ]
+    right, right_coded = right_terms(
+        flags,
+        late_strips,
+        [[(near, START), (far, START)], [(near_o, START), (far_o, START)]],
+        block,
+        4,
+        before=right,
+        last=True,
+    )
+    right_got = [send(right_coded[:, :half], to_line), send(right_coded[:, half:], to_line)]
+    right_coded, far_got = tie(right_coded, far_got)
+    far_out = add_up(flags, [far_product], far_got)[1]
+    sent = (send(far_out, far_straight), send(far_out, far_cross))
+    far_out, near = tie(far_out, near)
+    late_product, late_coded = left_terms(
+        flags, own, [[(near, START), (far, START)]], half, 2
+    )
+    late_got = send(late_coded, other_y)
+    late_coded, same_got = tie(late_coded, same_got)
     same_total, same_out = add_up(flags, same_products, same_got)
-    same_other = send(same_out, to_home)
-    same_out, near_got = tie(same_out, near_got)
-    near_total, near_out = add_up(flags, [near_product], near_got)
-    near_other = send(near_out, to_away)
-
-    right, near_out, end_home, far_o = tie(right, near_out, end_home, far_o)
-    far, end_home = tie(far, end_home)
-    end_away = send(columns(far, 2 * (1 - side), 2), outward)
-    end_home_o = send(end_home, beside)
-    strips = [
-        jnp.where(is_middle, strips_of([a])[0], strips_of([b], 2 * side * block)[0])
-        for a, b in ((far, end_home), (far_o, end_home_o))
-    ]
-
-    def last_right(end, end_o, start, at, steps):
-        return right_terms(
-            flags,
-            strips,
-            [[(end, start), (far, at)], [(end_o, start), (far_o, at)]],
-            block,
-            steps,
-            at=at,
-            before=right,
-            last=True,
-        )
-
-    right_home, home_coded = last_right(end_home, end_home_o, START, HOME, 2)
-    home_got = send(home_coded, to_line)
-    home_coded, end_home = tie(home_coded, end_home)
-    [far_product] = left_terms(
-        flags, own, [[(end_home, START), (far, HOME)]], block, 2, at=HOME, last=False
-    )
+    same_other = send(same_out, beside)
+    same_out, late_got = tie(same_out, late_got)
+    late_total, late_out = add_up(flags, [late_product], late_got)
+    late_other = send(late_out, beside)
+
     left_scale = 1.0 / denominator(left_counts).reshape(1)
     right_scale = 1.0 / denominator(right_counts)
     old = right_old[0]
-    far_product, near_other, same_other = tie(far_product, near_other, same_other)
-    left_done = finish_left(
-        flags, left_scale, left_old, same_total, same_other, near_total, near_other, True
-    )
-    left_done[0], home_got = tie(left_done[0], home_got)
-    right_done = finish_right(flags, right_scale, old, right_home, home_got, HOME, block, 2)
-
-    right_done[0], far_product, end_away = tie(right_done[0], far_product, end_away)
-    end_away_o = send(end_away, beside)
-    far_product, far_coded = left_terms(
-        flags, own, [[(end_away, START), (far, AWAY)]], block, 2, at=AWAY, before=[far_product]
-    )
-    far_got = send(far_coded, other_y)
-    far_coded, end_away_o = tie(far_coded, end_away_o)
-    right_away, away_coded = last_right(end_away, end_away_o, START, AWAY, 1)
-    away_got = send(away_coded, to_line)
-    away_coded, end_away_o = tie(away_coded, end_away_o)
-    right_last, last_coded = last_right(end_away, end_away_o, NEXT, LAST, 1)
-    last_got = send(last_coded, to_line)
-    last_coded, far_got = tie(last_coded, far_got)
-    far_total, far_out = add_up(flags, [far_product], far_got)
-    far_other = send(far_out, to_away)
-    far_out, away_got = tie(far_out, away_got)
-    right_done = finish_right(
-        flags, right_scale, old, right_away, away_got, AWAY, block, 1, right_done
-    )
-    right_done[0], far_other = tie(right_done[0], far_other)
+    late_out, same_other, late_other = tie(late_out, same_other, late_other)
+    lefts = (same_total, same_other, late_total, late_other)
+    left_done = finish_left(flags, left_scale, left_old, *lefts, (), True)
+    left_done[0], *sent = tie(left_done[0], *sent)
     left_state, left_fixed = finish_left(
-        flags, left_scale, left_old, same_total, same_other, far_total, far_other, False, left_done
-    )
-    left_state, last_got = tie(left_state, last_got)
+        flags, left_scale, left_old, *lefts, tuple(sent), False, left_done
+    )
+    left_state, share_got, *right_got = tie(left_state, share_got, *right_got)
+    right_done = finish_right(flags, right_scale, old, right, right_got[0], share_got, 0)
     right_state, right_fixed = finish_right(
-        flags, right_scale, old, right_last, last_got, LAST, block, 1, right_done
+        flags, right_scale, old, right, right_got[1], share_got, 1, right_done
     )
     return (left_state, left_fixed, right_state[None], right_fixed[None])
 

time: 320 us -> 363 us (1.13)
  waiting for transfers between devices: 135 us -> 194 us
  local copies, waits for them, and re-layouts: 25.4 us -> 12.9 us
    ppermute x24 -> x21, waiting for transfers between devices: 135 us -> 194 us  [send(): return lax.ppermute(value, AXES, pairs)]
    unnamed x35 -> x19, local copies, waits for them, and re-layouts: 11.1 us -> 3.02 us
    dynamic_slice x9 -> x6, local copies, waits for them, and re-layouts: 13.9 us -> 7.96 us  [strips_of(): return [lax.dynamic_slice_in_dim(part, at, strip, 1) for part in pair]]
    pallas_call x18 -> x14, Pallas kernels: 117 us -> 115 us  [kernel_call(): pl.pallas_call(body, grid_spec=pltpu.PrefetchScalarGridSpec(num_scalar_pr...]
    ppermute x24 -> x21, starting transfers between devices: 32.8 us -> 31 us  [send(): return lax.ppermute(value, AXES, pairs)]
  transfers between devices with their start and end apart: 24 -> 21, of which waited for: 11 -> 11; matrix products, arithmetic and copies ran while one was open for 6% -> 5% of each run, Pallas kernels for 35% -> 27%
where the time goes in v8:
time: 363 us; the launch traced here: 362 us
  waiting for transfers between devices  194 us (53%)
  Pallas kernels  115 us (32%)
  starting transfers between devices  31 us (9%)
  local copies, waits for them, and re-layouts  12.9 us (4%)
  other arithmetic  6.39 us (2%)
    ppermute x21, waiting for transfers between devices, send(): return lax.ppermute(value, AXES, pairs)  194 us
    pallas_call x14, Pallas kernels, kernel_call(): pl.pallas_call(body, grid_spec=pltpu.PrefetchScalarGridSpec(num_scalar_pr...  115 us
    ppermute x21, starting transfers between devices, send(): return lax.ppermute(value, AXES, pairs)  31 us
    dynamic_slice x6, local copies, waits for them, and re-layouts, strips_of(): return [lax.dynamic_slice_in_dim(part, at, strip, 1) for part in pair]  7.96 us
  transfers between devices with their start and end apart: 21, of which 11 were waited for; matrix products, arithmetic and copies ran while one was open for 5% of the time, Pallas kernels for 27%

profile of v8, /device:TPU:1, one launch (start us, length us, event | category | flops | bytes accessed | tf_op | source)
XLA Modules:
  0.0 361.9 jit_solution(14330054514854179662)
XLA Ops:
  0.6 3.7 %collective-permute-start = (bf16[512,3584]{1,0:T(8,128)(2,1)}, bf16[512,3584]{1,0:T(8,128)(2,1)}, u32[]{:S(2)}, u32[]{:S(2)}) collective-permute-start(bf16[512,3584]{1,0:T(8,128)(2,1)} %param.5), channel_id=1, source_target_pairs={{0,4},{1,6},{2,5},{3,7},{4,0},{5,2},{6,1},{7,3},{8,12},{9,14},{10,... | collective-permute-start | bytes 11010056 | tf_op jit(solution)/shard_map/ppermute | solution.py:434
  6.8 77.1 %collective-permute-done.refs_4_.refs_1_.first_ref = bf16[512,3584]{1,0:T(8,128)(2,1)} collective-permute-done((bf16[512,3584]{1,0:T(8,128)(2,1)}, bf16[512,3584]{1,0:T(8,128)(2,1)}, u32[]{:S(2)}, u32[]{:S(2)}) %collective-permute-start) | collective-permute-done | bytes 3670048 | tf_op jit(solution)/shard_map/ppermute | solution.py:434
  84.4 3.4 collective-permute-start.4
  87.9 2.6 collective-permute-start.8
  97.2 13.6 %shard_map.84.refs_4_ = f32[448,3584]{1,0:T(8,128)} custom-call(s32[6]{0:T(128)S(1)} %stack.27.flag_ref, bf16[512,448]{1,0:T(8,128)(2,1)S(1)} %get-tuple-element.105.refs_0_, bf16[512,448]{1,0:T(8,128)(2,1)S(1)} %constant_dynamic-slice_fusion.6.refs_1_, bf16[512,448]{1,0:T(8,128)(2,1)S(1)} %get-tuple-element.104.refs_2_, ...), custom_call_target="tpu_custom_call" | custom-call | flops 1 | bytes 1 | tf_op jit(solution)/shard_map/pallas_call | solution.py:148
  110.8 18.4 %collective-permute-done.4 = bf16[512,3584]{1,0:T(8,128)(2,1)} collective-permute-done((bf16[512,3584]{1,0:T(8,128)(2,1)}, bf16[512,3584]{1,0:T(8,128)(2,1)}, u32[]{:S(2)}, u32[]{:S(2)}) %collective-permute-start.4) | collective-permute-done | bytes 3670048 | tf_op jit(solution)/shard_map/ppermute | solution.py:434
  132.5 3.3 collective-permute-done.5
  135.9 2.5 collective-permute-done.6
  140.4 20.2 %shard_map.85 = (f32[1024,512]{1,0:T(8,128)S(1)}, f32[1024,512]{1,0:T(8,128)S(1)}, f32[1024,512]{1,0:T(8,128)}, s16[1568,512]{1,0:T(8,128)(2,1)}) custom-call(s32[6]{0:T(128)S(1)} %stack.27.flag_ref, bf16[512,3584]{1,0:T(8,128)(2,1)} %copy-done, bf16[512,3584]{1,0:T(8,128)(2,1)} %copy-done.7, bf16[512,3584]{1,0:T(8,128)(2,1)} %copy-done, ...), custom_call_target="tpu_custom_call" | custom-call | flops 1 | bytes 1 | tf_op jit(solution)/shard_map/pallas_call | solution.py:148
  162.4 9.8 %shard_map.86.refs_6_ = f32[448,3584]{1,0:T(8,128)} custom-call(s32[6]{0:T(128)S(1)} %stack.27.flag_ref, bf16[512,448]{1,0:T(8,128)(2,1)S(1)} %constant_dynamic-slice_fusion.3.refs_0_, bf16[512,448]{1,0:T(8,128)(2,1)S(1)} %constant_dynamic-slice_fusion.2.refs_1_, bf16[512,3584]{1,0:T(8,128)(2,1)S(1)} %copy-done.1, bf16[512,3584]{1,0:T(8,128)(2,1)} %copy-done.7, ...), custom_call_target="tpu_custom_call" | custom-call | flops 1 | bytes 1 | tf_op jit(solution)/shard_map/pallas_call | solution.py:148
  172.2 5.0 %collective-permute-done.7.refs_2_.refs_0_ = bf16[512,3584]{1,0:T(8,128)(2,1)} collective-permute-done((bf16[512,3584]{1,0:T(8,128)(2,1)}, bf16[512,3584]{1,0:T(8,128)(2,1)}, u32[]{:S(2)}, u32[]{:S(2)}) %collective-permute-start.7) | collective-permute-done | bytes 3670048 | tf_op jit(solution)/shard_map/ppermute | solution.py:434
  177.8 7.8 %shard_map.87 = (f32[1024,512]{1,0:T(8,128)S(1)}, s16[528,512]{1,0:T(8,128)(2,1)S(1)}) custom-call(s32[6]{0:T(128)S(1)} %stack.27.flag_ref, bf16[512,3584]{1,0:T(8,128)(2,1)} %collective-permute-done.refs_4_.refs_1_.first_ref, bf16[512,3584]{1,0:T(8,128)(2,1)} %collective-permute-done.2.refs_5_.second_ref, ...), custom_call_target="tpu_custom_call" | custom-call | flops 1 | bytes 1 | tf_op jit(solution)/shard_map/pallas_call | solution.py:148
  189.2 9.1 %shard_map.88 = s16[464,3584]{1,0:T(8,128)(2,1)} custom-call(s32[6]{0:T(128)S(1)} %stack.27.flag_ref, bf16[512,448]{1,0:T(8,128)(2,1)S(1)} %get-tuple-element.98.refs_0_, bf16[512,448]{1,0:T(8,128)(2,1)S(1)} %constant_dynamic-slice_fusion.1.refs_1_, bf16[512,3584]{1,0:T(8,128)(2,1)} %collective-permute-done.8.refs_0_.refs_2_.refs_3_.refs_1_, ...), custom_call_target="tpu_custom_call" | custom-call | flops 1 | bytes 1 | tf_op jit(solution)/shard_map/pallas_call | solution.py:148
  202.9 11.2 %shard_map.89 = (f32[448,3584]{1,0:T(8,128)}, s16[464,3584]{1,0:T(8,128)(2,1)S(1)}) custom-call(s32[6]{0:T(128)S(1)} %stack.27.flag_ref, bf16[512,448]{1,0:T(8,128)(2,1)S(1)} %get-tuple-element.99.refs_0_, bf16[512,448]{1,0:T(8,128)(2,1)S(1)} %dynamic-slice_select_fusion.refs_1_, bf16[512,3584]{1,0:T(8,128)(2,1)} %collective-permute-done.7.refs_2_.refs_0_, ...), custom_call_target="tpu_custom_call" | custom-call | flops 1 | bytes 1 | tf_op jit(solution)/shard_map/pallas_call | solution.py:148
  214.2 32.6 %collective-permute-done.11.refs_1_ = s16[528,512]{1,0:T(8,128)(2,1)S(1)} collective-permute-done((s16[528,512]{1,0:T(8,128)(2,1)S(1)}, s16[528,512]{1,0:T(8,128)(2,1)S(1)}, u32[]{:S(2)}, u32[]{:S(2)}) %collective-permute-start.11) | collective-permute-done | bytes 540704 | tf_op jit(solution)/shard_map/ppermute | solution.py:434
  248.6 8.4 %shard_map.91 = (f32[1024,512]{1,0:T(8,128)S(1)}, s16[528,512]{1,0:T(8,128)(2,1)S(1)}) custom-call(s32[6]{0:T(128)S(1)} %stack.27.flag_ref, bf16[512,3584]{1,0:T(8,128)(2,1)} %copy-done, bf16[512,3584]{1,0:T(8,128)(2,1)} %copy-done.7, bf16[512,3584]{1,0:T(8,128)(2,1)} %collective-permute-done.7.refs_2_.refs_0_, ...), custom_call_target="tpu_custom_call" | custom-call | flops 1 | bytes 1 | tf_op jit(solution)/shard_map/pallas_call | solution.py:148
  258.3 6.5 %shard_map.92 = (f32[1536,512]{1,0:T(8,128)}, s16[1568,512]{1,0:T(8,128)(2,1)}) custom-call(s32[6]{0:T(128)S(1)} %stack.27.flag_ref, f32[1024,512]{1,0:T(8,128)S(1)} %get-tuple-element.55.refs_0_, f32[1024,512]{1,0:T(8,128)} %copy-done.4, f32[1024,512]{1,0:T(8,128)} %get-tuple-element.57.refs_2_, s16[1568,512]{1,0:T(8,128)(2,1)} %collective-permute-done.12.refs_3_), custom_call_target="tpu_custom_call" | custom-call | flops 1 | bytes 1 | tf_op jit(solution)/shard_map/pallas_call | solution.py:148
  270.6 3.6 %collective-permute-start.20 = (s16[464,1792]{1,0:T(8,128)(2,1)S(1)}, s16[464,1792]{1,0:T(8,128)(2,1)S(1)}, u32[]{:S(2)}, u32[]{:S(2)}) collective-permute-start(s16[464,1792]{1,0:T(8,128)(2,1)S(1)} %get-tuple-element.102), channel_id=1, source_target_pairs={{1,2},{2,1},{5,6},{6,5},{9,10},{10,9},{13,14},{14,13},{17,18},{18,... | collective-permute-start | bytes 4988936 | tf_op jit(solution)/shard_map/ppermute | solution.py:434
  274.3 46.1 %collective-permute-done.13.refs_1_ = s16[528,512]{1,0:T(8,128)(2,1)S(1)} collective-permute-done((s16[528,512]{1,0:T(8,128)(2,1)S(1)}, s16[528,512]{1,0:T(8,128)(2,1)S(1)}, u32[]{:S(2)}, u32[]{:S(2)}) %collective-permute-start.13) | collective-permute-done | bytes 540704 | tf_op jit(solution)/shard_map/ppermute | solution.py:434
  329.4 5.1 %shard_map.94 = (f32[512,2048]{1,0:T(8,128)}, f32[512,2048]{1,0:T(8,128)}) custom-call(s32[6]{0:T(128)S(1)} %stack.27.flag_ref, f32[1]{0:T(128)} %bitcast.4.scale_ref, f32[512,2048]{1,0:T(8,128)} %old_ref.3, f32[1536,512]{1,0:T(8,128)} %get-tuple-element.74.same_ref, s16[1568,512]{1,0:T(8,128)(2,1)S(1)} %collective-permute-done.14.same_other_ref, ...), custom_call_target="tpu_custom_call" | custom-call | flops 1 | bytes 1 | tf_op jit(solution)/shard_map/pallas_call | solution.py:148
  334.5 4.6 %collective-permute-done.16.refs_0_ = s16[528,512]{1,0:T(8,128)(2,1)S(1)} collective-permute-done((s16[528,512]{1,0:T(8,128)(2,1)S(1)}, s16[528,512]{1,0:T(8,128)(2,1)S(1)}, u32[]{:S(2)}, u32[]{:S(2)}) %collective-permute-start.16) | collective-permute-done | bytes 540704 | tf_op jit(solution)/shard_map/ppermute | solution.py:434
  341.0 5.1 %shard_map.95 = (f32[512,2048]{1,0:T(8,128)}, f32[512,2048]{1,0:T(8,128)}) custom-call(s32[6]{0:T(128)S(1)} %stack.27.flag_ref, f32[1]{0:T(128)} %bitcast.4.scale_ref, f32[512,2048]{1,0:T(8,128)} %old_ref.3, f32[1536,512]{1,0:T(8,128)} %get-tuple-element.74.same_ref, ...), custom_call_target="tpu_custom_call", output_to_operand_aliasing={{0}: (9, {}), {1}: (10, {})} | custom-call | flops 1 | bytes 1 | tf_op jit(solution)/shard_map/pallas_call | solution.py:148
  346.1 7.9 %shard_map.96 = (f32[448,3584]{1,0:T(8,128)}, f32[448,3584]{1,0:T(8,128)}) custom-call(s32[6]{0:T(128)S(1)} %stack.27.flag_ref, f32[1]{0:T(128)S(6)} %div.21.scale_ref, f32[448,3584]{1,0:T(8,128)} %bitcast.8, f32[448,3584]{1,0:T(8,128)} %get-tuple-element.90.value_ref, s16[464,1792]{1,0:T(8,128)(2,1)S(1)} %collective-permute-done.19.coded_ref.level_ref, ...), custom_call_target="tpu_custom_call" | custom-call | flops 1 | bytes 1 | tf_op jit(solution)/shard_map/pallas_call | solution.py:148
  354.0 7.9 %shard_map.97 = (f32[448,3584]{1,0:T(8,128)}, f32[448,3584]{1,0:T(8,128)}) custom-call(s32[6]{0:T(128)S(1)} %stack.27.flag_ref, f32[1]{0:T(128)S(6)} %div.21.scale_ref, f32[448,3584]{1,0:T(8,128)} %bitcast.9, f32[448,3584]{1,0:T(8,128)} %get-tuple-element.90.value_ref, ...), custom_call_target="tpu_custom_call", output_to_operand_aliasing={{0}: (8, {}), {1}: (9, {})} | custom-call | flops 1 | bytes 1 | tf_op jit(solution)/shard_map/pallas_call | solution.py:148
  (64 shorter events, 44.2 us)
Async XLA Ops:
  0.6 83.2 %collective-permute-start = (bf16[512,3584]{1,0:T(8,128)(2,1)}, bf16[512,3584]{1,0:T(8,128)(2,1)}, u32[]{:S(2)}, u32[]{:S(2)}) collective-permute-start(bf16[512,3584]{1,0:T(8,128)(2,1)} %param.5), channel_id=1, source_target_pairs={{0,4},{1,6},{2,5},{3,7},{4,0},{5,2},{6,1},{7,3},{8,12},{9,14},{10,... | collective-permute-start | bytes 11010056 | tf_op jit(solution)/shard_map/ppermute | solution.py:434
  4.3 79.5 %collective-permute-start.1 = (bf16[512,3584]{1,0:T(8,128)(2,1)}, bf16[512,3584]{1,0:T(8,128)(2,1)}, u32[]{:S(2)}, u32[]{:S(2)}) collective-permute-start(bf16[512,3584]{1,0:T(8,128)(2,1)} %param.5), channel_id=1, source_target_pairs={{4,8},{5,10},{6,9},{7,11},{8,4},{9,6},{10,5},{11,7},{20,24},{21,26... | collective-permute-start | bytes 11010056 | tf_op jit(solution)/shard_map/ppermute | solution.py:434
  83.9 9.7 %collective-permute-start.3 = (bf16[512,3584]{1,0:T(8,128)(2,1)}, bf16[512,3584]{1,0:T(8,128)(2,1)}, u32[]{:S(2)}, u32[]{:S(2)}) collective-permute-start(bf16[512,3584]{1,0:T(8,128)(2,1)} %collective-permute-done.1.refs_6_.refs_2_), channel_id=1, source_target_pairs={{0,1},{1,0},{2,3},{3,2},{4,5},{5,4},{6,7},{7,6},{8,9},{9,8},{10,11... | collective-permute-start | bytes 11010056 | tf_op jit(solution)/shard_map/ppermute | solution.py:434
  83.9 12.0 %collective-permute-start.2 = (bf16[512,3584]{1,0:T(8,128)(2,1)}, bf16[512,3584]{1,0:T(8,128)(2,1)}, u32[]{:S(2)}, u32[]{:S(2)}) collective-permute-start(bf16[512,3584]{1,0:T(8,128)(2,1)} %collective-permute-done.refs_4_.refs_1_.first_ref), channel_id=1, source_target_pairs={{0,1},{1,0},{2,3},{3,2},{4,5},{5,4},{6,7},{7,6},{8,9},{9,8},{10,11... | collective-permute-start | bytes 11010056 | tf_op jit(solution)/shard_map/ppermute | solution.py:434
  84.4 44.8 %collective-permute-start.4 = (bf16[512,3584]{1,0:T(8,128)(2,1)}, bf16[512,3584]{1,0:T(8,128)(2,1)}, u32[]{:S(2)}, u32[]{:S(2)}) collective-permute-start(bf16[512,3584]{1,0:T(8,128)(2,1)} %param.5), channel_id=1, source_target_pairs={{1,2},{2,1},{5,6},{6,5},{9,10},{10,9},{13,14},{14,13},{17,18},{18,... | collective-permute-start | bytes 11010056 | tf_op jit(solution)/shard_map/ppermute | solution.py:434
  87.9 84.3 %collective-permute-start.8 = (bf16[512,3584]{1,0:T(8,128)(2,1)}, bf16[512,3584]{1,0:T(8,128)(2,1)}, u32[]{:S(2)}, u32[]{:S(2)}) collective-permute-start(bf16[512,3584]{1,0:T(8,128)(2,1)} %collective-permute-done.refs_4_.refs_1_.first_ref), channel_id=1, source_target_pairs={{4,8},{5,9},{6,10},{7,11},{8,4},{9,5},{10,6},{11,7},{20,24},{21,25... | collective-permute-start | bytes 11010056 | tf_op jit(solution)/shard_map/ppermute | solution.py:434
  90.5 86.7 %collective-permute-start.7 = (bf16[512,3584]{1,0:T(8,128)(2,1)}, bf16[512,3584]{1,0:T(8,128)(2,1)}, u32[]{:S(2)}, u32[]{:S(2)}) collective-permute-start(bf16[512,3584]{1,0:T(8,128)(2,1)} %collective-permute-done.1.refs_6_.refs_2_), channel_id=1, source_target_pairs={{4,0},{5,1},{6,2},{7,3},{8,12},{9,13},{10,14},{11,15},{20,16},{21,... | collective-permute-start | bytes 11010056 | tf_op jit(solution)/shard_map/ppermute | solution.py:434
  97.2 32.0 %copy-start.8 = (bf16[512,3584]{1,0:T(8,128)(2,1)S(1)}, bf16[512,3584]{1,0:T(8,128)(2,1)}, u32[]{:S(2)}) copy-start(bf16[512,3584]{1,0:T(8,128)(2,1)} %param.5) | copy-start | bytes 11010052
  131.9 3.9 %collective-permute-start.5 = (bf16[512,1792]{1,0:T(8,128)(2,1)S(1)}, bf16[512,1792]{1,0:T(8,128)(2,1)S(1)}, u32[]{:S(2)}, u32[]{:S(2)}) collective-permute-start(bf16[512,1792]{1,0:T(8,128)(2,1)S(1)} %get-tuple-element.101), channel_id=1, source_target_pairs={{0,1},{1,0},{2,3},{3,2},{4,5},{5,4},{6,7},{7,6},{8,9},{9,8},{10,11... | collective-permute-start | bytes 5505032 | tf_op jit(solution)/shard_map/ppermute | solution.py:434
  132.0 6.4 %collective-permute-start.6 = (bf16[512,1792]{1,0:T(8,128)(2,1)S(1)}, bf16[512,1792]{1,0:T(8,128)(2,1)S(1)}, u32[]{:S(2)}, u32[]{:S(2)}) collective-permute-start(bf16[512,1792]{1,0:T(8,128)(2,1)S(1)} %get-tuple-element.100), channel_id=1, source_target_pairs={{0,1},{1,0},{2,3},{3,2},{4,5},{5,4},{6,7},{7,6},{8,9},{9,8},{10,11... | collective-permute-start | bytes 5505032 | tf_op jit(solution)/shard_map/ppermute | solution.py:434
  140.4 22.0 %copy-start.1 = (bf16[512,3584]{1,0:T(8,128)(2,1)S(1)}, bf16[512,3584]{1,0:T(8,128)(2,1)}, u32[]{:S(2)}) copy-start(bf16[512,3584]{1,0:T(8,128)(2,1)} %copy-done) | copy-start | bytes 11010052
  177.2 10.7 %collective-permute-start.9 = (bf16[512,3584]{1,0:T(8,128)(2,1)}, bf16[512,3584]{1,0:T(8,128)(2,1)}, u32[]{:S(2)}, u32[]{:S(2)}) collective-permute-start(bf16[512,3584]{1,0:T(8,128)(2,1)} %collective-permute-done.8.refs_0_.refs_2_.refs_3_.refs_1_), channel_id=1, source_target_pairs={{0,1},{1,0},{2,3},{3,2},{4,5},{5,4},{6,7},{7,6},{8,9},{9,8},{10,11... | collective-permute-start | bytes 11010056 | tf_op jit(solution)/shard_map/ppermute | solution.py:434
  177.7 23.5 %collective-permute-start.10 = (bf16[512,3584]{1,0:T(8,128)(2,1)}, bf16[512,3584]{1,0:T(8,128)(2,1)}, u32[]{:S(2)}, u32[]{:S(2)}) collective-permute-start(bf16[512,3584]{1,0:T(8,128)(2,1)} %collective-permute-done.7.refs_2_.refs_0_), channel_id=1, source_target_pairs={{0,1},{1,0},{2,3},{3,2},{4,5},{5,4},{6,7},{7,6},{8,9},{9,8},{10,11... | collective-permute-start | bytes 11010056 | tf_op jit(solution)/shard_map/ppermute | solution.py:434
  177.7 80.6 %collective-permute-start.12 = (s16[1568,512]{1,0:T(8,128)(2,1)}, s16[1568,512]{1,0:T(8,128)(2,1)}, u32[]{:S(2)}, u32[]{:S(2)}) collective-permute-start(s16[1568,512]{1,0:T(8,128)(2,1)} %get-tuple-element.58), channel_id=1, source_target_pairs={{0,2},{1,3},{2,0},{3,1},{4,6},{5,7},{6,4},{7,5},{8,10},{9,11},{10,... | collective-permute-start | bytes 4816904 | tf_op jit(solution)/shard_map/ppermute | solution.py:434
  198.3 147.7 %collective-permute-start.18 = (s16[464,3584]{1,0:T(8,128)(2,1)}, s16[464,3584]{1,0:T(8,128)(2,1)S(1)}, u32[]{:S(2)}, u32[]{:S(2)}) collective-permute-start(s16[464,3584]{1,0:T(8,128)(2,1)} %shard_map.88), channel_id=1, source_target_pairs={{4,0},{5,2},{6,1},{7,3},{8,12},{9,14},{10,13},{11,15},{20,16},{21,... | collective-permute-start | bytes 9977864 | tf_op jit(solution)/shard_map/ppermute | solution.py:434
  199.8 47.0 %collective-permute-start.11 = (s16[528,512]{1,0:T(8,128)(2,1)S(1)}, s16[528,512]{1,0:T(8,128)(2,1)S(1)}, u32[]{:S(2)}, u32[]{:S(2)}) collective-permute-start(s16[528,512]{1,0:T(8,128)(2,1)S(1)} %get-tuple-element.64), channel_id=1, source_target_pairs={{0,2},{1,3},{2,0},{3,1},{4,6},{5,7},{6,4},{7,5},{8,10},{9,11},{10,... | collective-permute-start | bytes 1622024 | tf_op jit(solution)/shard_map/ppermute | solution.py:434
  264.8 55.6 %copy-start.3 = (f32[1024,512]{1,0:T(8,128)S(1)}, f32[1024,512]{1,0:T(8,128)}, u32[]{:S(2)}) copy-start(f32[1024,512]{1,0:T(8,128)} %copy-done.2) | copy-start | bytes 6291460
  264.8 61.6 %collective-permute-start.14 = (s16[1568,512]{1,0:T(8,128)(2,1)}, s16[1568,512]{1,0:T(8,128)(2,1)S(1)}, u32[]{:S(2)}, u32[]{:S(2)}) collective-permute-start(s16[1568,512]{1,0:T(8,128)(2,1)} %get-tuple-element.76), channel_id=1, source_target_pairs={{0,1},{1,0},{2,3},{3,2},{4,5},{5,4},{6,7},{7,6},{8,9},{9,8},{10,11... | collective-permute-start | bytes 4816904 | tf_op jit(solution)/shard_map/ppermute | solution.py:434
  268.7 77.4 %collective-permute-start.19 = (s16[464,1792]{1,0:T(8,128)(2,1)}, s16[464,1792]{1,0:T(8,128)(2,1)S(1)}, u32[]{:S(2)}, u32[]{:S(2)}) collective-permute-start(s16[464,1792]{1,0:T(8,128)(2,1)} %get-tuple-element.103), channel_id=1, source_target_pairs={{1,2},{2,1},{5,6},{6,5},{9,10},{10,9},{13,14},{14,13},{17,18},{18,... | collective-permute-start | bytes 4988936 | tf_op jit(solution)/shard_map/ppermute | solution.py:434
  270.6 75.5 %collective-permute-start.20 = (s16[464,1792]{1,0:T(8,128)(2,1)S(1)}, s16[464,1792]{1,0:T(8,128)(2,1)S(1)}, u32[]{:S(2)}, u32[]{:S(2)}) collective-permute-start(s16[464,1792]{1,0:T(8,128)(2,1)S(1)} %get-tuple-element.102), channel_id=1, source_target_pairs={{1,2},{2,1},{5,6},{6,5},{9,10},{10,9},{13,14},{14,13},{17,18},{18,... | collective-permute-start | bytes 4988936 | tf_op jit(solution)/shard_map/ppermute | solution.py:434
  274.2 46.2 %collective-permute-start.13 = (s16[528,512]{1,0:T(8,128)(2,1)S(1)}, s16[528,512]{1,0:T(8,128)(2,1)S(1)}, u32[]{:S(2)}, u32[]{:S(2)}) collective-permute-start(s16[528,512]{1,0:T(8,128)(2,1)S(1)} %copy-done.6), channel_id=1, source_target_pairs={{0,2},{1,3},{2,0},{3,1},{4,6},{5,7},{6,4},{7,5},{8,10},{9,11},{10,... | collective-permute-start | bytes 1622024 | tf_op jit(solution)/shard_map/ppermute | solution.py:434
  321.3 3.8 %collective-permute-start.15 = (s16[528,512]{1,0:T(8,128)(2,1)S(1)}, s16[528,512]{1,0:T(8,128)(2,1)S(1)}, u32[]{:S(2)}, u32[]{:S(2)}) collective-permute-start(s16[528,512]{1,0:T(8,128)(2,1)S(1)} %get-tuple-element.78), channel_id=1, source_target_pairs={{0,1},{1,0},{2,3},{3,2},{4,5},{5,4},{6,7},{7,6},{8,9},{9,8},{10,11... | collective-permute-start | bytes 1622024 | tf_op jit(solution)/shard_map/ppermute | solution.py:434
  325.1 13.9 %collective-permute-start.16 = (s16[528,512]{1,0:T(8,128)(2,1)S(1)}, s16[528,512]{1,0:T(8,128)(2,1)S(1)}, u32[]{:S(2)}, u32[]{:S(2)}) collective-permute-start(s16[528,512]{1,0:T(8,128)(2,1)S(1)} %get-tuple-element.70), channel_id=1, source_target_pairs={{5,1},{7,3},{8,12},{10,14},{21,17},{23,19},{24,28},{26,30}} | collective-permute-start | bytes 1622024 | tf_op jit(solution)/shard_map/ppermute | solution.py:434
  326.4 14.6 %collective-permute-start.17 = (s16[528,512]{1,0:T(8,128)(2,1)S(1)}, s16[528,512]{1,0:T(8,128)(2,1)S(1)}, u32[]{:S(2)}, u32[]{:S(2)}) collective-permute-start(s16[528,512]{1,0:T(8,128)(2,1)S(1)} %get-tuple-element.70), channel_id=1, source_target_pairs={{4,1},{6,3},{9,12},{11,14},{20,17},{22,19},{25,28},{27,30}} | collective-permute-start | bytes 1622024 | tf_op jit(solution)/shard_map/ppermute | solution.py:434
  (6 other events, 37.6 us)

commit v9 on v7

--- a/solution.py
+++ b/solution.py
@@ -237,25 +237,35 @@
     return kernel_call(body, flags, steps, ins, outs)
 
 
-def right_terms(flags, strips, columns, block, steps, at=START, before=None, last=False):
+def right_terms(
+    flags, strips, columns, block, steps, at=START, before=None, last=False, hand_on=False
+):
     wide = block * steps
-    rows, strip = strips[0].shape
-    many = len(strips)
+    given = not isinstance(strips, list)
+    if given:
+        many, strip, rows = strips.shape
+        strips = [strips]
+    else:
+        rows, strip = strips[0].shape
+        many = len(strips)
 
     def body(flag_ref, *refs):
-        strips_in, refs = refs[:many], refs[many:]
+        strips_in, refs = refs[: len(strips)], refs[len(strips) :]
         columns_in = []
         for choice in columns:
             columns_in.append(refs[: len(choice)])
             refs = refs[len(choice) :]
         if before is not None:
             before_in, refs = refs[0], refs[1:]
-        outs, turned = refs[:-1], refs[-1]
-
-        @pl.when(pl.program_id(0) == 0)
-        def _():
-            for index in range(many):
-                turned[index] = strips_in[index][...].T
+        if given:
+            outs, turned = refs, strips_in[0]
+        else:
+            outs, turned = refs[:-1], refs[-1]
+
+            @pl.when(pl.program_id(0) == 0)
+            def _():
+                for index in range(many):
+                    turned[index] = strips_in[index][...].T
 
         def add(choice):
             total = None if before is None else before_in[...]
@@ -275,7 +285,9 @@
             put_levels(pack(outs[0][...], outs[1], 0), outs[1], strip)
 
     here = lambda k, flags: k
-    ins = [(part, whole(part)) for part in strips]
+    shape = (many, strip, rows)
+    still = pl.BlockSpec(shape, lambda k, flags: (0, 0, 0))
+    ins = [(part, still if given else whole(part)) for part in strips]
     for choice in columns:
         ins += [
             (array, spec((rows, block), blocks_from(start, choice_of(choice, index))))
@@ -286,7 +298,11 @@
     outs = [((strip, wide), jnp.float32, spec((strip, block), here))]
     if last:
         outs.append(((strip + LEVELS, wide), jnp.int16, spec((strip + LEVELS, block), here)))
-    scratch = [pltpu.VMEM((many, strip, rows), jnp.bfloat16)]
+    scratch = []
+    if hand_on:
+        outs.append((shape, jnp.bfloat16, still))
+    elif not given:
+        scratch = [pltpu.VMEM(shape, jnp.bfloat16)]
     return kernel_call(body, flags, steps, ins, outs, scratch=scratch)
 
 
@@ -332,8 +348,8 @@
                 old_ref[...], unpack(coded_ref, 0, strip, 1), scale_ref[0], state_ref, fixed_ref, everything
             )
 
-    part = math.gcd(block * steps, 256)
-    there = lambda k, flags: k + flags[at] * block // part
+    part = block
+    there = lambda k, flags: k + flags[at]
     ins = [
         (scale, pl.BlockSpec(memory_space=pltpu.SMEM)),
         (old, spec((strip, part), there)),
@@ -345,7 +361,7 @@
         ins += [(array, pl.BlockSpec(memory_space=pl.ANY)) for array in written]
         aliases = {5: 0, 6: 1}
     outs = [((strip, wide), jnp.float32, spec((strip, part), there))] * 2
-    return kernel_call(body, flags, steps * block // part, ins, outs, aliases)
+    return kernel_call(body, flags, steps, ins, outs, aliases)
 
 
 def finish_left(flags, scale, old, same_total, same_other, total, other, inner, written=None):
@@ -544,16 +560,18 @@
     near_total, near_out = add_up(flags, [near_product], near_got)
     near_other = send(near_out, to_away)
 
+    far_t, near_out = tie(far, near_out)
+    far_away, near_out = tie(columns(far_t, 2 * (1 - side), 2), near_out)
     right, near_out, end_home, far_o = tie(right, near_out, end_home, far_o)
-    far, end_home = tie(far, end_home)
-    end_away = send(columns(far, 2 * (1 - side), 2), outward)
+    far_away, end_home = tie(far_away, end_home)
+    end_away = send(far_away, outward)
     end_home_o = send(end_home, beside)
     strips = [
         jnp.where(is_middle, strips_of([a])[0], strips_of([b], 2 * side * block)[0])
         for a, b in ((far, end_home), (far_o, end_home_o))
     ]
 
-    def last_right(end, end_o, start, at, steps):
+    def last_right(strips, end, end_o, start, at, steps):
         return right_terms(
             flags,
             strips,
@@ -563,9 +581,10 @@
             at=at,
             before=right,
             last=True,
+            hand_on=isinstance(strips, list),
         )
 
-    right_home, home_coded = last_right(end_home, end_home_o, START, HOME, 2)
+    right_home, home_coded, strips = last_right(strips, end_home, end_home_o, START, HOME, 2)
     home_got = send(home_coded, to_line)
     home_coded, end_home = tie(home_coded, end_home)
     [far_product] = left_terms(
@@ -588,10 +607,10 @@
     )
     far_got = send(far_coded, other_y)
     far_coded, end_away_o = tie(far_coded, end_away_o)
-    right_away, away_coded = last_right(end_away, end_away_o, START, AWAY, 1)
+    right_away, away_coded = last_right(strips, end_away, end_away_o, START, AWAY, 1)
     away_got = send(away_coded, to_line)
     away_coded, end_away_o = tie(away_coded, end_away_o)
-    right_last, last_coded = last_right(end_away, end_away_o, NEXT, LAST, 1)
+    right_last, last_coded = last_right(strips, end_away, end_away_o, NEXT, LAST, 1)
     last_got = send(last_coded, to_line)
     last_coded, far_got = tie(last_coded, far_got)
     far_total, far_out = add_up(flags, [far_product], far_got)

time: 320 us -> 314 us (0.981)
  waiting for transfers between devices: 135 us -> 128 us
  Pallas kernels: 117 us -> 113 us
  local copies, waits for them, and re-layouts: 25.4 us -> 28.6 us
    ppermute x24, waiting for transfers between devices: 135 us -> 128 us  [send(): return lax.ppermute(value, AXES, pairs)]
    pallas_call x18, Pallas kernels: 117 us -> 113 us  [kernel_call(): pl.pallas_call(body, grid_spec=pltpu.PrefetchScalarGridSpec(num_scalar_pr...]
    unnamed x35 -> x43, local copies, waits for them, and re-layouts: 11.1 us -> 12.4 us
  transfers between devices with their start and end apart: 24 -> 24, of which waited for: 11 -> 12; matrix products, arithmetic and copies ran while one was open for 6% -> 7% of each run, Pallas kernels for 35% -> 35%
where the time goes in v9:
time: 314 us; the launch traced here: 313 us
  waiting for transfers between devices  128 us (41%)
  Pallas kernels  113 us (36%)
  starting transfers between devices  34.7 us (11%)
  local copies, waits for them, and re-layouts  28.6 us (9%)
  other arithmetic  5.8 us (2%)
    ppermute x24, waiting for transfers between devices, send(): return lax.ppermute(value, AXES, pairs)  128 us
    pallas_call x18, Pallas kernels, kernel_call(): pl.pallas_call(body, grid_spec=pltpu.PrefetchScalarGridSpec(num_scalar_pr...  113 us
    ppermute x24, starting transfers between devices, send(): return lax.ppermute(value, AXES, pairs)  34.7 us
    unnamed x43, local copies, waits for them, and re-layouts  12.4 us
    dynamic_slice x7, local copies, waits for them, and re-layouts, strips_of(): lax.dynamic_slice_in_dim(part, strip_at - first, strip, 1)  9.32 us
    dynamic_slice x2, local copies, waits for them, and re-layouts, columns(): return lax.dynamic_slice_in_dim(value, first * block, count * block, 1)  6.4 us
  transfers between devices with their start and end apart: 24, of which 12 were waited for; matrix products, arithmetic and copies ran while one was open for 7% of the time, Pallas kernels for 35%

profile of v9, /device:TPU:1, one launch (start us, length us, event | category | flops | bytes accessed | tf_op | source)
XLA Modules:
  0.0 312.6 jit_solution(15727714924608510570)
XLA Ops:
  3.1 4.1 %collective-permute-start = (bf16[512,3584]{1,0:T(8,128)(2,1)}, bf16[512,3584]{1,0:T(8,128)(2,1)}, u32[]{:S(2)}, u32[]{:S(2)}) collective-permute-start(bf16[512,3584]{1,0:T(8,128)(2,1)} %param.5), channel_id=1, source_target_pairs={{0,4},{1,6},{2,5},{3,7},{4,0},{5,2},{6,1},{7,3},{8,12},{9,14},{10,... | collective-permute-start | bytes 11010056 | tf_op jit(solution)/shard_map/ppermute | solution.py:430
  7.2 79.7 %collective-permute-done.refs_4_.refs_1_ = bf16[512,3584]{1,0:T(8,128)(2,1)} collective-permute-done((bf16[512,3584]{1,0:T(8,128)(2,1)}, bf16[512,3584]{1,0:T(8,128)(2,1)}, u32[]{:S(2)}, u32[]{:S(2)}) %collective-permute-start) | collective-permute-done | bytes 3670048 | tf_op jit(solution)/shard_map/ppermute | solution.py:430
  87.5 3.8 %collective-permute-start.4 = (bf16[512,3584]{1,0:T(8,128)(2,1)}, bf16[512,3584]{1,0:T(8,128)(2,1)}, u32[]{:S(2)}, u32[]{:S(2)}) collective-permute-start(bf16[512,3584]{1,0:T(8,128)(2,1)} %param.5), channel_id=1, source_target_pairs={{1,2},{2,1},{5,6},{6,5},{9,10},{10,9},{13,14},{14,13},{17,18},{18,... | collective-permute-start | bytes 11010056 | tf_op jit(solution)/shard_map/ppermute | solution.py:430
  100.5 13.6 %shard_map.84.refs_4_ = f32[448,3584]{1,0:T(8,128)} custom-call(s32[9]{0:T(128)S(1)} %stack.39.flag_ref, bf16[512,448]{1,0:T(8,128)(2,1)S(1)} %get-tuple-element.141.refs_0_, bf16[512,448]{1,0:T(8,128)(2,1)S(1)} %constant_dynamic-slice_fusion.8.refs_1_, bf16[512,448]{1,0:T(8,128)(2,1)S(1)} %get-tuple-element.140.refs_2_, ...), custom_call_target="tpu_custom_call" | custom-call | flops 1 | bytes 1 | tf_op jit(solution)/shard_map/pallas_call | solution.py:149
  114.1 18.4 %collective-permute-done.4 = bf16[512,3584]{1,0:T(8,128)(2,1)} collective-permute-done((bf16[512,3584]{1,0:T(8,128)(2,1)}, bf16[512,3584]{1,0:T(8,128)(2,1)}, u32[]{:S(2)}, u32[]{:S(2)}) %collective-permute-start.4) | collective-permute-done | bytes 3670048 | tf_op jit(solution)/shard_map/ppermute | solution.py:430
  143.6 13.7 %shard_map.85 = (f32[1024,512]{1,0:T(8,128)S(1)}, f32[1024,512]{1,0:T(8,128)S(1)}, s16[1040,512]{1,0:T(8,128)(2,1)}) custom-call(s32[9]{0:T(128)S(1)} %stack.39.flag_ref, bf16[512,3584]{1,0:T(8,128)(2,1)} %copy-done, bf16[512,3584]{1,0:T(8,128)(2,1)} %copy-done.18, bf16[512,3584]{1,0:T(8,128)(2,1)} %copy-done, ...), custom_call_target="tpu_custom_call" | custom-call | flops 1 | bytes 1 | tf_op jit(solution)/shard_map/pallas_call | solution.py:149
  160.5 9.8 %shard_map.86.refs_4_ = f32[448,3584]{1,0:T(8,128)} custom-call(s32[9]{0:T(128)S(1)} %stack.39.flag_ref, bf16[512,448]{1,0:T(8,128)(2,1)S(1)} %constant_dynamic-slice_fusion.5.refs_0_, bf16[512,448]{1,0:T(8,128)(2,1)S(1)} %constant_dynamic-slice_fusion.4.refs_1_, bf16[512,3584]{1,0:T(8,128)(2,1)S(1)} %copy-done.1, bf16[512,3584]{1,0:T(8,128)(2,1)} %copy-done.18, ...), custom_call_target="tpu_custom_call" | custom-call | flops 1 | bytes 1 | tf_op jit(solution)/shard_map/pallas_call | solution.py:149
  170.3 6.5 %collective-permute-done.8.refs_0_.refs_2_ = bf16[512,3584]{1,0:T(8,128)(2,1)} collective-permute-done((bf16[512,3584]{1,0:T(8,128)(2,1)}, bf16[512,3584]{1,0:T(8,128)(2,1)}, u32[]{:S(2)}, u32[]{:S(2)}) %collective-permute-start.8) | collective-permute-done | bytes 3670048 | tf_op jit(solution)/shard_map/ppermute | solution.py:430
  182.5 9.2 %shard_map.87 = (f32[1024,512]{1,0:T(8,128)S(1)}, s16[528,512]{1,0:T(8,128)(2,1)}) custom-call(s32[9]{0:T(128)S(1)} %stack.39.flag_ref, bf16[512,3584]{1,0:T(8,128)(2,1)} %copy-done, bf16[512,3584]{1,0:T(8,128)(2,1)} %copy-done.18, bf16[512,3584]{1,0:T(8,128)(2,1)} %collective-permute-done.8.refs_0_.refs_2_, ...), custom_call_target="tpu_custom_call" | custom-call | flops 1 | bytes 1 | tf_op jit(solution)/shard_map/pallas_call | solution.py:149
  196.5 10.6 %shard_map.88.refs_6_.refs_5_ = f32[448,3584]{1,0:T(8,128)} custom-call(s32[9]{0:T(128)S(1)} %stack.39.flag_ref, bf16[512,448]{1,0:T(8,128)(2,1)S(1)} %constant_dynamic-slice_fusion.3.refs_0_, bf16[512,448]{1,0:T(8,128)(2,1)S(1)} %constant_dynamic-slice_fusion.2.refs_1_, bf16[512,3584]{1,0:T(8,128)(2,1)} %collective-permute-done.8.refs_0_.refs_2_, ...), custom_call_target="tpu_custom_call" | custom-call | flops 1 | bytes 1 | tf_op jit(solution)/shard_map/pallas_call | solution.py:149
  207.1 3.6 %shard_map.89 = (f32[1024,512]{1,0:T(8,128)S(1)}, s16[1040,512]{1,0:T(8,128)(2,1)S(1)}) custom-call(s32[9]{0:T(128)S(1)} %stack.39.flag_ref, f32[1024,512]{1,0:T(8,128)} %copy-done.6, f32[1024,512]{1,0:T(8,128)} %copy-done.7, s16[1040,512]{1,0:T(8,128)(2,1)S(1)} %collective-permute-done.7.refs_2_), custom_call_target="tpu_custom_call" | custom-call | flops 1 | bytes 1 | tf_op jit(solution)/shard_map/pallas_call | solution.py:149
  213.0 5.3 %collective-permute-done.11.refs_1_ = s16[528,512]{1,0:T(8,128)(2,1)S(1)} collective-permute-done((s16[528,512]{1,0:T(8,128)(2,1)}, s16[528,512]{1,0:T(8,128)(2,1)S(1)}, u32[]{:S(2)}, u32[]{:S(2)}) %collective-permute-start.11) | collective-permute-done | bytes 540704 | tf_op jit(solution)/shard_map/ppermute | solution.py:430
  219.2 3.5 %constant_dynamic-slice_fusion.1 = bf16[512,1792]{1,0:T(8,128)(2,1)} fusion(bf16[512,3584]{1,0:T(8,128)(2,1)} %collective-permute-done.9.refs_3_.refs_1_.refs_2_, s32[]{:T(128)S(6)} %select_n.64), kind=kLoop, calls=%fused_computation.6 | loop fusion | bytes 3670020 | tf_op jit(solution)/shard_map/dynamic_slice | solution.py:502
  230.2 7.4 %shard_map.91 = (f32[448,1792]{1,0:T(8,128)}, s16[464,1792]{1,0:T(8,128)(2,1)}, bf16[2,448,512]{2,1,0:T(8,128)(2,1)S(1)}) custom-call(s32[9]{0:T(128)S(1)} %stack.39.flag_ref, bf16[512,448]{1,0:T(8,128)(2,1)S(1)} %dynamic-slice_select_fusion.1.refs_0_, bf16[512,448]{1,0:T(8,128)(2,1)S(1)} %dynamic-slice_select_fusion.refs_1_, ...), custom_call_target="tpu_custom_call" | custom-call | flops 1 | bytes 1 | tf_op jit(solution)/shard_map/pallas_call | solution.py:149
  244.8 5.5 %shard_map.92.refs_2_ = f32[1024,512]{1,0:T(8,128)S(1)} custom-call(s32[9]{0:T(128)S(1)} %stack.39.flag_ref, bf16[512,3584]{1,0:T(8,128)(2,1)} %copy-done, bf16[512,3584]{1,0:T(8,128)(2,1)} %copy-done.18, bf16[512,1792]{1,0:T(8,128)(2,1)S(1)} %collective-permute-done.12.refs_2_.refs_0_, bf16[512,3584]{1,0:T(8,128)(2,1)} %collective-permute-done.9.refs_3_.refs_1_.refs_2_), custom_call_target="tpu_custom_call" | custom-call | flops 1 | bytes 1 | tf_op jit(solution)/shard_map/pallas_call | solution.py:149
  250.4 4.2 %shard_map.93 = (f32[512,2048]{1,0:T(8,128)}, f32[512,2048]{1,0:T(8,128)}) custom-call(s32[9]{0:T(128)S(1)} %stack.39.flag_ref, f32[1]{0:T(128)} %bitcast.7.scale_ref, f32[512,2048]{1,0:T(8,128)} %old_ref.3, f32[1024,512]{1,0:T(8,128)S(1)} %copy-done.3, s16[1040,512]{1,0:T(8,128)(2,1)S(1)} %collective-permute-done.16.same_other_ref, ...), custom_call_target="tpu_custom_call" | custom-call | flops 1 | bytes 1 | tf_op jit(solution)/shard_map/pallas_call | solution.py:149
  254.6 6.2 %collective-permute-done.17.coded_ref = s16[464,1792]{1,0:T(8,128)(2,1)S(1)} collective-permute-done((s16[464,1792]{1,0:T(8,128)(2,1)}, s16[464,1792]{1,0:T(8,128)(2,1)S(1)}, u32[]{:S(2)}, u32[]{:S(2)}) %collective-permute-start.17) | collective-permute-done | bytes 1663008 | tf_op jit(solution)/shard_map/ppermute | solution.py:430
  265.3 5.2 %shard_map.94 = (f32[448,3584]{1,0:T(8,128)}, f32[448,3584]{1,0:T(8,128)}) custom-call(s32[9]{0:T(128)S(1)} %stack.39.flag_ref, f32[1]{0:T(128)S(6)} %div.21.scale_ref, f32[448,3584]{1,0:T(8,128)} %bitcast.11, f32[448,1792]{1,0:T(8,128)S(1)} %copy-done.5, s16[464,1792]{1,0:T(8,128)(2,1)S(1)} %copy-done.11), custom_call_target="tpu_custom_call" | custom-call | flops 1 | bytes 1 | tf_op jit(solution)/shard_map/pallas_call | solution.py:149
  270.5 6.1 %shard_map.95 = (f32[1024,512]{1,0:T(8,128)S(1)}, s16[528,512]{1,0:T(8,128)(2,1)S(1)}) custom-call(s32[9]{0:T(128)S(1)} %stack.39.flag_ref, bf16[512,3584]{1,0:T(8,128)(2,1)} %copy-done, bf16[512,3584]{1,0:T(8,128)(2,1)} %copy-done.18, bf16[512,1792]{1,0:T(8,128)(2,1)S(1)} %collective-permute-done.18.refs_0_.refs_1_, ...), custom_call_target="tpu_custom_call" | custom-call | flops 1 | bytes 1 | tf_op jit(solution)/shard_map/pallas_call | solution.py:149
  278.6 5.2 %shard_map.96 = (f32[448,896]{1,0:T(8,128)S(1)}, s16[464,896]{1,0:T(8,128)(2,1)}) custom-call(s32[9]{0:T(128)S(1)} %stack.39.flag_ref, bf16[2,448,512]{2,1,0:T(8,128)(2,1)S(1)} %get-tuple-element.112.refs_0_, bf16[512,1792]{1,0:T(8,128)(2,1)S(1)} %collective-permute-done.18.refs_0_.refs_1_, bf16[512,3584]{1,0:T(8,128)(2,1)} %collective-permute-done.9.refs_3_.refs_1_.refs_2_, ...), custom_call_target="tpu_custom_call" | custom-call | flops 1 | bytes 1 | tf_op jit(solution)/shard_map/pallas_call | solution.py:149
  287.2 5.2 %shard_map.97 = (f32[448,896]{1,0:T(8,128)S(1)}, s16[464,896]{1,0:T(8,128)(2,1)}) custom-call(s32[9]{0:T(128)S(1)} %stack.39.flag_ref, bf16[2,448,512]{2,1,0:T(8,128)(2,1)S(1)} %get-tuple-element.112.refs_0_, bf16[512,1792]{1,0:T(8,128)(2,1)S(1)} %collective-permute-done.18.refs_0_.refs_1_, bf16[512,3584]{1,0:T(8,128)(2,1)} %collective-permute-done.9.refs_3_.refs_1_.refs_2_, ...), custom_call_target="tpu_custom_call" | custom-call | flops 1 | bytes 1 | tf_op jit(solution)/shard_map/pallas_call | solution.py:149
  299.6 4.1 %shard_map.99 = (f32[448,3584]{1,0:T(8,128)}, f32[448,3584]{1,0:T(8,128)}) custom-call(s32[9]{0:T(128)S(1)} %stack.39.flag_ref, f32[1]{0:T(128)S(6)} %div.21.scale_ref, f32[448,3584]{1,0:T(8,128)} %bitcast.12, f32[448,896]{1,0:T(8,128)S(1)} %get-tuple-element.120.value_ref, ...), custom_call_target="tpu_custom_call", output_to_operand_aliasing={{0}: (5, {}), {1}: (6, {})} | custom-call | flops 1 | bytes 1 | tf_op jit(solution)/shard_map/pallas_call | solution.py:149
  303.7 4.1 %shard_map.100 = (f32[512,2048]{1,0:T(8,128)}, f32[512,2048]{1,0:T(8,128)}) custom-call(s32[9]{0:T(128)S(1)} %stack.39.flag_ref, f32[1]{0:T(128)} %bitcast.7.scale_ref, f32[512,2048]{1,0:T(8,128)} %old_ref.3, f32[1024,512]{1,0:T(8,128)S(1)} %copy-done.3, ...), custom_call_target="tpu_custom_call", output_to_operand_aliasing={{0}: (7, {}), {1}: (8, {})} | custom-call | flops 1 | bytes 1 | tf_op jit(solution)/shard_map/pallas_call | solution.py:149
  308.5 4.1 %shard_map.101 = (f32[448,3584]{1,0:T(8,128)}, f32[448,3584]{1,0:T(8,128)}) custom-call(s32[9]{0:T(128)S(1)} %stack.39.flag_ref, f32[1]{0:T(128)S(6)} %div.21.scale_ref, f32[448,3584]{1,0:T(8,128)} %bitcast.13, f32[448,896]{1,0:T(8,128)S(1)} %get-tuple-element.132.value_ref, ...), custom_call_target="tpu_custom_call", output_to_operand_aliasing={{0}: (5, {}), {1}: (6, {})} | custom-call | flops 1 | bytes 1 | tf_op jit(solution)/shard_map/pallas_call | solution.py:149
  (100 shorter events, 70.9 us)
Async XLA Ops:
  0.6 6.6 %collective-permute-start.1 = (bf16[512,3584]{1,0:T(8,128)(2,1)}, bf16[512,3584]{1,0:T(8,128)(2,1)}, u32[]{:S(2)}, u32[]{:S(2)}) collective-permute-start(bf16[512,3584]{1,0:T(8,128)(2,1)} %param.5), channel_id=1, source_target_pairs={{4,8},{5,10},{6,9},{7,11},{8,4},{9,6},{10,5},{11,7},{20,24},{21,26... | collective-permute-start | bytes 11010056 | tf_op jit(solution)/shard_map/ppermute | solution.py:430
  3.1 83.8 %collective-permute-start = (bf16[512,3584]{1,0:T(8,128)(2,1)}, bf16[512,3584]{1,0:T(8,128)(2,1)}, u32[]{:S(2)}, u32[]{:S(2)}) collective-permute-start(bf16[512,3584]{1,0:T(8,128)(2,1)} %param.5), channel_id=1, source_target_pairs={{0,4},{1,6},{2,5},{3,7},{4,0},{5,2},{6,1},{7,3},{8,12},{9,14},{10,... | collective-permute-start | bytes 11010056 | tf_op jit(solution)/shard_map/ppermute | solution.py:430
  86.9 10.1 %collective-permute-start.2 = (bf16[512,3584]{1,0:T(8,128)(2,1)}, bf16[512,3584]{1,0:T(8,128)(2,1)}, u32[]{:S(2)}, u32[]{:S(2)}) collective-permute-start(bf16[512,3584]{1,0:T(8,128)(2,1)} %collective-permute-done.refs_4_.refs_1_), channel_id=1, source_target_pairs={{0,1},{1,0},{2,3},{3,2},{4,5},{5,4},{6,7},{7,6},{8,9},{9,8},{10,11... | collective-permute-start | bytes 11010056 | tf_op jit(solution)/shard_map/ppermute | solution.py:430
  87.5 11.6 %collective-permute-start.3 = (bf16[512,3584]{1,0:T(8,128)(2,1)}, bf16[512,3584]{1,0:T(8,128)(2,1)}, u32[]{:S(2)}, u32[]{:S(2)}) collective-permute-start(bf16[512,3584]{1,0:T(8,128)(2,1)} %collective-permute-done.1.refs_6_.refs_1_), channel_id=1, source_target_pairs={{0,1},{1,0},{2,3},{3,2},{4,5},{5,4},{6,7},{7,6},{8,9},{9,8},{10,11... | collective-permute-start | bytes 11010056 | tf_op jit(solution)/shard_map/ppermute | solution.py:430
  87.5 44.9 %collective-permute-start.4 = (bf16[512,3584]{1,0:T(8,128)(2,1)}, bf16[512,3584]{1,0:T(8,128)(2,1)}, u32[]{:S(2)}, u32[]{:S(2)}) collective-permute-start(bf16[512,3584]{1,0:T(8,128)(2,1)} %param.5), channel_id=1, source_target_pairs={{1,2},{2,1},{5,6},{6,5},{9,10},{10,9},{13,14},{14,13},{17,18},{18,... | collective-permute-start | bytes 11010056 | tf_op jit(solution)/shard_map/ppermute | solution.py:430
  91.4 78.9 %collective-permute-start.9 = (bf16[512,3584]{1,0:T(8,128)(2,1)}, bf16[512,3584]{1,0:T(8,128)(2,1)}, u32[]{:S(2)}, u32[]{:S(2)}) collective-permute-start(bf16[512,3584]{1,0:T(8,128)(2,1)} %collective-permute-done.refs_4_.refs_1_), channel_id=1, source_target_pairs={{4,8},{5,9},{6,10},{7,11},{8,4},{9,5},{10,6},{11,7},{20,24},{21,25... | collective-permute-start | bytes 11010056 | tf_op jit(solution)/shard_map/ppermute | solution.py:430
  94.0 82.9 %collective-permute-start.8 = (bf16[512,3584]{1,0:T(8,128)(2,1)}, bf16[512,3584]{1,0:T(8,128)(2,1)}, u32[]{:S(2)}, u32[]{:S(2)}) collective-permute-start(bf16[512,3584]{1,0:T(8,128)(2,1)} %collective-permute-done.1.refs_6_.refs_1_), channel_id=1, source_target_pairs={{4,0},{5,1},{6,2},{7,3},{8,12},{9,13},{10,14},{11,15},{20,16},{21,... | collective-permute-start | bytes 11010056 | tf_op jit(solution)/shard_map/ppermute | solution.py:430
  135.2 3.9 %collective-permute-start.5 = (bf16[512,1792]{1,0:T(8,128)(2,1)S(1)}, bf16[512,1792]{1,0:T(8,128)(2,1)S(1)}, u32[]{:S(2)}, u32[]{:S(2)}) collective-permute-start(bf16[512,1792]{1,0:T(8,128)(2,1)S(1)} %get-tuple-element.139), channel_id=1, source_target_pairs={{0,1},{1,0},{2,3},{3,2},{4,5},{5,4},{6,7},{7,6},{8,9},{9,8},{10,11... | collective-permute-start | bytes 5505032 | tf_op jit(solution)/shard_map/ppermute | solution.py:430
  135.2 6.4 %collective-permute-start.6 = (bf16[512,1792]{1,0:T(8,128)(2,1)S(1)}, bf16[512,1792]{1,0:T(8,128)(2,1)S(1)}, u32[]{:S(2)}, u32[]{:S(2)}) collective-permute-start(bf16[512,1792]{1,0:T(8,128)(2,1)S(1)} %get-tuple-element.138), channel_id=1, source_target_pairs={{0,1},{1,0},{2,3},{3,2},{4,5},{5,4},{6,7},{7,6},{8,9},{9,8},{10,11... | collective-permute-start | bytes 5505032 | tf_op jit(solution)/shard_map/ppermute | solution.py:430
  176.8 16.9 %collective-permute-start.10 = (bf16[512,3584]{1,0:T(8,128)(2,1)}, bf16[512,3584]{1,0:T(8,128)(2,1)}, u32[]{:S(2)}, u32[]{:S(2)}) collective-permute-start(bf16[512,3584]{1,0:T(8,128)(2,1)} %collective-permute-done.8.refs_0_.refs_2_), channel_id=1, source_target_pairs={{0,1},{1,0},{2,3},{3,2},{4,5},{5,4},{6,7},{7,6},{8,9},{9,8},{10,11... | collective-permute-start | bytes 11010056 | tf_op jit(solution)/shard_map/ppermute | solution.py:430
  177.2 46.3 %collective-permute-start.13 = (bf16[512,3584]{1,0:T(8,128)(2,1)}, bf16[512,3584]{1,0:T(8,128)(2,1)}, u32[]{:S(2)}, u32[]{:S(2)}) collective-permute-start(bf16[512,3584]{1,0:T(8,128)(2,1)} %collective-permute-done.9.refs_3_.refs_1_.refs_2_), channel_id=1, source_target_pairs={{0,1},{1,0},{2,3},{3,2},{4,5},{5,4},{6,7},{7,6},{8,9},{9,8},{10,11... | collective-permute-start | bytes 11010056 | tf_op jit(solution)/shard_map/ppermute | solution.py:430
  180.2 43.3 %collective-permute-start.12 = (bf16[512,1792]{1,0:T(8,128)(2,1)}, bf16[512,1792]{1,0:T(8,128)(2,1)S(1)}, u32[]{:S(2)}, u32[]{:S(2)}) collective-permute-start(bf16[512,1792]{1,0:T(8,128)(2,1)} %constant_dynamic-slice_fusion), channel_id=1, source_target_pairs={{4,0},{5,1},{6,2},{7,3},{8,12},{9,13},{10,14},{11,15},{20,16},{21,... | collective-permute-start | bytes 5505032 | tf_op jit(solution)/shard_map/ppermute | solution.py:430
  181.7 25.4 %collective-permute-start.7 = (s16[1040,512]{1,0:T(8,128)(2,1)}, s16[1040,512]{1,0:T(8,128)(2,1)S(1)}, u32[]{:S(2)}, u32[]{:S(2)}) collective-permute-start(s16[1040,512]{1,0:T(8,128)(2,1)} %get-tuple-element.77), channel_id=1, source_target_pairs={{0,2},{1,3},{2,0},{3,1},{4,6},{5,7},{6,4},{7,5},{8,10},{9,11},{10,... | collective-permute-start | bytes 3194888 | tf_op jit(solution)/shard_map/ppermute | solution.py:430
  192.9 25.3 %collective-permute-start.11 = (s16[528,512]{1,0:T(8,128)(2,1)}, s16[528,512]{1,0:T(8,128)(2,1)S(1)}, u32[]{:S(2)}, u32[]{:S(2)}) collective-permute-start(s16[528,512]{1,0:T(8,128)(2,1)} %get-tuple-element.81), channel_id=1, source_target_pairs={{0,2},{1,3},{2,0},{3,1},{4,6},{5,7},{6,4},{7,5},{8,10},{9,11},{10,... | collective-permute-start | bytes 1622024 | tf_op jit(solution)/shard_map/ppermute | solution.py:430
  223.6 4.8 %collective-permute-start.14 = (bf16[512,1792]{1,0:T(8,128)(2,1)S(1)}, bf16[512,1792]{1,0:T(8,128)(2,1)}, u32[]{:S(2)}, u32[]{:S(2)}) collective-permute-start(bf16[512,1792]{1,0:T(8,128)(2,1)S(1)} %collective-permute-done.12.refs_2_.refs_0_), channel_id=1, source_target_pairs={{0,1},{1,0},{2,3},{3,2},{4,5},{5,4},{6,7},{7,6},{8,9},{9,8},{10,11... | collective-permute-start | bytes 5505032 | tf_op jit(solution)/shard_map/ppermute | solution.py:430
  224.8 45.6 %collective-permute-start.18 = (bf16[512,1792]{1,0:T(8,128)(2,1)}, bf16[512,1792]{1,0:T(8,128)(2,1)S(1)}, u32[]{:S(2)}, u32[]{:S(2)}) collective-permute-start(bf16[512,1792]{1,0:T(8,128)(2,1)} %constant_dynamic-slice_fusion.1), channel_id=1, source_target_pairs={{4,0},{5,1},{6,2},{7,3},{8,12},{9,13},{10,14},{11,15},{20,16},{21,... | collective-permute-start | bytes 5505032 | tf_op jit(solution)/shard_map/ppermute | solution.py:430
  237.6 23.2 %collective-permute-start.17 = (s16[464,1792]{1,0:T(8,128)(2,1)}, s16[464,1792]{1,0:T(8,128)(2,1)S(1)}, u32[]{:S(2)}, u32[]{:S(2)}) collective-permute-start(s16[464,1792]{1,0:T(8,128)(2,1)} %get-tuple-element.98), channel_id=1, source_target_pairs={{1,2},{2,1},{5,6},{6,5},{9,10},{10,9},{13,14},{14,13},{17,18},{18,... | collective-permute-start | bytes 4988936 | tf_op jit(solution)/shard_map/ppermute | solution.py:430
  240.4 9.9 %collective-permute-start.16 = (s16[1040,512]{1,0:T(8,128)(2,1)S(1)}, s16[1040,512]{1,0:T(8,128)(2,1)S(1)}, u32[]{:S(2)}, u32[]{:S(2)}) collective-permute-start(s16[1040,512]{1,0:T(8,128)(2,1)S(1)} %copy-done.15), channel_id=1, source_target_pairs={{1,0},{3,2},{5,4},{7,6},{8,9},{10,11},{12,13},{14,15},{17,16},{19,... | collective-permute-start | bytes 3194888 | tf_op jit(solution)/shard_map/ppermute | solution.py:430
  241.8 8.5 %collective-permute-start.15 = (s16[528,512]{1,0:T(8,128)(2,1)S(1)}, s16[528,512]{1,0:T(8,128)(2,1)S(1)}, u32[]{:S(2)}, u32[]{:S(2)}) collective-permute-start(s16[528,512]{1,0:T(8,128)(2,1)S(1)} %copy-done.17), channel_id=1, source_target_pairs={{0,1},{2,3},{4,5},{6,7},{9,8},{11,10},{13,12},{15,14},{16,17},{18,... | collective-permute-start | bytes 1622024 | tf_op jit(solution)/shard_map/ppermute | solution.py:430
  270.5 6.9 %collective-permute-start.19 = (bf16[512,1792]{1,0:T(8,128)(2,1)S(1)}, bf16[512,1792]{1,0:T(8,128)(2,1)S(1)}, u32[]{:S(2)}, u32[]{:S(2)}) collective-permute-start(bf16[512,1792]{1,0:T(8,128)(2,1)S(1)} %collective-permute-done.18.refs_0_.refs_1_), channel_id=1, source_target_pairs={{0,1},{1,0},{2,3},{3,2},{4,5},{5,4},{6,7},{7,6},{8,9},{9,8},{10,11... | collective-permute-start | bytes 5505032 | tf_op jit(solution)/shard_map/ppermute | solution.py:430
  276.6 18.0 %collective-permute-start.20 = (s16[528,512]{1,0:T(8,128)(2,1)S(1)}, s16[528,512]{1,0:T(8,128)(2,1)S(1)}, u32[]{:S(2)}, u32[]{:S(2)}) collective-permute-start(s16[528,512]{1,0:T(8,128)(2,1)S(1)} %get-tuple-element.113), channel_id=1, source_target_pairs={{0,2},{1,3},{2,0},{3,1},{4,6},{5,7},{6,4},{7,5},{8,10},{9,11},{10,... | collective-permute-start | bytes 1622024 | tf_op jit(solution)/shard_map/ppermute | solution.py:430
  283.9 15.7 %collective-permute-start.21 = (s16[464,896]{1,0:T(8,128)(2,1)}, s16[464,896]{1,0:T(8,128)(2,1)S(1)}, u32[]{:S(2)}, u32[]{:S(2)}) collective-permute-start(s16[464,896]{1,0:T(8,128)(2,1)} %get-tuple-element.115), channel_id=1, source_target_pairs={{1,2},{2,1},{5,6},{6,5},{9,10},{10,9},{13,14},{14,13},{17,18},{18,... | collective-permute-start | bytes 2494472 | tf_op jit(solution)/shard_map/ppermute | solution.py:430
  292.4 16.1 %collective-permute-start.23 = (s16[464,896]{1,0:T(8,128)(2,1)}, s16[464,896]{1,0:T(8,128)(2,1)S(1)}, u32[]{:S(2)}, u32[]{:S(2)}) collective-permute-start(s16[464,896]{1,0:T(8,128)(2,1)} %get-tuple-element.117), channel_id=1, source_target_pairs={{1,2},{2,1},{5,6},{6,5},{9,10},{10,9},{13,14},{14,13},{17,18},{18,... | collective-permute-start | bytes 2494472 | tf_op jit(solution)/shard_map/ppermute | solution.py:430
  295.6 8.1 %collective-permute-start.22 = (s16[528,512]{1,0:T(8,128)(2,1)S(1)}, s16[528,512]{1,0:T(8,128)(2,1)S(1)}, u32[]{:S(2)}, u32[]{:S(2)}) collective-permute-start(s16[528,512]{1,0:T(8,128)(2,1)S(1)} %get-tuple-element.121), channel_id=1, source_target_pairs={{0,1},{2,3},{4,5},{6,7},{9,8},{11,10},{13,12},{15,14},{16,17},{18,... | collective-permute-start | bytes 1622024 | tf_op jit(solution)/shard_map/ppermute | solution.py:430
  (21 other events, 137.0 us)

commit v10 on v9

--- a/solution.py
+++ b/solution.py
@@ -130,7 +130,7 @@
     return (grouped * step[:, None, :]).reshape(rows, wide)
 
 
-PARAMS = pltpu.CompilerParams(vmem_limit_bytes=48 * 2**20)
+PARAMS = pltpu.CompilerParams(vmem_limit_bytes=64 * 2**20)
 FREE = pl.CostEstimate(flops=1, bytes_accessed=1, transcendentals=0)
 KEPT, START, NEXT, HOME, AWAY, LAST, SAME_HALF, MIDDLE, CORE = range(9)
 
@@ -553,15 +553,14 @@
     [right] = right_terms(
         flags, strips_of(nears), [one(part) for part in nears], block, 4, before=right
     )
-    same_got, right = tie(same_got, right)
+    far_t, right = tie(far, right)
+    far_away, same_got, right = tie(columns(far_t, 2 * (1 - side), 2), same_got, right)
     same_total, same_out = add_up(flags, same_products, same_got)
     same_other = send(same_out, to_home)
     same_out, near_got = tie(same_out, near_got)
     near_total, near_out = add_up(flags, [near_product], near_got)
     near_other = send(near_out, to_away)
 
-    far_t, near_out = tie(far, near_out)
-    far_away, near_out = tie(columns(far_t, 2 * (1 - side), 2), near_out)
     right, near_out, end_home, far_o = tie(right, near_out, end_home, far_o)
     far_away, end_home = tie(far_away, end_home)
     end_away = send(far_away, outward)

time: 314 us -> 322 us (1.025)
  Pallas kernels: 113 us -> 138 us
  waiting for transfers between devices: 128 us -> 110 us
    pallas_call x18, Pallas kernels: 113 us -> 138 us  [kernel_call(): pl.pallas_call(body, grid_spec=pltpu.PrefetchScalarGridSpec(num_scalar_pr...]
    ppermute x24, waiting for transfers between devices: 128 us -> 110 us  [send(): return lax.ppermute(value, AXES, pairs)]
    unnamed x43 -> x5, local copies, waits for them, and re-layouts: 12.4 us -> 2.66 us
    dynamic_slice x7, local copies, waits for them, and re-layouts: 9.32 us -> 14.7 us  [strips_of(): lax.dynamic_slice_in_dim(part, strip_at - first, strip, 1)]
  transfers between devices with their start and end apart: 24 -> 24, of which waited for: 12 -> 8; matrix products, arithmetic and copies ran while one was open for 7% -> 10% of each run, Pallas kernels for 35% -> 42%
where the time goes in v10:
time: 322 us; the launch traced here: 317 us
  Pallas kernels  138 us (43%)
  waiting for transfers between devices  110 us (34%)
  starting transfers between devices  35 us (11%)
  local copies, waits for them, and re-layouts  25.4 us (8%)
  other arithmetic  7.32 us (2%)
    pallas_call x18, Pallas kernels, kernel_call(): pl.pallas_call(body, grid_spec=pltpu.PrefetchScalarGridSpec(num_scalar_pr...  138 us
    ppermute x24, waiting for transfers between devices, send(): return lax.ppermute(value, AXES, pairs)  110 us
    ppermute x24, starting transfers between devices, send(): return lax.ppermute(value, AXES, pairs)  35 us
    dynamic_slice x7, local copies, waits for them, and re-layouts, strips_of(): lax.dynamic_slice_in_dim(part, strip_at - first, strip, 1)  14.7 us
  transfers between devices with their start and end apart: 24, of which 8 were waited for; matrix products, arithmetic and copies ran while one was open for 10% of the time, Pallas kernels for 42%

profile of v10, /device:TPU:1, one launch (start us, length us, event | category | flops | bytes accessed | tf_op | source)
XLA Modules:
  0.0 317.4 jit_solution(972272707230473923)
XLA Ops:
  3.1 4.1 %collective-permute-start = (bf16[512,3584]{1,0:T(8,128)(2,1)}, bf16[512,3584]{1,0:T(8,128)(2,1)}, u32[]{:S(2)}, u32[]{:S(2)}) collective-permute-start(bf16[512,3584]{1,0:T(8,128)(2,1)} %param.5), channel_id=1, source_target_pairs={{0,4},{1,6},{2,5},{3,7},{4,0},{5,2},{6,1},{7,3},{8,12},{9,14},{10,... | collective-permute-start | bytes 11010056 | tf_op jit(solution)/shard_map/ppermute | solution.py:430
  7.2 79.7 %collective-permute-done.refs_4_.refs_1_ = bf16[512,3584]{1,0:T(8,128)(2,1)} collective-permute-done((bf16[512,3584]{1,0:T(8,128)(2,1)}, bf16[512,3584]{1,0:T(8,128)(2,1)}, u32[]{:S(2)}, u32[]{:S(2)}) %collective-permute-start) | collective-permute-done | bytes 3670048 | tf_op jit(solution)/shard_map/ppermute | solution.py:430
  87.5 3.8 %collective-permute-start.4 = (bf16[512,3584]{1,0:T(8,128)(2,1)}, bf16[512,3584]{1,0:T(8,128)(2,1)}, u32[]{:S(2)}, u32[]{:S(2)}) collective-permute-start(bf16[512,3584]{1,0:T(8,128)(2,1)} %param.5), channel_id=1, source_target_pairs={{1,2},{2,1},{5,6},{6,5},{9,10},{10,9},{13,14},{14,13},{17,18},{18,... | collective-permute-start | bytes 11010056 | tf_op jit(solution)/shard_map/ppermute | solution.py:430
  102.7 14.3 %shard_map.84.refs_4_ = f32[448,3584]{1,0:T(8,128)} custom-call(s32[9]{0:T(128)} %stack.39.flag_ref, bf16[512,448]{1,0:T(8,128)(2,1)} %get-tuple-element.145.refs_0_, bf16[512,448]{1,0:T(8,128)(2,1)} %constant_dynamic-slice_fusion.8.refs_1_, bf16[512,448]{1,0:T(8,128)(2,1)} %get-tuple-element.144.refs_2_, ...), custom_call_target="tpu_custom_call" | custom-call | flops 1 | bytes 1 | tf_op jit(solution)/shard_map/pallas_call | solution.py:149
  117.1 15.4 %collective-permute-done.4 = bf16[512,3584]{1,0:T(8,128)(2,1)} collective-permute-done((bf16[512,3584]{1,0:T(8,128)(2,1)}, bf16[512,3584]{1,0:T(8,128)(2,1)}, u32[]{:S(2)}, u32[]{:S(2)}) %collective-permute-start.4) | collective-permute-done | bytes 3670048 | tf_op jit(solution)/shard_map/ppermute | solution.py:430
  144.1 14.9 %shard_map.85 = (f32[1024,512]{1,0:T(8,128)}, f32[1024,512]{1,0:T(8,128)}, s16[1040,512]{1,0:T(8,128)(2,1)}) custom-call(s32[9]{0:T(128)} %stack.39.flag_ref, bf16[512,3584]{1,0:T(8,128)(2,1)} %copy-done, bf16[512,3584]{1,0:T(8,128)(2,1)} %constant_dynamic-update-slice_fusion.second_ref.refs_3_, bf16[512,3584]{1,0:T(8,128)(2,1)} %copy-done, ...), custom_call_target="tpu_custom_call" | custom-call | flops 1 | bytes 1 | tf_op jit(solution)/shard_map/pallas_call | solution.py:149
  161.2 11.3 %shard_map.86.refs_4_ = f32[448,3584]{1,0:T(8,128)} custom-call(s32[9]{0:T(128)} %stack.39.flag_ref, bf16[512,448]{1,0:T(8,128)(2,1)} %constant_dynamic-slice_fusion.5.refs_0_, bf16[512,448]{1,0:T(8,128)(2,1)} %constant_dynamic-slice_fusion.4.refs_1_, bf16[512,3584]{1,0:T(8,128)(2,1)} %copy-done, ...), custom_call_target="tpu_custom_call" | custom-call | flops 1 | bytes 1 | tf_op jit(solution)/shard_map/pallas_call | solution.py:149
  172.5 4.8 %collective-permute-done.7.refs_0_.refs_2_ = bf16[512,3584]{1,0:T(8,128)(2,1)} collective-permute-done((bf16[512,3584]{1,0:T(8,128)(2,1)}, bf16[512,3584]{1,0:T(8,128)(2,1)}, u32[]{:S(2)}, u32[]{:S(2)}) %collective-permute-start.7) | collective-permute-done | bytes 3670048 | tf_op jit(solution)/shard_map/ppermute | solution.py:430
  183.0 10.0 %shard_map.87 = (f32[1024,512]{1,0:T(8,128)}, s16[528,512]{1,0:T(8,128)(2,1)}) custom-call(s32[9]{0:T(128)} %stack.39.flag_ref, bf16[512,3584]{1,0:T(8,128)(2,1)} %copy-done, bf16[512,3584]{1,0:T(8,128)(2,1)} %constant_dynamic-update-slice_fusion.second_ref.refs_3_, bf16[512,3584]{1,0:T(8,128)(2,1)} %collective-permute-done.7.refs_0_.refs_2_, ...), custom_call_target="tpu_custom_call" | custom-call | flops 1 | bytes 1 | tf_op jit(solution)/shard_map/pallas_call | solution.py:149
  198.0 11.3 %shard_map.88.refs_6_.refs_5_ = f32[448,3584]{1,0:T(8,128)} custom-call(s32[9]{0:T(128)} %stack.39.flag_ref, bf16[512,448]{1,0:T(8,128)(2,1)} %constant_dynamic-slice_fusion.3.refs_0_, bf16[512,448]{1,0:T(8,128)(2,1)} %constant_dynamic-slice_fusion.2.refs_1_, bf16[512,3584]{1,0:T(8,128)(2,1)} %collective-permute-done.7.refs_0_.refs_2_, ...), custom_call_target="tpu_custom_call" | custom-call | flops 1 | bytes 1 | tf_op jit(solution)/shard_map/pallas_call | solution.py:149
  212.2 5.5 %shard_map.89 = (f32[1024,512]{1,0:T(8,128)}, s16[1040,512]{1,0:T(8,128)(2,1)}) custom-call(s32[9]{0:T(128)} %stack.39.flag_ref, f32[1024,512]{1,0:T(8,128)} %get-tuple-element.77.refs_0_, f32[1024,512]{1,0:T(8,128)} %get-tuple-element.78.refs_1_, s16[1040,512]{1,0:T(8,128)(2,1)} %collective-permute-done.10.refs_2_), custom_call_target="tpu_custom_call" | custom-call | flops 1 | bytes 1 | tf_op jit(solution)/shard_map/pallas_call | solution.py:149
  218.9 3.8 %shard_map.90 = (f32[512,512]{1,0:T(8,128)}, s16[528,512]{1,0:T(8,128)(2,1)}) custom-call(s32[9]{0:T(128)} %stack.39.flag_ref, f32[1024,512]{1,0:T(8,128)} %get-tuple-element.94.refs_0_, s16[528,512]{1,0:T(8,128)(2,1)} %collective-permute-done.11.refs_1_), custom_call_target="tpu_custom_call" | custom-call | flops 1 | bytes 1 | tf_op jit(solution)/shard_map/pallas_call | solution.py:149
  232.8 8.2 %shard_map.91 = (f32[448,1792]{1,0:T(8,128)}, s16[464,1792]{1,0:T(8,128)(2,1)}, bf16[2,448,512]{2,1,0:T(8,128)(2,1)}) custom-call(s32[9]{0:T(128)} %stack.39.flag_ref, bf16[512,448]{1,0:T(8,128)(2,1)} %dynamic-slice_select_fusion.1.refs_0_, bf16[512,448]{1,0:T(8,128)(2,1)} %dynamic-slice_select_fusion.refs_1_, ...), custom_call_target="tpu_custom_call" | custom-call | flops 1 | bytes 1 | tf_op jit(solution)/shard_map/pallas_call | solution.py:149
  248.9 6.9 %shard_map.92.refs_2_ = f32[1024,512]{1,0:T(8,128)} custom-call(s32[9]{0:T(128)} %stack.39.flag_ref, bf16[512,3584]{1,0:T(8,128)(2,1)} %copy-done, bf16[512,3584]{1,0:T(8,128)(2,1)} %constant_dynamic-update-slice_fusion.second_ref.refs_3_, bf16[512,1792]{1,0:T(8,128)(2,1)} %collective-permute-done.12.refs_2_.refs_0_, ...), custom_call_target="tpu_custom_call" | custom-call | flops 1 | bytes 1 | tf_op jit(solution)/shard_map/pallas_call | solution.py:149
  255.8 5.7 %shard_map.93 = (f32[512,2048]{1,0:T(8,128)}, f32[512,2048]{1,0:T(8,128)}) custom-call(s32[9]{0:T(128)} %stack.39.flag_ref, f32[1]{0:T(128)} %bitcast.7.scale_ref, f32[512,2048]{1,0:T(8,128)} %old_ref.3, f32[1024,512]{1,0:T(8,128)} %get-tuple-element.91.same_ref, s16[1040,512]{1,0:T(8,128)(2,1)} %collective-permute-done.16.same_other_ref, ...), custom_call_target="tpu_custom_call" | custom-call | flops 1 | bytes 1 | tf_op jit(solution)/shard_map/pallas_call | solution.py:149
  264.3 6.0 %shard_map.94 = (f32[448,3584]{1,0:T(8,128)}, f32[448,3584]{1,0:T(8,128)}) custom-call(s32[9]{0:T(128)} %stack.39.flag_ref, f32[1]{0:T(128)S(6)} %div.21.scale_ref, f32[448,3584]{1,0:T(8,128)} %bitcast.11, f32[448,1792]{1,0:T(8,128)} %get-tuple-element.105.value_ref, s16[464,1792]{1,0:T(8,128)(2,1)} %collective-permute-done.17.coded_ref), custom_call_target="tpu_custom_call" | custom-call | flops 1 | bytes 1 | tf_op jit(solution)/shard_map/pallas_call | solution.py:149
  270.3 8.2 %shard_map.95 = (f32[1024,512]{1,0:T(8,128)}, s16[528,512]{1,0:T(8,128)(2,1)}) custom-call(s32[9]{0:T(128)} %stack.39.flag_ref, bf16[512,3584]{1,0:T(8,128)(2,1)} %copy-done, bf16[512,3584]{1,0:T(8,128)(2,1)} %constant_dynamic-update-slice_fusion.second_ref.refs_3_, bf16[512,1792]{1,0:T(8,128)(2,1)} %collective-permute-done.18.refs_0_.refs_1_, ...), custom_call_target="tpu_custom_call" | custom-call | flops 1 | bytes 1 | tf_op jit(solution)/shard_map/pallas_call | solution.py:149
  279.1 6.1 %shard_map.96 = (f32[448,896]{1,0:T(8,128)}, s16[464,896]{1,0:T(8,128)(2,1)}) custom-call(s32[9]{0:T(128)} %stack.39.flag_ref, bf16[2,448,512]{2,1,0:T(8,128)(2,1)} %get-tuple-element.116.refs_0_, bf16[512,1792]{1,0:T(8,128)(2,1)} %collective-permute-done.18.refs_0_.refs_1_, bf16[512,3584]{1,0:T(8,128)(2,1)} %collective-permute-done.8.refs_3_.refs_1_.refs_2_, ...), custom_call_target="tpu_custom_call" | custom-call | flops 1 | bytes 1 | tf_op jit(solution)/shard_map/pallas_call | solution.py:149
  285.1 3.5 %collective-permute-start.21 = (s16[464,896]{1,0:T(8,128)(2,1)}, s16[464,896]{1,0:T(8,128)(2,1)}, u32[]{:S(2)}, u32[]{:S(2)}) collective-permute-start(s16[464,896]{1,0:T(8,128)(2,1)} %get-tuple-element.119), channel_id=1, source_target_pairs={{1,2},{2,1},{5,6},{6,5},{9,10},{10,9},{13,14},{14,13},{17,18},{18,... | collective-permute-start | bytes 2494472 | tf_op jit(solution)/shard_map/ppermute | solution.py:430
  288.6 6.1 %shard_map.97 = (f32[448,896]{1,0:T(8,128)}, s16[464,896]{1,0:T(8,128)(2,1)}) custom-call(s32[9]{0:T(128)} %stack.39.flag_ref, bf16[2,448,512]{2,1,0:T(8,128)(2,1)} %get-tuple-element.116.refs_0_, bf16[512,1792]{1,0:T(8,128)(2,1)} %collective-permute-done.18.refs_0_.refs_1_, bf16[512,3584]{1,0:T(8,128)(2,1)} %collective-permute-done.8.refs_3_.refs_1_.refs_2_, ...), custom_call_target="tpu_custom_call" | custom-call | flops 1 | bytes 1 | tf_op jit(solution)/shard_map/pallas_call | solution.py:149
  296.8 3.9 %shard_map.98 = (f32[512,512]{1,0:T(8,128)}, s16[528,512]{1,0:T(8,128)(2,1)}) custom-call(s32[9]{0:T(128)} %stack.39.flag_ref, f32[1024,512]{1,0:T(8,128)} %get-tuple-element.115.refs_0_, s16[528,512]{1,0:T(8,128)(2,1)} %collective-permute-done.20.refs_1_), custom_call_target="tpu_custom_call" | custom-call | flops 1 | bytes 1 | tf_op jit(solution)/shard_map/pallas_call | solution.py:149
  301.9 4.9 %shard_map.99 = (f32[448,3584]{1,0:T(8,128)}, f32[448,3584]{1,0:T(8,128)}) custom-call(s32[9]{0:T(128)} %stack.39.flag_ref, f32[1]{0:T(128)S(6)} %div.21.scale_ref, f32[448,3584]{1,0:T(8,128)} %bitcast.12, f32[448,896]{1,0:T(8,128)} %get-tuple-element.124.value_ref, ...), custom_call_target="tpu_custom_call", output_to_operand_aliasing={{0}: (5, {}), {1}: (6, {})} | custom-call | flops 1 | bytes 1 | tf_op jit(solution)/shard_map/pallas_call | solution.py:149
  306.8 5.7 %shard_map.100 = (f32[512,2048]{1,0:T(8,128)}, f32[512,2048]{1,0:T(8,128)}) custom-call(s32[9]{0:T(128)} %stack.39.flag_ref, f32[1]{0:T(128)} %bitcast.7.scale_ref, f32[512,2048]{1,0:T(8,128)} %old_ref.3, f32[1024,512]{1,0:T(8,128)} %get-tuple-element.91.same_ref, ...), custom_call_target="tpu_custom_call", output_to_operand_aliasing={{0}: (7, {}), {1}: (8, {})} | custom-call | flops 1 | bytes 1 | tf_op jit(solution)/shard_map/pallas_call | solution.py:149
  312.6 4.9 %shard_map.101 = (f32[448,3584]{1,0:T(8,128)}, f32[448,3584]{1,0:T(8,128)}) custom-call(s32[9]{0:T(128)} %stack.39.flag_ref, f32[1]{0:T(128)S(6)} %div.21.scale_ref, f32[448,3584]{1,0:T(8,128)} %bitcast.13, f32[448,896]{1,0:T(8,128)} %get-tuple-element.136.value_ref, ...), custom_call_target="tpu_custom_call", output_to_operand_aliasing={{0}: (5, {}), {1}: (6, {})} | custom-call | flops 1 | bytes 1 | tf_op jit(solution)/shard_map/pallas_call | solution.py:149
  (62 shorter events, 66.4 us)
Async XLA Ops:
  0.6 6.6 %collective-permute-start.1 = (bf16[512,3584]{1,0:T(8,128)(2,1)}, bf16[512,3584]{1,0:T(8,128)(2,1)}, u32[]{:S(2)}, u32[]{:S(2)}) collective-permute-start(bf16[512,3584]{1,0:T(8,128)(2,1)} %param.5), channel_id=1, source_target_pairs={{4,8},{5,10},{6,9},{7,11},{8,4},{9,6},{10,5},{11,7},{20,24},{21,26... | collective-permute-start | bytes 11010056 | tf_op jit(solution)/shard_map/ppermute | solution.py:430
  3.1 83.8 %collective-permute-start = (bf16[512,3584]{1,0:T(8,128)(2,1)}, bf16[512,3584]{1,0:T(8,128)(2,1)}, u32[]{:S(2)}, u32[]{:S(2)}) collective-permute-start(bf16[512,3584]{1,0:T(8,128)(2,1)} %param.5), channel_id=1, source_target_pairs={{0,4},{1,6},{2,5},{3,7},{4,0},{5,2},{6,1},{7,3},{8,12},{9,14},{10,... | collective-permute-start | bytes 11010056 | tf_op jit(solution)/shard_map/ppermute | solution.py:430
  86.9 11.5 %collective-permute-start.2 = (bf16[512,3584]{1,0:T(8,128)(2,1)}, bf16[512,3584]{1,0:T(8,128)(2,1)}, u32[]{:S(2)}, u32[]{:S(2)}) collective-permute-start(bf16[512,3584]{1,0:T(8,128)(2,1)} %collective-permute-done.refs_4_.refs_1_), channel_id=1, source_target_pairs={{0,1},{1,0},{2,3},{3,2},{4,5},{5,4},{6,7},{7,6},{8,9},{9,8},{10,11... | collective-permute-start | bytes 11010056 | tf_op jit(solution)/shard_map/ppermute | solution.py:430
  87.5 13.1 %collective-permute-start.3 = (bf16[512,3584]{1,0:T(8,128)(2,1)}, bf16[512,3584]{1,0:T(8,128)(2,1)}, u32[]{:S(2)}, u32[]{:S(2)}) collective-permute-start(bf16[512,3584]{1,0:T(8,128)(2,1)} %collective-permute-done.1.refs_6_.refs_1_), channel_id=1, source_target_pairs={{0,1},{1,0},{2,3},{3,2},{4,5},{5,4},{6,7},{7,6},{8,9},{9,8},{10,11... | collective-permute-start | bytes 11010056 | tf_op jit(solution)/shard_map/ppermute | solution.py:430
  87.5 44.9 %collective-permute-start.4 = (bf16[512,3584]{1,0:T(8,128)(2,1)}, bf16[512,3584]{1,0:T(8,128)(2,1)}, u32[]{:S(2)}, u32[]{:S(2)}) collective-permute-start(bf16[512,3584]{1,0:T(8,128)(2,1)} %param.5), channel_id=1, source_target_pairs={{1,2},{2,1},{5,6},{6,5},{9,10},{10,9},{13,14},{14,13},{17,18},{18,... | collective-permute-start | bytes 11010056 | tf_op jit(solution)/shard_map/ppermute | solution.py:430
  91.9 80.5 %collective-permute-start.8 = (bf16[512,3584]{1,0:T(8,128)(2,1)}, bf16[512,3584]{1,0:T(8,128)(2,1)}, u32[]{:S(2)}, u32[]{:S(2)}) collective-permute-start(bf16[512,3584]{1,0:T(8,128)(2,1)} %collective-permute-done.refs_4_.refs_1_), channel_id=1, source_target_pairs={{4,8},{5,9},{6,10},{7,11},{8,4},{9,5},{10,6},{11,7},{20,24},{21,25... | collective-permute-start | bytes 11010056 | tf_op jit(solution)/shard_map/ppermute | solution.py:430
  94.4 82.9 %collective-permute-start.7 = (bf16[512,3584]{1,0:T(8,128)(2,1)}, bf16[512,3584]{1,0:T(8,128)(2,1)}, u32[]{:S(2)}, u32[]{:S(2)}) collective-permute-start(bf16[512,3584]{1,0:T(8,128)(2,1)} %collective-permute-done.1.refs_6_.refs_1_), channel_id=1, source_target_pairs={{4,0},{5,1},{6,2},{7,3},{8,12},{9,13},{10,14},{11,15},{20,16},{21,... | collective-permute-start | bytes 11010056 | tf_op jit(solution)/shard_map/ppermute | solution.py:430
  135.1 3.9 %collective-permute-start.5 = (bf16[512,1792]{1,0:T(8,128)(2,1)S(1)}, bf16[512,1792]{1,0:T(8,128)(2,1)S(1)}, u32[]{:S(2)}, u32[]{:S(2)}) collective-permute-start(bf16[512,1792]{1,0:T(8,128)(2,1)S(1)} %get-tuple-element.143), channel_id=1, source_target_pairs={{0,1},{1,0},{2,3},{3,2},{4,5},{5,4},{6,7},{7,6},{8,9},{9,8},{10,11... | collective-permute-start | bytes 5505032 | tf_op jit(solution)/shard_map/ppermute | solution.py:430
  135.2 6.4 %collective-permute-start.6 = (bf16[512,1792]{1,0:T(8,128)(2,1)S(1)}, bf16[512,1792]{1,0:T(8,128)(2,1)S(1)}, u32[]{:S(2)}, u32[]{:S(2)}) collective-permute-start(bf16[512,1792]{1,0:T(8,128)(2,1)S(1)} %get-tuple-element.142), channel_id=1, source_target_pairs={{0,1},{1,0},{2,3},{3,2},{4,5},{5,4},{6,7},{7,6},{8,9},{9,8},{10,11... | collective-permute-start | bytes 5505032 | tf_op jit(solution)/shard_map/ppermute | solution.py:430
  177.3 16.4 %collective-permute-start.9 = (bf16[512,3584]{1,0:T(8,128)(2,1)}, bf16[512,3584]{1,0:T(8,128)(2,1)}, u32[]{:S(2)}, u32[]{:S(2)}) collective-permute-start(bf16[512,3584]{1,0:T(8,128)(2,1)} %collective-permute-done.7.refs_0_.refs_2_), channel_id=1, source_target_pairs={{0,1},{1,0},{2,3},{3,2},{4,5},{5,4},{6,7},{7,6},{8,9},{9,8},{10,11... | collective-permute-start | bytes 11010056 | tf_op jit(solution)/shard_map/ppermute | solution.py:430
  177.7 46.5 %collective-permute-start.13 = (bf16[512,3584]{1,0:T(8,128)(2,1)}, bf16[512,3584]{1,0:T(8,128)(2,1)}, u32[]{:S(2)}, u32[]{:S(2)}) collective-permute-start(bf16[512,3584]{1,0:T(8,128)(2,1)} %collective-permute-done.8.refs_3_.refs_1_.refs_2_), channel_id=1, source_target_pairs={{0,1},{1,0},{2,3},{3,2},{4,5},{5,4},{6,7},{7,6},{8,9},{9,8},{10,11... | collective-permute-start | bytes 11010056 | tf_op jit(solution)/shard_map/ppermute | solution.py:430
  180.7 43.4 %collective-permute-start.12 = (bf16[512,1792]{1,0:T(8,128)(2,1)}, bf16[512,1792]{1,0:T(8,128)(2,1)}, u32[]{:S(2)}, u32[]{:S(2)}) collective-permute-start(bf16[512,1792]{1,0:T(8,128)(2,1)} %constant_dynamic-slice_fusion), channel_id=1, source_target_pairs={{4,0},{5,1},{6,2},{7,3},{8,12},{9,13},{10,14},{11,15},{20,16},{21,... | collective-permute-start | bytes 5505032 | tf_op jit(solution)/shard_map/ppermute | solution.py:430
  182.2 30.0 %collective-permute-start.10 = (s16[1040,512]{1,0:T(8,128)(2,1)}, s16[1040,512]{1,0:T(8,128)(2,1)}, u32[]{:S(2)}, u32[]{:S(2)}) collective-permute-start(s16[1040,512]{1,0:T(8,128)(2,1)} %get-tuple-element.79), channel_id=1, source_target_pairs={{0,2},{1,3},{2,0},{3,1},{4,6},{5,7},{6,4},{7,5},{8,10},{9,11},{10,... | collective-permute-start | bytes 3194888 | tf_op jit(solution)/shard_map/ppermute | solution.py:430
  192.9 25.9 %collective-permute-start.11 = (s16[528,512]{1,0:T(8,128)(2,1)}, s16[528,512]{1,0:T(8,128)(2,1)}, u32[]{:S(2)}, u32[]{:S(2)}) collective-permute-start(s16[528,512]{1,0:T(8,128)(2,1)} %get-tuple-element.84), channel_id=1, source_target_pairs={{0,2},{1,3},{2,0},{3,1},{4,6},{5,7},{6,4},{7,5},{8,10},{9,11},{10,... | collective-permute-start | bytes 1622024 | tf_op jit(solution)/shard_map/ppermute | solution.py:430
  224.1 5.1 %collective-permute-start.14 = (bf16[512,1792]{1,0:T(8,128)(2,1)}, bf16[512,1792]{1,0:T(8,128)(2,1)S(1)}, u32[]{:S(2)}, u32[]{:S(2)}) collective-permute-start(bf16[512,1792]{1,0:T(8,128)(2,1)} %collective-permute-done.12.refs_2_.refs_0_), channel_id=1, source_target_pairs={{0,1},{1,0},{2,3},{3,2},{4,5},{5,4},{6,7},{7,6},{8,9},{9,8},{10,11... | collective-permute-start | bytes 5505032 | tf_op jit(solution)/shard_map/ppermute | solution.py:430
  225.4 44.9 %collective-permute-start.18 = (bf16[512,1792]{1,0:T(8,128)(2,1)}, bf16[512,1792]{1,0:T(8,128)(2,1)}, u32[]{:S(2)}, u32[]{:S(2)}) collective-permute-start(bf16[512,1792]{1,0:T(8,128)(2,1)} %constant_dynamic-slice_fusion.1), channel_id=1, source_target_pairs={{4,0},{5,1},{6,2},{7,3},{8,12},{9,13},{10,14},{11,15},{20,16},{21,... | collective-permute-start | bytes 5505032 | tf_op jit(solution)/shard_map/ppermute | solution.py:430
  241.0 23.3 %collective-permute-start.17 = (s16[464,1792]{1,0:T(8,128)(2,1)}, s16[464,1792]{1,0:T(8,128)(2,1)}, u32[]{:S(2)}, u32[]{:S(2)}) collective-permute-start(s16[464,1792]{1,0:T(8,128)(2,1)} %get-tuple-element.102), channel_id=1, source_target_pairs={{1,2},{2,1},{5,6},{6,5},{9,10},{10,9},{13,14},{14,13},{17,18},{18,... | collective-permute-start | bytes 4988936 | tf_op jit(solution)/shard_map/ppermute | solution.py:430
  243.7 12.1 %collective-permute-start.16 = (s16[1040,512]{1,0:T(8,128)(2,1)}, s16[1040,512]{1,0:T(8,128)(2,1)}, u32[]{:S(2)}, u32[]{:S(2)}) collective-permute-start(s16[1040,512]{1,0:T(8,128)(2,1)} %get-tuple-element.95), channel_id=1, source_target_pairs={{1,0},{3,2},{5,4},{7,6},{8,9},{10,11},{12,13},{14,15},{17,16},{19,... | collective-permute-start | bytes 3194888 | tf_op jit(solution)/shard_map/ppermute | solution.py:430
  245.9 9.8 %collective-permute-start.15 = (s16[528,512]{1,0:T(8,128)(2,1)}, s16[528,512]{1,0:T(8,128)(2,1)}, u32[]{:S(2)}, u32[]{:S(2)}) collective-permute-start(s16[528,512]{1,0:T(8,128)(2,1)} %get-tuple-element.97), channel_id=1, source_target_pairs={{0,1},{2,3},{4,5},{6,7},{9,8},{11,10},{13,12},{15,14},{16,17},{18,... | collective-permute-start | bytes 1622024 | tf_op jit(solution)/shard_map/ppermute | solution.py:430
  270.3 8.8 %collective-permute-start.19 = (bf16[512,1792]{1,0:T(8,128)(2,1)}, bf16[512,1792]{1,0:T(8,128)(2,1)}, u32[]{:S(2)}, u32[]{:S(2)}) collective-permute-start(bf16[512,1792]{1,0:T(8,128)(2,1)} %collective-permute-done.18.refs_0_.refs_1_), channel_id=1, source_target_pairs={{0,1},{1,0},{2,3},{3,2},{4,5},{5,4},{6,7},{7,6},{8,9},{9,8},{10,11... | collective-permute-start | bytes 5505032 | tf_op jit(solution)/shard_map/ppermute | solution.py:430
  278.5 18.2 %collective-permute-start.20 = (s16[528,512]{1,0:T(8,128)(2,1)}, s16[528,512]{1,0:T(8,128)(2,1)}, u32[]{:S(2)}, u32[]{:S(2)}) collective-permute-start(s16[528,512]{1,0:T(8,128)(2,1)} %get-tuple-element.117), channel_id=1, source_target_pairs={{0,2},{1,3},{2,0},{3,1},{4,6},{5,7},{6,4},{7,5},{8,10},{9,11},{10,... | collective-permute-start | bytes 1622024 | tf_op jit(solution)/shard_map/ppermute | solution.py:430
  285.1 16.8 %collective-permute-start.21 = (s16[464,896]{1,0:T(8,128)(2,1)}, s16[464,896]{1,0:T(8,128)(2,1)}, u32[]{:S(2)}, u32[]{:S(2)}) collective-permute-start(s16[464,896]{1,0:T(8,128)(2,1)} %get-tuple-element.119), channel_id=1, source_target_pairs={{1,2},{2,1},{5,6},{6,5},{9,10},{10,9},{13,14},{14,13},{17,18},{18,... | collective-permute-start | bytes 2494472 | tf_op jit(solution)/shard_map/ppermute | solution.py:430
  294.7 17.9 %collective-permute-start.23 = (s16[464,896]{1,0:T(8,128)(2,1)}, s16[464,896]{1,0:T(8,128)(2,1)}, u32[]{:S(2)}, u32[]{:S(2)}) collective-permute-start(s16[464,896]{1,0:T(8,128)(2,1)} %get-tuple-element.121), channel_id=1, source_target_pairs={{1,2},{2,1},{5,6},{6,5},{9,10},{10,9},{13,14},{14,13},{17,18},{18,... | collective-permute-start | bytes 2494472 | tf_op jit(solution)/shard_map/ppermute | solution.py:430
  300.6 6.2 %collective-permute-start.22 = (s16[528,512]{1,0:T(8,128)(2,1)}, s16[528,512]{1,0:T(8,128)(2,1)}, u32[]{:S(2)}, u32[]{:S(2)}) collective-permute-start(s16[528,512]{1,0:T(8,128)(2,1)} %get-tuple-element.125), channel_id=1, source_target_pairs={{0,1},{2,3},{4,5},{6,7},{9,8},{11,10},{13,12},{15,14},{16,17},{18,... | collective-permute-start | bytes 1622024 | tf_op jit(solution)/shard_map/ppermute | solution.py:430
  (2 other events, 9.4 us)
